TPU v7x, 256 devices: a whole 4x4x8 slice. The times are simulated.
256 devices in a mesh: dp: 2 (over x_lo), row: 32 (over z, y), col: 4 (over x_hi, core).
Axes of the slice: x: 4 (x_hi: 2, x_lo: 2; x = x_hi * 2 + x_lo), y: 4, z: 8, core: 2. Of those that a mesh axis runs over, the one named last changes fastest.
Arguments:
- layer_input: bfloat16 [2048, 6144], P(('dp', 'row'), 'col'), may hold values from -0.8984375 to 0.8984375
- grad_output: bfloat16 [2048, 6144], P(('dp', 'row'), 'col'), may hold values from -3 to 3
- gate_saved: bfloat16 [2048, 16384], P(('dp', 'col'), 'row'), may hold values from -9 to 9
- up_saved: bfloat16 [2048, 16384], P(('dp', 'col'), 'row'), may hold values from -0.8984375 to 0.8984375
- w_gate: bfloat16 [6144, 16384], P('col', 'row'), may hold values from -0.078125 to 0.078125
- w_up: bfloat16 [6144, 16384], P('col', 'row'), may hold values from -0.078125 to 0.078125
- w_down: bfloat16 [16384, 6144], P('row', 'col'), may hold values from -0.046875 to 0.046875
Outputs:
- grad_input: bfloat16 [2048, 6144], P(('dp', 'row'), 'col')
- grad_gate: bfloat16 [6144, 16384], P('col', 'row')
- grad_up: bfloat16 [6144, 16384], P('col', 'row')
- grad_down: bfloat16 [16384, 6144], P('row', 'col')
All inputs are finite; a program needn't handle non-finite values.
Results may differ from a plain program's by a relative error of at most 0.022.
Values may be sent and summed in bfloat16 or wider, within the bound.
No kernel may reach another device: no remote copies, remote signals or barrier semaphores. Data moves between devices by JAX's collectives and lax.ppermute only.
A program may use at most 64 MiB of HBM per device.

v0:
```python
import functools

import jax
import jax.numpy as jnp
from jax import lax
from jax.experimental import pallas as pl
from jax.experimental.pallas import tpu as pltpu
from jax.sharding import Mesh, PartitionSpec as P

F32, BF16 = jnp.float32, jnp.bfloat16
NZ, NY = 8, 4
VMEM = pl.BlockSpec(memory_space=pltpu.VMEM)
SMEM = pl.BlockSpec(memory_space=pltpu.SMEM)


def dot(left, right, left_dim, right_dim):
    dims = (((left_dim,), (right_dim,)), ((), ()))
    return lax.dot_general(left, right, dims, preferred_element_type=F32)


def from_ahead(x, axis, n, k):
    return lax.ppermute(x, axis, [((d + k) % n, d) for d in range(n)])


def swap(x, axis):
    return lax.ppermute(x, axis, [(0, 1), (1, 0)])


def params(mib):
    return pltpu.CompilerParams(vmem_limit_bytes=mib << 20)


def arrange_kernel(n, slot, place, *refs):
    for k in range(n):
        refs[n][(place[slot] + k) % n] = refs[k][...]


def arrange(place, slot, parts):
    n = len(parts)
    rows, cols = parts[0].shape
    out = pl.pallas_call(
        functools.partial(arrange_kernel, n, slot),
        out_shape=jax.ShapeDtypeStruct((n, rows, cols), BF16),
        in_specs=[SMEM] + [VMEM] * n,
        out_specs=VMEM,
        compiler_params=params(16),
    )(place, *parts)
    return out.reshape(n * rows, cols)


def hidden_grad_kernel(place, go, w_down, mine, send):
    step = pl.program_id(0)
    half, side = step // 2, step % 2
    part = dot(go[...], w_down[...], 1, 1)

    @pl.when(side == place[3])
    def _():
        mine[half] = part

    @pl.when(side != place[3])
    def _():
        send[half] = part.astype(BF16)


def hidden_grad(place, go, w_down):
    whole = pl.BlockSpec((2, 256, 512), lambda i: (0, 0, 0))
    return pl.pallas_call(
        hidden_grad_kernel,
        grid=(4,),
        out_shape=(
            jax.ShapeDtypeStruct((2, 256, 512), F32),
            jax.ShapeDtypeStruct((2, 256, 512), BF16),
        ),
        in_specs=[
            SMEM,
            pl.BlockSpec((256, 1536), lambda i: (i, 0)),
            pl.BlockSpec((512, 1536), lambda i: (0, 0)),
        ],
        out_specs=(whole, whole),
        compiler_params=params(32),
        cost_estimate=pl.CostEstimate(flops=2 * 1024 * 1536 * 512, bytes_accessed=6 << 20, transcendentals=0),
    )(place, go, w_down)


def input_grad_kernel(place, gg, gg_other, gu, gu_other, w_gate, w_up, out):
    step = pl.program_id(0)
    half, side = step // 2, step % 2

    def emit(gate_ref, up_ref):
        total = dot(gate_ref[half], w_gate[...], 1, 1) + dot(up_ref[half], w_up[...], 1, 1)
        out[...] = total.astype(BF16)

    @pl.when(side == place[3])
    def _():
        emit(gg, gu)

    @pl.when(side != place[3])
    def _():
        emit(gg_other, gu_other)


def input_grad(place, gg, gg_other, gu, gu_other, w_gate, w_up):
    whole = pl.BlockSpec((2, 256, 512), lambda i: (0, 0, 0))
    weight = pl.BlockSpec((1536, 512), lambda i: (0, 0))
    return pl.pallas_call(
        input_grad_kernel,
        grid=(4,),
        out_shape=jax.ShapeDtypeStruct((1024, 1536), BF16),
        in_specs=[SMEM] + [whole] * 4 + [weight] * 2,
        out_specs=pl.BlockSpec((256, 1536), lambda i: (i, 0)),
        compiler_params=params(40),
        cost_estimate=pl.CostEstimate(flops=4 * 1024 * 1536 * 512, bytes_accessed=8 << 20, transcendentals=0),
    )(place, gg, gg_other, gu, gu_other, w_gate, w_up)


def fill_natural(place, own, other, rows, col):
    for half in range(2):
        base = half * 512
        start = pl.multiple_of(base + place[3] * 256, 256)
        rows[pl.ds(start, 256), col:col + 512] = own[half]
        start = pl.multiple_of(base + (1 - place[3]) * 256, 256)
        rows[pl.ds(start, 256), col:col + 512] = other[half]


def down_kernel(place, hidden, hidden_other, go, out, rows):
    @pl.when(pl.program_id(0) == 0)
    def _():
        fill_natural(place, hidden, hidden_other, rows, 0)

    out[...] = dot(rows[...], go[...], 0, 0).astype(BF16)


def down_grad(place, hidden, hidden_other, go):
    whole = pl.BlockSpec((2, 256, 512), lambda i: (0, 0, 0))
    return pl.pallas_call(
        down_kernel,
        grid=(3,),
        out_shape=jax.ShapeDtypeStruct((512, 1536), BF16),
        in_specs=[SMEM, whole, whole, pl.BlockSpec((1024, 512), lambda i: (0, i))],
        out_specs=pl.BlockSpec((512, 512), lambda i: (0, i)),
        scratch_shapes=[pltpu.VMEM((1024, 512), BF16)],
        compiler_params=params(32),
        cost_estimate=pl.CostEstimate(flops=2 * 1024 * 1536 * 512, bytes_accessed=6 << 20, transcendentals=0),
    )(place, hidden, hidden_other, go)


def fill_rolled(place, own, other, rows, col):
    for half in range(2):
        for pair in range(2):
            for y in range(NY):
                k = (y - place[1] + NY) % NY
                lines = pl.ds(pair * 128 + y * 32, 32)
                z_own = 4 * half + 2 * place[3] + pair
                rows[k, z_own, :, col:col + 512] = own[half, lines, :]
                z_other = 4 * half + 2 * (1 - place[3]) + pair
                rows[k, z_other, :, col:col + 512] = other[half, lines, :]


def weight_kernel(place, own, p0, p1, p2, p3, gg, gg_o, gu, gu_o, fgg, fgg_o, fgu, fgu_o, d_gate, d_up, near, far):
    @pl.when(pl.program_id(0) == 0)
    def _():
        fill_natural(place, gg, gg_o, near, 0)
        fill_natural(place, gu, gu_o, near, 512)
        fill_rolled(place, fgg, fgg_o, far, 0)
        fill_rolled(place, fgu, fgu_o, far, 512)

    total = dot(own[...], near[...], 0, 0)
    for k, piece in enumerate((p0, p1, p2, p3)):
        total = total + dot(piece[...], far[k].reshape(256, 1024), 0, 0)
    d_gate[...] = total[:, :512].astype(BF16)
    d_up[...] = total[:, 512:].astype(BF16)


def weight_grads(place, own, pieces, grads):
    whole = pl.BlockSpec((2, 256, 512), lambda i: (0, 0, 0))
    piece = pl.BlockSpec((256, 256), lambda i: (0, i))
    tile = pl.BlockSpec((256, 512), lambda i: (i, 0))
    shape = jax.ShapeDtypeStruct((1536, 512), BF16)
    return pl.pallas_call(
        weight_kernel,
        grid=(6,),
        out_shape=(shape, shape),
        in_specs=[SMEM, pl.BlockSpec((1024, 256), lambda i: (0, i))] + [piece] * 4 + [whole] * 8,
        out_specs=(tile, tile),
        scratch_shapes=[pltpu.VMEM((1024, 1024), BF16), pltpu.VMEM((NY, NZ, 32, 1024), BF16)],
        compiler_params=params(40),
        cost_estimate=pl.CostEstimate(flops=8 * 1024 * 1536 * 512, bytes_accessed=16 << 20, transcendentals=0),
    )(place, own, *pieces, *grads)


def ring(x, axis, n):
    ahead, behind = [], []
    up, down = x, x
    for step in range(1, n // 2 + 1):
        up = from_ahead(up, axis, n, 1)
        ahead.append(up)
        if step < n // 2:
            down = from_ahead(down, axis, n, n - 1)
            behind.append(down)
    return [x] + ahead + behind[::-1]


def ordered(mine, other, index):
    low = jnp.where(index == 0, mine, other)
    high = jnp.where(index == 0, other, mine)
    return jnp.stack([low, high], axis=0)


def body(layer_input, grad_output, gate_saved, up_saved, w_gate, w_up, w_down):
    place = jnp.stack([lax.axis_index(name) for name in ("z", "y", "xh", "core")]).astype(jnp.int32)
    xh = place[2]

    go_y = arrange(place, 1, [grad_output] + [from_ahead(grad_output, "y", NY, k) for k in (1, 2, 3)])
    go = lax.all_gather(go_y, "z", axis=0, tiled=True)

    gate = ordered(gate_saved, swap(gate_saved, "xh"), xh)
    up = ordered(up_saved, swap(up_saved, "xh"), xh)
    gate_val, up_val = gate.astype(F32), up.astype(F32)
    hidden = (gate_val * jax.nn.sigmoid(gate_val) * up_val).astype(BF16)
    hidden_other = swap(hidden, "core")
    partner = swap(layer_input, "dp")
    partner_z = arrange(place, 0, ring(partner, "z", NZ))
    own_y = arrange(place, 1, [layer_input] + [from_ahead(layer_input, "y", NY, k) for k in (1, 2, 3)])

    go, gate, up, hidden, hidden_other, partner_z, own_y = lax.optimization_barrier(
        (go, gate, up, hidden, hidden_other, partner_z, own_y)
    )

    own_input = lax.all_gather(own_y, "z", axis=0, tiled=True)
    mine, send = hidden_grad(place, go, w_down)
    chip = mine + swap(send, "core").astype(F32)
    chip_far = swap(chip.astype(BF16), "xh")
    part_down = down_grad(place, hidden, hidden_other, go)
    piece1 = from_ahead(partner_z, "y", NY, 1)
    piece3 = from_ahead(partner_z, "y", NY, 3)

    chip, chip_far, part_down, piece1, piece3 = lax.optimization_barrier(
        (chip, chip_far, part_down, piece1, piece3)
    )

    grad_hidden = chip + chip_far.astype(F32)
    gate_val, up_val = gate.astype(F32), up.astype(F32)
    sigma = jax.nn.sigmoid(gate_val)
    gg = (grad_hidden * up_val * sigma * (1.0 + gate_val * (1.0 - sigma))).astype(BF16)
    gu = (grad_hidden * gate_val * sigma).astype(BF16)
    gg_other, gu_other = swap(gg, "core"), swap(gu, "core")
    gg_far, gu_far = swap(gg, "dp"), swap(gu, "dp")
    partial_in = input_grad(place, gg, gg_other, gu, gu_other, w_gate, w_up)
    in_z = lax.psum_scatter(partial_in, "z", scatter_dimension=0, tiled=True).reshape(NY, 32, 1536)

    piece2 = from_ahead(partner_z, "y", NY, 2)
    gg_far, gu_far, part_down, piece2 = lax.optimization_barrier((gg_far, gu_far, part_down, piece2))
    down_far = swap(part_down, "dp")
    grads = (gg, gg_other, gu, gu_other, gg_far, swap(gg_far, "core"), gu_far, swap(gu_far, "core"))
    grad_gate, grad_up = weight_grads(place, own_input, (partner_z, piece1, piece2, piece3), grads)
    grad_down = (part_down.astype(F32) + down_far.astype(F32)).astype(BF16)
    in_z, grad_gate, grad_up, grad_down = lax.optimization_barrier((in_z, grad_gate, grad_up, grad_down))

    y = place[1]
    total = lax.dynamic_index_in_dim(in_z, y, 0, keepdims=False).astype(F32)
    for k in range(1, NY):
        slab = lax.dynamic_index_in_dim(in_z, (y + k) % NY, 0, keepdims=False)
        total = total + from_ahead(slab, "y", NY, NY - k).astype(F32)
    return total.astype(BF16), grad_gate, grad_up, grad_down


def solution(mesh):
    fine = Mesh(mesh.devices.reshape(2, NZ, NY, 2, 2), ("dp", "z", "y", "xh", "core"))
    tokens, col, row = ("dp", "z", "y"), ("xh", "core"), ("z", "y")
    in_specs = (
        P(tokens, col),
        P(tokens, col),
        P(("dp",) + col, row),
        P(("dp",) + col, row),
        P(col, row),
        P(col, row),
        P(row, col),
    )
    out_specs = (P(tokens, col), P(col, row), P(col, row), P(row, col))
    return jax.shard_map(body, mesh=fine, in_specs=in_specs, out_specs=out_specs, check_vma=False)
```

profile of v0, /device:TPU:2, one launch (start us, length us, event | category | flops | bytes accessed | tf_op | source)
XLA Modules:
  0.0 219.1 jit_solution(4600743820956366490)
XLA Ops:
  7.2 3.1 %collective-permute-start = (bf16[32,1536]{1,0:T(8,128)(2,1)}, bf16[32,1536]{1,0:T(8,128)(2,1)S(1)}, u32[]{:S(2)}, u32[]{:S(2)}) collective-permute-start(bf16[32,1536]{1,0:T(8,128)(2,1)} %refs_0_.2), channel_id=1, source_target_pairs={{4,0},{8,4},{12,8},{0,12},{5,1},{9,5},{13,9},{1,13},{6,2},{10,6},{... | collective-permute-start | bytes 294920 | tf_op jit(solution)/shard_map/ppermute | solution.py:22
  12.0 2.8 %collective-permute-done.refs_1_ = bf16[32,1536]{1,0:T(8,128)(2,1)S(1)} collective-permute-done((bf16[32,1536]{1,0:T(8,128)(2,1)}, bf16[32,1536]{1,0:T(8,128)(2,1)S(1)}, u32[]{:S(2)}, u32[]{:S(2)}) %collective-permute-start) | collective-permute-done | bytes 98336 | tf_op jit(solution)/shard_map/ppermute | solution.py:22
  14.8 2.6 %collective-permute-done.1.refs_2_ = bf16[32,1536]{1,0:T(8,128)(2,1)S(1)} collective-permute-done((bf16[32,1536]{1,0:T(8,128)(2,1)}, bf16[32,1536]{1,0:T(8,128)(2,1)S(1)}, u32[]{:S(2)}, u32[]{:S(2)}) %collective-permute-start.1) | collective-permute-done | bytes 98336 | tf_op jit(solution)/shard_map/ppermute | solution.py:22
  19.3 1.3 shard_map.102
  20.7 2.2 %collective-permute-start.4 = (bf16[256,512]{1,0:T(8,128)(2,1)}, bf16[256,512]{1,0:T(8,128)(2,1)S(1)}, u32[]{:S(2)}, u32[]{:S(2)}) collective-permute-start(bf16[256,512]{1,0:T(8,128)(2,1)} %param.10), channel_id=1, source_target_pairs={{0,2},{2,0},{1,3},{3,1},{4,6},{6,4},{5,7},{7,5},{8,10},{10,8},{9,1... | collective-permute-start | bytes 786440 | tf_op jit(solution)/shard_map/ppermute | solution.py:26
  22.9 1.4 collective-permute-start.3
  24.8 6.9 %collective-permute-done.4 = bf16[256,512]{1,0:T(8,128)(2,1)S(1)} collective-permute-done((bf16[256,512]{1,0:T(8,128)(2,1)}, bf16[256,512]{1,0:T(8,128)(2,1)S(1)}, u32[]{:S(2)}, u32[]{:S(2)}) %collective-permute-start.4) | collective-permute-done | bytes 262176 | tf_op jit(solution)/shard_map/ppermute | solution.py:26
  32.7 4.1 %collective-permute-done.3 = bf16[256,512]{1,0:T(8,128)(2,1)S(1)} collective-permute-done((bf16[256,512]{1,0:T(8,128)(2,1)}, bf16[256,512]{1,0:T(8,128)(2,1)S(1)}, u32[]{:S(2)}, u32[]{:S(2)}) %collective-permute-start.3) | collective-permute-done | bytes 262176 | tf_op jit(solution)/shard_map/ppermute | solution.py:26
  37.9 5.9 %collective-permute-start.7 = (bf16[32,1536]{1,0:T(8,128)(2,1)S(1)}, bf16[32,1536]{1,0:T(8,128)(2,1)S(1)}, u32[]{:S(2)}, u32[]{:S(2)}) collective-permute-start(bf16[32,1536]{1,0:T(8,128)(2,1)S(1)} %collective-permute-done.6.refs_0_), channel_id=1, source_target_pairs={{16,0},{32,16},{48,32},{64,48},{80,64},{96,80},{112,96},{0,112},{1... | collective-permute-start | bytes 294920 | tf_op jit(solution)/shard_map/ppermute | solution.py:22
  43.8 4.8 %collective-permute-done.7.refs_1_ = bf16[32,1536]{1,0:T(8,128)(2,1)S(1)} collective-permute-done((bf16[32,1536]{1,0:T(8,128)(2,1)S(1)}, bf16[32,1536]{1,0:T(8,128)(2,1)S(1)}, u32[]{:S(2)}, u32[]{:S(2)}) %collective-permute-start.7) | collective-permute-done | bytes 98336 | tf_op jit(solution)/shard_map/ppermute | solution.py:22
  48.6 3.7 %collective-permute-start.8 = (bf16[32,1536]{1,0:T(8,128)(2,1)S(1)}, bf16[32,1536]{1,0:T(8,128)(2,1)S(1)}, u32[]{:S(2)}, u32[]{:S(2)}) collective-permute-start(bf16[32,1536]{1,0:T(8,128)(2,1)S(1)} %collective-permute-done.7.refs_1_), channel_id=1, source_target_pairs={{16,0},{32,16},{48,32},{64,48},{80,64},{96,80},{112,96},{0,112},{1... | collective-permute-start | bytes 294920 | tf_op jit(solution)/shard_map/ppermute | solution.py:22
  52.9 4.0 %collective-permute-done.8.refs_2_ = bf16[32,1536]{1,0:T(8,128)(2,1)S(1)} collective-permute-done((bf16[32,1536]{1,0:T(8,128)(2,1)S(1)}, bf16[32,1536]{1,0:T(8,128)(2,1)S(1)}, u32[]{:S(2)}, u32[]{:S(2)}) %collective-permute-start.8) | collective-permute-done | bytes 98336 | tf_op jit(solution)/shard_map/ppermute | solution.py:22
  56.9 3.7 %collective-permute-start.9 = (bf16[32,1536]{1,0:T(8,128)(2,1)S(1)}, bf16[32,1536]{1,0:T(8,128)(2,1)S(1)}, u32[]{:S(2)}, u32[]{:S(2)}) collective-permute-start(bf16[32,1536]{1,0:T(8,128)(2,1)S(1)} %collective-permute-done.8.refs_2_), channel_id=1, source_target_pairs={{16,0},{32,16},{48,32},{64,48},{80,64},{96,80},{112,96},{0,112},{1... | collective-permute-start | bytes 294920 | tf_op jit(solution)/shard_map/ppermute | solution.py:22
  60.6 1.3 shard_map.104
  61.9 3.0 %collective-permute-done.9.refs_3_ = bf16[32,1536]{1,0:T(8,128)(2,1)S(1)} collective-permute-done((bf16[32,1536]{1,0:T(8,128)(2,1)S(1)}, bf16[32,1536]{1,0:T(8,128)(2,1)S(1)}, u32[]{:S(2)}, u32[]{:S(2)}) %collective-permute-start.9) | collective-permute-done | bytes 98336 | tf_op jit(solution)/shard_map/ppermute | solution.py:22
  64.9 3.7 %collective-permute-start.10 = (bf16[32,1536]{1,0:T(8,128)(2,1)S(1)}, bf16[32,1536]{1,0:T(8,128)(2,1)S(1)}, u32[]{:S(2)}, u32[]{:S(2)}) collective-permute-start(bf16[32,1536]{1,0:T(8,128)(2,1)S(1)} %collective-permute-done.9.refs_3_), channel_id=1, source_target_pairs={{16,0},{32,16},{48,32},{64,48},{80,64},{96,80},{112,96},{0,112},{1... | collective-permute-start | bytes 294920 | tf_op jit(solution)/shard_map/ppermute | solution.py:22
  68.6 1.1 pad_maximum_fusion
  69.8 2.2 %collective-permute-done.10.refs_4_ = bf16[32,1536]{1,0:T(8,128)(2,1)S(1)} collective-permute-done((bf16[32,1536]{1,0:T(8,128)(2,1)S(1)}, bf16[32,1536]{1,0:T(8,128)(2,1)S(1)}, u32[]{:S(2)}, u32[]{:S(2)}) %collective-permute-start.10) | collective-permute-done | bytes 98336 | tf_op jit(solution)/shard_map/ppermute | solution.py:22
  73.7 1.9 copy-done.3
  75.6 1.4 copy-done.4
  77.0 3.1 %shard_map.105 = (f32[2,256,512]{2,1,0:T(8,128)S(1)}, bf16[2,256,512]{2,1,0:T(8,128)(2,1)S(1)}) custom-call(s32[4]{0:T(128)S(1)} %pad_add_fusion.place, bf16[1024,1536]{1,0:T(8,128)(2,1)S(1)} %copy-done.3, bf16[512,1536]{1,0:T(8,128)(2,1)S(1)} %copy-done.4), custom_call_target="tpu_custom_call" | custom-call | flops 1610612736 | bytes 6291456 | tf_op jit(solution)/shard_map/pallas_call | solution.py:67
  80.2 2.1 collective-permute-start.19
  82.6 2.5 %collective-permute-start.18 = (bf16[2,256,512]{2,1,0:T(8,128)(2,1)S(1)}, bf16[2,256,512]{2,1,0:T(8,128)(2,1)S(1)}, u32[]{:S(2)}, u32[]{:S(2)}) collective-permute-start(bf16[2,256,512]{2,1,0:T(8,128)(2,1)S(1)} %get-tuple-element.52), channel_id=1, source_target_pairs={{0,2},{2,0},{1,3},{3,1},{4,6},{6,4},{5,7},{7,5},{8,10},{10,8},{9,1... | collective-permute-start | bytes 1572872 | tf_op jit(solution)/shard_map/ppermute | solution.py:26
  85.0 3.1 %shard_map.106 = bf16[512,1536]{1,0:T(8,128)(2,1)S(1)} custom-call(s32[4]{0:T(128)S(1)} %pad_add_fusion.place, bf16[2,256,512]{2,1,0:T(8,128)(2,1)S(1)} %fusion.12.hidden, bf16[2,256,512]{2,1,0:T(8,128)(2,1)S(1)} %collective-permute-done.5.hidden_other, bf16[1024,1536]{1,0:T(8,128)(2,1)S(1)} %copy-done.3), custom_call_target="tpu_custom_call" | custom-call | flops 1610612736 | bytes 6291456 | tf_op jit(solution)/shard_map/pallas_call | solution.py:135
  88.1 12.1 %collective-permute-done.19.p1 = bf16[256,1536]{1,0:T(8,128)(2,1)S(1)} collective-permute-done((bf16[256,1536]{1,0:T(8,128)(2,1)S(1)}, bf16[256,1536]{1,0:T(8,128)(2,1)S(1)}, u32[]{:S(2)}, u32[]{:S(2)}) %collective-permute-start.19) | collective-permute-done | bytes 786464 | tf_op jit(solution)/shard_map/ppermute | solution.py:22
  100.2 3.0 %collective-permute-done.20.p3 = bf16[256,1536]{1,0:T(8,128)(2,1)S(1)} collective-permute-done((bf16[256,1536]{1,0:T(8,128)(2,1)S(1)}, bf16[256,1536]{1,0:T(8,128)(2,1)S(1)}, u32[]{:S(2)}, u32[]{:S(2)}) %collective-permute-start.20) | collective-permute-done | bytes 786464 | tf_op jit(solution)/shard_map/ppermute | solution.py:22
  104.6 1.4 collective-permute-done.21.gg_other.gg_o
  106.7 5.6 %shard_map.107 = bf16[1024,1536]{1,0:T(8,128)(2,1)} custom-call(s32[4]{0:T(128)S(1)} %pad_add_fusion.place, bf16[2,256,512]{2,1,0:T(8,128)(2,1)S(1)} %get-tuple-element.55.gg, bf16[2,256,512]{2,1,0:T(8,128)(2,1)S(1)} %collective-permute-done.21.gg_other.gg_o, bf16[2,256,512]{2,1,0:T(8,128)(2,1)S(1)} %get-tuple-element.54.gu, ...), custom_call_target="tpu_custom_call" | custom-call | flops 3221225472 | bytes 8388608 | tf_op jit(solution)/shard_map/pallas_call | solution.py:105
  114.8 1.4 collective-permute-start.24
  116.2 19.0 %collective-permute-done.25.p2 = bf16[256,1536]{1,0:T(8,128)(2,1)S(1)} collective-permute-done((bf16[256,1536]{1,0:T(8,128)(2,1)S(1)}, bf16[256,1536]{1,0:T(8,128)(2,1)S(1)}, u32[]{:S(2)}, u32[]{:S(2)}) %collective-permute-start.25) | collective-permute-done | bytes 786464 | tf_op jit(solution)/shard_map/ppermute | solution.py:22
  136.1 3.3 %collective-permute-done.24.fgu = bf16[2,256,512]{2,1,0:T(8,128)(2,1)S(1)} collective-permute-done((bf16[2,256,512]{2,1,0:T(8,128)(2,1)S(1)}, bf16[2,256,512]{2,1,0:T(8,128)(2,1)S(1)}, u32[]{:S(2)}, u32[]{:S(2)}) %collective-permute-start.24) | collective-permute-done | bytes 524320 | tf_op jit(solution)/shard_map/ppermute | solution.py:26
  141.3 34.7 %collective-permute-done.28 = bf16[512,1536]{1,0:T(8,128)(2,1)} collective-permute-done((bf16[512,1536]{1,0:T(8,128)(2,1)S(1)}, bf16[512,1536]{1,0:T(8,128)(2,1)}, u32[]{:S(2)}, u32[]{:S(2)}) %collective-permute-start.28) | collective-permute-done | bytes 1572896 | tf_op jit(solution)/shard_map/ppermute | solution.py:26
  176.0 3.0 %add_convert_fusion = bf16[512,1536]{1,0:T(8,128)(2,1)} fusion(bf16[512,1536]{1,0:T(8,128)(2,1)} %collective-permute-done.28, bf16[512,1536]{1,0:T(8,128)(2,1)S(1)} %shard_map.106), kind=kLoop, calls=%fused_computation | loop fusion | flops 3145728 | bytes 4718592 | tf_op jit(solution)/shard_map/convert_element_type | solution.py:256
  180.7 1.9 copy-done.2
  182.6 1.1 copy-done.8
  183.7 1.1 copy-done.10
  184.9 1.1 copy-done.12
  186.0 1.0 copy-done.14
  187.0 1.0 copy-done.16
  188.1 1.0 copy-done.18
  189.1 1.0 copy-done.20
  190.2 1.0 copy-done.22
  191.2 1.0 copy-done.24
  192.2 10.0 %shard_map.108 = (bf16[1536,512]{1,0:T(8,128)(2,1)}, bf16[1536,512]{1,0:T(8,128)(2,1)}) custom-call(s32[4]{0:T(128)S(1)} %pad_add_fusion.place, bf16[1024,1536]{1,0:T(8,128)(2,1)S(1)} %copy-done.2, bf16[256,1536]{1,0:T(8,128)(2,1)S(1)} %bitcast.28, bf16[256,1536]{1,0:T(8,128)(2,1)S(1)} %copy-done.8, bf16[256,1536]{1,0:T(8,128)(2,1)S(1)} %copy-done.12, ...), custom_call_target="tpu_custom_call" | custom-call | flops 6442450944 | bytes 16777216 | tf_op jit(solution)/shard_map/pallas_call | solution.py:179
  204.0 2.2 %collective-permute-start.30 = (bf16[32,1536]{1,0:T(8,128)(2,1)S(1)}, bf16[32,1536]{1,0:T(8,128)(2,1)S(1)}, u32[]{:S(2)}, u32[]{:S(2)}) collective-permute-start(bf16[32,1536]{1,0:T(8,128)(2,1)S(1)} %get-tuple-element.62), channel_id=1, source_target_pairs={{8,0},{12,4},{0,8},{4,12},{9,1},{13,5},{1,9},{5,13},{10,2},{14,6},... | collective-permute-start | bytes 294920 | tf_op jit(solution)/shard_map/ppermute | solution.py:22
  206.2 2.5 %collective-permute-start.31 = (bf16[32,1536]{1,0:T(8,128)(2,1)S(1)}, bf16[32,1536]{1,0:T(8,128)(2,1)S(1)}, u32[]{:S(2)}, u32[]{:S(2)}) collective-permute-start(bf16[32,1536]{1,0:T(8,128)(2,1)S(1)} %get-tuple-element.61), channel_id=1, source_target_pairs={{4,0},{8,4},{12,8},{0,12},{5,1},{9,5},{13,9},{1,13},{6,2},{10,6},{... | collective-permute-start | bytes 294920 | tf_op jit(solution)/shard_map/ppermute | solution.py:22
  209.1 1.0 collective-permute-done.30
  211.0 1.6 fusion.15
  (98 shorter events, 21.1 us)
Async XLA Ops:
  7.2 66.5 %all-gather.3.cloned.1.call-start = ((), (), s32[]{:S(2)}) async-start(), calls=%async_computation.1 | async-start | bytes 3538944 | tf_op jit(solution)/shard_map/all_gather | solution.py:214
  7.2 7.6 %collective-permute-start = (bf16[32,1536]{1,0:T(8,128)(2,1)}, bf16[32,1536]{1,0:T(8,128)(2,1)S(1)}, u32[]{:S(2)}, u32[]{:S(2)}) collective-permute-start(bf16[32,1536]{1,0:T(8,128)(2,1)} %refs_0_.2), channel_id=1, source_target_pairs={{4,0},{8,4},{12,8},{0,12},{5,1},{9,5},{13,9},{1,13},{6,2},{10,6},{... | collective-permute-start | bytes 294920 | tf_op jit(solution)/shard_map/ppermute | solution.py:22
  10.3 7.1 %collective-permute-start.1 = (bf16[32,1536]{1,0:T(8,128)(2,1)}, bf16[32,1536]{1,0:T(8,128)(2,1)S(1)}, u32[]{:S(2)}, u32[]{:S(2)}) collective-permute-start(bf16[32,1536]{1,0:T(8,128)(2,1)} %refs_0_.2), channel_id=1, source_target_pairs={{8,0},{12,4},{0,8},{4,12},{9,1},{13,5},{1,9},{5,13},{10,2},{14,6},... | collective-permute-start | bytes 294920 | tf_op jit(solution)/shard_map/ppermute | solution.py:22
  10.9 7.4 %collective-permute-start.2 = (bf16[32,1536]{1,0:T(8,128)(2,1)}, bf16[32,1536]{1,0:T(8,128)(2,1)S(1)}, u32[]{:S(2)}, u32[]{:S(2)}) collective-permute-start(bf16[32,1536]{1,0:T(8,128)(2,1)} %refs_0_.2), channel_id=1, source_target_pairs={{12,0},{0,4},{4,8},{8,12},{13,1},{1,5},{5,9},{9,13},{14,2},{2,6},{... | collective-permute-start | bytes 294920 | tf_op jit(solution)/shard_map/ppermute | solution.py:22
  19.3 17.6 %copy-start.27 = (bf16[256,512]{1,0:T(8,128)(2,1)S(1)}, bf16[256,512]{1,0:T(8,128)(2,1)}, u32[]{:S(2)}) copy-start(bf16[256,512]{1,0:T(8,128)(2,1)} %param.9) | copy-start | bytes 786436
  20.6 160.1 %all-gather.5.cloned.1.call-start = ((), (), s32[]{:S(2)}) async-start(), calls=%async_computation.3 | async-start | bytes 3538944 | tf_op jit(solution)/shard_map/all_gather | solution.py:229
  20.7 11.0 %collective-permute-start.4 = (bf16[256,512]{1,0:T(8,128)(2,1)}, bf16[256,512]{1,0:T(8,128)(2,1)S(1)}, u32[]{:S(2)}, u32[]{:S(2)}) collective-permute-start(bf16[256,512]{1,0:T(8,128)(2,1)} %param.10), channel_id=1, source_target_pairs={{0,2},{2,0},{1,3},{3,1},{4,6},{6,4},{5,7},{7,5},{8,10},{10,8},{9,1... | collective-permute-start | bytes 786440 | tf_op jit(solution)/shard_map/ppermute | solution.py:26
  22.9 14.0 %collective-permute-start.3 = (bf16[256,512]{1,0:T(8,128)(2,1)}, bf16[256,512]{1,0:T(8,128)(2,1)S(1)}, u32[]{:S(2)}, u32[]{:S(2)}) collective-permute-start(bf16[256,512]{1,0:T(8,128)(2,1)} %param.9), channel_id=1, source_target_pairs={{0,2},{2,0},{1,3},{3,1},{4,6},{6,4},{5,7},{7,5},{8,10},{10,8},{9,1... | collective-permute-start | bytes 786440 | tf_op jit(solution)/shard_map/ppermute | solution.py:26
  24.3 13.6 %collective-permute-start.6 = (bf16[32,1536]{1,0:T(8,128)(2,1)}, bf16[32,1536]{1,0:T(8,128)(2,1)S(1)}, u32[]{:S(2)}, u32[]{:S(2)}) collective-permute-start(bf16[32,1536]{1,0:T(8,128)(2,1)} %refs_0_.3), channel_id=1, source_target_pairs={{0,128},{128,0},{1,129},{129,1},{2,130},{130,2},{3,131},{131,3},{4... | collective-permute-start | bytes 294920 | tf_op jit(solution)/shard_map/ppermute | solution.py:26
  32.7 11.1 %copy-start.1 = (bf16[32,1536]{1,0:T(8,128)(2,1)S(1)}, bf16[32,1536]{1,0:T(8,128)(2,1)}, u32[]{:S(2)}) copy-start(bf16[32,1536]{1,0:T(8,128)(2,1)} %refs_0_.3) | copy-start | bytes 294916
  37.2 35.4 %collective-permute-start.5 = (bf16[2,256,512]{2,1,0:T(8,128)(2,1)S(1)}, bf16[2,256,512]{2,1,0:T(8,128)(2,1)S(1)}, u32[]{:S(2)}, u32[]{:S(2)}) collective-permute-start(bf16[2,256,512]{2,1,0:T(8,128)(2,1)S(1)} %fusion.12.hidden), channel_id=1, source_target_pairs={{0,1},{1,0},{2,3},{3,2},{4,5},{5,4},{6,7},{7,6},{8,9},{9,8},{10,11... | collective-permute-start | bytes 1572872 | tf_op jit(solution)/shard_map/ppermute | solution.py:26
  37.9 10.7 %collective-permute-start.7 = (bf16[32,1536]{1,0:T(8,128)(2,1)S(1)}, bf16[32,1536]{1,0:T(8,128)(2,1)S(1)}, u32[]{:S(2)}, u32[]{:S(2)}) collective-permute-start(bf16[32,1536]{1,0:T(8,128)(2,1)S(1)} %collective-permute-done.6.refs_0_), channel_id=1, source_target_pairs={{16,0},{32,16},{48,32},{64,48},{80,64},{96,80},{112,96},{0,112},{1... | collective-permute-start | bytes 294920 | tf_op jit(solution)/shard_map/ppermute | solution.py:22
  43.8 8.5 %collective-permute-start.14 = (bf16[32,1536]{1,0:T(8,128)(2,1)S(1)}, bf16[32,1536]{1,0:T(8,128)(2,1)S(1)}, u32[]{:S(2)}, u32[]{:S(2)}) collective-permute-start(bf16[32,1536]{1,0:T(8,128)(2,1)S(1)} %copy-done.1), channel_id=1, source_target_pairs={{4,0},{8,4},{12,8},{0,12},{5,1},{9,5},{13,9},{1,13},{6,2},{10,6},{... | collective-permute-start | bytes 294920 | tf_op jit(solution)/shard_map/ppermute | solution.py:22
  43.8 9.1 %collective-permute-start.11 = (bf16[32,1536]{1,0:T(8,128)(2,1)S(1)}, bf16[32,1536]{1,0:T(8,128)(2,1)S(1)}, u32[]{:S(2)}, u32[]{:S(2)}) collective-permute-start(bf16[32,1536]{1,0:T(8,128)(2,1)S(1)} %collective-permute-done.6.refs_0_), channel_id=1, source_target_pairs={{112,0},{0,16},{16,32},{32,48},{48,64},{64,80},{80,96},{96,112},{1... | collective-permute-start | bytes 294920 | tf_op jit(solution)/shard_map/ppermute | solution.py:22
  48.6 8.3 %collective-permute-start.8 = (bf16[32,1536]{1,0:T(8,128)(2,1)S(1)}, bf16[32,1536]{1,0:T(8,128)(2,1)S(1)}, u32[]{:S(2)}, u32[]{:S(2)}) collective-permute-start(bf16[32,1536]{1,0:T(8,128)(2,1)S(1)} %collective-permute-done.7.refs_1_), channel_id=1, source_target_pairs={{16,0},{32,16},{48,32},{64,48},{80,64},{96,80},{112,96},{0,112},{1... | collective-permute-start | bytes 294920 | tf_op jit(solution)/shard_map/ppermute | solution.py:22
  52.3 8.3 %collective-permute-start.15 = (bf16[32,1536]{1,0:T(8,128)(2,1)S(1)}, bf16[32,1536]{1,0:T(8,128)(2,1)S(1)}, u32[]{:S(2)}, u32[]{:S(2)}) collective-permute-start(bf16[32,1536]{1,0:T(8,128)(2,1)S(1)} %copy-done.1), channel_id=1, source_target_pairs={{8,0},{12,4},{0,8},{4,12},{9,1},{13,5},{1,9},{5,13},{10,2},{14,6},... | collective-permute-start | bytes 294920 | tf_op jit(solution)/shard_map/ppermute | solution.py:22
  52.3 8.3 %collective-permute-start.16 = (bf16[32,1536]{1,0:T(8,128)(2,1)S(1)}, bf16[32,1536]{1,0:T(8,128)(2,1)S(1)}, u32[]{:S(2)}, u32[]{:S(2)}) collective-permute-start(bf16[32,1536]{1,0:T(8,128)(2,1)S(1)} %copy-done.1), channel_id=1, source_target_pairs={{12,0},{0,4},{4,8},{8,12},{13,1},{1,5},{5,9},{9,13},{14,2},{2,6},{... | collective-permute-start | bytes 294920 | tf_op jit(solution)/shard_map/ppermute | solution.py:22
  52.9 9.0 %collective-permute-start.12 = (bf16[32,1536]{1,0:T(8,128)(2,1)S(1)}, bf16[32,1536]{1,0:T(8,128)(2,1)S(1)}, u32[]{:S(2)}, u32[]{:S(2)}) collective-permute-start(bf16[32,1536]{1,0:T(8,128)(2,1)S(1)} %collective-permute-done.11.refs_7_), channel_id=1, source_target_pairs={{112,0},{0,16},{16,32},{32,48},{48,64},{64,80},{80,96},{96,112},{1... | collective-permute-start | bytes 294920 | tf_op jit(solution)/shard_map/ppermute | solution.py:22
  56.9 8.0 %collective-permute-start.9 = (bf16[32,1536]{1,0:T(8,128)(2,1)S(1)}, bf16[32,1536]{1,0:T(8,128)(2,1)S(1)}, u32[]{:S(2)}, u32[]{:S(2)}) collective-permute-start(bf16[32,1536]{1,0:T(8,128)(2,1)S(1)} %collective-permute-done.8.refs_2_), channel_id=1, source_target_pairs={{16,0},{32,16},{48,32},{64,48},{80,64},{96,80},{112,96},{0,112},{1... | collective-permute-start | bytes 294920 | tf_op jit(solution)/shard_map/ppermute | solution.py:22
  61.9 7.9 %collective-permute-start.13 = (bf16[32,1536]{1,0:T(8,128)(2,1)S(1)}, bf16[32,1536]{1,0:T(8,128)(2,1)S(1)}, u32[]{:S(2)}, u32[]{:S(2)}) collective-permute-start(bf16[32,1536]{1,0:T(8,128)(2,1)S(1)} %collective-permute-done.12.refs_6_), channel_id=1, source_target_pairs={{112,0},{0,16},{16,32},{32,48},{48,64},{64,80},{80,96},{96,112},{1... | collective-permute-start | bytes 294920 | tf_op jit(solution)/shard_map/ppermute | solution.py:22
  64.9 7.1 %collective-permute-start.10 = (bf16[32,1536]{1,0:T(8,128)(2,1)S(1)}, bf16[32,1536]{1,0:T(8,128)(2,1)S(1)}, u32[]{:S(2)}, u32[]{:S(2)}) collective-permute-start(bf16[32,1536]{1,0:T(8,128)(2,1)S(1)} %collective-permute-done.9.refs_3_), channel_id=1, source_target_pairs={{16,0},{32,16},{48,32},{64,48},{80,64},{96,80},{112,96},{0,112},{1... | collective-permute-start | bytes 294920 | tf_op jit(solution)/shard_map/ppermute | solution.py:22
  73.7 128.5 %reduce-scatter.2.cloned.1.call-start = ((), (), s32[]{:S(2)}) async-start(), calls=%async_computation.2 | async-start | bytes 3538944 | tf_op jit(solution)/shard_map/reduce_scatter | solution.py:249
  73.7 1.9 copy-start.3
  75.6 1.4 copy-start.4
  80.1 2.2 %collective-permute-start.17 = (bf16[2,256,512]{2,1,0:T(8,128)(2,1)S(1)}, bf16[2,256,512]{2,1,0:T(8,128)(2,1)S(1)}, u32[]{:S(2)}, u32[]{:S(2)}) collective-permute-start(bf16[2,256,512]{2,1,0:T(8,128)(2,1)S(1)} %get-tuple-element.30), channel_id=1, source_target_pairs={{0,1},{1,0},{2,3},{3,2},{4,5},{5,4},{6,7},{7,6},{8,9},{9,8},{10,11... | collective-permute-start | bytes 1572872 | tf_op jit(solution)/shard_map/ppermute | solution.py:26
  80.2 20.0 %collective-permute-start.19 = (bf16[256,1536]{1,0:T(8,128)(2,1)S(1)}, bf16[256,1536]{1,0:T(8,128)(2,1)S(1)}, u32[]{:S(2)}, u32[]{:S(2)}) collective-permute-start(bf16[256,1536]{1,0:T(8,128)(2,1)S(1)} %bitcast.25), channel_id=1, source_target_pairs={{4,0},{8,4},{12,8},{0,12},{5,1},{9,5},{13,9},{1,13},{6,2},{10,6},{... | collective-permute-start | bytes 2359304 | tf_op jit(solution)/shard_map/ppermute | solution.py:22
  82.3 20.8 %collective-permute-start.20 = (bf16[256,1536]{1,0:T(8,128)(2,1)S(1)}, bf16[256,1536]{1,0:T(8,128)(2,1)S(1)}, u32[]{:S(2)}, u32[]{:S(2)}) collective-permute-start(bf16[256,1536]{1,0:T(8,128)(2,1)S(1)} %bitcast.26), channel_id=1, source_target_pairs={{12,0},{0,4},{4,8},{8,12},{13,1},{1,5},{5,9},{9,13},{14,2},{2,6},{... | collective-permute-start | bytes 2359304 | tf_op jit(solution)/shard_map/ppermute | solution.py:22
  82.5 20.6 %copy-start.25 = (bf16[2,256,512]{2,1,0:T(8,128)(2,1)S(1)}, bf16[2,256,512]{2,1,0:T(8,128)(2,1)}, u32[]{:S(2)}) copy-start(bf16[2,256,512]{2,1,0:T(8,128)(2,1)} %get-tuple-element.37) | copy-start | bytes 1572868
  82.6 20.6 %copy-start.26 = (bf16[2,256,512]{2,1,0:T(8,128)(2,1)S(1)}, bf16[2,256,512]{2,1,0:T(8,128)(2,1)}, u32[]{:S(2)}) copy-start(bf16[2,256,512]{2,1,0:T(8,128)(2,1)} %get-tuple-element.36) | copy-start | bytes 1572868
  82.6 20.6 %collective-permute-start.18 = (bf16[2,256,512]{2,1,0:T(8,128)(2,1)S(1)}, bf16[2,256,512]{2,1,0:T(8,128)(2,1)S(1)}, u32[]{:S(2)}, u32[]{:S(2)}) collective-permute-start(bf16[2,256,512]{2,1,0:T(8,128)(2,1)S(1)} %get-tuple-element.52), channel_id=1, source_target_pairs={{0,2},{2,0},{1,3},{3,1},{4,6},{6,4},{5,7},{7,5},{8,10},{10,8},{9,1... | collective-permute-start | bytes 1572872 | tf_op jit(solution)/shard_map/ppermute | solution.py:26
  100.2 3.6 %copy-start.7 = (bf16[256,1536]{1,0:T(8,128)(2,1)}, bf16[256,1536]{1,0:T(8,128)(2,1)S(1)}, u32[]{:S(2)}) copy-start(bf16[256,1536]{1,0:T(8,128)(2,1)S(1)} %collective-permute-done.19.p1) | copy-start | bytes 2359300
  103.1 3.6 %copy-start.5 = (bf16[1536,512]{1,0:T(8,128)(2,1)S(1)}, bf16[1536,512]{1,0:T(8,128)(2,1)}, u32[]{:S(2)}) copy-start(bf16[1536,512]{1,0:T(8,128)(2,1)} %w_gate.1) | copy-start | bytes 4718596
  103.2 3.6 %copy-start.6 = (bf16[1536,512]{1,0:T(8,128)(2,1)S(1)}, bf16[1536,512]{1,0:T(8,128)(2,1)}, u32[]{:S(2)}) copy-start(bf16[1536,512]{1,0:T(8,128)(2,1)} %w_up.1) | copy-start | bytes 4718596
  104.1 1.9 collective-permute-start.21
  104.1 2.7 %collective-permute-start.22 = (bf16[2,256,512]{2,1,0:T(8,128)(2,1)S(1)}, bf16[2,256,512]{2,1,0:T(8,128)(2,1)S(1)}, u32[]{:S(2)}, u32[]{:S(2)}) collective-permute-start(bf16[2,256,512]{2,1,0:T(8,128)(2,1)S(1)} %get-tuple-element.54.gu), channel_id=1, source_target_pairs={{0,1},{1,0},{2,3},{3,2},{4,5},{5,4},{6,7},{7,6},{8,9},{9,8},{10,11... | collective-permute-start | bytes 1572872 | tf_op jit(solution)/shard_map/ppermute | solution.py:26
  114.0 21.2 %collective-permute-start.25 = (bf16[256,1536]{1,0:T(8,128)(2,1)S(1)}, bf16[256,1536]{1,0:T(8,128)(2,1)S(1)}, u32[]{:S(2)}, u32[]{:S(2)}) collective-permute-start(bf16[256,1536]{1,0:T(8,128)(2,1)S(1)} %bitcast.27), channel_id=1, source_target_pairs={{8,0},{12,4},{0,8},{4,12},{9,1},{13,5},{1,9},{5,13},{10,2},{14,6},... | collective-permute-start | bytes 2359304 | tf_op jit(solution)/shard_map/ppermute | solution.py:22
  114.1 22.0 %collective-permute-start.23 = (bf16[2,256,512]{2,1,0:T(8,128)(2,1)S(1)}, bf16[2,256,512]{2,1,0:T(8,128)(2,1)S(1)}, u32[]{:S(2)}, u32[]{:S(2)}) collective-permute-start(bf16[2,256,512]{2,1,0:T(8,128)(2,1)S(1)} %get-tuple-element.55.gg), channel_id=1, source_target_pairs={{0,128},{128,0},{1,129},{129,1},{2,130},{130,2},{3,131},{131,3},{4... | collective-permute-start | bytes 1572872 | tf_op jit(solution)/shard_map/ppermute | solution.py:26
  114.8 24.6 %collective-permute-start.24 = (bf16[2,256,512]{2,1,0:T(8,128)(2,1)S(1)}, bf16[2,256,512]{2,1,0:T(8,128)(2,1)S(1)}, u32[]{:S(2)}, u32[]{:S(2)}) collective-permute-start(bf16[2,256,512]{2,1,0:T(8,128)(2,1)S(1)} %get-tuple-element.54.gu), channel_id=1, source_target_pairs={{0,128},{128,0},{1,129},{129,1},{2,130},{130,2},{3,131},{131,3},{4... | collective-permute-start | bytes 1572872 | tf_op jit(solution)/shard_map/ppermute | solution.py:26
  136.0 3.3 %copy-start.17 = (bf16[2,256,512]{2,1,0:T(8,128)(2,1)}, bf16[2,256,512]{2,1,0:T(8,128)(2,1)S(1)}, u32[]{:S(2)}) copy-start(bf16[2,256,512]{2,1,0:T(8,128)(2,1)S(1)} %collective-permute-done.23.fgg) | copy-start | bytes 1572868
  140.2 35.8 %collective-permute-start.28 = (bf16[512,1536]{1,0:T(8,128)(2,1)S(1)}, bf16[512,1536]{1,0:T(8,128)(2,1)}, u32[]{:S(2)}, u32[]{:S(2)}) collective-permute-start(bf16[512,1536]{1,0:T(8,128)(2,1)S(1)} %shard_map.106), channel_id=1, source_target_pairs={{0,128},{128,0},{1,129},{129,1},{2,130},{130,2},{3,131},{131,3},{4... | collective-permute-start | bytes 4718600 | tf_op jit(solution)/shard_map/ppermute | solution.py:26
  140.8 38.3 %collective-permute-start.26 = (bf16[2,256,512]{2,1,0:T(8,128)(2,1)}, bf16[2,256,512]{2,1,0:T(8,128)(2,1)S(1)}, u32[]{:S(2)}, u32[]{:S(2)}) collective-permute-start(bf16[2,256,512]{2,1,0:T(8,128)(2,1)} %copy-done.17), channel_id=1, source_target_pairs={{0,1},{1,0},{2,3},{3,2},{4,5},{5,4},{6,7},{7,6},{8,9},{9,8},{10,11... | collective-permute-start | bytes 1572872 | tf_op jit(solution)/shard_map/ppermute | solution.py:26
  140.8 39.1 %collective-permute-start.27 = (bf16[2,256,512]{2,1,0:T(8,128)(2,1)}, bf16[2,256,512]{2,1,0:T(8,128)(2,1)S(1)}, u32[]{:S(2)}, u32[]{:S(2)}) collective-permute-start(bf16[2,256,512]{2,1,0:T(8,128)(2,1)} %copy-done.19), channel_id=1, source_target_pairs={{0,1},{1,0},{2,3},{3,2},{4,5},{5,4},{6,7},{7,6},{8,9},{9,8},{10,11... | collective-permute-start | bytes 1572872 | tf_op jit(solution)/shard_map/ppermute | solution.py:26
  180.7 1.9 copy-start.2
  182.6 1.1 copy-start.8
  183.7 1.1 copy-start.10
  203.2 5.9 %collective-permute-start.29 = (bf16[32,1536]{1,0:T(8,128)(2,1)S(1)}, bf16[32,1536]{1,0:T(8,128)(2,1)S(1)}, u32[]{:S(2)}, u32[]{:S(2)}) collective-permute-start(bf16[32,1536]{1,0:T(8,128)(2,1)S(1)} %get-tuple-element.60), channel_id=1, source_target_pairs={{12,0},{0,4},{4,8},{8,12},{13,1},{1,5},{5,9},{9,13},{14,2},{2,6},{... | collective-permute-start | bytes 294920 | tf_op jit(solution)/shard_map/ppermute | solution.py:22
  204.0 6.2 %collective-permute-start.30 = (bf16[32,1536]{1,0:T(8,128)(2,1)S(1)}, bf16[32,1536]{1,0:T(8,128)(2,1)S(1)}, u32[]{:S(2)}, u32[]{:S(2)}) collective-permute-start(bf16[32,1536]{1,0:T(8,128)(2,1)S(1)} %get-tuple-element.62), channel_id=1, source_target_pairs={{8,0},{12,4},{0,8},{4,12},{9,1},{13,5},{1,9},{5,13},{10,2},{14,6},... | collective-permute-start | bytes 294920 | tf_op jit(solution)/shard_map/ppermute | solution.py:22
  206.2 4.8 %collective-permute-start.31 = (bf16[32,1536]{1,0:T(8,128)(2,1)S(1)}, bf16[32,1536]{1,0:T(8,128)(2,1)S(1)}, u32[]{:S(2)}, u32[]{:S(2)}) collective-permute-start(bf16[32,1536]{1,0:T(8,128)(2,1)S(1)} %get-tuple-element.61), channel_id=1, source_target_pairs={{4,0},{8,4},{12,8},{0,12},{5,1},{9,5},{13,9},{1,13},{6,2},{10,6},{... | collective-permute-start | bytes 294920 | tf_op jit(solution)/shard_map/ppermute | solution.py:22
  (15 other events, 14.2 us)
Sparse Core Ops, SparseCore 0:
  20.7 52.8 all-gather.2
  75.4 44.5 all-gather.4
  122.6 45.3 reduce-scatter.1
where the time goes:
time: 221 us; the launch traced here: 219 us
  waiting for transfers between devices  110 us (50%)
  starting transfers between devices  40.6 us (18%)
  Pallas kernels  25 us (11%)
  local copies, waits for them, and re-layouts  22 us (10%)
  between operations  14 us (6%)
  other arithmetic  7.95 us (4%)
    ppermute x19, waiting for transfers between devices, from_ahead(): return lax.ppermute(x, axis, [((d + k) % n, d) for d in range(n)])  56.8 us
    ppermute x13, waiting for transfers between devices, swap(): return lax.ppermute(x, axis, [(0, 1), (1, 0)])  51.8 us
    ppermute x19, starting transfers between devices, from_ahead(): return lax.ppermute(x, axis, [((d + k) % n, d) for d in range(n)])  30 us
    unnamed x56, local copies, waits for them, and re-layouts  21 us
    ppermute x13, starting transfers between devices, swap(): return lax.ppermute(x, axis, [(0, 1), (1, 0)])  10.5 us
    pallas_call x1, Pallas kernels, weight_grads(): pl.pallas_call(weight_kernel, grid=(6,), out_shape=(shape, shape), in_spe...  9.96 us
    pallas_call x1, Pallas kernels, input_grad(): pl.pallas_call(input_grad_kernel, grid=(4,), out_shape=jax.ShapeDtypeStru...  5.6 us
  transfers between devices with their start and end apart: 35, of which 22 were waited for; matrix products, arithmetic and copies ran while one was open for 3% of the time, Pallas kernels for 11%

commit v1 on v0

--- a/solution.py
+++ b/solution.py
@@ -11,6 +11,7 @@
 NZ, NY = 8, 4
 VMEM = pl.BlockSpec(memory_space=pltpu.VMEM)
 SMEM = pl.BlockSpec(memory_space=pltpu.SMEM)
+HBM = pl.BlockSpec(memory_space=pltpu.HBM)
 
 
 def dot(left, right, left_dim, right_dim):
@@ -48,36 +49,38 @@
     return out.reshape(n * rows, cols)
 
 
-def hidden_grad_kernel(place, go, w_down, mine, send):
-    step = pl.program_id(0)
-    half, side = step // 2, step % 2
-    part = dot(go[...], w_down[...], 1, 1)
-
-    @pl.when(side == place[3])
-    def _():
-        mine[half] = part
-
-    @pl.when(side != place[3])
-    def _():
-        send[half] = part.astype(BF16)
+def hidden_grad_kernel(place, go, w_down, mine, send, rows, sems):
+    copies = [
+        pltpu.make_async_copy(go.at[pl.ds(256 * block, 256)], rows.at[block], sems.at[block])
+        for block in range(4)
+    ]
+    for copy in copies:
+        copy.start()
+    for block, copy in enumerate(copies):
+        copy.wait()
+        half, side = block // 2, block % 2
+        part = dot(rows[block], w_down[...], 1, 1)
+
+        @pl.when(side == place[3])
+        def _():
+            mine[half] = part
+
+        @pl.when(side != place[3])
+        def _():
+            send[half] = part.astype(BF16)
 
 
 def hidden_grad(place, go, w_down):
-    whole = pl.BlockSpec((2, 256, 512), lambda i: (0, 0, 0))
     return pl.pallas_call(
         hidden_grad_kernel,
-        grid=(4,),
         out_shape=(
             jax.ShapeDtypeStruct((2, 256, 512), F32),
             jax.ShapeDtypeStruct((2, 256, 512), BF16),
         ),
-        in_specs=[
-            SMEM,
-            pl.BlockSpec((256, 1536), lambda i: (i, 0)),
-            pl.BlockSpec((512, 1536), lambda i: (0, 0)),
-        ],
-        out_specs=(whole, whole),
-        compiler_params=params(32),
+        in_specs=[SMEM, HBM, VMEM],
+        out_specs=(VMEM, VMEM),
+        scratch_shapes=[pltpu.VMEM((4, 256, 1536), BF16), pltpu.SemaphoreType.DMA((4,))],
+        compiler_params=params(24),
         cost_estimate=pl.CostEstimate(flops=2 * 1024 * 1536 * 512, bytes_accessed=6 << 20, transcendentals=0),
     )(place, go, w_down)
 
@@ -100,15 +103,13 @@
 
 
 def input_grad(place, gg, gg_other, gu, gu_other, w_gate, w_up):
-    whole = pl.BlockSpec((2, 256, 512), lambda i: (0, 0, 0))
-    weight = pl.BlockSpec((1536, 512), lambda i: (0, 0))
     return pl.pallas_call(
         input_grad_kernel,
         grid=(4,),
         out_shape=jax.ShapeDtypeStruct((1024, 1536), BF16),
-        in_specs=[SMEM] + [whole] * 4 + [weight] * 2,
+        in_specs=[SMEM] + [VMEM] * 6,
         out_specs=pl.BlockSpec((256, 1536), lambda i: (i, 0)),
-        compiler_params=params(40),
+        compiler_params=params(24),
         cost_estimate=pl.CostEstimate(flops=4 * 1024 * 1536 * 512, bytes_accessed=8 << 20, transcendentals=0),
     )(place, gg, gg_other, gu, gu_other, w_gate, w_up)
 
@@ -131,12 +132,11 @@
 
 
 def down_grad(place, hidden, hidden_other, go):
-    whole = pl.BlockSpec((2, 256, 512), lambda i: (0, 0, 0))
     return pl.pallas_call(
         down_kernel,
         grid=(3,),
         out_shape=jax.ShapeDtypeStruct((512, 1536), BF16),
-        in_specs=[SMEM, whole, whole, pl.BlockSpec((1024, 512), lambda i: (0, i))],
+        in_specs=[SMEM, VMEM, VMEM, pl.BlockSpec((1024, 512), lambda i: (0, i))],
         out_specs=pl.BlockSpec((512, 512), lambda i: (0, i)),
         scratch_shapes=[pltpu.VMEM((1024, 512), BF16)],
         compiler_params=params(32),
@@ -156,48 +156,42 @@
                 rows[k, z_other, :, col:col + 512] = other[half, lines, :]
 
 
-def weight_kernel(place, own, p0, p1, p2, p3, gg, gg_o, gu, gu_o, fgg, fgg_o, fgu, fgu_o, d_gate, d_up, near, far):
+def weight_kernel(place, *refs):
+    pieces, grads, (d_gate, d_up, rows) = refs[:8], refs[8:16], refs[16:]
+
     @pl.when(pl.program_id(0) == 0)
     def _():
-        fill_natural(place, gg, gg_o, near, 0)
-        fill_natural(place, gu, gu_o, near, 512)
-        fill_rolled(place, fgg, fgg_o, far, 0)
-        fill_rolled(place, fgu, fgu_o, far, 512)
-
-    total = dot(own[...], near[...], 0, 0)
-    for k, piece in enumerate((p0, p1, p2, p3)):
-        total = total + dot(piece[...], far[k].reshape(256, 1024), 0, 0)
+        for replica in range(2):
+            fill_rolled(place, *grads[4 * replica:4 * replica + 2], rows.at[replica], 0)
+            fill_rolled(place, *grads[4 * replica + 2:4 * replica + 4], rows.at[replica], 512)
+
+    total = jnp.zeros((256, 1024), F32)
+    for k, piece in enumerate(pieces):
+        total = total + dot(piece[...], rows[k // NY, k % NY].reshape(256, 1024), 0, 0)
     d_gate[...] = total[:, :512].astype(BF16)
     d_up[...] = total[:, 512:].astype(BF16)
 
 
-def weight_grads(place, own, pieces, grads):
-    whole = pl.BlockSpec((2, 256, 512), lambda i: (0, 0, 0))
-    piece = pl.BlockSpec((256, 256), lambda i: (0, i))
+def weight_grads(place, pieces, grads):
     tile = pl.BlockSpec((256, 512), lambda i: (i, 0))
     shape = jax.ShapeDtypeStruct((1536, 512), BF16)
     return pl.pallas_call(
         weight_kernel,
         grid=(6,),
         out_shape=(shape, shape),
-        in_specs=[SMEM, pl.BlockSpec((1024, 256), lambda i: (0, i))] + [piece] * 4 + [whole] * 8,
+        in_specs=[SMEM] + [pl.BlockSpec((256, 256), lambda i: (0, i))] * 8 + [VMEM] * 8,
         out_specs=(tile, tile),
-        scratch_shapes=[pltpu.VMEM((1024, 1024), BF16), pltpu.VMEM((NY, NZ, 32, 1024), BF16)],
-        compiler_params=params(40),
+        scratch_shapes=[pltpu.VMEM((2, NY, NZ, 32, 1024), BF16)],
+        compiler_params=params(28),
         cost_estimate=pl.CostEstimate(flops=8 * 1024 * 1536 * 512, bytes_accessed=16 << 20, transcendentals=0),
-    )(place, own, *pieces, *grads)
-
-
-def ring(x, axis, n):
-    ahead, behind = [], []
-    up, down = x, x
-    for step in range(1, n // 2 + 1):
-        up = from_ahead(up, axis, n, 1)
-        ahead.append(up)
-        if step < n // 2:
-            down = from_ahead(down, axis, n, n - 1)
-            behind.append(down)
-    return [x] + ahead + behind[::-1]
+    )(place, *pieces, *grads)
+
+
+def gather_z(x):
+    f1, f2, b1, b2 = (from_ahead(x, "z", NZ, k) for k in (1, 2, 7, 6))
+    f3, b3 = from_ahead(f2, "z", NZ, 1), from_ahead(b2, "z", NZ, 7)
+    f4 = from_ahead(f2, "z", NZ, 2)
+    return [x, f1, f2, f3, f4, b3, b2, b1]
 
 
 def ordered(mine, other, index):
@@ -218,25 +212,21 @@
     gate_val, up_val = gate.astype(F32), up.astype(F32)
     hidden = (gate_val * jax.nn.sigmoid(gate_val) * up_val).astype(BF16)
     hidden_other = swap(hidden, "core")
-    partner = swap(layer_input, "dp")
-    partner_z = arrange(place, 0, ring(partner, "z", NZ))
-    own_y = arrange(place, 1, [layer_input] + [from_ahead(layer_input, "y", NY, k) for k in (1, 2, 3)])
-
-    go, gate, up, hidden, hidden_other, partner_z, own_y = lax.optimization_barrier(
-        (go, gate, up, hidden, hidden_other, partner_z, own_y)
+    own_z = arrange(place, 0, gather_z(layer_input))
+    partner_z = swap(own_z, "dp")
+    own1, own3 = from_ahead(own_z, "y", NY, 1), from_ahead(own_z, "y", NY, 3)
+
+    go, gate, up, hidden, hidden_other, partner_z, own1, own3 = lax.optimization_barrier(
+        (go, gate, up, hidden, hidden_other, partner_z, own1, own3)
     )
 
-    own_input = lax.all_gather(own_y, "z", axis=0, tiled=True)
+    own2 = from_ahead(own_z, "y", NY, 2)
     mine, send = hidden_grad(place, go, w_down)
     chip = mine + swap(send, "core").astype(F32)
     chip_far = swap(chip.astype(BF16), "xh")
     part_down = down_grad(place, hidden, hidden_other, go)
-    piece1 = from_ahead(partner_z, "y", NY, 1)
-    piece3 = from_ahead(partner_z, "y", NY, 3)
-
-    chip, chip_far, part_down, piece1, piece3 = lax.optimization_barrier(
-        (chip, chip_far, part_down, piece1, piece3)
-    )
+
+    chip, chip_far, part_down, own2 = lax.optimization_barrier((chip, chip_far, part_down, own2))
 
     grad_hidden = chip + chip_far.astype(F32)
     gate_val, up_val = gate.astype(F32), up.astype(F32)
@@ -245,16 +235,16 @@
     gu = (grad_hidden * gate_val * sigma).astype(BF16)
     gg_other, gu_other = swap(gg, "core"), swap(gu, "core")
     gg_far, gu_far = swap(gg, "dp"), swap(gu, "dp")
+    partner = [partner_z] + [from_ahead(partner_z, "y", NY, k) for k in (1, 2, 3)]
     partial_in = input_grad(place, gg, gg_other, gu, gu_other, w_gate, w_up)
     in_z = lax.psum_scatter(partial_in, "z", scatter_dimension=0, tiled=True).reshape(NY, 32, 1536)
 
-    piece2 = from_ahead(partner_z, "y", NY, 2)
-    gg_far, gu_far, part_down, piece2 = lax.optimization_barrier((gg_far, gu_far, part_down, piece2))
+    gg_far, gu_far, part_down = lax.optimization_barrier((gg_far, gu_far, part_down))
     down_far = swap(part_down, "dp")
     grads = (gg, gg_other, gu, gu_other, gg_far, swap(gg_far, "core"), gu_far, swap(gu_far, "core"))
-    grad_gate, grad_up = weight_grads(place, own_input, (partner_z, piece1, piece2, piece3), grads)
+    grad_gate, grad_up = weight_grads(place, [own_z, own1, own2, own3] + partner, grads)
+    grad_gate, grad_up, down_far = lax.optimization_barrier((grad_gate, grad_up, down_far))
     grad_down = (part_down.astype(F32) + down_far.astype(F32)).astype(BF16)
-    in_z, grad_gate, grad_up, grad_down = lax.optimization_barrier((in_z, grad_gate, grad_up, grad_down))
 
     y = place[1]
     total = lax.dynamic_index_in_dim(in_z, y, 0, keepdims=False).astype(F32)

time: 221 us -> 211 us (0.955)
  local copies, waits for them, and re-layouts: 22 us -> 17.2 us
  starting transfers between devices: 40.6 us -> 36.6 us
    ppermute x19, waiting for transfers between devices: 56.8 us -> 71.7 us  [from_ahead(): return lax.ppermute(x, axis, [((d + k) % n, d) for d in range(n)])]
    ppermute x13, waiting for transfers between devices: 51.8 us -> 37 us  [swap(): return lax.ppermute(x, axis, [(0, 1), (1, 0)])]
    ppermute x19, starting transfers between devices: 30 us -> 24.7 us  [from_ahead(): return lax.ppermute(x, axis, [((d + k) % n, d) for d in range(n)])]
    unnamed x56 -> x50, local copies, waits for them, and re-layouts: 21 us -> 16.2 us
  transfers between devices with their start and end apart: 35 -> 34, of which waited for: 22 -> 24; matrix products, arithmetic and copies ran while one was open for 3% -> 2% of each run, Pallas kernels for 11% -> 7%
where the time goes in v1:
time: 211 us; the launch traced here: 210 us
  waiting for transfers between devices  110 us (52%)
  starting transfers between devices  36.6 us (17%)
  Pallas kernels  25 us (12%)
  local copies, waits for them, and re-layouts  17.2 us (8%)
  between operations  14.3 us (7%)
  other arithmetic  7.01 us (3%)
    ppermute x19, waiting for transfers between devices, from_ahead(): return lax.ppermute(x, axis, [((d + k) % n, d) for d in range(n)])  71.7 us
    ppermute x13, waiting for transfers between devices, swap(): return lax.ppermute(x, axis, [(0, 1), (1, 0)])  37 us
    ppermute x19, starting transfers between devices, from_ahead(): return lax.ppermute(x, axis, [((d + k) % n, d) for d in range(n)])  24.7 us
    unnamed x50, local copies, waits for them, and re-layouts  16.2 us
    ppermute x13, starting transfers between devices, swap(): return lax.ppermute(x, axis, [(0, 1), (1, 0)])  11.9 us
    pallas_call x1, Pallas kernels, weight_grads(): pl.pallas_call(weight_kernel, grid=(6,), out_shape=(shape, shape), in_spe...  11.1 us
    pallas_call x1, Pallas kernels, input_grad(): pl.pallas_call(input_grad_kernel, grid=(4,), out_shape=jax.ShapeDtypeStru...  5.62 us
  transfers between devices with their start and end apart: 34, of which 24 were waited for; matrix products, arithmetic and copies ran while one was open for 2% of the time, Pallas kernels for 7%

profile of v1, /device:TPU:2, one launch (start us, length us, event | category | flops | bytes accessed | tf_op | source)
XLA Modules:
  0.0 210.3 jit_solution(478926600163046430)
XLA Ops:
  7.2 3.1 %collective-permute-start = (bf16[32,1536]{1,0:T(8,128)(2,1)}, bf16[32,1536]{1,0:T(8,128)(2,1)S(1)}, u32[]{:S(2)}, u32[]{:S(2)}) collective-permute-start(bf16[32,1536]{1,0:T(8,128)(2,1)} %refs_0_.2), channel_id=1, source_target_pairs={{4,0},{8,4},{12,8},{0,12},{5,1},{9,5},{13,9},{1,13},{6,2},{10,6},{... | collective-permute-start | bytes 294920 | tf_op jit(solution)/shard_map/ppermute | solution.py:23
  10.9 1.0 collective-permute-start.2
  12.0 2.8 %collective-permute-done.refs_1_ = bf16[32,1536]{1,0:T(8,128)(2,1)S(1)} collective-permute-done((bf16[32,1536]{1,0:T(8,128)(2,1)}, bf16[32,1536]{1,0:T(8,128)(2,1)S(1)}, u32[]{:S(2)}, u32[]{:S(2)}) %collective-permute-start) | collective-permute-done | bytes 98336 | tf_op jit(solution)/shard_map/ppermute | solution.py:23
  14.8 2.6 %collective-permute-done.1.refs_2_ = bf16[32,1536]{1,0:T(8,128)(2,1)S(1)} collective-permute-done((bf16[32,1536]{1,0:T(8,128)(2,1)}, bf16[32,1536]{1,0:T(8,128)(2,1)S(1)}, u32[]{:S(2)}, u32[]{:S(2)}) %collective-permute-start.1) | collective-permute-done | bytes 98336 | tf_op jit(solution)/shard_map/ppermute | solution.py:23
  17.4 1.0 collective-permute-done.2.refs_3_
  19.3 1.3 shard_map.102
  20.7 2.2 %collective-permute-start.4 = (bf16[256,512]{1,0:T(8,128)(2,1)}, bf16[256,512]{1,0:T(8,128)(2,1)S(1)}, u32[]{:S(2)}, u32[]{:S(2)}) collective-permute-start(bf16[256,512]{1,0:T(8,128)(2,1)} %param.10), channel_id=1, source_target_pairs={{0,2},{2,0},{1,3},{3,1},{4,6},{6,4},{5,7},{7,5},{8,10},{10,8},{9,1... | collective-permute-start | bytes 786440 | tf_op jit(solution)/shard_map/ppermute | solution.py:27
  22.9 6.3 %collective-permute-start.7 = (bf16[32,1536]{1,0:T(8,128)(2,1)}, bf16[32,1536]{1,0:T(8,128)(2,1)S(1)}, u32[]{:S(2)}, u32[]{:S(2)}) collective-permute-start(bf16[32,1536]{1,0:T(8,128)(2,1)} %refs_0_.3), channel_id=1, source_target_pairs={{32,0},{48,16},{64,32},{80,48},{96,64},{112,80},{0,96},{16,112},{3... | collective-permute-start | bytes 294920 | tf_op jit(solution)/shard_map/ppermute | solution.py:23
  29.2 1.0 collective-permute-start.12
  30.2 2.7 %collective-permute-start.6 = (bf16[32,1536]{1,0:T(8,128)(2,1)}, bf16[32,1536]{1,0:T(8,128)(2,1)S(1)}, u32[]{:S(2)}, u32[]{:S(2)}) collective-permute-start(bf16[32,1536]{1,0:T(8,128)(2,1)} %refs_0_.3), channel_id=1, source_target_pairs={{16,0},{32,16},{48,32},{64,48},{80,64},{96,80},{112,96},{0,112},{1... | collective-permute-start | bytes 294920 | tf_op jit(solution)/shard_map/ppermute | solution.py:23
  33.7 3.0 %collective-permute-start.8 = (bf16[32,1536]{1,0:T(8,128)(2,1)S(1)}, bf16[32,1536]{1,0:T(8,128)(2,1)S(1)}, u32[]{:S(2)}, u32[]{:S(2)}) collective-permute-start(bf16[32,1536]{1,0:T(8,128)(2,1)S(1)} %collective-permute-done.7.refs_2_), channel_id=1, source_target_pairs={{16,0},{32,16},{48,32},{64,48},{80,64},{96,80},{112,96},{0,112},{1... | collective-permute-start | bytes 294920 | tf_op jit(solution)/shard_map/ppermute | solution.py:23
  36.7 1.9 collective-permute-done.10.refs_6_
  38.6 3.3 %collective-permute-done.12.refs_7_ = bf16[32,1536]{1,0:T(8,128)(2,1)S(1)} collective-permute-done((bf16[32,1536]{1,0:T(8,128)(2,1)}, bf16[32,1536]{1,0:T(8,128)(2,1)S(1)}, u32[]{:S(2)}, u32[]{:S(2)}) %collective-permute-start.12) | collective-permute-done | bytes 98336 | tf_op jit(solution)/shard_map/ppermute | solution.py:23
  43.2 5.1 %collective-permute-done.9.refs_4_ = bf16[32,1536]{1,0:T(8,128)(2,1)S(1)} collective-permute-done((bf16[32,1536]{1,0:T(8,128)(2,1)S(1)}, bf16[32,1536]{1,0:T(8,128)(2,1)S(1)}, u32[]{:S(2)}, u32[]{:S(2)}) %collective-permute-start.9) | collective-permute-done | bytes 98336 | tf_op jit(solution)/shard_map/ppermute | solution.py:23
  48.4 1.5 collective-permute-done.11.refs_5_
  51.4 2.2 %collective-permute-start.13 = (bf16[256,1536]{1,0:T(8,128)(2,1)S(1)}, bf16[256,1536]{1,0:T(8,128)(2,1)S(1)}, u32[]{:S(2)}, u32[]{:S(2)}) collective-permute-start(bf16[256,1536]{1,0:T(8,128)(2,1)S(1)} %bitcast.24), channel_id=1, source_target_pairs={{0,128},{128,0},{1,129},{129,1},{2,130},{130,2},{3,131},{131,3},{4... | collective-permute-start | bytes 2359304 | tf_op jit(solution)/shard_map/ppermute | solution.py:27
  53.6 2.0 collective-permute-start.15
  56.4 1.1 pad_maximum_fusion
  58.3 9.4 %collective-permute-done.13.refs_4_ = bf16[256,1536]{1,0:T(8,128)(2,1)S(1)} collective-permute-done((bf16[256,1536]{1,0:T(8,128)(2,1)S(1)}, bf16[256,1536]{1,0:T(8,128)(2,1)S(1)}, u32[]{:S(2)}, u32[]{:S(2)}) %collective-permute-start.13) | collective-permute-done | bytes 786464 | tf_op jit(solution)/shard_map/ppermute | solution.py:27
  67.7 1.0 collective-permute-done.14.refs_1_
  70.9 1.5 all-gather.2.cloned.1.call-done.go
  72.4 1.9 copy-done.2
  74.3 3.3 %shard_map.104 = (f32[2,256,512]{2,1,0:T(8,128)S(1)}, bf16[2,256,512]{2,1,0:T(8,128)(2,1)S(1)}) custom-call(s32[4]{0:T(128)S(1)} %pad_add_fusion.place, bf16[1024,1536]{1,0:T(8,128)(2,1)S(1)} %copy-done.2, bf16[512,1536]{1,0:T(8,128)(2,1)S(1)} %copy-done.4), custom_call_target="tpu_custom_call" | custom-call | flops 1610612736 | bytes 6291456 | tf_op jit(solution)/shard_map/pallas_call | solution.py:74
  78.1 1.5 collective-permute-done.16
  79.8 1.5 collective-permute-start.17
  81.5 3.1 %shard_map.105 = bf16[512,1536]{1,0:T(8,128)(2,1)S(1)} custom-call(s32[4]{0:T(128)S(1)} %pad_add_fusion.place, bf16[2,256,512]{2,1,0:T(8,128)(2,1)S(1)} %fusion.12.hidden, bf16[2,256,512]{2,1,0:T(8,128)(2,1)S(1)} %collective-permute-done.5.hidden_other, bf16[1024,1536]{1,0:T(8,128)(2,1)S(1)} %copy-done.3), custom_call_target="tpu_custom_call" | custom-call | flops 1610612736 | bytes 6291456 | tf_op jit(solution)/shard_map/pallas_call | solution.py:135
  84.5 14.6 %collective-permute-done.18.refs_2_ = bf16[256,1536]{1,0:T(8,128)(2,1)S(1)} collective-permute-done((bf16[256,1536]{1,0:T(8,128)(2,1)S(1)}, bf16[256,1536]{1,0:T(8,128)(2,1)S(1)}, u32[]{:S(2)}, u32[]{:S(2)}) %collective-permute-start.18) | collective-permute-done | bytes 786464 | tf_op jit(solution)/shard_map/ppermute | solution.py:23
  100.5 1.4 collective-permute-done.19.gg_other.refs_9_
  102.7 5.6 %shard_map.106 = bf16[1024,1536]{1,0:T(8,128)(2,1)} custom-call(s32[4]{0:T(128)S(1)} %pad_add_fusion.place, bf16[2,256,512]{2,1,0:T(8,128)(2,1)S(1)} %get-tuple-element.51.gg.refs_8_, bf16[2,256,512]{2,1,0:T(8,128)(2,1)S(1)} %collective-permute-done.19.gg_other.refs_9_, bf16[2,256,512]{2,1,0:T(8,128)(2,1)S(1)} %get-tuple-element.50.gu.refs_10_, ...), custom_call_target="tpu_custom_call" | custom-call | flops 3221225472 | bytes 8388608 | tf_op jit(solution)/shard_map/pallas_call | solution.py:106
  109.9 1.6 collective-permute-start.27
  112.2 12.7 %collective-permute-done.27.refs_12_ = bf16[2,256,512]{2,1,0:T(8,128)(2,1)} collective-permute-done((bf16[2,256,512]{2,1,0:T(8,128)(2,1)S(1)}, bf16[2,256,512]{2,1,0:T(8,128)(2,1)}, u32[]{:S(2)}, u32[]{:S(2)}) %collective-permute-start.27) | collective-permute-done | bytes 524320 | tf_op jit(solution)/shard_map/ppermute | solution.py:27
  124.9 10.4 %collective-permute-done.28.refs_14_ = bf16[2,256,512]{2,1,0:T(8,128)(2,1)} collective-permute-done((bf16[2,256,512]{2,1,0:T(8,128)(2,1)S(1)}, bf16[2,256,512]{2,1,0:T(8,128)(2,1)}, u32[]{:S(2)}, u32[]{:S(2)}) %collective-permute-start.28) | collective-permute-done | bytes 524320 | tf_op jit(solution)/shard_map/ppermute | solution.py:27
  135.3 1.5 collective-permute-start.31
  139.3 19.8 %collective-permute-done.25.refs_6_ = bf16[256,1536]{1,0:T(8,128)(2,1)} collective-permute-done((bf16[256,1536]{1,0:T(8,128)(2,1)}, bf16[256,1536]{1,0:T(8,128)(2,1)}, u32[]{:S(2)}, u32[]{:S(2)}) %collective-permute-start.25) | collective-permute-done | bytes 786464 | tf_op jit(solution)/shard_map/ppermute | solution.py:23
  159.1 14.6 %collective-permute-done.26.refs_7_ = bf16[256,1536]{1,0:T(8,128)(2,1)} collective-permute-done((bf16[256,1536]{1,0:T(8,128)(2,1)}, bf16[256,1536]{1,0:T(8,128)(2,1)}, u32[]{:S(2)}, u32[]{:S(2)}) %collective-permute-start.26) | collective-permute-done | bytes 786464 | tf_op jit(solution)/shard_map/ppermute | solution.py:23
  173.7 1.1 copy-done.8
  174.8 1.1 copy-done.10
  175.9 1.1 copy-done.12
  177.1 1.1 copy-done.14
  178.2 1.1 copy-done.16
  179.3 1.0 copy-done.18
  180.4 1.0 copy-done.20
  181.4 11.1 %shard_map.107 = (bf16[1536,512]{1,0:T(8,128)(2,1)}, bf16[1536,512]{1,0:T(8,128)(2,1)}) custom-call(s32[4]{0:T(128)S(1)} %pad_add_fusion.place, bf16[256,1536]{1,0:T(8,128)(2,1)S(1)} %bitcast.28, bf16[256,1536]{1,0:T(8,128)(2,1)S(1)} %copy-done.10, bf16[256,1536]{1,0:T(8,128)(2,1)S(1)} %copy-done.14, bf16[256,1536]{1,0:T(8,128)(2,1)S(1)} %copy-done.12, ...), custom_call_target="tpu_custom_call" | custom-call | flops 6442450944 | bytes 16777216 | tf_op jit(solution)/shard_map/pallas_call | solution.py:178
  192.5 1.0 dynamic-slice_bitcast_fusion.2
  193.6 2.3 %collective-permute-start.22 = (bf16[32,1536]{1,0:T(8,128)(2,1)S(1)}, bf16[32,1536]{1,0:T(8,128)(2,1)S(1)}, u32[]{:S(2)}, u32[]{:S(2)}) collective-permute-start(bf16[32,1536]{1,0:T(8,128)(2,1)S(1)} %get-tuple-element.58), channel_id=1, source_target_pairs={{8,0},{12,4},{0,8},{4,12},{9,1},{13,5},{1,9},{5,13},{10,2},{14,6},... | collective-permute-start | bytes 294920 | tf_op jit(solution)/shard_map/ppermute | solution.py:23
  196.9 3.0 %add_convert_fusion = bf16[512,1536]{1,0:T(8,128)(2,1)} fusion(bf16[512,1536]{1,0:T(8,128)(2,1)} %collective-permute-done.31, bf16[512,1536]{1,0:T(8,128)(2,1)S(1)} %shard_map.105), kind=kLoop, calls=%fused_computation | loop fusion | flops 3145728 | bytes 4718592 | tf_op jit(solution)/shard_map/convert_element_type | solution.py:247
  199.9 1.4 collective-permute-done.21
  201.9 1.6 fusion.15
  (88 shorter events, 18.3 us)
Async XLA Ops:
  7.2 65.2 %all-gather.2.cloned.1.call-start = ((), (), s32[]{:S(2)}) async-start(), calls=%async_computation.1 | async-start | bytes 3538944 | tf_op jit(solution)/shard_map/all_gather | solution.py:208
  7.2 7.6 %collective-permute-start = (bf16[32,1536]{1,0:T(8,128)(2,1)}, bf16[32,1536]{1,0:T(8,128)(2,1)S(1)}, u32[]{:S(2)}, u32[]{:S(2)}) collective-permute-start(bf16[32,1536]{1,0:T(8,128)(2,1)} %refs_0_.2), channel_id=1, source_target_pairs={{4,0},{8,4},{12,8},{0,12},{5,1},{9,5},{13,9},{1,13},{6,2},{10,6},{... | collective-permute-start | bytes 294920 | tf_op jit(solution)/shard_map/ppermute | solution.py:23
  10.3 7.1 %collective-permute-start.1 = (bf16[32,1536]{1,0:T(8,128)(2,1)}, bf16[32,1536]{1,0:T(8,128)(2,1)S(1)}, u32[]{:S(2)}, u32[]{:S(2)}) collective-permute-start(bf16[32,1536]{1,0:T(8,128)(2,1)} %refs_0_.2), channel_id=1, source_target_pairs={{8,0},{12,4},{0,8},{4,12},{9,1},{13,5},{1,9},{5,13},{10,2},{14,6},... | collective-permute-start | bytes 294920 | tf_op jit(solution)/shard_map/ppermute | solution.py:23
  10.9 7.4 %collective-permute-start.2 = (bf16[32,1536]{1,0:T(8,128)(2,1)}, bf16[32,1536]{1,0:T(8,128)(2,1)S(1)}, u32[]{:S(2)}, u32[]{:S(2)}) collective-permute-start(bf16[32,1536]{1,0:T(8,128)(2,1)} %refs_0_.2), channel_id=1, source_target_pairs={{12,0},{0,4},{4,8},{8,12},{13,1},{1,5},{5,9},{9,13},{14,2},{2,6},{... | collective-permute-start | bytes 294920 | tf_op jit(solution)/shard_map/ppermute | solution.py:23
  19.3 36.4 %copy-start.23 = (bf16[256,512]{1,0:T(8,128)(2,1)S(1)}, bf16[256,512]{1,0:T(8,128)(2,1)}, u32[]{:S(2)}) copy-start(bf16[256,512]{1,0:T(8,128)(2,1)} %param.10) | copy-start | bytes 786436
  20.6 35.1 %copy-start.24 = (bf16[256,512]{1,0:T(8,128)(2,1)S(1)}, bf16[256,512]{1,0:T(8,128)(2,1)}, u32[]{:S(2)}) copy-start(bf16[256,512]{1,0:T(8,128)(2,1)} %param.9) | copy-start | bytes 786436
  20.6 171.9 %reduce-scatter.2.cloned.1.call-start = ((), (), s32[]{:S(2)}) async-start(), calls=%async_computation.2 | async-start | bytes 3538944 | tf_op jit(solution)/shard_map/reduce_scatter | solution.py:240
  20.7 35.0 %collective-permute-start.4 = (bf16[256,512]{1,0:T(8,128)(2,1)}, bf16[256,512]{1,0:T(8,128)(2,1)S(1)}, u32[]{:S(2)}, u32[]{:S(2)}) collective-permute-start(bf16[256,512]{1,0:T(8,128)(2,1)} %param.10), channel_id=1, source_target_pairs={{0,2},{2,0},{1,3},{3,1},{4,6},{6,4},{5,7},{7,5},{8,10},{10,8},{9,1... | collective-permute-start | bytes 786440 | tf_op jit(solution)/shard_map/ppermute | solution.py:27
  22.9 10.8 %collective-permute-start.7 = (bf16[32,1536]{1,0:T(8,128)(2,1)}, bf16[32,1536]{1,0:T(8,128)(2,1)S(1)}, u32[]{:S(2)}, u32[]{:S(2)}) collective-permute-start(bf16[32,1536]{1,0:T(8,128)(2,1)} %refs_0_.3), channel_id=1, source_target_pairs={{32,0},{48,16},{64,32},{80,48},{96,64},{112,80},{0,96},{16,112},{3... | collective-permute-start | bytes 294920 | tf_op jit(solution)/shard_map/ppermute | solution.py:23
  29.2 9.4 %collective-permute-start.10 = (bf16[32,1536]{1,0:T(8,128)(2,1)}, bf16[32,1536]{1,0:T(8,128)(2,1)S(1)}, u32[]{:S(2)}, u32[]{:S(2)}) collective-permute-start(bf16[32,1536]{1,0:T(8,128)(2,1)} %refs_0_.3), channel_id=1, source_target_pairs={{96,0},{112,16},{0,32},{16,48},{32,64},{48,80},{64,96},{80,112},{9... | collective-permute-start | bytes 294920 | tf_op jit(solution)/shard_map/ppermute | solution.py:23
  29.2 12.8 %collective-permute-start.12 = (bf16[32,1536]{1,0:T(8,128)(2,1)}, bf16[32,1536]{1,0:T(8,128)(2,1)S(1)}, u32[]{:S(2)}, u32[]{:S(2)}) collective-permute-start(bf16[32,1536]{1,0:T(8,128)(2,1)} %refs_0_.3), channel_id=1, source_target_pairs={{112,0},{0,16},{16,32},{32,48},{48,64},{64,80},{80,96},{96,112},{1... | collective-permute-start | bytes 294920 | tf_op jit(solution)/shard_map/ppermute | solution.py:23
  30.2 11.8 %collective-permute-start.6 = (bf16[32,1536]{1,0:T(8,128)(2,1)}, bf16[32,1536]{1,0:T(8,128)(2,1)S(1)}, u32[]{:S(2)}, u32[]{:S(2)}) collective-permute-start(bf16[32,1536]{1,0:T(8,128)(2,1)} %refs_0_.3), channel_id=1, source_target_pairs={{16,0},{32,16},{48,32},{64,48},{80,64},{96,80},{112,96},{0,112},{1... | collective-permute-start | bytes 294920 | tf_op jit(solution)/shard_map/ppermute | solution.py:23
  33.7 9.6 %collective-permute-start.8 = (bf16[32,1536]{1,0:T(8,128)(2,1)S(1)}, bf16[32,1536]{1,0:T(8,128)(2,1)S(1)}, u32[]{:S(2)}, u32[]{:S(2)}) collective-permute-start(bf16[32,1536]{1,0:T(8,128)(2,1)S(1)} %collective-permute-done.7.refs_2_), channel_id=1, source_target_pairs={{16,0},{32,16},{48,32},{64,48},{80,64},{96,80},{112,96},{0,112},{1... | collective-permute-start | bytes 294920 | tf_op jit(solution)/shard_map/ppermute | solution.py:23
  38.6 9.7 %collective-permute-start.9 = (bf16[32,1536]{1,0:T(8,128)(2,1)S(1)}, bf16[32,1536]{1,0:T(8,128)(2,1)S(1)}, u32[]{:S(2)}, u32[]{:S(2)}) collective-permute-start(bf16[32,1536]{1,0:T(8,128)(2,1)S(1)} %collective-permute-done.7.refs_2_), channel_id=1, source_target_pairs={{32,0},{48,16},{64,32},{80,48},{96,64},{112,80},{0,96},{16,112},{3... | collective-permute-start | bytes 294920 | tf_op jit(solution)/shard_map/ppermute | solution.py:23
  42.0 7.9 %collective-permute-start.11 = (bf16[32,1536]{1,0:T(8,128)(2,1)S(1)}, bf16[32,1536]{1,0:T(8,128)(2,1)S(1)}, u32[]{:S(2)}, u32[]{:S(2)}) collective-permute-start(bf16[32,1536]{1,0:T(8,128)(2,1)S(1)} %collective-permute-done.10.refs_6_), channel_id=1, source_target_pairs={{112,0},{0,16},{16,32},{32,48},{48,64},{64,80},{80,96},{96,112},{1... | collective-permute-start | bytes 294920 | tf_op jit(solution)/shard_map/ppermute | solution.py:23
  42.0 13.7 %collective-permute-start.3 = (bf16[256,512]{1,0:T(8,128)(2,1)}, bf16[256,512]{1,0:T(8,128)(2,1)S(1)}, u32[]{:S(2)}, u32[]{:S(2)}) collective-permute-start(bf16[256,512]{1,0:T(8,128)(2,1)} %param.9), channel_id=1, source_target_pairs={{0,2},{2,0},{1,3},{3,1},{4,6},{6,4},{5,7},{7,5},{8,10},{10,8},{9,1... | collective-permute-start | bytes 786440 | tf_op jit(solution)/shard_map/ppermute | solution.py:27
  51.4 16.4 %collective-permute-start.13 = (bf16[256,1536]{1,0:T(8,128)(2,1)S(1)}, bf16[256,1536]{1,0:T(8,128)(2,1)S(1)}, u32[]{:S(2)}, u32[]{:S(2)}) collective-permute-start(bf16[256,1536]{1,0:T(8,128)(2,1)S(1)} %bitcast.24), channel_id=1, source_target_pairs={{0,128},{128,0},{1,129},{129,1},{2,130},{130,2},{3,131},{131,3},{4... | collective-permute-start | bytes 2359304 | tf_op jit(solution)/shard_map/ppermute | solution.py:27
  53.6 15.2 %collective-permute-start.14 = (bf16[256,1536]{1,0:T(8,128)(2,1)S(1)}, bf16[256,1536]{1,0:T(8,128)(2,1)S(1)}, u32[]{:S(2)}, u32[]{:S(2)}) collective-permute-start(bf16[256,1536]{1,0:T(8,128)(2,1)S(1)} %bitcast.25), channel_id=1, source_target_pairs={{4,0},{8,4},{12,8},{0,12},{5,1},{9,5},{13,9},{1,13},{6,2},{10,6},{... | collective-permute-start | bytes 2359304 | tf_op jit(solution)/shard_map/ppermute | solution.py:23
  53.6 16.4 %collective-permute-start.15 = (bf16[256,1536]{1,0:T(8,128)(2,1)S(1)}, bf16[256,1536]{1,0:T(8,128)(2,1)S(1)}, u32[]{:S(2)}, u32[]{:S(2)}) collective-permute-start(bf16[256,1536]{1,0:T(8,128)(2,1)S(1)} %bitcast.26), channel_id=1, source_target_pairs={{12,0},{0,4},{4,8},{8,12},{13,1},{1,5},{5,9},{9,13},{14,2},{2,6},{... | collective-permute-start | bytes 2359304 | tf_op jit(solution)/shard_map/ppermute | solution.py:23
  55.8 16.6 %copy-start.4 = (bf16[512,1536]{1,0:T(8,128)(2,1)S(1)}, bf16[512,1536]{1,0:T(8,128)(2,1)}, u32[]{:S(2)}) copy-start(bf16[512,1536]{1,0:T(8,128)(2,1)} %w_down.1) | copy-start | bytes 4718596
  56.1 2.2 %collective-permute-start.5 = (bf16[2,256,512]{2,1,0:T(8,128)(2,1)S(1)}, bf16[2,256,512]{2,1,0:T(8,128)(2,1)S(1)}, u32[]{:S(2)}, u32[]{:S(2)}) collective-permute-start(bf16[2,256,512]{2,1,0:T(8,128)(2,1)S(1)} %fusion.12.hidden), channel_id=1, source_target_pairs={{0,1},{1,0},{2,3},{3,2},{4,5},{5,4},{6,7},{7,6},{8,9},{9,8},{10,11... | collective-permute-start | bytes 1572872 | tf_op jit(solution)/shard_map/ppermute | solution.py:27
  72.4 1.9 copy-start.2
  77.6 2.0 collective-permute-start.16
  77.7 21.5 %collective-permute-start.18 = (bf16[256,1536]{1,0:T(8,128)(2,1)S(1)}, bf16[256,1536]{1,0:T(8,128)(2,1)S(1)}, u32[]{:S(2)}, u32[]{:S(2)}) collective-permute-start(bf16[256,1536]{1,0:T(8,128)(2,1)S(1)} %bitcast.27), channel_id=1, source_target_pairs={{8,0},{12,4},{0,8},{4,12},{9,1},{13,5},{1,9},{5,13},{10,2},{14,6},... | collective-permute-start | bytes 2359304 | tf_op jit(solution)/shard_map/ppermute | solution.py:23
  79.6 1.9 copy-start.3
  79.8 19.4 %copy-start.21 = (bf16[2,256,512]{2,1,0:T(8,128)(2,1)S(1)}, bf16[2,256,512]{2,1,0:T(8,128)(2,1)}, u32[]{:S(2)}) copy-start(bf16[2,256,512]{2,1,0:T(8,128)(2,1)} %get-tuple-element.34) | copy-start | bytes 1572868
  79.8 19.4 %copy-start.22 = (bf16[2,256,512]{2,1,0:T(8,128)(2,1)S(1)}, bf16[2,256,512]{2,1,0:T(8,128)(2,1)}, u32[]{:S(2)}) copy-start(bf16[2,256,512]{2,1,0:T(8,128)(2,1)} %get-tuple-element.33) | copy-start | bytes 1572868
  79.8 19.3 %collective-permute-start.17 = (bf16[2,256,512]{2,1,0:T(8,128)(2,1)S(1)}, bf16[2,256,512]{2,1,0:T(8,128)(2,1)S(1)}, u32[]{:S(2)}, u32[]{:S(2)}) collective-permute-start(bf16[2,256,512]{2,1,0:T(8,128)(2,1)S(1)} %get-tuple-element.48), channel_id=1, source_target_pairs={{0,2},{2,0},{1,3},{3,1},{4,6},{6,4},{5,7},{7,5},{8,10},{10,8},{9,1... | collective-permute-start | bytes 1572872 | tf_op jit(solution)/shard_map/ppermute | solution.py:27
  99.1 3.5 %copy-start.5 = (bf16[1536,512]{1,0:T(8,128)(2,1)S(1)}, bf16[1536,512]{1,0:T(8,128)(2,1)}, u32[]{:S(2)}) copy-start(bf16[1536,512]{1,0:T(8,128)(2,1)} %w_gate.1) | copy-start | bytes 4718596
  99.2 3.5 %copy-start.6 = (bf16[1536,512]{1,0:T(8,128)(2,1)S(1)}, bf16[1536,512]{1,0:T(8,128)(2,1)}, u32[]{:S(2)}) copy-start(bf16[1536,512]{1,0:T(8,128)(2,1)} %w_up.1) | copy-start | bytes 4718596
  100.0 1.9 collective-permute-start.19
  100.0 2.7 %collective-permute-start.20 = (bf16[2,256,512]{2,1,0:T(8,128)(2,1)S(1)}, bf16[2,256,512]{2,1,0:T(8,128)(2,1)S(1)}, u32[]{:S(2)}, u32[]{:S(2)}) collective-permute-start(bf16[2,256,512]{2,1,0:T(8,128)(2,1)S(1)} %get-tuple-element.50.gu.refs_10_), channel_id=1, source_target_pairs={{0,1},{1,0},{2,3},{3,2},{4,5},{5,4},{6,7},{7,6},{8,9},{9,8},{10,11... | collective-permute-start | bytes 1572872 | tf_op jit(solution)/shard_map/ppermute | solution.py:27
  109.9 15.0 %collective-permute-start.27 = (bf16[2,256,512]{2,1,0:T(8,128)(2,1)S(1)}, bf16[2,256,512]{2,1,0:T(8,128)(2,1)}, u32[]{:S(2)}, u32[]{:S(2)}) collective-permute-start(bf16[2,256,512]{2,1,0:T(8,128)(2,1)S(1)} %get-tuple-element.51.gg.refs_8_), channel_id=1, source_target_pairs={{0,128},{128,0},{1,129},{129,1},{2,130},{130,2},{3,131},{131,3},{4... | collective-permute-start | bytes 1572872 | tf_op jit(solution)/shard_map/ppermute | solution.py:27
  111.5 23.8 %collective-permute-start.28 = (bf16[2,256,512]{2,1,0:T(8,128)(2,1)S(1)}, bf16[2,256,512]{2,1,0:T(8,128)(2,1)}, u32[]{:S(2)}, u32[]{:S(2)}) collective-permute-start(bf16[2,256,512]{2,1,0:T(8,128)(2,1)S(1)} %get-tuple-element.50.gu.refs_10_), channel_id=1, source_target_pairs={{0,128},{128,0},{1,129},{129,1},{2,130},{130,2},{3,131},{131,3},{4... | collective-permute-start | bytes 1572872 | tf_op jit(solution)/shard_map/ppermute | solution.py:27
  112.1 25.8 %collective-permute-start.24 = (bf16[256,1536]{1,0:T(8,128)(2,1)}, bf16[256,1536]{1,0:T(8,128)(2,1)S(1)}, u32[]{:S(2)}, u32[]{:S(2)}) collective-permute-start(bf16[256,1536]{1,0:T(8,128)(2,1)} %copy-done.7), channel_id=1, source_target_pairs={{4,0},{8,4},{12,8},{0,12},{5,1},{9,5},{13,9},{1,13},{6,2},{10,6},{... | collective-permute-start | bytes 2359304 | tf_op jit(solution)/shard_map/ppermute | solution.py:23
  135.3 57.2 %collective-permute-start.31 = (bf16[512,1536]{1,0:T(8,128)(2,1)S(1)}, bf16[512,1536]{1,0:T(8,128)(2,1)}, u32[]{:S(2)}, u32[]{:S(2)}) collective-permute-start(bf16[512,1536]{1,0:T(8,128)(2,1)S(1)} %shard_map.105), channel_id=1, source_target_pairs={{0,128},{128,0},{1,129},{129,1},{2,130},{130,2},{3,131},{131,3},{4... | collective-permute-start | bytes 4718600 | tf_op jit(solution)/shard_map/ppermute | solution.py:27
  136.8 22.3 %collective-permute-start.25 = (bf16[256,1536]{1,0:T(8,128)(2,1)}, bf16[256,1536]{1,0:T(8,128)(2,1)}, u32[]{:S(2)}, u32[]{:S(2)}) collective-permute-start(bf16[256,1536]{1,0:T(8,128)(2,1)} %copy-done.7), channel_id=1, source_target_pairs={{8,0},{12,4},{0,8},{4,12},{9,1},{13,5},{1,9},{5,13},{10,2},{14,6},... | collective-permute-start | bytes 2359304 | tf_op jit(solution)/shard_map/ppermute | solution.py:23
  137.1 36.6 %collective-permute-start.26 = (bf16[256,1536]{1,0:T(8,128)(2,1)}, bf16[256,1536]{1,0:T(8,128)(2,1)}, u32[]{:S(2)}, u32[]{:S(2)}) collective-permute-start(bf16[256,1536]{1,0:T(8,128)(2,1)} %copy-done.7), channel_id=1, source_target_pairs={{12,0},{0,4},{4,8},{8,12},{13,1},{1,5},{5,9},{9,13},{14,2},{2,6},{... | collective-permute-start | bytes 2359304 | tf_op jit(solution)/shard_map/ppermute | solution.py:23
  137.8 35.9 %collective-permute-start.29 = (bf16[2,256,512]{2,1,0:T(8,128)(2,1)}, bf16[2,256,512]{2,1,0:T(8,128)(2,1)}, u32[]{:S(2)}, u32[]{:S(2)}) collective-permute-start(bf16[2,256,512]{2,1,0:T(8,128)(2,1)} %collective-permute-done.27.refs_12_), channel_id=1, source_target_pairs={{0,1},{1,0},{2,3},{3,2},{4,5},{5,4},{6,7},{7,6},{8,9},{9,8},{10,11... | collective-permute-start | bytes 1572872 | tf_op jit(solution)/shard_map/ppermute | solution.py:27
  138.8 34.9 %collective-permute-start.30 = (bf16[2,256,512]{2,1,0:T(8,128)(2,1)}, bf16[2,256,512]{2,1,0:T(8,128)(2,1)}, u32[]{:S(2)}, u32[]{:S(2)}) collective-permute-start(bf16[2,256,512]{2,1,0:T(8,128)(2,1)} %collective-permute-done.28.refs_14_), channel_id=1, source_target_pairs={{0,1},{1,0},{2,3},{3,2},{4,5},{5,4},{6,7},{7,6},{8,9},{9,8},{10,11... | collective-permute-start | bytes 1572872 | tf_op jit(solution)/shard_map/ppermute | solution.py:27
  173.7 1.1 copy-start.8
  174.8 1.1 copy-start.10
  175.9 1.1 copy-start.12
  177.1 1.1 copy-start.14
  178.2 1.1 copy-start.16
  193.5 7.8 %collective-permute-start.21 = (bf16[32,1536]{1,0:T(8,128)(2,1)S(1)}, bf16[32,1536]{1,0:T(8,128)(2,1)S(1)}, u32[]{:S(2)}, u32[]{:S(2)}) collective-permute-start(bf16[32,1536]{1,0:T(8,128)(2,1)S(1)} %get-tuple-element.56), channel_id=1, source_target_pairs={{12,0},{0,4},{4,8},{8,12},{13,1},{1,5},{5,9},{9,13},{14,2},{2,6},{... | collective-permute-start | bytes 294920 | tf_op jit(solution)/shard_map/ppermute | solution.py:23
  193.6 7.7 %collective-permute-start.22 = (bf16[32,1536]{1,0:T(8,128)(2,1)S(1)}, bf16[32,1536]{1,0:T(8,128)(2,1)S(1)}, u32[]{:S(2)}, u32[]{:S(2)}) collective-permute-start(bf16[32,1536]{1,0:T(8,128)(2,1)S(1)} %get-tuple-element.58), channel_id=1, source_target_pairs={{8,0},{12,4},{0,8},{4,12},{9,1},{13,5},{1,9},{5,13},{10,2},{14,6},... | collective-permute-start | bytes 294920 | tf_op jit(solution)/shard_map/ppermute | solution.py:23
  196.0 5.9 %collective-permute-start.23 = (bf16[32,1536]{1,0:T(8,128)(2,1)S(1)}, bf16[32,1536]{1,0:T(8,128)(2,1)S(1)}, u32[]{:S(2)}, u32[]{:S(2)}) collective-permute-start(bf16[32,1536]{1,0:T(8,128)(2,1)S(1)} %get-tuple-element.57), channel_id=1, source_target_pairs={{4,0},{8,4},{12,8},{0,12},{5,1},{9,5},{13,9},{1,13},{6,2},{10,6},{... | collective-permute-start | bytes 294920 | tf_op jit(solution)/shard_map/ppermute | solution.py:23
  (11 other events, 10.1 us)
Sparse Core Ops, SparseCore 0:
  20.7 51.5 all-gather.1
  110.1 43.0 reduce-scatter.1

commit v2 on v1

v2 whole, which is shorter than its diff:
```python
import functools

import jax
import jax.numpy as jnp
from jax import lax
from jax.experimental import pallas as pl
from jax.experimental.pallas import tpu as pltpu
from jax.sharding import Mesh, PartitionSpec as P

F32, BF16 = jnp.float32, jnp.bfloat16
NZ, NY = 8, 4
WIDE, SIDE = 1024, 512
FIRST = 64
VMEM = pl.BlockSpec(memory_space=pltpu.VMEM)
SMEM = pl.BlockSpec(memory_space=pltpu.SMEM)
HBM = pl.BlockSpec(memory_space=pltpu.HBM)


def dot(left, right, left_dim, right_dim):
    dims = (((left_dim,), (right_dim,)), ((), ()))
    return lax.dot_general(left, right, dims, preferred_element_type=F32)


def from_ahead(x, axis, n, k):
    return lax.ppermute(x, axis, [((d + k) % n, d) for d in range(n)])


def swap(x, axis):
    return lax.ppermute(x, axis, [(0, 1), (1, 0)])


def params(mib):
    return pltpu.CompilerParams(vmem_limit_bytes=mib << 20)


def prepare_kernel(layer_input, grad_output, wide, mixed):
    wide[...] = grad_output[:, :WIDE]
    mixed[:, :1536] = layer_input[...]
    mixed[:, 1536:] = grad_output[:, WIDE:]


def prepare(layer_input, grad_output):
    return pl.pallas_call(
        prepare_kernel,
        out_shape=(
            jax.ShapeDtypeStruct((32, WIDE), BF16),
            jax.ShapeDtypeStruct((32, 1536 + SIDE), BF16),
        ),
        in_specs=[VMEM] * 2,
        out_specs=(VMEM,) * 2,
        compiler_params=params(4),
    )(layer_input, grad_output)


def arrange_kernel(n, slot, cuts, place, *refs):
    for k in range(n):
        there = (place[slot] + k) % n
        for out, (low, high) in zip(refs[n:], cuts):
            out[there] = refs[k][:, low:high]


def arrange(place, slot, parts, cuts):
    n, rows = len(parts), parts[0].shape[0]
    outs = pl.pallas_call(
        functools.partial(arrange_kernel, n, slot, cuts),
        out_shape=tuple(jax.ShapeDtypeStruct((n, rows, high - low), BF16) for low, high in cuts),
        in_specs=[SMEM] + [VMEM] * n,
        out_specs=(VMEM,) * len(cuts),
        compiler_params=params(6),
    )(place, *parts)
    return [out.reshape(n * rows, -1) for out in outs]


def hidden_grad_kernel(place, go, s0, s1, s2, s3, w_down, mine, send, side, rows, sems):
    copies = [
        pltpu.make_async_copy(go.at[pl.ds(512 * half, 512)], rows.at[half], sems.at[half])
        for half in range(2)
    ]
    for copy in copies:
        copy.start()
    for k, piece in enumerate((s0, s1, s2, s3)):
        there = (place[1] + k) % NY
        for z in range(NZ):
            side[z, there] = piece[32 * z:32 * z + 32, :]
    for half, copy in enumerate(copies):
        copy.wait()
        part = dot(rows[half], w_down[:, :WIDE], 1, 1)
        part = part + dot(side[4 * half:4 * half + 4].reshape(512, SIDE), w_down[:, WIDE:], 1, 1)
        for which in range(2):
            block = part[256 * which:256 * which + 256]

            @pl.when(place[3] == which)
            def _():
                mine[half] = block

            @pl.when(place[3] != which)
            def _():
                send[half] = block.astype(BF16)


def hidden_grad(place, go, sides, w_down):
    return pl.pallas_call(
        hidden_grad_kernel,
        out_shape=(
            jax.ShapeDtypeStruct((2, 256, 512), F32),
            jax.ShapeDtypeStruct((2, 256, 512), BF16),
            jax.ShapeDtypeStruct((NZ, NY, 32, SIDE), BF16),
        ),
        in_specs=[SMEM, HBM] + [VMEM] * 5,
        out_specs=(VMEM,) * 3,
        scratch_shapes=[pltpu.VMEM((2, 512, WIDE), BF16), pltpu.SemaphoreType.DMA((2,))],
        compiler_params=params(16),
    )(place, go, *sides, w_down)


def input_grad_kernel(place, gg, gg_other, gu, gu_other, w_gate, w_up, out):
    def emit(gate_ref, up_ref, core):
        gate_rows, up_rows = gate_ref[...].reshape(512, 512), up_ref[...].reshape(512, 512)
        total = (dot(gate_rows, w_gate[...], 1, 1) + dot(up_rows, w_up[...], 1, 1)).astype(BF16)
        for half in range(2):
            start = pl.multiple_of(512 * half + 256 * core, 256)
            out[pl.ds(start, 256), :] = total[256 * half:256 * half + 256]

    emit(gg, gu, place[3])
    emit(gg_other, gu_other, 1 - place[3])


def input_grad(place, gg, gg_other, gu, gu_other, w_gate, w_up):
    weight = pl.BlockSpec((512, 512), lambda i: (i, 0))
    return pl.pallas_call(
        input_grad_kernel,
        grid=(3,),
        out_shape=jax.ShapeDtypeStruct((1024, 1536), BF16),
        in_specs=[SMEM] + [VMEM] * 4 + [weight] * 2,
        out_specs=pl.BlockSpec((1024, 512), lambda i: (0, i)),
        compiler_params=params(16),
    )(place, gg, gg_other, gu, gu_other, w_gate, w_up)


def fill_natural(place, own, other, rows, col):
    for half in range(2):
        base = half * 512
        start = pl.multiple_of(base + place[3] * 256, 256)
        rows[pl.ds(start, 256), col:col + 512] = own[half]
        start = pl.multiple_of(base + (1 - place[3]) * 256, 256)
        rows[pl.ds(start, 256), col:col + 512] = other[half]


def down_kernel(place, hidden, hidden_other, go, side, first, rest, rows):
    step = pl.program_id(0)

    @pl.when(step == 0)
    def _():
        fill_natural(place, hidden, hidden_other, rows, 0)

    def emit(right):
        total = dot(rows[...], right, 0, 0).astype(BF16)
        first[...] = total[:FIRST]
        rest[...] = total[FIRST:]

    @pl.when(step < WIDE // 512)
    def _():
        emit(go[...])

    @pl.when(step == WIDE // 512)
    def _():
        emit(side[...].reshape(1024, SIDE))


def down_grad(place, hidden, hidden_other, go, side):
    return pl.pallas_call(
        down_kernel,
        grid=(3,),
        out_shape=(
            jax.ShapeDtypeStruct((FIRST, 1536), BF16),
            jax.ShapeDtypeStruct((512 - FIRST, 1536), BF16),
        ),
        in_specs=[SMEM, VMEM, VMEM, pl.BlockSpec((1024, 512), lambda i: (0, jnp.minimum(i, 1))), VMEM],
        out_specs=(
            pl.BlockSpec((FIRST, 512), lambda i: (0, i)),
            pl.BlockSpec((512 - FIRST, 512), lambda i: (0, i)),
        ),
        scratch_shapes=[pltpu.VMEM((1024, 512), BF16)],
        compiler_params=params(12),
    )(place, hidden, hidden_other, go, side)


def fill_rolled(place, own, other, rows, col):
    for half in range(2):
        for pair in range(2):
            for y in range(NY):
                k = (y - place[1] + NY) % NY
                lines = pl.ds(pair * 128 + y * 32, 32)
                z_own = 4 * half + 2 * place[3] + pair
                rows[k, z_own, :, col:col + 512] = own[half, lines, :]
                z_other = 4 * half + 2 * (1 - place[3]) + pair
                rows[k, z_other, :, col:col + 512] = other[half, lines, :]


def weight_kernel(place, *refs):
    pieces, grads, (d_gate, d_up, rows) = refs[:8], refs[8:16], refs[16:]

    @pl.when(pl.program_id(0) == 0)
    def _():
        for replica in range(2):
            fill_rolled(place, *grads[4 * replica:4 * replica + 2], rows.at[replica], 0)
            fill_rolled(place, *grads[4 * replica + 2:4 * replica + 4], rows.at[replica], 512)

    total = jnp.zeros((256, 1024), F32)
    for k, piece in enumerate(pieces):
        total = total + dot(piece[...], rows[k // NY, k % NY].reshape(256, 1024), 0, 0)
    d_gate[...] = total[:, :512].astype(BF16)
    d_up[...] = total[:, 512:].astype(BF16)


def weight_grads(place, pieces, grads):
    tile = pl.BlockSpec((256, 512), lambda i: (i, 0))
    shape = jax.ShapeDtypeStruct((1536, 512), BF16)
    return pl.pallas_call(
        weight_kernel,
        grid=(6,),
        out_shape=(shape, shape),
        in_specs=[SMEM] + [pl.BlockSpec((256, 256), lambda i: (0, i))] * 8 + [VMEM] * 8,
        out_specs=(tile, tile),
        scratch_shapes=[pltpu.VMEM((2, NY, NZ, 32, 1024), BF16)],
        compiler_params=params(18),
    )(place, *pieces, *grads)


def gather_z_near(x):
    return [from_ahead(x, "z", NZ, k) for k in (1, 2, 6, 7)]


def gather_z_far(x, f1, f2, b2, b1):
    f3, b3 = from_ahead(f2, "z", NZ, 1), from_ahead(b2, "z", NZ, 7)
    f4 = from_ahead(f2, "z", NZ, 2)
    return [x, f1, f2, f3, f4, b3, b2, b1]


def ordered(mine, other, index):
    low = jnp.where(index == 0, mine, other)
    high = jnp.where(index == 0, other, mine)
    return jnp.stack([low, high], axis=0)


def body(layer_input, grad_output, gate_saved, up_saved, w_gate, w_up, w_down):
    place = jnp.stack([lax.axis_index(name) for name in ("z", "y", "xh", "core")]).astype(jnp.int32)
    xh = place[2]

    wide, mixed = prepare(layer_input, grad_output)
    wide_parts = [from_ahead(wide, "y", NY, k) for k in (1, 2, 3)]
    near = gather_z_near(mixed)
    wide_parts, near = lax.optimization_barrier((wide_parts, near))
    (go_y,) = arrange(place, 1, [wide] + wide_parts, ((0, WIDE),))
    go = lax.all_gather(go_y, "z", axis=0, tiled=True)
    own_z, side_z = arrange(place, 0, gather_z_far(mixed, *near), ((0, 1536), (1536, 1536 + SIDE)))
    sides = [side_z] + [from_ahead(side_z, "y", NY, k) for k in (1, 2, 3)]
    partner_z = swap(own_z, "dp")

    gate = ordered(gate_saved, swap(gate_saved, "xh"), xh)
    up = ordered(up_saved, swap(up_saved, "xh"), xh)
    gate_val, up_val = gate.astype(F32), up.astype(F32)
    hidden = (gate_val * jax.nn.sigmoid(gate_val) * up_val).astype(BF16)
    hidden_other = swap(hidden, "core")
    go, gate, up, hidden, hidden_other, own_z, partner_z, *sides = lax.optimization_barrier(
        (go, gate, up, hidden, hidden_other, own_z, partner_z, *sides)
    )

    own1, own3 = from_ahead(own_z, "y", NY, 1), from_ahead(own_z, "y", NY, 3)
    mine, send, side = hidden_grad(place, go, sides, w_down)
    chip = mine + swap(send, "core").astype(F32)
    chip_far = swap(chip.astype(BF16), "xh")
    down_first, down_rest = down_grad(place, hidden, hidden_other, go, side)

    chip, chip_far, down_first, down_rest = lax.optimization_barrier((chip, chip_far, down_first, down_rest))

    first_far = swap(down_first, "dp")
    grad_hidden = chip + chip_far.astype(F32)
    gate_val, up_val = gate.astype(F32), up.astype(F32)
    sigma = jax.nn.sigmoid(gate_val)
    gg = (grad_hidden * up_val * sigma * (1.0 + gate_val * (1.0 - sigma))).astype(BF16)
    gu = (grad_hidden * gate_val * sigma).astype(BF16)
    gg_other, gu_other = swap(gg, "core"), swap(gu, "core")
    gg_other, gu_other, own1, own3, first_far = lax.optimization_barrier((gg_other, gu_other, own1, own3, first_far))
    partial_in = input_grad(place, gg, gg_other, gu, gu_other, w_gate, w_up)
    in_z = lax.psum_scatter(partial_in, "z", scatter_dimension=0, tiled=True).reshape(NY, 32, 1536)

    gg_far, gu_far = swap(gg, "dp"), swap(gu, "dp")
    partner1, partner3 = from_ahead(partner_z, "y", NY, 1), from_ahead(partner_z, "y", NY, 3)
    own2 = from_ahead(own_z, "y", NY, 2)
    gg_far, gu_far, down_rest, partner1, partner3 = lax.optimization_barrier(
        (gg_far, gu_far, down_rest, partner1, partner3)
    )
    rest_far = swap(down_rest, "dp")
    partner2 = from_ahead(partner_z, "y", NY, 2)
    gg_far_other, gu_far_other = swap(gg_far, "core"), swap(gu_far, "core")

    y = place[1]
    slabs = [lax.dynamic_index_in_dim(in_z, (y + k) % NY, 0, keepdims=False) for k in range(NY)]
    total = slabs[0].astype(F32)
    for k in range(1, NY):
        total = total + from_ahead(slabs[k], "y", NY, NY - k).astype(F32)
    grad_input = total.astype(BF16)
    grad_input, own2, partner2, gg_far_other, gu_far_other = lax.optimization_barrier(
        (grad_input, own2, partner2, gg_far_other, gu_far_other)
    )
    pieces = (own_z, own1, own2, own3, partner_z, partner1, partner2, partner3)
    grads = (gg, gg_other, gu, gu_other, gg_far, gg_far_other, gu_far, gu_far_other)
    grad_gate, grad_up = weight_grads(place, pieces, grads)
    grad_gate, grad_up, rest_far = lax.optimization_barrier((grad_gate, grad_up, rest_far))
    first = down_first.astype(F32) + first_far.astype(F32)
    rest = down_rest.astype(F32) + rest_far.astype(F32)
    grad_down = jnp.concatenate([first, rest], axis=0).astype(BF16)
    return grad_input, grad_gate, grad_up, grad_down


def solution(mesh):
    fine = Mesh(mesh.devices.reshape(2, NZ, NY, 2, 2), ("dp", "z", "y", "xh", "core"))
    tokens, col, row = ("dp", "z", "y"), ("xh", "core"), ("z", "y")
    in_specs = (
        P(tokens, col),
        P(tokens, col),
        P(("dp",) + col, row),
        P(("dp",) + col, row),
        P(col, row),
        P(col, row),
        P(row, col),
    )
    out_specs = (P(tokens, col), P(col, row), P(col, row), P(row, col))
    return jax.shard_map(body, mesh=fine, in_specs=in_specs, out_specs=out_specs, check_vma=False)
```

time: 211 us -> 229 us (1.085)
  starting transfers between devices: 36.6 us -> 45.4 us
  local copies, waits for them, and re-layouts: 17.2 us -> 21.5 us
  waiting for transfers between devices: 110 us -> 114 us
    ppermute x13 -> x14, waiting for transfers between devices: 37 us -> 12.8 us  [swap(): return lax.ppermute(x, axis, [(0, 1), (1, 0)])]
    reduce_scatter x1, waiting for transfers between devices: 0.02 us -> 15.4 us  [body(): lax.psum_scatter(partial_in, 'z', scatter_dimension=0, tiled=True)]
    ppermute x19 -> x22, waiting for transfers between devices: 71.7 us -> 84 us  [from_ahead(): return lax.ppermute(x, axis, [((d + k) % n, d) for d in range(n)])]
    ppermute x19 -> x22, starting transfers between devices: 24.7 us -> 31.2 us  [from_ahead(): return lax.ppermute(x, axis, [((d + k) % n, d) for d in range(n)])]
    unnamed x50 -> x70, local copies, waits for them, and re-layouts: 16.2 us -> 19.8 us
    convert_element_type x2 -> x1, other arithmetic: 4.62 us -> 1.73 us  [body(): grad_input = total.astype(BF16)]
    another operation x0 -> x2, other arithmetic: none -> 2.74 us
    ppermute x13 -> x14, starting transfers between devices: 11.9 us -> 14.2 us  [swap(): return lax.ppermute(x, axis, [(0, 1), (1, 0)])]
  transfers between devices with their start and end apart: 34 -> 38, of which waited for: 24 -> 19; matrix products, arithmetic and copies ran while one was open for 2% -> 3% of each run, Pallas kernels for 7% -> 7%
where the time goes in v2:
time: 229 us; the launch traced here: 228 us
  waiting for transfers between devices  114 us (50%)
  starting transfers between devices  45.4 us (20%)
  Pallas kernels  24.5 us (11%)
  local copies, waits for them, and re-layouts  21.5 us (9%)
  between operations  14.3 us (6%)
  other arithmetic  8.11 us (4%)
    ppermute x22, waiting for transfers between devices, from_ahead(): return lax.ppermute(x, axis, [((d + k) % n, d) for d in range(n)])  84 us
    ppermute x22, starting transfers between devices, from_ahead(): return lax.ppermute(x, axis, [((d + k) % n, d) for d in range(n)])  31.2 us
    unnamed x70, local copies, waits for them, and re-layouts  19.8 us
    reduce_scatter x1, waiting for transfers between devices, body(): lax.psum_scatter(partial_in, 'z', scatter_dimension=0, tiled=True)  15.4 us
    ppermute x14, starting transfers between devices, swap(): return lax.ppermute(x, axis, [(0, 1), (1, 0)])  14.2 us
    ppermute x14, waiting for transfers between devices, swap(): return lax.ppermute(x, axis, [(0, 1), (1, 0)])  12.8 us
    pallas_call x1, Pallas kernels, weight_grads(): pl.pallas_call(weight_kernel, grid=(6,), out_shape=(shape, shape), in_spe...  10.2 us
    pallas_call x1, Pallas kernels, input_grad(): pl.pallas_call(input_grad_kernel, grid=(3,), out_shape=jax.ShapeDtypeStru...  5.52 us
  transfers between devices with their start and end apart: 38, of which 19 were waited for; matrix products, arithmetic and copies ran while one was open for 3% of the time, Pallas kernels for 7%

profile of v2, /device:TPU:2, one launch (start us, length us, event | category | flops | bytes accessed | tf_op | source)
XLA Modules:
  0.0 227.9 jit_solution(14010499916171929860)
XLA Ops:
  9.0 3.1 %collective-permute-start = (bf16[32,1024]{1,0:T(8,128)(2,1)S(1)}, bf16[32,1024]{1,0:T(8,128)(2,1)S(1)}, u32[]{:S(2)}, u32[]{:S(2)}) collective-permute-start(bf16[32,1024]{1,0:T(8,128)(2,1)S(1)} %get-tuple-element.55.refs_0_), channel_id=1, source_target_pairs={{4,0},{8,4},{12,8},{0,12},{5,1},{9,5},{13,9},{1,13},{6,2},{10,6},{... | collective-permute-start | bytes 196616 | tf_op jit(solution)/shard_map/ppermute | solution.py:25
  12.7 5.9 %collective-permute-start.3 = (bf16[32,2048]{1,0:T(8,128)(2,1)S(1)}, bf16[32,2048]{1,0:T(8,128)(2,1)S(1)}, u32[]{:S(2)}, u32[]{:S(2)}) collective-permute-start(bf16[32,2048]{1,0:T(8,128)(2,1)S(1)} %get-tuple-element.56.refs_0_), channel_id=1, source_target_pairs={{16,0},{32,16},{48,32},{64,48},{80,64},{96,80},{112,96},{0,112},{1... | collective-permute-start | bytes 393224 | tf_op jit(solution)/shard_map/ppermute | solution.py:25
  18.6 1.5 collective-permute-start.4
  20.0 1.5 collective-permute-start.5
  22.7 4.4 %collective-permute-done.2.refs_3_ = bf16[32,1024]{1,0:T(8,128)(2,1)S(1)} collective-permute-done((bf16[32,1024]{1,0:T(8,128)(2,1)S(1)}, bf16[32,1024]{1,0:T(8,128)(2,1)S(1)}, u32[]{:S(2)}, u32[]{:S(2)}) %collective-permute-start.2) | collective-permute-done | bytes 65568 | tf_op jit(solution)/shard_map/ppermute | solution.py:25
  27.1 2.6 %collective-permute-done.5.refs_6_ = bf16[32,2048]{1,0:T(8,128)(2,1)S(1)} collective-permute-done((bf16[32,2048]{1,0:T(8,128)(2,1)S(1)}, bf16[32,2048]{1,0:T(8,128)(2,1)S(1)}, u32[]{:S(2)}, u32[]{:S(2)}) %collective-permute-start.5) | collective-permute-done | bytes 131104 | tf_op jit(solution)/shard_map/ppermute | solution.py:25
  29.7 1.8 collective-permute-done.6.refs_7_
  31.4 1.3 shard_map.103
  32.8 2.2 collective-permute-start.7
  35.9 1.5 collective-permute-start.12
  37.4 1.4 collective-permute-start.8
  38.8 3.1 %collective-permute-done.10.refs_3_ = bf16[32,2048]{1,0:T(8,128)(2,1)S(1)} collective-permute-done((bf16[32,2048]{1,0:T(8,128)(2,1)S(1)}, bf16[32,2048]{1,0:T(8,128)(2,1)S(1)}, u32[]{:S(2)}, u32[]{:S(2)}) %collective-permute-start.10) | collective-permute-done | bytes 131104 | tf_op jit(solution)/shard_map/ppermute | solution.py:25
  41.9 5.4 %collective-permute-done.11.refs_4_ = bf16[32,2048]{1,0:T(8,128)(2,1)S(1)} collective-permute-done((bf16[32,2048]{1,0:T(8,128)(2,1)S(1)}, bf16[32,2048]{1,0:T(8,128)(2,1)S(1)}, u32[]{:S(2)}, u32[]{:S(2)}) %collective-permute-start.11) | collective-permute-done | bytes 131104 | tf_op jit(solution)/shard_map/ppermute | solution.py:25
  47.2 1.5 shard_map.104
  48.7 1.9 collective-permute-start.13
  51.3 3.0 %collective-permute-start.15 = (bf16[256,512]{1,0:T(8,128)(2,1)S(1)}, bf16[256,512]{1,0:T(8,128)(2,1)S(1)}, u32[]{:S(2)}, u32[]{:S(2)}) collective-permute-start(bf16[256,512]{1,0:T(8,128)(2,1)S(1)} %bitcast.26), channel_id=1, source_target_pairs={{8,0},{12,4},{0,8},{4,12},{9,1},{13,5},{1,9},{5,13},{10,2},{14,6},... | collective-permute-start | bytes 786440 | tf_op jit(solution)/shard_map/ppermute | solution.py:25
  54.3 1.3 collective-permute-start.16
  56.7 3.7 %collective-permute-done.14.s1 = bf16[256,512]{1,0:T(8,128)(2,1)S(1)} collective-permute-done((bf16[256,512]{1,0:T(8,128)(2,1)S(1)}, bf16[256,512]{1,0:T(8,128)(2,1)S(1)}, u32[]{:S(2)}, u32[]{:S(2)}) %collective-permute-start.14) | collective-permute-done | bytes 262176 | tf_op jit(solution)/shard_map/ppermute | solution.py:25
  62.8 4.3 %collective-permute-done.16.s3 = bf16[256,512]{1,0:T(8,128)(2,1)S(1)} collective-permute-done((bf16[256,512]{1,0:T(8,128)(2,1)S(1)}, bf16[256,512]{1,0:T(8,128)(2,1)S(1)}, u32[]{:S(2)}, u32[]{:S(2)}) %collective-permute-start.16) | collective-permute-done | bytes 262176 | tf_op jit(solution)/shard_map/ppermute | solution.py:25
  68.6 1.8 all-gather.2.cloned.1.call-done.go
  70.4 1.6 copy-done
  74.8 2.9 %shard_map.105 = (f32[2,256,512]{2,1,0:T(8,128)S(1)}, bf16[2,256,512]{2,1,0:T(8,128)(2,1)S(1)}, bf16[8,4,32,512]{3,2,1,0:T(8,128)(2,1)S(1)}) custom-call(s32[4]{0:T(128)S(1)} %pad_add_fusion.place, bf16[1024,1024]{1,0:T(8,128)(2,1)S(1)} %copy-done, bf16[256,512]{1,0:T(8,128)(2,1)S(1)} %bitcast.28, bf16[256,512]{1,0:T(8,128)(2,1)S(1)} %copy-done.22, ...), custom_call_target="tpu_custom_call" | custom-call | tf_op jit(solution)/shard_map/pallas_call | solution.py:102
  77.8 1.9 collective-permute-done.17
  79.9 2.7 %collective-permute-start.18 = (bf16[2,256,512]{2,1,0:T(8,128)(2,1)S(1)}, bf16[2,256,512]{2,1,0:T(8,128)(2,1)S(1)}, u32[]{:S(2)}, u32[]{:S(2)}) collective-permute-start(bf16[2,256,512]{2,1,0:T(8,128)(2,1)S(1)} %get-tuple-element.106), channel_id=1, source_target_pairs={{0,2},{2,0},{1,3},{3,1},{4,6},{6,4},{5,7},{7,5},{8,10},{10,8},{9,1... | collective-permute-start | bytes 1572872 | tf_op jit(solution)/shard_map/ppermute | solution.py:29
  82.6 2.4 %collective-permute-start.21 = (bf16[256,1536]{1,0:T(8,128)(2,1)}, bf16[256,1536]{1,0:T(8,128)(2,1)S(1)}, u32[]{:S(2)}, u32[]{:S(2)}) collective-permute-start(bf16[256,1536]{1,0:T(8,128)(2,1)} %bitcast.9.refs_0_), channel_id=1, source_target_pairs={{4,0},{8,4},{12,8},{0,12},{5,1},{9,5},{13,9},{1,13},{6,2},{10,6},{... | collective-permute-start | bytes 2359304 | tf_op jit(solution)/shard_map/ppermute | solution.py:25
  85.1 3.1 %shard_map.106 = (bf16[64,1536]{1,0:T(8,128)(2,1)S(1)}, bf16[448,1536]{1,0:T(8,128)(2,1)S(1)}) custom-call(s32[4]{0:T(128)S(1)} %pad_add_fusion.place, bf16[2,256,512]{2,1,0:T(8,128)(2,1)S(1)} %fusion.12.hidden, bf16[2,256,512]{2,1,0:T(8,128)(2,1)S(1)} %copy-done.14, bf16[1024,1024]{1,0:T(8,128)(2,1)S(1)} %copy-done.1, ...), custom_call_target="tpu_custom_call" | custom-call | tf_op jit(solution)/shard_map/pallas_call | solution.py:171
  88.2 7.3 %collective-permute-done.18 = bf16[2,256,512]{2,1,0:T(8,128)(2,1)S(1)} collective-permute-done((bf16[2,256,512]{2,1,0:T(8,128)(2,1)S(1)}, bf16[2,256,512]{2,1,0:T(8,128)(2,1)S(1)}, u32[]{:S(2)}, u32[]{:S(2)}) %collective-permute-start.18) | collective-permute-done | bytes 524320 | tf_op jit(solution)/shard_map/ppermute | solution.py:29
  96.7 1.2 collective-permute-start.23
  98.0 4.2 %collective-permute-done.21.refs_1_ = bf16[256,1536]{1,0:T(8,128)(2,1)S(1)} collective-permute-done((bf16[256,1536]{1,0:T(8,128)(2,1)}, bf16[256,1536]{1,0:T(8,128)(2,1)S(1)}, u32[]{:S(2)}, u32[]{:S(2)}) %collective-permute-start.21) | collective-permute-done | bytes 786464 | tf_op jit(solution)/shard_map/ppermute | solution.py:25
  103.1 2.4 %collective-permute-done.22.refs_3_ = bf16[256,1536]{1,0:T(8,128)(2,1)S(1)} collective-permute-done((bf16[256,1536]{1,0:T(8,128)(2,1)}, bf16[256,1536]{1,0:T(8,128)(2,1)S(1)}, u32[]{:S(2)}, u32[]{:S(2)}) %collective-permute-start.22) | collective-permute-done | bytes 786464 | tf_op jit(solution)/shard_map/ppermute | solution.py:25
  107.1 5.5 %shard_map.107 = bf16[1024,1536]{1,0:T(8,128)(2,1)} custom-call(s32[4]{0:T(128)S(1)} %pad_add_fusion.place, bf16[2,256,512]{2,1,0:T(8,128)(2,1)S(1)} %get-tuple-element.109.gg.refs_8_, bf16[2,256,512]{2,1,0:T(8,128)(2,1)S(1)} %collective-permute-done.19.gg_other.refs_9_, bf16[2,256,512]{2,1,0:T(8,128)(2,1)S(1)} %get-tuple-element.108.gu.refs_10_, ...), custom_call_target="tpu_custom_call" | custom-call | tf_op jit(solution)/shard_map/pallas_call | solution.py:130
  112.6 1.2 collective-permute-start.31
  114.7 1.4 collective-permute-start.29
  116.7 14.3 %collective-permute-done.31.refs_5_ = bf16[256,1536]{1,0:T(8,128)(2,1)S(1)} collective-permute-done((bf16[256,1536]{1,0:T(8,128)(2,1)}, bf16[256,1536]{1,0:T(8,128)(2,1)S(1)}, u32[]{:S(2)}, u32[]{:S(2)}) %collective-permute-start.31) | collective-permute-done | bytes 786464 | tf_op jit(solution)/shard_map/ppermute | solution.py:25
  131.9 1.5 collective-permute-done.32.refs_7_
  134.3 3.6 %collective-permute-done.30.refs_14_ = bf16[2,256,512]{2,1,0:T(8,128)(2,1)S(1)} collective-permute-done((bf16[2,256,512]{2,1,0:T(8,128)(2,1)S(1)}, bf16[2,256,512]{2,1,0:T(8,128)(2,1)S(1)}, u32[]{:S(2)}, u32[]{:S(2)}) %collective-permute-start.30) | collective-permute-done | bytes 524320 | tf_op jit(solution)/shard_map/ppermute | solution.py:29
  138.7 1.4 collective-permute-start.35
  140.2 15.4 %reduce-scatter.2.cloned.1.call-done = bf16[128,1536]{1,0:T(8,128)(2,1)} async-done(((bf16[1024,1536]{1,0:T(8,128)(2,1)}), bf16[128,1536]{1,0:T(8,128)(2,1)}) %reduce-scatter.2.cloned.1.call-update) | async-done | bytes 393232 | tf_op jit(solution)/shard_map/reduce_scatter | solution.py:286
  155.6 1.7 dynamic-slice_bitcast_fusion.2
  157.3 2.8 %collective-permute-start.26 = (bf16[32,1536]{1,0:T(8,128)(2,1)}, bf16[32,1536]{1,0:T(8,128)(2,1)}, u32[]{:S(2)}, u32[]{:S(2)}) collective-permute-start(bf16[32,1536]{1,0:T(8,128)(2,1)} %get-tuple-element.115), channel_id=1, source_target_pairs={{4,0},{8,4},{12,8},{0,12},{5,1},{9,5},{13,9},{1,13},{6,2},{10,6},{... | collective-permute-start | bytes 294920 | tf_op jit(solution)/shard_map/ppermute | solution.py:25
  161.7 1.9 collective-permute-start.27
  163.6 25.1 %collective-permute-done.26 = bf16[32,1536]{1,0:T(8,128)(2,1)} collective-permute-done((bf16[32,1536]{1,0:T(8,128)(2,1)}, bf16[32,1536]{1,0:T(8,128)(2,1)}, u32[]{:S(2)}, u32[]{:S(2)}) %collective-permute-start.26) | collective-permute-done | bytes 98336 | tf_op jit(solution)/shard_map/ppermute | solution.py:25
  190.3 1.7 fusion.15
  192.0 10.4 %collective-permute-done.28.refs_6_ = bf16[256,1536]{1,0:T(8,128)(2,1)S(1)} collective-permute-done((bf16[256,1536]{1,0:T(8,128)(2,1)}, bf16[256,1536]{1,0:T(8,128)(2,1)S(1)}, u32[]{:S(2)}, u32[]{:S(2)}) %collective-permute-start.28) | collective-permute-done | bytes 786464 | tf_op jit(solution)/shard_map/ppermute | solution.py:25
  203.5 1.1 copy-done.10
  207.9 10.2 %shard_map.108 = (bf16[1536,512]{1,0:T(8,128)(2,1)}, bf16[1536,512]{1,0:T(8,128)(2,1)}) custom-call(s32[4]{0:T(128)S(1)} %pad_add_fusion.place, bf16[256,1536]{1,0:T(8,128)(2,1)} %bitcast.9.refs_0_, bf16[256,1536]{1,0:T(8,128)(2,1)S(1)} %copy-done.6, bf16[256,1536]{1,0:T(8,128)(2,1)S(1)} %collective-permute-done.27.refs_2_, bf16[256,1536]{1,0:T(8,128)(2,1)S(1)} %copy-done.8, ...), custom_call_target="tpu_custom_call" | custom-call | tf_op jit(solution)/shard_map/pallas_call | solution.py:219
  218.1 1.7 add_convert_fusion
  219.8 1.2 pad_maximum_fusion
  (119 shorter events, 28.7 us)
Async XLA Ops:
  7.2 63.2 %all-gather.2.cloned.1.call-start = ((), (), s32[]{:S(2)}) async-start(), calls=%async_computation.1 | async-start | bytes 2359296 | tf_op jit(solution)/shard_map/all_gather | solution.py:255
  9.0 41.7 %copy-start.32 = (bf16[256,512]{1,0:T(8,128)(2,1)S(1)}, bf16[256,512]{1,0:T(8,128)(2,1)}, u32[]{:S(2)}) copy-start(bf16[256,512]{1,0:T(8,128)(2,1)} %param.9) | copy-start | bytes 786436
  9.0 41.7 %copy-start.33 = (bf16[256,512]{1,0:T(8,128)(2,1)S(1)}, bf16[256,512]{1,0:T(8,128)(2,1)}, u32[]{:S(2)}) copy-start(bf16[256,512]{1,0:T(8,128)(2,1)} %param.10) | copy-start | bytes 786436
  9.0 12.5 %collective-permute-start = (bf16[32,1024]{1,0:T(8,128)(2,1)S(1)}, bf16[32,1024]{1,0:T(8,128)(2,1)S(1)}, u32[]{:S(2)}, u32[]{:S(2)}) collective-permute-start(bf16[32,1024]{1,0:T(8,128)(2,1)S(1)} %get-tuple-element.55.refs_0_), channel_id=1, source_target_pairs={{4,0},{8,4},{12,8},{0,12},{5,1},{9,5},{13,9},{1,13},{6,2},{10,6},{... | collective-permute-start | bytes 196616 | tf_op jit(solution)/shard_map/ppermute | solution.py:25
  12.1 9.4 %collective-permute-start.1 = (bf16[32,1024]{1,0:T(8,128)(2,1)S(1)}, bf16[32,1024]{1,0:T(8,128)(2,1)S(1)}, u32[]{:S(2)}, u32[]{:S(2)}) collective-permute-start(bf16[32,1024]{1,0:T(8,128)(2,1)S(1)} %get-tuple-element.55.refs_0_), channel_id=1, source_target_pairs={{8,0},{12,4},{0,8},{4,12},{9,1},{13,5},{1,9},{5,13},{10,2},{14,6},... | collective-permute-start | bytes 196616 | tf_op jit(solution)/shard_map/ppermute | solution.py:25
  12.7 14.4 %collective-permute-start.3 = (bf16[32,2048]{1,0:T(8,128)(2,1)S(1)}, bf16[32,2048]{1,0:T(8,128)(2,1)S(1)}, u32[]{:S(2)}, u32[]{:S(2)}) collective-permute-start(bf16[32,2048]{1,0:T(8,128)(2,1)S(1)} %get-tuple-element.56.refs_0_), channel_id=1, source_target_pairs={{16,0},{32,16},{48,32},{64,48},{80,64},{96,80},{112,96},{0,112},{1... | collective-permute-start | bytes 393224 | tf_op jit(solution)/shard_map/ppermute | solution.py:25
  18.6 8.5 %collective-permute-start.4 = (bf16[32,2048]{1,0:T(8,128)(2,1)S(1)}, bf16[32,2048]{1,0:T(8,128)(2,1)S(1)}, u32[]{:S(2)}, u32[]{:S(2)}) collective-permute-start(bf16[32,2048]{1,0:T(8,128)(2,1)S(1)} %get-tuple-element.56.refs_0_), channel_id=1, source_target_pairs={{32,0},{48,16},{64,32},{80,48},{96,64},{112,80},{0,96},{16,112},{3... | collective-permute-start | bytes 393224 | tf_op jit(solution)/shard_map/ppermute | solution.py:25
  20.0 9.6 %collective-permute-start.5 = (bf16[32,2048]{1,0:T(8,128)(2,1)S(1)}, bf16[32,2048]{1,0:T(8,128)(2,1)S(1)}, u32[]{:S(2)}, u32[]{:S(2)}) collective-permute-start(bf16[32,2048]{1,0:T(8,128)(2,1)S(1)} %get-tuple-element.56.refs_0_), channel_id=1, source_target_pairs={{96,0},{112,16},{0,32},{16,48},{32,64},{48,80},{64,96},{80,112},{9... | collective-permute-start | bytes 393224 | tf_op jit(solution)/shard_map/ppermute | solution.py:25
  21.5 9.9 %collective-permute-start.6 = (bf16[32,2048]{1,0:T(8,128)(2,1)S(1)}, bf16[32,2048]{1,0:T(8,128)(2,1)S(1)}, u32[]{:S(2)}, u32[]{:S(2)}) collective-permute-start(bf16[32,2048]{1,0:T(8,128)(2,1)S(1)} %get-tuple-element.56.refs_0_), channel_id=1, source_target_pairs={{112,0},{0,16},{16,32},{32,48},{48,64},{64,80},{80,96},{96,112},{1... | collective-permute-start | bytes 393224 | tf_op jit(solution)/shard_map/ppermute | solution.py:25
  21.5 5.6 %collective-permute-start.2 = (bf16[32,1024]{1,0:T(8,128)(2,1)S(1)}, bf16[32,1024]{1,0:T(8,128)(2,1)S(1)}, u32[]{:S(2)}, u32[]{:S(2)}) collective-permute-start(bf16[32,1024]{1,0:T(8,128)(2,1)S(1)} %get-tuple-element.55.refs_0_), channel_id=1, source_target_pairs={{12,0},{0,4},{4,8},{8,12},{13,1},{1,5},{5,9},{9,13},{14,2},{2,6},{... | collective-permute-start | bytes 196616 | tf_op jit(solution)/shard_map/ppermute | solution.py:25
  32.7 122.9 %reduce-scatter.2.cloned.1.call-start = ((), (), s32[]{:S(2)}) async-start(), calls=%async_computation.2 | async-start | bytes 3538944 | tf_op jit(solution)/shard_map/reduce_scatter | solution.py:286
  32.8 17.9 %collective-permute-start.7 = (bf16[256,512]{1,0:T(8,128)(2,1)}, bf16[256,512]{1,0:T(8,128)(2,1)S(1)}, u32[]{:S(2)}, u32[]{:S(2)}) collective-permute-start(bf16[256,512]{1,0:T(8,128)(2,1)} %param.9), channel_id=1, source_target_pairs={{0,2},{2,0},{1,3},{3,1},{4,6},{6,4},{5,7},{7,5},{8,10},{10,8},{9,1... | collective-permute-start | bytes 786440 | tf_op jit(solution)/shard_map/ppermute | solution.py:29
  35.0 6.9 %collective-permute-start.10 = (bf16[32,2048]{1,0:T(8,128)(2,1)S(1)}, bf16[32,2048]{1,0:T(8,128)(2,1)S(1)}, u32[]{:S(2)}, u32[]{:S(2)}) collective-permute-start(bf16[32,2048]{1,0:T(8,128)(2,1)S(1)} %collective-permute-done.4.refs_2_), channel_id=1, source_target_pairs={{16,0},{32,16},{48,32},{64,48},{80,64},{96,80},{112,96},{0,112},{1... | collective-permute-start | bytes 393224 | tf_op jit(solution)/shard_map/ppermute | solution.py:25
  35.9 11.3 %collective-permute-start.11 = (bf16[32,2048]{1,0:T(8,128)(2,1)S(1)}, bf16[32,2048]{1,0:T(8,128)(2,1)S(1)}, u32[]{:S(2)}, u32[]{:S(2)}) collective-permute-start(bf16[32,2048]{1,0:T(8,128)(2,1)S(1)} %collective-permute-done.4.refs_2_), channel_id=1, source_target_pairs={{32,0},{48,16},{64,32},{80,48},{96,64},{112,80},{0,96},{16,112},{3... | collective-permute-start | bytes 393224 | tf_op jit(solution)/shard_map/ppermute | solution.py:25
  35.9 11.3 %collective-permute-start.12 = (bf16[32,2048]{1,0:T(8,128)(2,1)S(1)}, bf16[32,2048]{1,0:T(8,128)(2,1)S(1)}, u32[]{:S(2)}, u32[]{:S(2)}) collective-permute-start(bf16[32,2048]{1,0:T(8,128)(2,1)S(1)} %collective-permute-done.5.refs_6_), channel_id=1, source_target_pairs={{112,0},{0,16},{16,32},{32,48},{48,64},{64,80},{80,96},{96,112},{1... | collective-permute-start | bytes 393224 | tf_op jit(solution)/shard_map/ppermute | solution.py:25
  37.4 13.3 %collective-permute-start.8 = (bf16[256,512]{1,0:T(8,128)(2,1)}, bf16[256,512]{1,0:T(8,128)(2,1)S(1)}, u32[]{:S(2)}, u32[]{:S(2)}) collective-permute-start(bf16[256,512]{1,0:T(8,128)(2,1)} %param.10), channel_id=1, source_target_pairs={{0,2},{2,0},{1,3},{3,1},{4,6},{6,4},{5,7},{7,5},{8,10},{10,8},{9,1... | collective-permute-start | bytes 786440 | tf_op jit(solution)/shard_map/ppermute | solution.py:29
  48.7 19.8 %collective-permute-start.13 = (bf16[256,1536]{1,0:T(8,128)(2,1)}, bf16[256,1536]{1,0:T(8,128)(2,1)}, u32[]{:S(2)}, u32[]{:S(2)}) collective-permute-start(bf16[256,1536]{1,0:T(8,128)(2,1)} %bitcast.9.refs_0_), channel_id=1, source_target_pairs={{0,128},{128,0},{1,129},{129,1},{2,130},{130,2},{3,131},{131,3},{4... | collective-permute-start | bytes 2359304 | tf_op jit(solution)/shard_map/ppermute | solution.py:29
  50.8 19.6 %copy-start.2 = (bf16[512,1536]{1,0:T(8,128)(2,1)S(1)}, bf16[512,1536]{1,0:T(8,128)(2,1)}, u32[]{:S(2)}) copy-start(bf16[512,1536]{1,0:T(8,128)(2,1)} %w_down.1) | copy-start | bytes 4718596
  51.1 16.6 %collective-permute-start.9 = (bf16[2,256,512]{2,1,0:T(8,128)(2,1)S(1)}, bf16[2,256,512]{2,1,0:T(8,128)(2,1)S(1)}, u32[]{:S(2)}, u32[]{:S(2)}) collective-permute-start(bf16[2,256,512]{2,1,0:T(8,128)(2,1)S(1)} %fusion.12.hidden), channel_id=1, source_target_pairs={{0,1},{1,0},{2,3},{3,2},{4,5},{5,4},{6,7},{7,6},{8,9},{9,8},{10,11... | collective-permute-start | bytes 1572872 | tf_op jit(solution)/shard_map/ppermute | solution.py:29
  51.2 9.2 %collective-permute-start.14 = (bf16[256,512]{1,0:T(8,128)(2,1)S(1)}, bf16[256,512]{1,0:T(8,128)(2,1)S(1)}, u32[]{:S(2)}, u32[]{:S(2)}) collective-permute-start(bf16[256,512]{1,0:T(8,128)(2,1)S(1)} %bitcast.25), channel_id=1, source_target_pairs={{4,0},{8,4},{12,8},{0,12},{5,1},{9,5},{13,9},{1,13},{6,2},{10,6},{... | collective-permute-start | bytes 786440 | tf_op jit(solution)/shard_map/ppermute | solution.py:25
  51.3 10.8 %collective-permute-start.15 = (bf16[256,512]{1,0:T(8,128)(2,1)S(1)}, bf16[256,512]{1,0:T(8,128)(2,1)S(1)}, u32[]{:S(2)}, u32[]{:S(2)}) collective-permute-start(bf16[256,512]{1,0:T(8,128)(2,1)S(1)} %bitcast.26), channel_id=1, source_target_pairs={{8,0},{12,4},{0,8},{4,12},{9,1},{13,5},{1,9},{5,13},{10,2},{14,6},... | collective-permute-start | bytes 786440 | tf_op jit(solution)/shard_map/ppermute | solution.py:25
  54.3 12.8 %collective-permute-start.16 = (bf16[256,512]{1,0:T(8,128)(2,1)S(1)}, bf16[256,512]{1,0:T(8,128)(2,1)S(1)}, u32[]{:S(2)}, u32[]{:S(2)}) collective-permute-start(bf16[256,512]{1,0:T(8,128)(2,1)S(1)} %bitcast.27), channel_id=1, source_target_pairs={{12,0},{0,4},{4,8},{8,12},{13,1},{1,5},{5,9},{9,13},{14,2},{2,6},{... | collective-permute-start | bytes 786440 | tf_op jit(solution)/shard_map/ppermute | solution.py:25
  55.6 14.7 %copy-start.20 = (bf16[8,32,512]{2,1,0:T(8,128)(2,1)S(1)}, bf16[8,32,512]{2,1,0:T(8,128)(2,1)}, u32[]{:S(2)}) copy-start(bf16[8,32,512]{2,1,0:T(8,128)(2,1)} %copy-done.19) | copy-start | bytes 786436
  77.7 2.0 collective-permute-start.17
  79.9 15.6 %collective-permute-start.18 = (bf16[2,256,512]{2,1,0:T(8,128)(2,1)S(1)}, bf16[2,256,512]{2,1,0:T(8,128)(2,1)S(1)}, u32[]{:S(2)}, u32[]{:S(2)}) collective-permute-start(bf16[2,256,512]{2,1,0:T(8,128)(2,1)S(1)} %get-tuple-element.106), channel_id=1, source_target_pairs={{0,2},{2,0},{1,3},{3,1},{4,6},{6,4},{5,7},{7,5},{8,10},{10,8},{9,1... | collective-permute-start | bytes 1572872 | tf_op jit(solution)/shard_map/ppermute | solution.py:29
  82.6 19.5 %collective-permute-start.21 = (bf16[256,1536]{1,0:T(8,128)(2,1)}, bf16[256,1536]{1,0:T(8,128)(2,1)S(1)}, u32[]{:S(2)}, u32[]{:S(2)}) collective-permute-start(bf16[256,1536]{1,0:T(8,128)(2,1)} %bitcast.9.refs_0_), channel_id=1, source_target_pairs={{4,0},{8,4},{12,8},{0,12},{5,1},{9,5},{13,9},{1,13},{6,2},{10,6},{... | collective-permute-start | bytes 2359304 | tf_op jit(solution)/shard_map/ppermute | solution.py:25
  85.0 20.4 %collective-permute-start.22 = (bf16[256,1536]{1,0:T(8,128)(2,1)}, bf16[256,1536]{1,0:T(8,128)(2,1)S(1)}, u32[]{:S(2)}, u32[]{:S(2)}) collective-permute-start(bf16[256,1536]{1,0:T(8,128)(2,1)} %bitcast.9.refs_0_), channel_id=1, source_target_pairs={{12,0},{0,4},{4,8},{8,12},{13,1},{1,5},{5,9},{9,13},{14,2},{2,6},{... | collective-permute-start | bytes 2359304 | tf_op jit(solution)/shard_map/ppermute | solution.py:25
  85.0 10.5 %copy-start.30 = (bf16[2,256,512]{2,1,0:T(8,128)(2,1)S(1)}, bf16[2,256,512]{2,1,0:T(8,128)(2,1)}, u32[]{:S(2)}) copy-start(bf16[2,256,512]{2,1,0:T(8,128)(2,1)} %get-tuple-element.81) | copy-start | bytes 1572868
  85.1 10.4 %copy-start.31 = (bf16[2,256,512]{2,1,0:T(8,128)(2,1)S(1)}, bf16[2,256,512]{2,1,0:T(8,128)(2,1)}, u32[]{:S(2)}) copy-start(bf16[2,256,512]{2,1,0:T(8,128)(2,1)} %get-tuple-element.80) | copy-start | bytes 1572868
  88.2 8.5 %copy-start.27 = (bf16[64,1536]{1,0:T(8,128)(2,1)}, bf16[64,1536]{1,0:T(8,128)(2,1)S(1)}, u32[]{:S(2)}) copy-start(bf16[64,1536]{1,0:T(8,128)(2,1)S(1)} %get-tuple-element.83) | copy-start | bytes 589828
  95.5 11.6 %copy-start.3 = (bf16[1536,512]{1,0:T(8,128)(2,1)S(1)}, bf16[1536,512]{1,0:T(8,128)(2,1)}, u32[]{:S(2)}) copy-start(bf16[1536,512]{1,0:T(8,128)(2,1)} %w_gate.1) | copy-start | bytes 4718596
  95.5 11.6 %copy-start.4 = (bf16[1536,512]{1,0:T(8,128)(2,1)S(1)}, bf16[1536,512]{1,0:T(8,128)(2,1)}, u32[]{:S(2)}) copy-start(bf16[1536,512]{1,0:T(8,128)(2,1)} %w_up.1) | copy-start | bytes 4718596
  96.1 10.2 %collective-permute-start.19 = (bf16[2,256,512]{2,1,0:T(8,128)(2,1)S(1)}, bf16[2,256,512]{2,1,0:T(8,128)(2,1)S(1)}, u32[]{:S(2)}, u32[]{:S(2)}) collective-permute-start(bf16[2,256,512]{2,1,0:T(8,128)(2,1)S(1)} %get-tuple-element.109.gg.refs_8_), channel_id=1, source_target_pairs={{0,1},{1,0},{2,3},{3,2},{4,5},{5,4},{6,7},{7,6},{8,9},{9,8},{10,11... | collective-permute-start | bytes 1572872 | tf_op jit(solution)/shard_map/ppermute | solution.py:29
  96.2 10.8 %collective-permute-start.20 = (bf16[2,256,512]{2,1,0:T(8,128)(2,1)S(1)}, bf16[2,256,512]{2,1,0:T(8,128)(2,1)S(1)}, u32[]{:S(2)}, u32[]{:S(2)}) collective-permute-start(bf16[2,256,512]{2,1,0:T(8,128)(2,1)S(1)} %get-tuple-element.108.gu.refs_10_), channel_id=1, source_target_pairs={{0,1},{1,0},{2,3},{3,2},{4,5},{5,4},{6,7},{7,6},{8,9},{9,8},{10,11... | collective-permute-start | bytes 1572872 | tf_op jit(solution)/shard_map/ppermute | solution.py:29
  96.7 9.6 %collective-permute-start.23 = (bf16[64,1536]{1,0:T(8,128)(2,1)S(1)}, bf16[64,1536]{1,0:T(8,128)(2,1)S(1)}, u32[]{:S(2)}, u32[]{:S(2)}) collective-permute-start(bf16[64,1536]{1,0:T(8,128)(2,1)S(1)} %get-tuple-element.83), channel_id=1, source_target_pairs={{0,128},{128,0},{1,129},{129,1},{2,130},{130,2},{3,131},{131,3},{4... | collective-permute-start | bytes 589832 | tf_op jit(solution)/shard_map/ppermute | solution.py:29
  112.6 18.4 %collective-permute-start.31 = (bf16[256,1536]{1,0:T(8,128)(2,1)}, bf16[256,1536]{1,0:T(8,128)(2,1)S(1)}, u32[]{:S(2)}, u32[]{:S(2)}) collective-permute-start(bf16[256,1536]{1,0:T(8,128)(2,1)} %collective-permute-done.13.refs_4_), channel_id=1, source_target_pairs={{4,0},{8,4},{12,8},{0,12},{5,1},{9,5},{13,9},{1,13},{6,2},{10,6},{... | collective-permute-start | bytes 2359304 | tf_op jit(solution)/shard_map/ppermute | solution.py:25
  113.9 19.6 %collective-permute-start.32 = (bf16[256,1536]{1,0:T(8,128)(2,1)}, bf16[256,1536]{1,0:T(8,128)(2,1)S(1)}, u32[]{:S(2)}, u32[]{:S(2)}) collective-permute-start(bf16[256,1536]{1,0:T(8,128)(2,1)} %collective-permute-done.13.refs_4_), channel_id=1, source_target_pairs={{12,0},{0,4},{4,8},{8,12},{13,1},{1,5},{5,9},{9,13},{14,2},{2,6},{... | collective-permute-start | bytes 2359304 | tf_op jit(solution)/shard_map/ppermute | solution.py:25
  114.7 19.6 %collective-permute-start.29 = (bf16[2,256,512]{2,1,0:T(8,128)(2,1)S(1)}, bf16[2,256,512]{2,1,0:T(8,128)(2,1)S(1)}, u32[]{:S(2)}, u32[]{:S(2)}) collective-permute-start(bf16[2,256,512]{2,1,0:T(8,128)(2,1)S(1)} %get-tuple-element.109.gg.refs_8_), channel_id=1, source_target_pairs={{0,128},{128,0},{1,129},{129,1},{2,130},{130,2},{3,131},{131,3},{4... | collective-permute-start | bytes 1572872 | tf_op jit(solution)/shard_map/ppermute | solution.py:29
  116.2 21.7 %collective-permute-start.30 = (bf16[2,256,512]{2,1,0:T(8,128)(2,1)S(1)}, bf16[2,256,512]{2,1,0:T(8,128)(2,1)S(1)}, u32[]{:S(2)}, u32[]{:S(2)}) collective-permute-start(bf16[2,256,512]{2,1,0:T(8,128)(2,1)S(1)} %get-tuple-element.108.gu.refs_10_), channel_id=1, source_target_pairs={{0,128},{128,0},{1,129},{129,1},{2,130},{130,2},{3,131},{131,3},{4... | collective-permute-start | bytes 1572872 | tf_op jit(solution)/shard_map/ppermute | solution.py:29
  138.7 79.4 %collective-permute-start.35 = (bf16[448,1536]{1,0:T(8,128)(2,1)S(1)}, bf16[448,1536]{1,0:T(8,128)(2,1)}, u32[]{:S(2)}, u32[]{:S(2)}) collective-permute-start(bf16[448,1536]{1,0:T(8,128)(2,1)S(1)} %get-tuple-element.101), channel_id=1, source_target_pairs={{0,128},{128,0},{1,129},{129,1},{2,130},{130,2},{3,131},{131,3},{4... | collective-permute-start | bytes 4128776 | tf_op jit(solution)/shard_map/ppermute | solution.py:29
  157.3 31.4 %collective-permute-start.26 = (bf16[32,1536]{1,0:T(8,128)(2,1)}, bf16[32,1536]{1,0:T(8,128)(2,1)}, u32[]{:S(2)}, u32[]{:S(2)}) collective-permute-start(bf16[32,1536]{1,0:T(8,128)(2,1)} %get-tuple-element.115), channel_id=1, source_target_pairs={{4,0},{8,4},{12,8},{0,12},{5,1},{9,5},{13,9},{1,13},{6,2},{10,6},{... | collective-permute-start | bytes 294920 | tf_op jit(solution)/shard_map/ppermute | solution.py:25
  160.1 28.6 %collective-permute-start.25 = (bf16[32,1536]{1,0:T(8,128)(2,1)}, bf16[32,1536]{1,0:T(8,128)(2,1)}, u32[]{:S(2)}, u32[]{:S(2)}) collective-permute-start(bf16[32,1536]{1,0:T(8,128)(2,1)} %get-tuple-element.116), channel_id=1, source_target_pairs={{8,0},{12,4},{0,8},{4,12},{9,1},{13,5},{1,9},{5,13},{10,2},{14,6},... | collective-permute-start | bytes 294920 | tf_op jit(solution)/shard_map/ppermute | solution.py:25
  160.8 27.9 %collective-permute-start.24 = (bf16[32,1536]{1,0:T(8,128)(2,1)}, bf16[32,1536]{1,0:T(8,128)(2,1)}, u32[]{:S(2)}, u32[]{:S(2)}) collective-permute-start(bf16[32,1536]{1,0:T(8,128)(2,1)} %get-tuple-element.114), channel_id=1, source_target_pairs={{12,0},{0,4},{4,8},{8,12},{13,1},{1,5},{5,9},{9,13},{14,2},{2,6},{... | collective-permute-start | bytes 294920 | tf_op jit(solution)/shard_map/ppermute | solution.py:25
  161.7 40.7 %copy-start.6 = (bf16[256,1536]{1,0:T(8,128)(2,1)S(1)}, bf16[256,1536]{1,0:T(8,128)(2,1)}, u32[]{:S(2)}) copy-start(bf16[256,1536]{1,0:T(8,128)(2,1)} %copy-done.5) | copy-start | bytes 2359300
  161.7 30.3 %collective-permute-start.27 = (bf16[256,1536]{1,0:T(8,128)(2,1)}, bf16[256,1536]{1,0:T(8,128)(2,1)S(1)}, u32[]{:S(2)}, u32[]{:S(2)}) collective-permute-start(bf16[256,1536]{1,0:T(8,128)(2,1)} %bitcast.9.refs_0_), channel_id=1, source_target_pairs={{8,0},{12,4},{0,8},{4,12},{9,1},{13,5},{1,9},{5,13},{10,2},{14,6},... | collective-permute-start | bytes 2359304 | tf_op jit(solution)/shard_map/ppermute | solution.py:25
  188.7 13.7 %collective-permute-start.28 = (bf16[256,1536]{1,0:T(8,128)(2,1)}, bf16[256,1536]{1,0:T(8,128)(2,1)S(1)}, u32[]{:S(2)}, u32[]{:S(2)}) collective-permute-start(bf16[256,1536]{1,0:T(8,128)(2,1)} %collective-permute-done.13.refs_4_), channel_id=1, source_target_pairs={{8,0},{12,4},{0,8},{4,12},{9,1},{13,5},{1,9},{5,13},{10,2},{14,6},... | collective-permute-start | bytes 2359304 | tf_op jit(solution)/shard_map/ppermute | solution.py:25
  188.7 13.7 %collective-permute-start.33 = (bf16[2,256,512]{2,1,0:T(8,128)(2,1)}, bf16[2,256,512]{2,1,0:T(8,128)(2,1)S(1)}, u32[]{:S(2)}, u32[]{:S(2)}) collective-permute-start(bf16[2,256,512]{2,1,0:T(8,128)(2,1)} %copy-done.15), channel_id=1, source_target_pairs={{0,1},{1,0},{2,3},{3,2},{4,5},{5,4},{6,7},{7,6},{8,9},{9,8},{10,11... | collective-permute-start | bytes 1572872 | tf_op jit(solution)/shard_map/ppermute | solution.py:29
  188.7 13.7 %collective-permute-start.34 = (bf16[2,256,512]{2,1,0:T(8,128)(2,1)}, bf16[2,256,512]{2,1,0:T(8,128)(2,1)S(1)}, u32[]{:S(2)}, u32[]{:S(2)}) collective-permute-start(bf16[2,256,512]{2,1,0:T(8,128)(2,1)} %copy-done.17), channel_id=1, source_target_pairs={{0,1},{1,0},{2,3},{3,2},{4,5},{5,4},{6,7},{7,6},{8,9},{9,8},{10,11... | collective-permute-start | bytes 1572872 | tf_op jit(solution)/shard_map/ppermute | solution.py:29
  (25 other events, 39.5 us)
Sparse Core Ops, SparseCore 0:
  32.9 37.4 all-gather.1
  112.7 42.8 reduce-scatter.1

commit v3 on v1

v3 whole, which is shorter than its diff:
```python
import functools

import jax
import jax.numpy as jnp
from jax import lax
from jax.experimental import pallas as pl
from jax.experimental.pallas import tpu as pltpu
from jax.sharding import Mesh, PartitionSpec as P

F32, BF16 = jnp.float32, jnp.bfloat16
NZ, NY = 8, 4
HALF = 768
VMEM = pl.BlockSpec(memory_space=pltpu.VMEM)
SMEM = pl.BlockSpec(memory_space=pltpu.SMEM)
HBM = pl.BlockSpec(memory_space=pltpu.HBM)


def dot(left, right, left_dim, right_dim):
    dims = (((left_dim,), (right_dim,)), ((), ()))
    return lax.dot_general(left, right, dims, preferred_element_type=F32)


def from_ahead(x, axis, n, k):
    return lax.ppermute(x, axis, [((d + k) % n, d) for d in range(n)])


def swap(x, axis):
    return lax.ppermute(x, axis, [(0, 1), (1, 0)])


def grant(mib):
    return pltpu.CompilerParams(vmem_limit_bytes=mib << 20)


def in_hbm(x):
    return pltpu.with_memory_space_constraint(x, pltpu.HBM)


def prepare_kernel(grad_output, layer_input, mixed):
    mixed[:, :1536] = grad_output[...]
    mixed[:, 1536:] = layer_input[:, :HALF]


def prepare(grad_output, layer_input):
    return pl.pallas_call(
        prepare_kernel,
        out_shape=jax.ShapeDtypeStruct((32, 1536 + HALF), BF16),
        in_specs=[VMEM] * 2,
        out_specs=VMEM,
        compiler_params=grant(4),
    )(grad_output, layer_input)


def arrange_kernel(n, slot, cuts, place, *refs):
    for k in range(n):
        there = (place[slot] + k) % n
        for out, (low, high) in zip(refs[n:], cuts):
            out[there] = refs[k][:, low:high]


def arrange(place, slot, parts, cuts):
    n, rows = len(parts), parts[0].shape[0]
    outs = pl.pallas_call(
        functools.partial(arrange_kernel, n, slot, cuts),
        out_shape=tuple(jax.ShapeDtypeStruct((n, rows, high - low), BF16) for low, high in cuts),
        in_specs=[SMEM] + [VMEM] * n,
        out_specs=(VMEM,) * len(cuts),
        compiler_params=grant(6),
    )(place, *parts)
    return [out.reshape(n * rows, -1) for out in outs]


def hidden_grad_kernel(place, go, w_down, mine, send, rows, sems):
    copies = [
        pltpu.make_async_copy(go.at[pl.ds(512 * half, 512)], rows.at[half], sems.at[half])
        for half in range(2)
    ]
    for copy in copies:
        copy.start()
    for half, copy in enumerate(copies):
        copy.wait()
        part = dot(rows[half], w_down[...], 1, 1)
        for which in range(2):
            block = part[256 * which:256 * which + 256]

            @pl.when(place[3] == which)
            def _():
                mine[half] = block

            @pl.when(place[3] != which)
            def _():
                send[half] = block.astype(BF16)


def hidden_grad(place, go, w_down):
    return pl.pallas_call(
        hidden_grad_kernel,
        out_shape=(
            jax.ShapeDtypeStruct((2, 256, 512), F32),
            jax.ShapeDtypeStruct((2, 256, 512), BF16),
        ),
        in_specs=[SMEM, HBM, VMEM],
        out_specs=(VMEM,) * 2,
        scratch_shapes=[pltpu.VMEM((2, 512, 1536), BF16), pltpu.SemaphoreType.DMA((2,))],
        compiler_params=grant(16),
    )(place, in_hbm(go), w_down)


def input_grad_kernel(place, gg, gg_other, gu, gu_other, w_gate, w_up, out):
    def emit(gate_ref, up_ref, core):
        gate_rows, up_rows = gate_ref[...].reshape(512, 512), up_ref[...].reshape(512, 512)
        total = (dot(gate_rows, w_gate[...], 1, 1) + dot(up_rows, w_up[...], 1, 1)).astype(BF16)
        for half in range(2):
            start = pl.multiple_of(512 * half + 256 * core, 256)
            out[pl.ds(start, 256), :] = total[256 * half:256 * half + 256]

    emit(gg, gu, place[3])
    emit(gg_other, gu_other, 1 - place[3])


def input_grad(place, gg, gg_other, gu, gu_other, w_gate, w_up):
    weight = pl.BlockSpec((512, 512), lambda i: (i, 0))
    return pl.pallas_call(
        input_grad_kernel,
        grid=(3,),
        out_shape=jax.ShapeDtypeStruct((1024, 1536), BF16),
        in_specs=[SMEM] + [VMEM] * 4 + [weight] * 2,
        out_specs=pl.BlockSpec((1024, 512), lambda i: (0, i)),
        compiler_params=grant(16),
    )(place, gg, gg_other, gu, gu_other, w_gate, w_up)


def fill_natural(place, own, other, rows, col):
    for half in range(2):
        base = half * 512
        start = pl.multiple_of(base + place[3] * 256, 256)
        rows[pl.ds(start, 256), col:col + 512] = own[half]
        start = pl.multiple_of(base + (1 - place[3]) * 256, 256)
        rows[pl.ds(start, 256), col:col + 512] = other[half]


def down_kernel(place, hidden, hidden_other, go, out, rows):
    @pl.when(pl.program_id(0) == 0)
    def _():
        fill_natural(place, hidden, hidden_other, rows, 0)

    out[...] = dot(rows[...], go[...], 0, 0).astype(BF16)


def down_grad(place, hidden, hidden_other, go):
    return pl.pallas_call(
        down_kernel,
        grid=(3,),
        out_shape=jax.ShapeDtypeStruct((512, 1536), BF16),
        in_specs=[SMEM, VMEM, VMEM, pl.BlockSpec((1024, 512), lambda i: (0, i))],
        out_specs=pl.BlockSpec((512, 512), lambda i: (0, i)),
        scratch_shapes=[pltpu.VMEM((1024, 512), BF16)],
        compiler_params=grant(12),
    )(place, hidden, hidden_other, in_hbm(go))


def fill_rolled(place, own, other, rows, col):
    for half in range(2):
        for pair in range(2):
            for y in range(NY):
                k = (y - place[1] + NY) % NY
                lines = pl.ds(pair * 128 + y * 32, 32)
                z_own = 4 * half + 2 * place[3] + pair
                rows[k, z_own, :, col:col + 512] = own[half, lines, :]
                z_other = 4 * half + 2 * (1 - place[3]) + pair
                rows[k, z_other, :, col:col + 512] = other[half, lines, :]


def weight_kernel(place, own, *refs):
    pieces, grads, (d_gate, d_up, natural, rows) = refs[:8], refs[8:16], refs[16:]
    step = pl.program_id(0)

    @pl.when(step == 0)
    def _():
        fill_natural(place, *grads[0:2], natural, 0)
        fill_natural(place, *grads[2:4], natural, 512)
        for replica in range(2):
            fill_rolled(place, *grads[4 * replica:4 * replica + 2], rows.at[replica], 0)
            fill_rolled(place, *grads[4 * replica + 2:4 * replica + 4], rows.at[replica], 512)

    def rolled(replica):
        total = jnp.zeros((256, 1024), F32)
        for k in range(NY):
            total = total + dot(pieces[NY * replica + k][...], rows[replica, k].reshape(256, 1024), 0, 0)
        return total

    def emit(total):
        d_gate[...] = total[:, :512].astype(BF16)
        d_up[...] = total[:, 512:].astype(BF16)

    @pl.when(step < 3)
    def _():
        emit(dot(own[...], natural[...], 0, 0) + rolled(1))

    @pl.when(step >= 3)
    def _():
        emit(rolled(0) + rolled(1))


def weight_grads(place, own, own_pieces, partner_pieces, grads):
    tile = pl.BlockSpec((256, 512), lambda i: (i, 0))
    shape = jax.ShapeDtypeStruct((1536, 512), BF16)
    low = pl.BlockSpec((1024, 256), lambda i: (0, jnp.minimum(i, 2)))
    high = pl.BlockSpec((256, 256), lambda i: (0, jnp.maximum(i - 3, 0)))
    every = pl.BlockSpec((256, 256), lambda i: (0, i))
    high0, high1, high2, high3 = own_pieces
    partner0, partner1, partner2, partner3 = partner_pieces
    early = [in_hbm(x) for x in (own, high0, high1)]
    partner = [in_hbm(x) for x in (high3, partner0, partner1)]
    partner3 = in_hbm(partner3)
    near = [in_hbm(x) for x in grads[:4]]
    return pl.pallas_call(
        weight_kernel,
        grid=(6,),
        out_shape=(shape, shape),
        in_specs=[SMEM, low] + [high] * 4 + [every] * 4 + [VMEM] * 8,
        out_specs=(tile, tile),
        scratch_shapes=[pltpu.VMEM((1024, 1024), BF16), pltpu.VMEM((2, NY, NZ, 32, 1024), BF16)],
        compiler_params=grant(24),
    )(place, *early, high2, *partner, partner2, partner3, *near, *grads[4:])


def ring(x, axis, n):
    ahead, behind = [], []
    up, down = x, x
    for step in range(1, n // 2 + 1):
        up = from_ahead(up, axis, n, 1)
        ahead.append(up)
        if step < n // 2:
            down = from_ahead(down, axis, n, n - 1)
            behind.append(down)
    return [x] + ahead + behind[::-1]


def ordered(mine, other, index):
    low = jnp.where(index == 0, mine, other)
    high = jnp.where(index == 0, other, mine)
    return jnp.stack([low, high], axis=0)


def body(layer_input, grad_output, gate_saved, up_saved, w_gate, w_up, w_down):
    place = jnp.stack([lax.axis_index(name) for name in ("z", "y", "xh", "core")]).astype(jnp.int32)
    xh = place[2]

    mixed = prepare(grad_output, layer_input)
    mixed_parts = [mixed] + [from_ahead(mixed, "y", NY, k) for k in (1, 2, 3)]
    go_y, own_y = arrange(place, 1, mixed_parts, ((0, 1536), (1536, 1536 + HALF)))
    go = lax.all_gather(go_y, "z", axis=0, tiled=True)
    own_z, high_z = arrange(place, 0, ring(layer_input, "z", NZ), ((0, 1536), (HALF, 1536)))
    partner_z = swap(own_z, "dp")
    high1, high3 = from_ahead(high_z, "y", NY, 1), from_ahead(high_z, "y", NY, 3)

    gate = ordered(gate_saved, swap(gate_saved, "xh"), xh)
    up = ordered(up_saved, swap(up_saved, "xh"), xh)
    gate_val, up_val = gate.astype(F32), up.astype(F32)
    hidden = (gate_val * jax.nn.sigmoid(gate_val) * up_val).astype(BF16)
    hidden_other = swap(hidden, "core")
    go, gate, up, hidden, hidden_other, own_y, high_z, partner_z, high1, high3 = lax.optimization_barrier(
        (go, gate, up, hidden, hidden_other, own_y, high_z, partner_z, high1, high3)
    )

    own_low = lax.all_gather(own_y, "z", axis=0, tiled=True)
    partner1, partner3 = from_ahead(partner_z, "y", NY, 1), from_ahead(partner_z, "y", NY, 3)
    mine, send = hidden_grad(place, go, w_down)
    chip = mine + swap(send, "core").astype(F32)
    chip_far = swap(chip.astype(BF16), "xh")
    part_down = down_grad(place, hidden, hidden_other, go)

    chip, chip_far, part_down = lax.optimization_barrier((chip, chip_far, part_down))

    grad_hidden = chip + chip_far.astype(F32)
    gate_val, up_val = gate.astype(F32), up.astype(F32)
    sigma = jax.nn.sigmoid(gate_val)
    gg = (grad_hidden * up_val * sigma * (1.0 + gate_val * (1.0 - sigma))).astype(BF16)
    gu = (grad_hidden * gate_val * sigma).astype(BF16)
    gg_other, gu_other = swap(gg, "core"), swap(gu, "core")
    gg_other, gu_other, partner1, partner3 = lax.optimization_barrier((gg_other, gu_other, partner1, partner3))
    partial_in = input_grad(place, gg, gg_other, gu, gu_other, w_gate, w_up)
    in_z = lax.psum_scatter(partial_in, "z", scatter_dimension=0, tiled=True).reshape(NY, 32, 1536)

    gg_far, gu_far = swap(gg, "dp"), swap(gu, "dp")
    high2, partner2 = from_ahead(high_z, "y", NY, 2), from_ahead(partner_z, "y", NY, 2)
    gg_far, gu_far, part_down, high2 = lax.optimization_barrier((gg_far, gu_far, part_down, high2))
    down_far = swap(part_down, "dp")
    grads = (gg, gg_other, gu, gu_other, gg_far, swap(gg_far, "core"), gu_far, swap(gu_far, "core"))
    own_pieces, partner_pieces = (high_z, high1, high2, high3), (partner_z, partner1, partner2, partner3)
    grad_gate, grad_up = weight_grads(place, own_low, own_pieces, partner_pieces, grads)
    in_z, grad_gate, grad_up = lax.optimization_barrier((in_z, grad_gate, grad_up))

    y = place[1]
    total = lax.dynamic_index_in_dim(in_z, y, 0, keepdims=False).astype(F32)
    for k in range(1, NY):
        slab = lax.dynamic_index_in_dim(in_z, (y + k) % NY, 0, keepdims=False)
        total = total + from_ahead(slab, "y", NY, NY - k).astype(F32)
    grad_input = total.astype(BF16)
    grad_input, down_far = lax.optimization_barrier((grad_input, down_far))
    grad_down = (part_down.astype(F32) + down_far.astype(F32)).astype(BF16)
    return grad_input, grad_gate, grad_up, grad_down


def solution(mesh):
    fine = Mesh(mesh.devices.reshape(2, NZ, NY, 2, 2), ("dp", "z", "y", "xh", "core"))
    tokens, col, row = ("dp", "z", "y"), ("xh", "core"), ("z", "y")
    in_specs = (
        P(tokens, col),
        P(tokens, col),
        P(("dp",) + col, row),
        P(("dp",) + col, row),
        P(col, row),
        P(col, row),
        P(row, col),
    )
    out_specs = (P(tokens, col), P(col, row), P(col, row), P(row, col))
    return jax.shard_map(body, mesh=fine, in_specs=in_specs, out_specs=out_specs, check_vma=False)
```

time: 211 us -> 182 us (0.86)
  waiting for transfers between devices: 110 us -> 77.9 us
  local copies, waits for them, and re-layouts: 17.2 us -> 6.34 us
  starting transfers between devices: 36.6 us -> 47.2 us
  Pallas kernels: 25 us -> 28.4 us
    ppermute x13, waiting for transfers between devices: 37 us -> 18.3 us  [swap(): return lax.ppermute(x, axis, [(0, 1), (1, 0)])]
    ppermute x19, waiting for transfers between devices: 71.7 us -> 53.1 us  [from_ahead(): return lax.ppermute(x, axis, [((d + k) % n, d) for d in range(n)])]
    unnamed x50 -> x34, local copies, waits for them, and re-layouts: 16.2 us -> 5.34 us
    ppermute x19, starting transfers between devices: 24.7 us -> 35 us  [from_ahead(): return lax.ppermute(x, axis, [((d + k) % n, d) for d in range(n)])]
    reduce_scatter x1, waiting for transfers between devices: 0.02 us -> 6.43 us  [body(): lax.psum_scatter(partial_in, 'z', scatter_dimension=0, tiled=True)]
    pallas_call x3 -> x4, Pallas kernels: 7.54 us -> 8.26 us  [the longest x1 5.48 us: input_grad(): pl.pallas_call(input_grad_kernel, grid=(3,), out_shape=jax.ShapeDtypeStru...]
  transfers between devices with their start and end apart: 34 -> 35, of which waited for: 24 -> 24; matrix products, arithmetic and copies ran while one was open for 2% -> 3% of each run, Pallas kernels for 7% -> 15%
where the time goes in v3:
time: 182 us
  waiting for transfers between devices  77.9 us (43%)
  starting transfers between devices  47.2 us (26%)
  Pallas kernels  28.4 us (16%)
  between operations  14 us (8%)
  other arithmetic  7.83 us (4%)
  local copies, waits for them, and re-layouts  6.34 us (3%)
    ppermute x19, waiting for transfers between devices, from_ahead(): return lax.ppermute(x, axis, [((d + k) % n, d) for d in range(n)])  53.1 us
    ppermute x19, starting transfers between devices, from_ahead(): return lax.ppermute(x, axis, [((d + k) % n, d) for d in range(n)])  35 us
    ppermute x13, waiting for transfers between devices, swap(): return lax.ppermute(x, axis, [(0, 1), (1, 0)])  18.3 us
    ppermute x13, starting transfers between devices, swap(): return lax.ppermute(x, axis, [(0, 1), (1, 0)])  12.1 us
    pallas_call x1, Pallas kernels, weight_grads(): pl.pallas_call(weight_kernel, grid=(6,), out_shape=(shape, shape), in_spe...  12 us
    reduce_scatter x1, waiting for transfers between devices, body(): lax.psum_scatter(partial_in, 'z', scatter_dimension=0, tiled=True)  6.43 us
    pallas_call x1, Pallas kernels, input_grad(): pl.pallas_call(input_grad_kernel, grid=(3,), out_shape=jax.ShapeDtypeStru...  5.48 us
    unnamed x34, local copies, waits for them, and re-layouts  5.34 us
  transfers between devices with their start and end apart: 35, of which 24 were waited for; matrix products, arithmetic and copies ran while one was open for 3% of the time, Pallas kernels for 15%

profile of v3, /device:TPU:2, one launch (start us, length us, event | category | flops | bytes accessed | tf_op | source)
XLA Modules:
  0.0 181.7 jit_solution(9275943839253825760)
XLA Ops:
  9.0 3.1 %collective-permute-start = (bf16[32,2304]{1,0:T(8,128)(2,1)S(1)}, bf16[32,2304]{1,0:T(8,128)(2,1)S(1)}, u32[]{:S(2)}, u32[]{:S(2)}) collective-permute-start(bf16[32,2304]{1,0:T(8,128)(2,1)S(1)} %shard_map.102.refs_0_), channel_id=1, source_target_pairs={{4,0},{8,4},{12,8},{0,12},{5,1},{9,5},{13,9},{1,13},{6,2},{10,6},{... | collective-permute-start | bytes 442376 | tf_op jit(solution)/shard_map/ppermute | solution.py:24
  13.8 4.6 %collective-permute-done.refs_1_ = bf16[32,2304]{1,0:T(8,128)(2,1)S(1)} collective-permute-done((bf16[32,2304]{1,0:T(8,128)(2,1)S(1)}, bf16[32,2304]{1,0:T(8,128)(2,1)S(1)}, u32[]{:S(2)}, u32[]{:S(2)}) %collective-permute-start) | collective-permute-done | bytes 147488 | tf_op jit(solution)/shard_map/ppermute | solution.py:24
  18.4 2.0 %collective-permute-done.1.refs_2_ = bf16[32,2304]{1,0:T(8,128)(2,1)S(1)} collective-permute-done((bf16[32,2304]{1,0:T(8,128)(2,1)S(1)}, bf16[32,2304]{1,0:T(8,128)(2,1)S(1)}, u32[]{:S(2)}, u32[]{:S(2)}) %collective-permute-start.1) | collective-permute-done | bytes 147488 | tf_op jit(solution)/shard_map/ppermute | solution.py:24
  20.4 1.7 collective-permute-done.2.refs_3_
  22.1 1.4 shard_map.103
  23.5 5.9 %collective-permute-start.6 = (bf16[32,1536]{1,0:T(8,128)(2,1)}, bf16[32,1536]{1,0:T(8,128)(2,1)S(1)}, u32[]{:S(2)}, u32[]{:S(2)}) collective-permute-start(bf16[32,1536]{1,0:T(8,128)(2,1)} %refs_0_.1), channel_id=1, source_target_pairs={{16,0},{32,16},{48,32},{64,48},{80,64},{96,80},{112,96},{0,112},{1... | collective-permute-start | bytes 294920 | tf_op jit(solution)/shard_map/ppermute | solution.py:24
  29.5 2.1 %collective-permute-start.4 = (bf16[256,512]{1,0:T(8,128)(2,1)}, bf16[256,512]{1,0:T(8,128)(2,1)S(1)}, u32[]{:S(2)}, u32[]{:S(2)}) collective-permute-start(bf16[256,512]{1,0:T(8,128)(2,1)} %param.10), channel_id=1, source_target_pairs={{0,2},{2,0},{1,3},{3,1},{4,6},{6,4},{5,7},{7,5},{8,10},{10,8},{9,1... | collective-permute-start | bytes 786440 | tf_op jit(solution)/shard_map/ppermute | solution.py:28
  32.0 3.6 %collective-permute-start.7 = (bf16[32,1536]{1,0:T(8,128)(2,1)S(1)}, bf16[32,1536]{1,0:T(8,128)(2,1)S(1)}, u32[]{:S(2)}, u32[]{:S(2)}) collective-permute-start(bf16[32,1536]{1,0:T(8,128)(2,1)S(1)} %collective-permute-done.6.refs_1_), channel_id=1, source_target_pairs={{16,0},{32,16},{48,32},{64,48},{80,64},{96,80},{112,96},{0,112},{1... | collective-permute-start | bytes 294920 | tf_op jit(solution)/shard_map/ppermute | solution.py:24
  35.6 2.0 %collective-permute-done.10.refs_7_ = bf16[32,1536]{1,0:T(8,128)(2,1)S(1)} collective-permute-done((bf16[32,1536]{1,0:T(8,128)(2,1)}, bf16[32,1536]{1,0:T(8,128)(2,1)S(1)}, u32[]{:S(2)}, u32[]{:S(2)}) %collective-permute-start.10) | collective-permute-done | bytes 98336 | tf_op jit(solution)/shard_map/ppermute | solution.py:24
  37.6 2.3 %collective-permute-done.7.refs_2_ = bf16[32,1536]{1,0:T(8,128)(2,1)S(1)} collective-permute-done((bf16[32,1536]{1,0:T(8,128)(2,1)S(1)}, bf16[32,1536]{1,0:T(8,128)(2,1)S(1)}, u32[]{:S(2)}, u32[]{:S(2)}) %collective-permute-start.7) | collective-permute-done | bytes 98336 | tf_op jit(solution)/shard_map/ppermute | solution.py:24
  40.0 3.7 %collective-permute-start.8 = (bf16[32,1536]{1,0:T(8,128)(2,1)S(1)}, bf16[32,1536]{1,0:T(8,128)(2,1)S(1)}, u32[]{:S(2)}, u32[]{:S(2)}) collective-permute-start(bf16[32,1536]{1,0:T(8,128)(2,1)S(1)} %collective-permute-done.7.refs_2_), channel_id=1, source_target_pairs={{16,0},{32,16},{48,32},{64,48},{80,64},{96,80},{112,96},{0,112},{1... | collective-permute-start | bytes 294920 | tf_op jit(solution)/shard_map/ppermute | solution.py:24
  43.7 2.2 %collective-permute-start.3 = (bf16[256,512]{1,0:T(8,128)(2,1)}, bf16[256,512]{1,0:T(8,128)(2,1)S(1)}, u32[]{:S(2)}, u32[]{:S(2)}) collective-permute-start(bf16[256,512]{1,0:T(8,128)(2,1)} %param.9), channel_id=1, source_target_pairs={{0,2},{2,0},{1,3},{3,1},{4,6},{6,4},{5,7},{7,5},{8,10},{10,8},{9,1... | collective-permute-start | bytes 786440 | tf_op jit(solution)/shard_map/ppermute | solution.py:28
  45.8 1.8 collective-permute-done.8.refs_3_
  47.6 3.7 %collective-permute-start.9 = (bf16[32,1536]{1,0:T(8,128)(2,1)S(1)}, bf16[32,1536]{1,0:T(8,128)(2,1)S(1)}, u32[]{:S(2)}, u32[]{:S(2)}) collective-permute-start(bf16[32,1536]{1,0:T(8,128)(2,1)S(1)} %collective-permute-done.8.refs_3_), channel_id=1, source_target_pairs={{16,0},{32,16},{48,32},{64,48},{80,64},{96,80},{112,96},{0,112},{1... | collective-permute-start | bytes 294920 | tf_op jit(solution)/shard_map/ppermute | solution.py:24
  51.3 1.0 select_bitcast_fusion.1
  52.3 1.4 collective-permute-done.12.refs_5_
  53.7 1.8 collective-permute-done.9.refs_4_
  55.5 1.4 shard_map.104
  58.5 2.0 %collective-permute-start.15 = (bf16[256,768]{1,0:T(8,128)(2,1)}, bf16[256,768]{1,0:T(8,128)(2,1)}, u32[]{:S(2)}, u32[]{:S(2)}) collective-permute-start(bf16[256,768]{1,0:T(8,128)(2,1)} %bitcast.10.refs_0_), channel_id=1, source_target_pairs={{12,0},{0,4},{4,8},{8,12},{13,1},{1,5},{5,9},{9,13},{14,2},{2,6},{... | collective-permute-start | bytes 1179656 | tf_op jit(solution)/shard_map/ppermute | solution.py:24
  60.5 1.1 pad_maximum_fusion
  61.5 8.7 %collective-permute-done.14.refs_1_ = bf16[256,768]{1,0:T(8,128)(2,1)} collective-permute-done((bf16[256,768]{1,0:T(8,128)(2,1)}, bf16[256,768]{1,0:T(8,128)(2,1)}, u32[]{:S(2)}, u32[]{:S(2)}) %collective-permute-start.14) | collective-permute-done | bytes 393248 | tf_op jit(solution)/shard_map/ppermute | solution.py:24
  70.2 1.2 collective-permute-done.15.refs_3_
  71.4 1.7 collective-permute-done.13.refs_4_
  73.3 4.1 %shard_map.105 = (f32[2,256,512]{2,1,0:T(8,128)S(1)}, bf16[2,256,512]{2,1,0:T(8,128)(2,1)S(1)}) custom-call(s32[4]{0:T(128)S(1)} %pad_add_fusion.place, bf16[1024,1536]{1,0:T(8,128)(2,1)} %all-gather.3.cloned.1.call-done.go, bf16[512,1536]{1,0:T(8,128)(2,1)S(1)} %copy-done.4), custom_call_target="tpu_custom_call" | custom-call | tf_op jit(solution)/shard_map/pallas_call | solution.py:96
  77.5 1.9 %collective-permute-done.16 = bf16[2,256,512]{2,1,0:T(8,128)(2,1)S(1)} collective-permute-done((bf16[2,256,512]{2,1,0:T(8,128)(2,1)S(1)}, bf16[2,256,512]{2,1,0:T(8,128)(2,1)S(1)}, u32[]{:S(2)}, u32[]{:S(2)}) %collective-permute-start.16) | collective-permute-done | bytes 524320 | tf_op jit(solution)/shard_map/ppermute | solution.py:28
  79.7 2.2 %collective-permute-start.17 = (bf16[2,256,512]{2,1,0:T(8,128)(2,1)S(1)}, bf16[2,256,512]{2,1,0:T(8,128)(2,1)S(1)}, u32[]{:S(2)}, u32[]{:S(2)}) collective-permute-start(bf16[2,256,512]{2,1,0:T(8,128)(2,1)S(1)} %get-tuple-element.72), channel_id=1, source_target_pairs={{0,2},{2,0},{1,3},{3,1},{4,6},{6,4},{5,7},{7,5},{8,10},{10,8},{9,1... | collective-permute-start | bytes 1572872 | tf_op jit(solution)/shard_map/ppermute | solution.py:28
  81.8 1.7 collective-permute-start.20
  83.8 4.1 %shard_map.106 = bf16[512,1536]{1,0:T(8,128)(2,1)S(1)} custom-call(s32[4]{0:T(128)S(1)} %pad_add_fusion.place, bf16[2,256,512]{2,1,0:T(8,128)(2,1)S(1)} %fusion.12.hidden, bf16[2,256,512]{2,1,0:T(8,128)(2,1)S(1)} %collective-permute-done.5.hidden_other, bf16[1024,1536]{1,0:T(8,128)(2,1)} %all-gather.3.cloned.1.call-done.go), custom_call_target="tpu_custom_call" | custom-call | tf_op jit(solution)/shard_map/pallas_call | solution.py:151
  87.9 7.3 %collective-permute-done.17 = bf16[2,256,512]{2,1,0:T(8,128)(2,1)S(1)} collective-permute-done((bf16[2,256,512]{2,1,0:T(8,128)(2,1)S(1)}, bf16[2,256,512]{2,1,0:T(8,128)(2,1)S(1)}, u32[]{:S(2)}, u32[]{:S(2)}) %collective-permute-start.17) | collective-permute-done | bytes 524320 | tf_op jit(solution)/shard_map/ppermute | solution.py:28
  96.5 4.9 %collective-permute-done.20.refs_5_ = bf16[256,1536]{1,0:T(8,128)(2,1)S(1)} collective-permute-done((bf16[256,1536]{1,0:T(8,128)(2,1)}, bf16[256,1536]{1,0:T(8,128)(2,1)S(1)}, u32[]{:S(2)}, u32[]{:S(2)}) %collective-permute-start.20) | collective-permute-done | bytes 786464 | tf_op jit(solution)/shard_map/ppermute | solution.py:24
  101.3 2.6 %collective-permute-done.21.refs_7_ = bf16[256,1536]{1,0:T(8,128)(2,1)S(1)} collective-permute-done((bf16[256,1536]{1,0:T(8,128)(2,1)}, bf16[256,1536]{1,0:T(8,128)(2,1)S(1)}, u32[]{:S(2)}, u32[]{:S(2)}) %collective-permute-start.21) | collective-permute-done | bytes 786464 | tf_op jit(solution)/shard_map/ppermute | solution.py:24
  104.9 5.5 %shard_map.107 = bf16[1024,1536]{1,0:T(8,128)(2,1)} custom-call(s32[4]{0:T(128)S(1)} %pad_add_fusion.place, bf16[2,256,512]{2,1,0:T(8,128)(2,1)S(1)} %get-tuple-element.75.gg.refs_8_, bf16[2,256,512]{2,1,0:T(8,128)(2,1)S(1)} %collective-permute-done.18.gg_other.refs_9_, bf16[2,256,512]{2,1,0:T(8,128)(2,1)S(1)} %get-tuple-element.74.gu.refs_10_, ...), custom_call_target="tpu_custom_call" | custom-call | tf_op jit(solution)/shard_map/pallas_call | solution.py:123
  111.3 1.3 collective-permute-start.22
  113.4 3.5 %collective-permute-start.25 = (bf16[256,1536]{1,0:T(8,128)(2,1)}, bf16[256,1536]{1,0:T(8,128)(2,1)S(1)}, u32[]{:S(2)}, u32[]{:S(2)}) collective-permute-start(bf16[256,1536]{1,0:T(8,128)(2,1)} %collective-permute-done.13.refs_4_), channel_id=1, source_target_pairs={{8,0},{12,4},{0,8},{4,12},{9,1},{13,5},{1,9},{5,13},{10,2},{14,6},... | collective-permute-start | bytes 2359304 | tf_op jit(solution)/shard_map/ppermute | solution.py:24
  116.9 10.2 %collective-permute-done.24.refs_2_ = bf16[256,768]{1,0:T(8,128)(2,1)S(1)} collective-permute-done((bf16[256,768]{1,0:T(8,128)(2,1)}, bf16[256,768]{1,0:T(8,128)(2,1)S(1)}, u32[]{:S(2)}, u32[]{:S(2)}) %collective-permute-start.24) | collective-permute-done | bytes 393248 | tf_op jit(solution)/shard_map/ppermute | solution.py:24
  127.9 7.3 %collective-permute-done.23.refs_14_ = bf16[2,256,512]{2,1,0:T(8,128)(2,1)} collective-permute-done((bf16[2,256,512]{2,1,0:T(8,128)(2,1)S(1)}, bf16[2,256,512]{2,1,0:T(8,128)(2,1)}, u32[]{:S(2)}, u32[]{:S(2)}) %collective-permute-start.23) | collective-permute-done | bytes 524320 | tf_op jit(solution)/shard_map/ppermute | solution.py:28
  135.2 1.3 collective-permute-start.31
  137.0 4.1 %collective-permute-done.25.refs_6_ = bf16[256,1536]{1,0:T(8,128)(2,1)S(1)} collective-permute-done((bf16[256,1536]{1,0:T(8,128)(2,1)}, bf16[256,1536]{1,0:T(8,128)(2,1)S(1)}, u32[]{:S(2)}, u32[]{:S(2)}) %collective-permute-start.25) | collective-permute-done | bytes 786464 | tf_op jit(solution)/shard_map/ppermute | solution.py:24
  141.2 1.0 copy-done.10
  142.2 12.0 %shard_map.108 = (bf16[1536,512]{1,0:T(8,128)(2,1)}, bf16[1536,512]{1,0:T(8,128)(2,1)}) custom-call(s32[4]{0:T(128)S(1)} %pad_add_fusion.place, bf16[1024,768]{1,0:T(8,128)(2,1)} %all-gather.5.cloned.1.call-done.own, bf16[256,768]{1,0:T(8,128)(2,1)} %bitcast.10.refs_0_, bf16[256,768]{1,0:T(8,128)(2,1)} %collective-permute-done.14.refs_1_, ...), custom_call_target="tpu_custom_call" | custom-call | tf_op jit(solution)/shard_map/pallas_call | solution.py:217
  154.2 6.4 %reduce-scatter.2.cloned.1.call-done = bf16[128,1536]{1,0:T(8,128)(2,1)} async-done(((bf16[1024,1536]{1,0:T(8,128)(2,1)}), bf16[128,1536]{1,0:T(8,128)(2,1)}) %reduce-scatter.2.cloned.1.call-update) | async-done | bytes 393232 | tf_op jit(solution)/shard_map/reduce_scatter | solution.py:284
  160.6 1.0 dynamic-slice_bitcast_fusion.2
  161.6 1.6 collective-permute-start.28
  163.1 2.8 %collective-permute-start.29 = (bf16[32,1536]{1,0:T(8,128)(2,1)S(1)}, bf16[32,1536]{1,0:T(8,128)(2,1)S(1)}, u32[]{:S(2)}, u32[]{:S(2)}) collective-permute-start(bf16[32,1536]{1,0:T(8,128)(2,1)S(1)} %get-tuple-element.82), channel_id=1, source_target_pairs={{8,0},{12,4},{0,8},{4,12},{9,1},{13,5},{1,9},{5,13},{10,2},{14,6},... | collective-permute-start | bytes 294920 | tf_op jit(solution)/shard_map/ppermute | solution.py:24
  166.0 1.3 collective-permute-start.30
  167.5 2.1 %collective-permute-done.29 = bf16[32,1536]{1,0:T(8,128)(2,1)S(1)} collective-permute-done((bf16[32,1536]{1,0:T(8,128)(2,1)S(1)}, bf16[32,1536]{1,0:T(8,128)(2,1)S(1)}, u32[]{:S(2)}, u32[]{:S(2)}) %collective-permute-start.29) | collective-permute-done | bytes 98336 | tf_op jit(solution)/shard_map/ppermute | solution.py:24
  170.6 1.6 fusion.15
  172.2 2.9 %add_convert_fusion = bf16[512,1536]{1,0:T(8,128)(2,1)} fusion(bf16[512,1536]{1,0:T(8,128)(2,1)} %collective-permute-done.31, bf16[512,1536]{1,0:T(8,128)(2,1)S(1)} %shard_map.106), kind=kLoop, calls=%fused_computation | loop fusion | flops 3145728 | bytes 4718592 | tf_op jit(solution)/shard_map/convert_element_type | solution.py:302
  (76 shorter events, 12.5 us)
Async XLA Ops:
  7.2 66.1 %all-gather.3.cloned.1.call-start = ((), (), s32[]{:S(2)}) async-start(), calls=%async_computation.1 | async-start | bytes 3538944 | tf_op jit(solution)/shard_map/all_gather | solution.py:253
  9.0 46.5 %copy-start.8 = (bf16[32,1536]{1,0:T(8,128)(2,1)S(1)}, bf16[32,1536]{1,0:T(8,128)(2,1)}, u32[]{:S(2)}) copy-start(bf16[32,1536]{1,0:T(8,128)(2,1)} %refs_0_.1) | copy-start | bytes 294916
  9.0 48.9 %copy-start.16 = (bf16[256,512]{1,0:T(8,128)(2,1)S(1)}, bf16[256,512]{1,0:T(8,128)(2,1)}, u32[]{:S(2)}) copy-start(bf16[256,512]{1,0:T(8,128)(2,1)} %param.9) | copy-start | bytes 786436
  9.0 9.4 %collective-permute-start = (bf16[32,2304]{1,0:T(8,128)(2,1)S(1)}, bf16[32,2304]{1,0:T(8,128)(2,1)S(1)}, u32[]{:S(2)}, u32[]{:S(2)}) collective-permute-start(bf16[32,2304]{1,0:T(8,128)(2,1)S(1)} %shard_map.102.refs_0_), channel_id=1, source_target_pairs={{4,0},{8,4},{12,8},{0,12},{5,1},{9,5},{13,9},{1,13},{6,2},{10,6},{... | collective-permute-start | bytes 442376 | tf_op jit(solution)/shard_map/ppermute | solution.py:24
  12.1 8.3 %collective-permute-start.1 = (bf16[32,2304]{1,0:T(8,128)(2,1)S(1)}, bf16[32,2304]{1,0:T(8,128)(2,1)S(1)}, u32[]{:S(2)}, u32[]{:S(2)}) collective-permute-start(bf16[32,2304]{1,0:T(8,128)(2,1)S(1)} %shard_map.102.refs_0_), channel_id=1, source_target_pairs={{8,0},{12,4},{0,8},{4,12},{9,1},{13,5},{1,9},{5,13},{10,2},{14,6},... | collective-permute-start | bytes 442376 | tf_op jit(solution)/shard_map/ppermute | solution.py:24
  12.7 9.3 %collective-permute-start.2 = (bf16[32,2304]{1,0:T(8,128)(2,1)S(1)}, bf16[32,2304]{1,0:T(8,128)(2,1)S(1)}, u32[]{:S(2)}, u32[]{:S(2)}) collective-permute-start(bf16[32,2304]{1,0:T(8,128)(2,1)S(1)} %shard_map.102.refs_0_), channel_id=1, source_target_pairs={{12,0},{0,4},{4,8},{8,12},{13,1},{1,5},{5,9},{9,13},{14,2},{2,6},{... | collective-permute-start | bytes 442376 | tf_op jit(solution)/shard_map/ppermute | solution.py:24
  23.5 117.6 %all-gather.5.cloned.1.call-start = ((), (), s32[]{:S(2)}) async-start(), calls=%async_computation.3 | async-start | bytes 1769472 | tf_op jit(solution)/shard_map/all_gather | solution.py:267
  23.5 8.5 %collective-permute-start.6 = (bf16[32,1536]{1,0:T(8,128)(2,1)}, bf16[32,1536]{1,0:T(8,128)(2,1)S(1)}, u32[]{:S(2)}, u32[]{:S(2)}) collective-permute-start(bf16[32,1536]{1,0:T(8,128)(2,1)} %refs_0_.1), channel_id=1, source_target_pairs={{16,0},{32,16},{48,32},{64,48},{80,64},{96,80},{112,96},{0,112},{1... | collective-permute-start | bytes 294920 | tf_op jit(solution)/shard_map/ppermute | solution.py:24
  29.5 21.9 %collective-permute-start.4 = (bf16[256,512]{1,0:T(8,128)(2,1)}, bf16[256,512]{1,0:T(8,128)(2,1)S(1)}, u32[]{:S(2)}, u32[]{:S(2)}) collective-permute-start(bf16[256,512]{1,0:T(8,128)(2,1)} %param.10), channel_id=1, source_target_pairs={{0,2},{2,0},{1,3},{3,1},{4,6},{6,4},{5,7},{7,5},{8,10},{10,8},{9,1... | collective-permute-start | bytes 786440 | tf_op jit(solution)/shard_map/ppermute | solution.py:28
  31.6 6.0 %collective-permute-start.10 = (bf16[32,1536]{1,0:T(8,128)(2,1)}, bf16[32,1536]{1,0:T(8,128)(2,1)S(1)}, u32[]{:S(2)}, u32[]{:S(2)}) collective-permute-start(bf16[32,1536]{1,0:T(8,128)(2,1)} %refs_0_.1), channel_id=1, source_target_pairs={{112,0},{0,16},{16,32},{32,48},{48,64},{64,80},{80,96},{96,112},{1... | collective-permute-start | bytes 294920 | tf_op jit(solution)/shard_map/ppermute | solution.py:24
  32.0 7.9 %collective-permute-start.7 = (bf16[32,1536]{1,0:T(8,128)(2,1)S(1)}, bf16[32,1536]{1,0:T(8,128)(2,1)S(1)}, u32[]{:S(2)}, u32[]{:S(2)}) collective-permute-start(bf16[32,1536]{1,0:T(8,128)(2,1)S(1)} %collective-permute-done.6.refs_1_), channel_id=1, source_target_pairs={{16,0},{32,16},{48,32},{64,48},{80,64},{96,80},{112,96},{0,112},{1... | collective-permute-start | bytes 294920 | tf_op jit(solution)/shard_map/ppermute | solution.py:24
  37.6 8.2 %collective-permute-start.11 = (bf16[32,1536]{1,0:T(8,128)(2,1)S(1)}, bf16[32,1536]{1,0:T(8,128)(2,1)S(1)}, u32[]{:S(2)}, u32[]{:S(2)}) collective-permute-start(bf16[32,1536]{1,0:T(8,128)(2,1)S(1)} %collective-permute-done.10.refs_7_), channel_id=1, source_target_pairs={{112,0},{0,16},{16,32},{32,48},{48,64},{64,80},{80,96},{96,112},{1... | collective-permute-start | bytes 294920 | tf_op jit(solution)/shard_map/ppermute | solution.py:24
  40.0 7.7 %collective-permute-start.8 = (bf16[32,1536]{1,0:T(8,128)(2,1)S(1)}, bf16[32,1536]{1,0:T(8,128)(2,1)S(1)}, u32[]{:S(2)}, u32[]{:S(2)}) collective-permute-start(bf16[32,1536]{1,0:T(8,128)(2,1)S(1)} %collective-permute-done.7.refs_2_), channel_id=1, source_target_pairs={{16,0},{32,16},{48,32},{64,48},{80,64},{96,80},{112,96},{0,112},{1... | collective-permute-start | bytes 294920 | tf_op jit(solution)/shard_map/ppermute | solution.py:24
  43.7 14.2 %collective-permute-start.3 = (bf16[256,512]{1,0:T(8,128)(2,1)}, bf16[256,512]{1,0:T(8,128)(2,1)S(1)}, u32[]{:S(2)}, u32[]{:S(2)}) collective-permute-start(bf16[256,512]{1,0:T(8,128)(2,1)} %param.9), channel_id=1, source_target_pairs={{0,2},{2,0},{1,3},{3,1},{4,6},{6,4},{5,7},{7,5},{8,10},{10,8},{9,1... | collective-permute-start | bytes 786440 | tf_op jit(solution)/shard_map/ppermute | solution.py:28
  45.8 7.9 %collective-permute-start.12 = (bf16[32,1536]{1,0:T(8,128)(2,1)S(1)}, bf16[32,1536]{1,0:T(8,128)(2,1)S(1)}, u32[]{:S(2)}, u32[]{:S(2)}) collective-permute-start(bf16[32,1536]{1,0:T(8,128)(2,1)S(1)} %collective-permute-done.11.refs_6_), channel_id=1, source_target_pairs={{112,0},{0,16},{16,32},{32,48},{48,64},{64,80},{80,96},{96,112},{1... | collective-permute-start | bytes 294920 | tf_op jit(solution)/shard_map/ppermute | solution.py:24
  47.6 7.9 %collective-permute-start.9 = (bf16[32,1536]{1,0:T(8,128)(2,1)S(1)}, bf16[32,1536]{1,0:T(8,128)(2,1)S(1)}, u32[]{:S(2)}, u32[]{:S(2)}) collective-permute-start(bf16[32,1536]{1,0:T(8,128)(2,1)S(1)} %collective-permute-done.8.refs_3_), channel_id=1, source_target_pairs={{16,0},{32,16},{48,32},{64,48},{80,64},{96,80},{112,96},{0,112},{1... | collective-permute-start | bytes 294920 | tf_op jit(solution)/shard_map/ppermute | solution.py:24
  56.9 16.2 %collective-permute-start.13 = (bf16[256,1536]{1,0:T(8,128)(2,1)S(1)}, bf16[256,1536]{1,0:T(8,128)(2,1)}, u32[]{:S(2)}, u32[]{:S(2)}) collective-permute-start(bf16[256,1536]{1,0:T(8,128)(2,1)S(1)} %bitcast.26), channel_id=1, source_target_pairs={{0,128},{128,0},{1,129},{129,1},{2,130},{130,2},{3,131},{131,3},{4... | collective-permute-start | bytes 2359304 | tf_op jit(solution)/shard_map/ppermute | solution.py:28
  57.9 15.4 %copy-start.4 = (bf16[512,1536]{1,0:T(8,128)(2,1)S(1)}, bf16[512,1536]{1,0:T(8,128)(2,1)}, u32[]{:S(2)}) copy-start(bf16[512,1536]{1,0:T(8,128)(2,1)} %w_down.1) | copy-start | bytes 4718596
  58.3 3.3 %collective-permute-start.5 = (bf16[2,256,512]{2,1,0:T(8,128)(2,1)S(1)}, bf16[2,256,512]{2,1,0:T(8,128)(2,1)S(1)}, u32[]{:S(2)}, u32[]{:S(2)}) collective-permute-start(bf16[2,256,512]{2,1,0:T(8,128)(2,1)S(1)} %fusion.12.hidden), channel_id=1, source_target_pairs={{0,1},{1,0},{2,3},{3,2},{4,5},{5,4},{6,7},{7,6},{8,9},{9,8},{10,11... | collective-permute-start | bytes 1572872 | tf_op jit(solution)/shard_map/ppermute | solution.py:28
  58.4 11.8 %collective-permute-start.14 = (bf16[256,768]{1,0:T(8,128)(2,1)}, bf16[256,768]{1,0:T(8,128)(2,1)}, u32[]{:S(2)}, u32[]{:S(2)}) collective-permute-start(bf16[256,768]{1,0:T(8,128)(2,1)} %bitcast.10.refs_0_), channel_id=1, source_target_pairs={{4,0},{8,4},{12,8},{0,12},{5,1},{9,5},{13,9},{1,13},{6,2},{10,6},{... | collective-permute-start | bytes 1179656 | tf_op jit(solution)/shard_map/ppermute | solution.py:24
  58.5 13.0 %collective-permute-start.15 = (bf16[256,768]{1,0:T(8,128)(2,1)}, bf16[256,768]{1,0:T(8,128)(2,1)}, u32[]{:S(2)}, u32[]{:S(2)}) collective-permute-start(bf16[256,768]{1,0:T(8,128)(2,1)} %bitcast.10.refs_0_), channel_id=1, source_target_pairs={{12,0},{0,4},{4,8},{8,12},{13,1},{1,5},{5,9},{9,13},{14,2},{2,6},{... | collective-permute-start | bytes 1179656 | tf_op jit(solution)/shard_map/ppermute | solution.py:24
  73.3 87.3 %reduce-scatter.2.cloned.1.call-start = ((), (), s32[]{:S(2)}) async-start(), calls=%async_computation.2 | async-start | bytes 3538944 | tf_op jit(solution)/shard_map/reduce_scatter | solution.py:284
  77.4 2.0 %collective-permute-start.16 = (bf16[2,256,512]{2,1,0:T(8,128)(2,1)S(1)}, bf16[2,256,512]{2,1,0:T(8,128)(2,1)S(1)}, u32[]{:S(2)}, u32[]{:S(2)}) collective-permute-start(bf16[2,256,512]{2,1,0:T(8,128)(2,1)S(1)} %get-tuple-element.44), channel_id=1, source_target_pairs={{0,1},{1,0},{2,3},{3,2},{4,5},{5,4},{6,7},{7,6},{8,9},{9,8},{10,11... | collective-permute-start | bytes 1572872 | tf_op jit(solution)/shard_map/ppermute | solution.py:28
  79.6 15.6 %copy-start.12 = (bf16[2,256,512]{2,1,0:T(8,128)(2,1)S(1)}, bf16[2,256,512]{2,1,0:T(8,128)(2,1)}, u32[]{:S(2)}) copy-start(bf16[2,256,512]{2,1,0:T(8,128)(2,1)} %get-tuple-element.50) | copy-start | bytes 1572868
  79.6 15.6 %copy-start.13 = (bf16[2,256,512]{2,1,0:T(8,128)(2,1)S(1)}, bf16[2,256,512]{2,1,0:T(8,128)(2,1)}, u32[]{:S(2)}) copy-start(bf16[2,256,512]{2,1,0:T(8,128)(2,1)} %get-tuple-element.49) | copy-start | bytes 1572868
  79.7 15.6 %collective-permute-start.17 = (bf16[2,256,512]{2,1,0:T(8,128)(2,1)S(1)}, bf16[2,256,512]{2,1,0:T(8,128)(2,1)S(1)}, u32[]{:S(2)}, u32[]{:S(2)}) collective-permute-start(bf16[2,256,512]{2,1,0:T(8,128)(2,1)S(1)} %get-tuple-element.72), channel_id=1, source_target_pairs={{0,2},{2,0},{1,3},{3,1},{4,6},{6,4},{5,7},{7,5},{8,10},{10,8},{9,1... | collective-permute-start | bytes 1572872 | tf_op jit(solution)/shard_map/ppermute | solution.py:28
  81.8 19.5 %collective-permute-start.20 = (bf16[256,1536]{1,0:T(8,128)(2,1)}, bf16[256,1536]{1,0:T(8,128)(2,1)S(1)}, u32[]{:S(2)}, u32[]{:S(2)}) collective-permute-start(bf16[256,1536]{1,0:T(8,128)(2,1)} %collective-permute-done.13.refs_4_), channel_id=1, source_target_pairs={{4,0},{8,4},{12,8},{0,12},{5,1},{9,5},{13,9},{1,13},{6,2},{10,6},{... | collective-permute-start | bytes 2359304 | tf_op jit(solution)/shard_map/ppermute | solution.py:24
  83.5 20.4 %collective-permute-start.21 = (bf16[256,1536]{1,0:T(8,128)(2,1)}, bf16[256,1536]{1,0:T(8,128)(2,1)S(1)}, u32[]{:S(2)}, u32[]{:S(2)}) collective-permute-start(bf16[256,1536]{1,0:T(8,128)(2,1)} %collective-permute-done.13.refs_4_), channel_id=1, source_target_pairs={{12,0},{0,4},{4,8},{8,12},{13,1},{1,5},{5,9},{9,13},{14,2},{2,6},{... | collective-permute-start | bytes 2359304 | tf_op jit(solution)/shard_map/ppermute | solution.py:24
  95.2 9.7 %copy-start.5 = (bf16[1536,512]{1,0:T(8,128)(2,1)S(1)}, bf16[1536,512]{1,0:T(8,128)(2,1)}, u32[]{:S(2)}) copy-start(bf16[1536,512]{1,0:T(8,128)(2,1)} %w_gate.1) | copy-start | bytes 4718596
  95.2 9.7 %copy-start.6 = (bf16[1536,512]{1,0:T(8,128)(2,1)S(1)}, bf16[1536,512]{1,0:T(8,128)(2,1)}, u32[]{:S(2)}) copy-start(bf16[1536,512]{1,0:T(8,128)(2,1)} %w_up.1) | copy-start | bytes 4718596
  95.8 15.4 %copy-start.1 = (bf16[2,256,512]{2,1,0:T(8,128)(2,1)}, bf16[2,256,512]{2,1,0:T(8,128)(2,1)S(1)}, u32[]{:S(2)}) copy-start(bf16[2,256,512]{2,1,0:T(8,128)(2,1)S(1)} %get-tuple-element.75.gg.refs_8_) | copy-start | bytes 1572868
  95.8 16.7 %copy-start = (bf16[2,256,512]{2,1,0:T(8,128)(2,1)}, bf16[2,256,512]{2,1,0:T(8,128)(2,1)S(1)}, u32[]{:S(2)}) copy-start(bf16[2,256,512]{2,1,0:T(8,128)(2,1)S(1)} %get-tuple-element.74.gu.refs_10_) | copy-start | bytes 1572868
  95.9 8.1 %collective-permute-start.18 = (bf16[2,256,512]{2,1,0:T(8,128)(2,1)S(1)}, bf16[2,256,512]{2,1,0:T(8,128)(2,1)S(1)}, u32[]{:S(2)}, u32[]{:S(2)}) collective-permute-start(bf16[2,256,512]{2,1,0:T(8,128)(2,1)S(1)} %get-tuple-element.75.gg.refs_8_), channel_id=1, source_target_pairs={{0,1},{1,0},{2,3},{3,2},{4,5},{5,4},{6,7},{7,6},{8,9},{9,8},{10,11... | collective-permute-start | bytes 1572872 | tf_op jit(solution)/shard_map/ppermute | solution.py:28
  96.0 9.0 %collective-permute-start.19 = (bf16[2,256,512]{2,1,0:T(8,128)(2,1)S(1)}, bf16[2,256,512]{2,1,0:T(8,128)(2,1)S(1)}, u32[]{:S(2)}, u32[]{:S(2)}) collective-permute-start(bf16[2,256,512]{2,1,0:T(8,128)(2,1)S(1)} %get-tuple-element.74.gu.refs_10_), channel_id=1, source_target_pairs={{0,1},{1,0},{2,3},{3,2},{4,5},{5,4},{6,7},{7,6},{8,9},{9,8},{10,11... | collective-permute-start | bytes 1572872 | tf_op jit(solution)/shard_map/ppermute | solution.py:28
  101.3 2.6 %copy-start.14 = (bf16[256,1536]{1,0:T(8,128)(2,1)}, bf16[256,1536]{1,0:T(8,128)(2,1)S(1)}, u32[]{:S(2)}) copy-start(bf16[256,1536]{1,0:T(8,128)(2,1)S(1)} %collective-permute-done.20.refs_5_) | copy-start | bytes 2359300
  104.0 1.0 copy-start.15
  104.9 5.5 %copy-start.2 = (bf16[2,256,512]{2,1,0:T(8,128)(2,1)}, bf16[2,256,512]{2,1,0:T(8,128)(2,1)S(1)}, u32[]{:S(2)}) copy-start(bf16[2,256,512]{2,1,0:T(8,128)(2,1)S(1)} %collective-permute-done.18.gg_other.refs_9_) | copy-start | bytes 1572868
  111.3 16.6 %collective-permute-start.22 = (bf16[2,256,512]{2,1,0:T(8,128)(2,1)S(1)}, bf16[2,256,512]{2,1,0:T(8,128)(2,1)}, u32[]{:S(2)}, u32[]{:S(2)}) collective-permute-start(bf16[2,256,512]{2,1,0:T(8,128)(2,1)S(1)} %get-tuple-element.75.gg.refs_8_), channel_id=1, source_target_pairs={{0,128},{128,0},{1,129},{129,1},{2,130},{130,2},{3,131},{131,3},{4... | collective-permute-start | bytes 1572872 | tf_op jit(solution)/shard_map/ppermute | solution.py:28
  112.6 22.7 %collective-permute-start.23 = (bf16[2,256,512]{2,1,0:T(8,128)(2,1)S(1)}, bf16[2,256,512]{2,1,0:T(8,128)(2,1)}, u32[]{:S(2)}, u32[]{:S(2)}) collective-permute-start(bf16[2,256,512]{2,1,0:T(8,128)(2,1)S(1)} %get-tuple-element.74.gu.refs_10_), channel_id=1, source_target_pairs={{0,128},{128,0},{1,129},{129,1},{2,130},{130,2},{3,131},{131,3},{4... | collective-permute-start | bytes 1572872 | tf_op jit(solution)/shard_map/ppermute | solution.py:28
  113.4 13.8 %collective-permute-start.24 = (bf16[256,768]{1,0:T(8,128)(2,1)}, bf16[256,768]{1,0:T(8,128)(2,1)S(1)}, u32[]{:S(2)}, u32[]{:S(2)}) collective-permute-start(bf16[256,768]{1,0:T(8,128)(2,1)} %bitcast.10.refs_0_), channel_id=1, source_target_pairs={{8,0},{12,4},{0,8},{4,12},{9,1},{13,5},{1,9},{5,13},{10,2},{14,6},... | collective-permute-start | bytes 1179656 | tf_op jit(solution)/shard_map/ppermute | solution.py:24
  113.4 27.7 %collective-permute-start.25 = (bf16[256,1536]{1,0:T(8,128)(2,1)}, bf16[256,1536]{1,0:T(8,128)(2,1)S(1)}, u32[]{:S(2)}, u32[]{:S(2)}) collective-permute-start(bf16[256,1536]{1,0:T(8,128)(2,1)} %collective-permute-done.13.refs_4_), channel_id=1, source_target_pairs={{8,0},{12,4},{0,8},{4,12},{9,1},{13,5},{1,9},{5,13},{10,2},{14,6},... | collective-permute-start | bytes 2359304 | tf_op jit(solution)/shard_map/ppermute | solution.py:24
  135.2 37.0 %collective-permute-start.31 = (bf16[512,1536]{1,0:T(8,128)(2,1)S(1)}, bf16[512,1536]{1,0:T(8,128)(2,1)}, u32[]{:S(2)}, u32[]{:S(2)}) collective-permute-start(bf16[512,1536]{1,0:T(8,128)(2,1)S(1)} %shard_map.106), channel_id=1, source_target_pairs={{0,128},{128,0},{1,129},{129,1},{2,130},{130,2},{3,131},{131,3},{4... | collective-permute-start | bytes 4718600 | tf_op jit(solution)/shard_map/ppermute | solution.py:28
  136.5 4.6 %collective-permute-start.26 = (bf16[2,256,512]{2,1,0:T(8,128)(2,1)}, bf16[2,256,512]{2,1,0:T(8,128)(2,1)S(1)}, u32[]{:S(2)}, u32[]{:S(2)}) collective-permute-start(bf16[2,256,512]{2,1,0:T(8,128)(2,1)} %collective-permute-done.22.refs_12_), channel_id=1, source_target_pairs={{0,1},{1,0},{2,3},{3,2},{4,5},{5,4},{6,7},{7,6},{8,9},{9,8},{10,11... | collective-permute-start | bytes 1572872 | tf_op jit(solution)/shard_map/ppermute | solution.py:28
  136.5 4.6 %collective-permute-start.27 = (bf16[2,256,512]{2,1,0:T(8,128)(2,1)}, bf16[2,256,512]{2,1,0:T(8,128)(2,1)S(1)}, u32[]{:S(2)}, u32[]{:S(2)}) collective-permute-start(bf16[2,256,512]{2,1,0:T(8,128)(2,1)} %collective-permute-done.23.refs_14_), channel_id=1, source_target_pairs={{0,1},{1,0},{2,3},{3,2},{4,5},{5,4},{6,7},{7,6},{8,9},{9,8},{10,11... | collective-permute-start | bytes 1572872 | tf_op jit(solution)/shard_map/ppermute | solution.py:28
  141.2 1.0 copy-start.10
  161.6 5.9 %collective-permute-start.28 = (bf16[32,1536]{1,0:T(8,128)(2,1)S(1)}, bf16[32,1536]{1,0:T(8,128)(2,1)S(1)}, u32[]{:S(2)}, u32[]{:S(2)}) collective-permute-start(bf16[32,1536]{1,0:T(8,128)(2,1)S(1)} %get-tuple-element.80), channel_id=1, source_target_pairs={{12,0},{0,4},{4,8},{8,12},{13,1},{1,5},{5,9},{9,13},{14,2},{2,6},{... | collective-permute-start | bytes 294920 | tf_op jit(solution)/shard_map/ppermute | solution.py:24
  163.1 6.5 %collective-permute-start.29 = (bf16[32,1536]{1,0:T(8,128)(2,1)S(1)}, bf16[32,1536]{1,0:T(8,128)(2,1)S(1)}, u32[]{:S(2)}, u32[]{:S(2)}) collective-permute-start(bf16[32,1536]{1,0:T(8,128)(2,1)S(1)} %get-tuple-element.82), channel_id=1, source_target_pairs={{8,0},{12,4},{0,8},{4,12},{9,1},{13,5},{1,9},{5,13},{10,2},{14,6},... | collective-permute-start | bytes 294920 | tf_op jit(solution)/shard_map/ppermute | solution.py:24
  166.0 4.6 %collective-permute-start.30 = (bf16[32,1536]{1,0:T(8,128)(2,1)S(1)}, bf16[32,1536]{1,0:T(8,128)(2,1)S(1)}, u32[]{:S(2)}, u32[]{:S(2)}) collective-permute-start(bf16[32,1536]{1,0:T(8,128)(2,1)S(1)} %get-tuple-element.81), channel_id=1, source_target_pairs={{4,0},{8,4},{12,8},{0,12},{5,1},{9,5},{13,9},{1,13},{6,2},{10,6},{... | collective-permute-start | bytes 294920 | tf_op jit(solution)/shard_map/ppermute | solution.py:24
  (4 other events, 3.4 us)
Sparse Core Ops, SparseCore 0:
  23.6 49.5 all-gather.2
  75.0 37.1 all-gather.4
  114.8 45.7 reduce-scatter.1

commit v4 on v3

--- a/solution.py
+++ b/solution.py
@@ -48,7 +48,7 @@
         in_specs=[VMEM] * 2,
         out_specs=VMEM,
         compiler_params=grant(4),
-    )(grad_output, layer_input)
+    )(in_hbm(grad_output), in_hbm(layer_input))
 
 
 def arrange_kernel(n, slot, cuts, place, *refs):
@@ -171,23 +171,15 @@
                 rows[k, z_other, :, col:col + 512] = other[half, lines, :]
 
 
-def weight_kernel(place, own, *refs):
-    pieces, grads, (d_gate, d_up, natural, rows) = refs[:8], refs[8:16], refs[16:]
+def own_kernel(place, own, p0, p1, p2, p3, gg, gg_other, gu, gu_other, d_gate, d_up, natural, rows):
     step = pl.program_id(0)
 
     @pl.when(step == 0)
     def _():
-        fill_natural(place, *grads[0:2], natural, 0)
-        fill_natural(place, *grads[2:4], natural, 512)
-        for replica in range(2):
-            fill_rolled(place, *grads[4 * replica:4 * replica + 2], rows.at[replica], 0)
-            fill_rolled(place, *grads[4 * replica + 2:4 * replica + 4], rows.at[replica], 512)
-
-    def rolled(replica):
-        total = jnp.zeros((256, 1024), F32)
-        for k in range(NY):
-            total = total + dot(pieces[NY * replica + k][...], rows[replica, k].reshape(256, 1024), 0, 0)
-        return total
+        fill_natural(place, gg, gg_other, natural, 0)
+        fill_natural(place, gu, gu_other, natural, 512)
+        fill_rolled(place, gg, gg_other, rows, 0)
+        fill_rolled(place, gu, gu_other, rows, 512)
 
     def emit(total):
         d_gate[...] = total[:, :512].astype(BF16)
@@ -195,40 +187,80 @@
 
     @pl.when(step < 3)
     def _():
-        emit(dot(own[...], natural[...], 0, 0) + rolled(1))
+        emit(dot(own[...], natural[...], 0, 0))
 
     @pl.when(step >= 3)
     def _():
-        emit(rolled(0) + rolled(1))
-
-
-def weight_grads(place, own, own_pieces, partner_pieces, grads):
-    tile = pl.BlockSpec((256, 512), lambda i: (i, 0))
-    shape = jax.ShapeDtypeStruct((1536, 512), BF16)
+        total = jnp.zeros((256, 1024), F32)
+        for k, piece in enumerate((p0, p1, p2, p3)):
+            total = total + dot(piece[...], rows[k].reshape(256, 1024), 0, 0)
+        emit(total)
+
+
+def partner_kernel(place, p0, p1, p2, p3, gg, gg_other, gu, gu_other, own_gate, own_up, d_gate, d_up, rows):
+    @pl.when(pl.program_id(0) == 0)
+    def _():
+        fill_rolled(place, gg, gg_other, rows, 0)
+        fill_rolled(place, gu, gu_other, rows, 512)
+
+    total = jnp.zeros((256, 1024), F32)
+    for k, piece in enumerate((p0, p1, p2, p3)):
+        total = total + dot(piece[...], rows[k].reshape(256, 1024), 0, 0)
+    d_gate[...] = (total[:, :512].astype(BF16).astype(F32) + own_gate[...].astype(F32)).astype(BF16)
+    d_up[...] = (total[:, 512:].astype(BF16).astype(F32) + own_up[...].astype(F32)).astype(BF16)
+
+
+TILE = pl.BlockSpec((256, 512), lambda i: (i, 0))
+WEIGHT = jax.ShapeDtypeStruct((1536, 512), BF16)
+ROLLED = pltpu.VMEM((NY, NZ, 32, 1024), BF16)
+
+
+def own_weight_grads(place, own, pieces, grads):
     low = pl.BlockSpec((1024, 256), lambda i: (0, jnp.minimum(i, 2)))
     high = pl.BlockSpec((256, 256), lambda i: (0, jnp.maximum(i - 3, 0)))
+    return pl.pallas_call(
+        own_kernel,
+        grid=(6,),
+        out_shape=(WEIGHT, WEIGHT),
+        in_specs=[SMEM, low] + [high] * 4 + [VMEM] * 4,
+        out_specs=(TILE, TILE),
+        scratch_shapes=[pltpu.VMEM((1024, 1024), BF16), ROLLED],
+        compiler_params=grant(16),
+    )(place, in_hbm(own), *(in_hbm(x) for x in pieces), *grads)
+
+
+def partner_weight_grads(place, pieces, grads, own_gate, own_up):
     every = pl.BlockSpec((256, 256), lambda i: (0, i))
-    high0, high1, high2, high3 = own_pieces
-    partner0, partner1, partner2, partner3 = partner_pieces
-    early = [in_hbm(x) for x in (own, high0, high1)]
-    partner = [in_hbm(x) for x in (high3, partner0, partner1)]
-    partner3 = in_hbm(partner3)
-    near = [in_hbm(x) for x in grads[:4]]
-    return pl.pallas_call(
-        weight_kernel,
+    return pl.pallas_call(
+        partner_kernel,
         grid=(6,),
-        out_shape=(shape, shape),
-        in_specs=[SMEM, low] + [high] * 4 + [every] * 4 + [VMEM] * 8,
-        out_specs=(tile, tile),
-        scratch_shapes=[pltpu.VMEM((1024, 1024), BF16), pltpu.VMEM((2, NY, NZ, 32, 1024), BF16)],
-        compiler_params=grant(24),
-    )(place, *early, high2, *partner, partner2, partner3, *near, *grads[4:])
-
-
-def ring(x, axis, n):
-    ahead, behind = [], []
-    up, down = x, x
-    for step in range(1, n // 2 + 1):
+        out_shape=(WEIGHT, WEIGHT),
+        in_specs=[SMEM] + [every] * 4 + [VMEM] * 4 + [TILE] * 2,
+        out_specs=(TILE, TILE),
+        scratch_shapes=[ROLLED],
+        compiler_params=grant(16),
+    )(place, *(x if k == 2 else in_hbm(x) for k, x in enumerate(pieces)), *grads, own_gate, own_up)
+
+
+def add_kernel(left, right, out):
+    out[...] = (left[...].astype(F32) + right[...].astype(F32)).astype(BF16)
+
+
+def add(left, right):
+    block = pl.BlockSpec((128, 1536), lambda i: (i, 0))
+    return pl.pallas_call(
+        add_kernel,
+        grid=(4,),
+        out_shape=jax.ShapeDtypeStruct((512, 1536), BF16),
+        in_specs=[block] * 2,
+        out_specs=block,
+        compiler_params=grant(8),
+    )(left, right)
+
+
+def ring(x, up, down, axis, n):
+    ahead, behind = [up], [down]
+    for step in range(2, n // 2 + 1):
         up = from_ahead(up, axis, n, 1)
         ahead.append(up)
         if step < n // 2:
@@ -249,9 +281,11 @@
 
     mixed = prepare(grad_output, layer_input)
     mixed_parts = [mixed] + [from_ahead(mixed, "y", NY, k) for k in (1, 2, 3)]
+    z_up, z_down = from_ahead(layer_input, "z", NZ, 1), from_ahead(layer_input, "z", NZ, NZ - 1)
+    mixed_parts, z_up, z_down = lax.optimization_barrier((mixed_parts, z_up, z_down))
     go_y, own_y = arrange(place, 1, mixed_parts, ((0, 1536), (1536, 1536 + HALF)))
     go = lax.all_gather(go_y, "z", axis=0, tiled=True)
-    own_z, high_z = arrange(place, 0, ring(layer_input, "z", NZ), ((0, 1536), (HALF, 1536)))
+    own_z, high_z = arrange(place, 0, ring(layer_input, z_up, z_down, "z", NZ), ((0, 1536), (HALF, 1536)))
     partner_z = swap(own_z, "dp")
     high1, high3 = from_ahead(high_z, "y", NY, 1), from_ahead(high_z, "y", NY, 3)
 
@@ -279,17 +313,18 @@
     gg = (grad_hidden * up_val * sigma * (1.0 + gate_val * (1.0 - sigma))).astype(BF16)
     gu = (grad_hidden * gate_val * sigma).astype(BF16)
     gg_other, gu_other = swap(gg, "core"), swap(gu, "core")
-    gg_other, gu_other, partner1, partner3 = lax.optimization_barrier((gg_other, gu_other, partner1, partner3))
     partial_in = input_grad(place, gg, gg_other, gu, gu_other, w_gate, w_up)
+    partial_in, partner1, partner3 = lax.optimization_barrier((partial_in, partner1, partner3))
     in_z = lax.psum_scatter(partial_in, "z", scatter_dimension=0, tiled=True).reshape(NY, 32, 1536)
 
     gg_far, gu_far = swap(gg, "dp"), swap(gu, "dp")
     high2, partner2 = from_ahead(high_z, "y", NY, 2), from_ahead(partner_z, "y", NY, 2)
     gg_far, gu_far, part_down, high2 = lax.optimization_barrier((gg_far, gu_far, part_down, high2))
     down_far = swap(part_down, "dp")
-    grads = (gg, gg_other, gu, gu_other, gg_far, swap(gg_far, "core"), gu_far, swap(gu_far, "core"))
     own_pieces, partner_pieces = (high_z, high1, high2, high3), (partner_z, partner1, partner2, partner3)
-    grad_gate, grad_up = weight_grads(place, own_low, own_pieces, partner_pieces, grads)
+    own_gate, own_up = own_weight_grads(place, own_low, own_pieces, (gg, gg_other, gu, gu_other))
+    far = (gg_far, swap(gg_far, "core"), gu_far, swap(gu_far, "core"))
+    grad_gate, grad_up = partner_weight_grads(place, partner_pieces, far, own_gate, own_up)
     in_z, grad_gate, grad_up = lax.optimization_barrier((in_z, grad_gate, grad_up))
 
     y = place[1]
@@ -299,7 +334,7 @@
         total = total + from_ahead(slab, "y", NY, NY - k).astype(F32)
     grad_input = total.astype(BF16)
     grad_input, down_far = lax.optimization_barrier((grad_input, down_far))
-    grad_down = (part_down.astype(F32) + down_far.astype(F32)).astype(BF16)
+    grad_down = add(part_down, down_far)
     return grad_input, grad_gate, grad_up, grad_down
 
 

time: 182 us -> 181 us (level)
  Pallas kernels: 28.4 us -> 35.6 us
  starting transfers between devices: 47.2 us -> 43.4 us
  other arithmetic: 7.83 us -> 4.89 us
  local copies, waits for them, and re-layouts: 6.34 us -> 3.64 us
    ppermute x19, waiting for transfers between devices: 53.1 us -> 41.3 us  [from_ahead(): return lax.ppermute(x, axis, [((d + k) % n, d) for d in range(n)])]
    pallas_call x1 -> x3, Pallas kernels: 12 us -> 18.9 us  [the longest x1 8.32 us: partner_weight_grads(): pl.pallas_call(partner_kernel, grid=(6,), out_shape=(WEIGHT, WEIGHT), in_...]
    reduce_scatter x1, waiting for transfers between devices: 6.43 us -> 12.4 us  [body(): lax.psum_scatter(partial_in, 'z', scatter_dimension=0, tiled=True)]
    all_gather x1, waiting for transfers between devices: 0.1 us -> 4.3 us  [body(): go = lax.all_gather(go_y, 'z', axis=0, tiled=True)]
    convert_element_type x1 -> x0, other arithmetic: 2.93 us -> none  [body(): grad_down = (part_down.astype(F32) + down_far.astype(F32)).astype(BF16)]
    ppermute x13, waiting for transfers between devices: 18.3 us -> 21.1 us  [swap(): return lax.ppermute(x, axis, [(0, 1), (1, 0)])]
    unnamed x34 -> x26, local copies, waits for them, and re-layouts: 5.34 us -> 2.63 us
    ppermute x19, starting transfers between devices: 35 us -> 32.4 us  [from_ahead(): return lax.ppermute(x, axis, [((d + k) % n, d) for d in range(n)])]
  transfers between devices with their start and end apart: 35 -> 35, of which waited for: 24 -> 19; matrix products, arithmetic and copies ran while one was open for 3% -> 3% of each run, Pallas kernels for 15% -> 16%
where the time goes in v4:
time: 181 us
  waiting for transfers between devices  79.1 us (44%)
  starting transfers between devices  43.4 us (24%)
  Pallas kernels  35.6 us (20%)
  between operations  14 us (8%)
  other arithmetic  4.89 us (3%)
  local copies, waits for them, and re-layouts  3.64 us (2%)
    ppermute x19, waiting for transfers between devices, from_ahead(): return lax.ppermute(x, axis, [((d + k) % n, d) for d in range(n)])  41.3 us
    ppermute x19, starting transfers between devices, from_ahead(): return lax.ppermute(x, axis, [((d + k) % n, d) for d in range(n)])  32.4 us
    ppermute x13, waiting for transfers between devices, swap(): return lax.ppermute(x, axis, [(0, 1), (1, 0)])  21.1 us
    reduce_scatter x1, waiting for transfers between devices, body(): lax.psum_scatter(partial_in, 'z', scatter_dimension=0, tiled=True)  12.4 us
    ppermute x13, starting transfers between devices, swap(): return lax.ppermute(x, axis, [(0, 1), (1, 0)])  11 us
    pallas_call x1, Pallas kernels, partner_weight_grads(): pl.pallas_call(partner_kernel, grid=(6,), out_shape=(WEIGHT, WEIGHT), in_...  8.32 us
    pallas_call x1, Pallas kernels, own_weight_grads(): pl.pallas_call(own_kernel, grid=(6,), out_shape=(WEIGHT, WEIGHT), in_spec...  6.89 us
    pallas_call x1, Pallas kernels, input_grad(): pl.pallas_call(input_grad_kernel, grid=(3,), out_shape=jax.ShapeDtypeStru...  5.45 us
  transfers between devices with their start and end apart: 35, of which 19 were waited for; matrix products, arithmetic and copies ran while one was open for 3% of the time, Pallas kernels for 16%

profile of v4, /device:TPU:2, one launch (start us, length us, event | category | flops | bytes accessed | tf_op | source)
XLA Modules:
  0.0 180.6 jit_solution(3753918844830943087)
XLA Ops:
  7.2 1.0 shard_map.102.refs_0_
  8.2 3.1 %collective-permute-start = (bf16[32,2304]{1,0:T(8,128)(2,1)S(1)}, bf16[32,2304]{1,0:T(8,128)(2,1)S(1)}, u32[]{:S(2)}, u32[]{:S(2)}) collective-permute-start(bf16[32,2304]{1,0:T(8,128)(2,1)S(1)} %shard_map.102.refs_0_), channel_id=1, source_target_pairs={{4,0},{8,4},{12,8},{0,12},{5,1},{9,5},{13,9},{1,13},{6,2},{10,6},{... | collective-permute-start | bytes 442376 | tf_op jit(solution)/shard_map/ppermute | solution.py:24
  12.0 1.0 collective-permute-start.2
  12.9 5.9 %collective-permute-start.3 = (bf16[32,1536]{1,0:T(8,128)(2,1)}, bf16[32,1536]{1,0:T(8,128)(2,1)S(1)}, u32[]{:S(2)}, u32[]{:S(2)}) collective-permute-start(bf16[32,1536]{1,0:T(8,128)(2,1)} %refs_0_.1), channel_id=1, source_target_pairs={{16,0},{32,16},{48,32},{64,48},{80,64},{96,80},{112,96},{0,112},{1... | collective-permute-start | bytes 294920 | tf_op jit(solution)/shard_map/ppermute | solution.py:24
  18.9 2.4 %collective-permute-done.3.refs_1_ = bf16[32,1536]{1,0:T(8,128)(2,1)S(1)} collective-permute-done((bf16[32,1536]{1,0:T(8,128)(2,1)}, bf16[32,1536]{1,0:T(8,128)(2,1)S(1)}, u32[]{:S(2)}, u32[]{:S(2)}) %collective-permute-start.3) | collective-permute-done | bytes 98336 | tf_op jit(solution)/shard_map/ppermute | solution.py:24
  21.3 3.5 %collective-permute-done.4.refs_7_ = bf16[32,1536]{1,0:T(8,128)(2,1)S(1)} collective-permute-done((bf16[32,1536]{1,0:T(8,128)(2,1)}, bf16[32,1536]{1,0:T(8,128)(2,1)S(1)}, u32[]{:S(2)}, u32[]{:S(2)}) %collective-permute-start.4) | collective-permute-done | bytes 98336 | tf_op jit(solution)/shard_map/ppermute | solution.py:24
  24.8 1.4 shard_map.103
  26.3 2.2 %collective-permute-start.5 = (bf16[256,512]{1,0:T(8,128)(2,1)}, bf16[256,512]{1,0:T(8,128)(2,1)S(1)}, u32[]{:S(2)}, u32[]{:S(2)}) collective-permute-start(bf16[256,512]{1,0:T(8,128)(2,1)} %param.9), channel_id=1, source_target_pairs={{0,2},{2,0},{1,3},{3,1},{4,6},{6,4},{5,7},{7,5},{8,10},{10,8},{9,1... | collective-permute-start | bytes 786440 | tf_op jit(solution)/shard_map/ppermute | solution.py:28
  28.5 2.3 %collective-permute-start.8 = (bf16[32,1536]{1,0:T(8,128)(2,1)S(1)}, bf16[32,1536]{1,0:T(8,128)(2,1)S(1)}, u32[]{:S(2)}, u32[]{:S(2)}) collective-permute-start(bf16[32,1536]{1,0:T(8,128)(2,1)S(1)} %collective-permute-done.3.refs_1_), channel_id=1, source_target_pairs={{16,0},{32,16},{48,32},{64,48},{80,64},{96,80},{112,96},{0,112},{1... | collective-permute-start | bytes 294920 | tf_op jit(solution)/shard_map/ppermute | solution.py:24
  30.9 2.3 %collective-permute-done.8.refs_2_ = bf16[32,1536]{1,0:T(8,128)(2,1)S(1)} collective-permute-done((bf16[32,1536]{1,0:T(8,128)(2,1)S(1)}, bf16[32,1536]{1,0:T(8,128)(2,1)S(1)}, u32[]{:S(2)}, u32[]{:S(2)}) %collective-permute-start.8) | collective-permute-done | bytes 98336 | tf_op jit(solution)/shard_map/ppermute | solution.py:24
  33.2 3.5 %collective-permute-start.9 = (bf16[32,1536]{1,0:T(8,128)(2,1)S(1)}, bf16[32,1536]{1,0:T(8,128)(2,1)S(1)}, u32[]{:S(2)}, u32[]{:S(2)}) collective-permute-start(bf16[32,1536]{1,0:T(8,128)(2,1)S(1)} %collective-permute-done.8.refs_2_), channel_id=1, source_target_pairs={{16,0},{32,16},{48,32},{64,48},{80,64},{96,80},{112,96},{0,112},{1... | collective-permute-start | bytes 294920 | tf_op jit(solution)/shard_map/ppermute | solution.py:24
  36.7 1.4 collective-permute-start.6
  38.1 3.0 %collective-permute-done.9.refs_3_ = bf16[32,1536]{1,0:T(8,128)(2,1)S(1)} collective-permute-done((bf16[32,1536]{1,0:T(8,128)(2,1)S(1)}, bf16[32,1536]{1,0:T(8,128)(2,1)S(1)}, u32[]{:S(2)}, u32[]{:S(2)}) %collective-permute-start.9) | collective-permute-done | bytes 98336 | tf_op jit(solution)/shard_map/ppermute | solution.py:24
  41.1 3.7 %collective-permute-start.10 = (bf16[32,1536]{1,0:T(8,128)(2,1)S(1)}, bf16[32,1536]{1,0:T(8,128)(2,1)S(1)}, u32[]{:S(2)}, u32[]{:S(2)}) collective-permute-start(bf16[32,1536]{1,0:T(8,128)(2,1)S(1)} %collective-permute-done.9.refs_3_), channel_id=1, source_target_pairs={{16,0},{32,16},{48,32},{64,48},{80,64},{96,80},{112,96},{0,112},{1... | collective-permute-start | bytes 294920 | tf_op jit(solution)/shard_map/ppermute | solution.py:24
  44.8 1.0 select_bitcast_fusion.3
  46.2 2.7 %collective-permute-done.10.refs_4_ = bf16[32,1536]{1,0:T(8,128)(2,1)S(1)} collective-permute-done((bf16[32,1536]{1,0:T(8,128)(2,1)S(1)}, bf16[32,1536]{1,0:T(8,128)(2,1)S(1)}, u32[]{:S(2)}, u32[]{:S(2)}) %collective-permute-start.10) | collective-permute-done | bytes 98336 | tf_op jit(solution)/shard_map/ppermute | solution.py:24
  50.7 2.2 %collective-permute-start.14 = (bf16[256,768]{1,0:T(8,128)(2,1)S(1)}, bf16[256,768]{1,0:T(8,128)(2,1)S(1)}, u32[]{:S(2)}, u32[]{:S(2)}) collective-permute-start(bf16[256,768]{1,0:T(8,128)(2,1)S(1)} %bitcast.26), channel_id=1, source_target_pairs={{4,0},{8,4},{12,8},{0,12},{5,1},{9,5},{13,9},{1,13},{6,2},{10,6},{... | collective-permute-start | bytes 1179656 | tf_op jit(solution)/shard_map/ppermute | solution.py:24
  52.9 1.1 pad_maximum_fusion
  54.0 8.3 %collective-permute-done.14.p1 = bf16[256,768]{1,0:T(8,128)(2,1)S(1)} collective-permute-done((bf16[256,768]{1,0:T(8,128)(2,1)S(1)}, bf16[256,768]{1,0:T(8,128)(2,1)S(1)}, u32[]{:S(2)}, u32[]{:S(2)}) %collective-permute-start.14) | collective-permute-done | bytes 393248 | tf_op jit(solution)/shard_map/ppermute | solution.py:24
  62.3 3.0 %collective-permute-done.15.p3 = bf16[256,768]{1,0:T(8,128)(2,1)S(1)} collective-permute-done((bf16[256,768]{1,0:T(8,128)(2,1)S(1)}, bf16[256,768]{1,0:T(8,128)(2,1)S(1)}, u32[]{:S(2)}, u32[]{:S(2)}) %collective-permute-start.15) | collective-permute-done | bytes 393248 | tf_op jit(solution)/shard_map/ppermute | solution.py:24
  66.1 4.3 %all-gather.3.cloned.1.call-done.go = bf16[1024,1536]{1,0:T(8,128)(2,1)} async-done(((bf16[128,1536]{1,0:T(8,128)(2,1)}), bf16[1024,1536]{1,0:T(8,128)(2,1)}) %all-gather.3.cloned.1.call-update) | async-done | bytes 3145744 | tf_op jit(solution)/shard_map/all_gather | solution.py:287
  70.4 4.1 %shard_map.105 = (f32[2,256,512]{2,1,0:T(8,128)S(1)}, bf16[2,256,512]{2,1,0:T(8,128)(2,1)S(1)}) custom-call(s32[4]{0:T(128)S(1)} %pad_add_fusion.place, bf16[1024,1536]{1,0:T(8,128)(2,1)} %all-gather.3.cloned.1.call-done.go, bf16[512,1536]{1,0:T(8,128)(2,1)S(1)} %copy-done.2), custom_call_target="tpu_custom_call" | custom-call | tf_op jit(solution)/shard_map/pallas_call | solution.py:96
  74.7 1.9 %collective-permute-done.16 = bf16[2,256,512]{2,1,0:T(8,128)(2,1)S(1)} collective-permute-done((bf16[2,256,512]{2,1,0:T(8,128)(2,1)S(1)}, bf16[2,256,512]{2,1,0:T(8,128)(2,1)S(1)}, u32[]{:S(2)}, u32[]{:S(2)}) %collective-permute-start.16) | collective-permute-done | bytes 524320 | tf_op jit(solution)/shard_map/ppermute | solution.py:28
  76.8 2.2 %collective-permute-start.17 = (bf16[2,256,512]{2,1,0:T(8,128)(2,1)S(1)}, bf16[2,256,512]{2,1,0:T(8,128)(2,1)S(1)}, u32[]{:S(2)}, u32[]{:S(2)}) collective-permute-start(bf16[2,256,512]{2,1,0:T(8,128)(2,1)S(1)} %get-tuple-element.86), channel_id=1, source_target_pairs={{0,2},{2,0},{1,3},{3,1},{4,6},{6,4},{5,7},{7,5},{8,10},{10,8},{9,1... | collective-permute-start | bytes 1572872 | tf_op jit(solution)/shard_map/ppermute | solution.py:28
  79.0 1.7 collective-permute-start.20
  81.0 4.1 %shard_map.106.left = bf16[512,1536]{1,0:T(8,128)(2,1)S(1)} custom-call(s32[4]{0:T(128)S(1)} %pad_add_fusion.place, bf16[2,256,512]{2,1,0:T(8,128)(2,1)S(1)} %fusion.12.hidden, bf16[2,256,512]{2,1,0:T(8,128)(2,1)S(1)} %collective-permute-done.7.hidden_other, bf16[1024,1536]{1,0:T(8,128)(2,1)} %all-gather.3.cloned.1.call-done.go), custom_call_target="tpu_custom_call" | custom-call | tf_op jit(solution)/shard_map/pallas_call | solution.py:151
  85.1 7.3 %collective-permute-done.17 = bf16[2,256,512]{2,1,0:T(8,128)(2,1)S(1)} collective-permute-done((bf16[2,256,512]{2,1,0:T(8,128)(2,1)S(1)}, bf16[2,256,512]{2,1,0:T(8,128)(2,1)S(1)}, u32[]{:S(2)}, u32[]{:S(2)}) %collective-permute-start.17) | collective-permute-done | bytes 524320 | tf_op jit(solution)/shard_map/ppermute | solution.py:28
  93.6 1.4 collective-permute-done.18.gg_other
  95.7 5.4 %shard_map.107 = bf16[1024,1536]{1,0:T(8,128)(2,1)} custom-call(s32[4]{0:T(128)S(1)} %pad_add_fusion.place, bf16[2,256,512]{2,1,0:T(8,128)(2,1)S(1)} %get-tuple-element.89.gg, bf16[2,256,512]{2,1,0:T(8,128)(2,1)S(1)} %collective-permute-done.18.gg_other, bf16[2,256,512]{2,1,0:T(8,128)(2,1)S(1)} %get-tuple-element.88.gu, ...), custom_call_target="tpu_custom_call" | custom-call | tf_op jit(solution)/shard_map/pallas_call | solution.py:123
  101.2 0.8 copy-done
  102.0 1.1 collective-permute-start.23
  103.1 1.0 collective-permute-start.24
  104.1 2.2 %collective-permute-start.25 = (bf16[256,768]{1,0:T(8,128)(2,1)S(1)}, bf16[256,768]{1,0:T(8,128)(2,1)S(1)}, u32[]{:S(2)}, u32[]{:S(2)}) collective-permute-start(bf16[256,768]{1,0:T(8,128)(2,1)S(1)} %bitcast.28), channel_id=1, source_target_pairs={{8,0},{12,4},{0,8},{4,12},{9,1},{13,5},{1,9},{5,13},{10,2},{14,6},... | collective-permute-start | bytes 1179656 | tf_op jit(solution)/shard_map/ppermute | solution.py:24
  106.3 1.4 collective-permute-start.22
  107.6 10.0 %collective-permute-done.25.p2 = bf16[256,768]{1,0:T(8,128)(2,1)S(1)} collective-permute-done((bf16[256,768]{1,0:T(8,128)(2,1)S(1)}, bf16[256,768]{1,0:T(8,128)(2,1)S(1)}, u32[]{:S(2)}, u32[]{:S(2)}) %collective-permute-start.25) | collective-permute-done | bytes 393248 | tf_op jit(solution)/shard_map/ppermute | solution.py:24
  117.7 9.7 %collective-permute-done.24.gu = bf16[2,256,512]{2,1,0:T(8,128)(2,1)} collective-permute-done((bf16[2,256,512]{2,1,0:T(8,128)(2,1)S(1)}, bf16[2,256,512]{2,1,0:T(8,128)(2,1)}, u32[]{:S(2)}, u32[]{:S(2)}) %collective-permute-start.24) | collective-permute-done | bytes 524320 | tf_op jit(solution)/shard_map/ppermute | solution.py:28
  127.4 1.0 collective-permute-start.31
  129.0 1.0 copy-done.1
  130.0 6.9 %shard_map.108 = (bf16[1536,512]{1,0:T(8,128)(2,1)S(1)}, bf16[1536,512]{1,0:T(8,128)(2,1)S(1)}) custom-call(s32[4]{0:T(128)S(1)} %pad_add_fusion.place, bf16[1024,768]{1,0:T(8,128)(2,1)} %all-gather.5.cloned.1.call-done.own, bf16[256,768]{1,0:T(8,128)(2,1)} %bitcast.29, bf16[256,768]{1,0:T(8,128)(2,1)} %copy-done.9, bf16[256,768]{1,0:T(8,128)(2,1)} %copy-done.11, ...), custom_call_target="tpu_custom_call" | custom-call | tf_op jit(solution)/shard_map/pallas_call | solution.py:221
  136.9 8.3 %shard_map.109 = (bf16[1536,512]{1,0:T(8,128)(2,1)}, bf16[1536,512]{1,0:T(8,128)(2,1)}) custom-call(s32[4]{0:T(128)S(1)} %pad_add_fusion.place, bf16[256,1536]{1,0:T(8,128)(2,1)} %collective-permute-done.13.p0, bf16[256,1536]{1,0:T(8,128)(2,1)} %collective-permute-done.20.p1, bf16[256,1536]{1,0:T(8,128)(2,1)} %collective-permute-done.22.p2, ...), custom_call_target="tpu_custom_call" | custom-call | tf_op jit(solution)/shard_map/pallas_call | solution.py:234
  145.3 12.4 %reduce-scatter.2.cloned.1.call-done = bf16[128,1536]{1,0:T(8,128)(2,1)} async-done(((bf16[1024,1536]{1,0:T(8,128)(2,1)}), bf16[128,1536]{1,0:T(8,128)(2,1)}) %reduce-scatter.2.cloned.1.call-update) | async-done | bytes 393232 | tf_op jit(solution)/shard_map/reduce_scatter | solution.py:318
  157.6 1.0 dynamic-slice_bitcast_fusion.2
  158.7 3.0 %collective-permute-start.30 = (bf16[32,1536]{1,0:T(8,128)(2,1)S(1)}, bf16[32,1536]{1,0:T(8,128)(2,1)S(1)}, u32[]{:S(2)}, u32[]{:S(2)}) collective-permute-start(bf16[32,1536]{1,0:T(8,128)(2,1)S(1)} %get-tuple-element.95), channel_id=1, source_target_pairs={{4,0},{8,4},{12,8},{0,12},{5,1},{9,5},{13,9},{1,13},{6,2},{10,6},{... | collective-permute-start | bytes 294920 | tf_op jit(solution)/shard_map/ppermute | solution.py:24
  161.6 0.9 collective-permute-start.29
  163.9 3.9 %collective-permute-done.29 = bf16[32,1536]{1,0:T(8,128)(2,1)S(1)} collective-permute-done((bf16[32,1536]{1,0:T(8,128)(2,1)S(1)}, bf16[32,1536]{1,0:T(8,128)(2,1)S(1)}, u32[]{:S(2)}, u32[]{:S(2)}) %collective-permute-start.29) | collective-permute-done | bytes 98336 | tf_op jit(solution)/shard_map/ppermute | solution.py:24
  167.8 1.0 collective-permute-done.28
  168.8 1.6 fusion.15
  170.4 3.7 %shard_map.110 = bf16[512,1536]{1,0:T(8,128)(2,1)} custom-call(bf16[512,1536]{1,0:T(8,128)(2,1)S(1)} %shard_map.106.left, bf16[512,1536]{1,0:T(8,128)(2,1)} %collective-permute-done.31.right), custom_call_target="tpu_custom_call" | custom-call | tf_op jit(solution)/shard_map/pallas_call | solution.py:251
  (69 shorter events, 8.4 us)
Async XLA Ops:
  7.2 41.6 %copy-start.5 = (bf16[32,1536]{1,0:T(8,128)(2,1)S(1)}, bf16[32,1536]{1,0:T(8,128)(2,1)}, u32[]{:S(2)}) copy-start(bf16[32,1536]{1,0:T(8,128)(2,1)} %refs_0_.1) | copy-start | bytes 294916
  7.2 43.0 %copy-start.12 = (bf16[256,512]{1,0:T(8,128)(2,1)S(1)}, bf16[256,512]{1,0:T(8,128)(2,1)}, u32[]{:S(2)}) copy-start(bf16[256,512]{1,0:T(8,128)(2,1)} %param.10) | copy-start | bytes 786436
  7.2 63.2 %all-gather.3.cloned.1.call-start = ((), (), s32[]{:S(2)}) async-start(), calls=%async_computation.1 | async-start | bytes 3538944 | tf_op jit(solution)/shard_map/all_gather | solution.py:287
  8.2 16.6 %collective-permute-start = (bf16[32,2304]{1,0:T(8,128)(2,1)S(1)}, bf16[32,2304]{1,0:T(8,128)(2,1)S(1)}, u32[]{:S(2)}, u32[]{:S(2)}) collective-permute-start(bf16[32,2304]{1,0:T(8,128)(2,1)S(1)} %shard_map.102.refs_0_), channel_id=1, source_target_pairs={{4,0},{8,4},{12,8},{0,12},{5,1},{9,5},{13,9},{1,13},{6,2},{10,6},{... | collective-permute-start | bytes 442376 | tf_op jit(solution)/shard_map/ppermute | solution.py:24
  11.3 13.5 %collective-permute-start.1 = (bf16[32,2304]{1,0:T(8,128)(2,1)S(1)}, bf16[32,2304]{1,0:T(8,128)(2,1)S(1)}, u32[]{:S(2)}, u32[]{:S(2)}) collective-permute-start(bf16[32,2304]{1,0:T(8,128)(2,1)S(1)} %shard_map.102.refs_0_), channel_id=1, source_target_pairs={{8,0},{12,4},{0,8},{4,12},{9,1},{13,5},{1,9},{5,13},{10,2},{14,6},... | collective-permute-start | bytes 442376 | tf_op jit(solution)/shard_map/ppermute | solution.py:24
  12.0 12.9 %collective-permute-start.2 = (bf16[32,2304]{1,0:T(8,128)(2,1)S(1)}, bf16[32,2304]{1,0:T(8,128)(2,1)S(1)}, u32[]{:S(2)}, u32[]{:S(2)}) collective-permute-start(bf16[32,2304]{1,0:T(8,128)(2,1)S(1)} %shard_map.102.refs_0_), channel_id=1, source_target_pairs={{12,0},{0,4},{4,8},{8,12},{13,1},{1,5},{5,9},{9,13},{14,2},{2,6},{... | collective-permute-start | bytes 442376 | tf_op jit(solution)/shard_map/ppermute | solution.py:24
  12.9 8.4 %collective-permute-start.3 = (bf16[32,1536]{1,0:T(8,128)(2,1)}, bf16[32,1536]{1,0:T(8,128)(2,1)S(1)}, u32[]{:S(2)}, u32[]{:S(2)}) collective-permute-start(bf16[32,1536]{1,0:T(8,128)(2,1)} %refs_0_.1), channel_id=1, source_target_pairs={{16,0},{32,16},{48,32},{64,48},{80,64},{96,80},{112,96},{0,112},{1... | collective-permute-start | bytes 294920 | tf_op jit(solution)/shard_map/ppermute | solution.py:24
  18.8 6.0 %collective-permute-start.4 = (bf16[32,1536]{1,0:T(8,128)(2,1)}, bf16[32,1536]{1,0:T(8,128)(2,1)S(1)}, u32[]{:S(2)}, u32[]{:S(2)}) collective-permute-start(bf16[32,1536]{1,0:T(8,128)(2,1)} %refs_0_.1), channel_id=1, source_target_pairs={{112,0},{0,16},{16,32},{32,48},{48,64},{64,80},{80,96},{96,112},{1... | collective-permute-start | bytes 294920 | tf_op jit(solution)/shard_map/ppermute | solution.py:24
  26.3 102.7 %all-gather.5.cloned.1.call-start = ((), (), s32[]{:S(2)}) async-start(), calls=%async_computation.3 | async-start | bytes 1769472 | tf_op jit(solution)/shard_map/all_gather | solution.py:301
  26.3 18.5 %collective-permute-start.5 = (bf16[256,512]{1,0:T(8,128)(2,1)}, bf16[256,512]{1,0:T(8,128)(2,1)S(1)}, u32[]{:S(2)}, u32[]{:S(2)}) collective-permute-start(bf16[256,512]{1,0:T(8,128)(2,1)} %param.9), channel_id=1, source_target_pairs={{0,2},{2,0},{1,3},{3,1},{4,6},{6,4},{5,7},{7,5},{8,10},{10,8},{9,1... | collective-permute-start | bytes 786440 | tf_op jit(solution)/shard_map/ppermute | solution.py:28
  28.5 4.6 %collective-permute-start.8 = (bf16[32,1536]{1,0:T(8,128)(2,1)S(1)}, bf16[32,1536]{1,0:T(8,128)(2,1)S(1)}, u32[]{:S(2)}, u32[]{:S(2)}) collective-permute-start(bf16[32,1536]{1,0:T(8,128)(2,1)S(1)} %collective-permute-done.3.refs_1_), channel_id=1, source_target_pairs={{16,0},{32,16},{48,32},{64,48},{80,64},{96,80},{112,96},{0,112},{1... | collective-permute-start | bytes 294920 | tf_op jit(solution)/shard_map/ppermute | solution.py:24
  30.9 7.2 %collective-permute-start.11 = (bf16[32,1536]{1,0:T(8,128)(2,1)S(1)}, bf16[32,1536]{1,0:T(8,128)(2,1)S(1)}, u32[]{:S(2)}, u32[]{:S(2)}) collective-permute-start(bf16[32,1536]{1,0:T(8,128)(2,1)S(1)} %collective-permute-done.4.refs_7_), channel_id=1, source_target_pairs={{112,0},{0,16},{16,32},{32,48},{48,64},{64,80},{80,96},{96,112},{1... | collective-permute-start | bytes 294920 | tf_op jit(solution)/shard_map/ppermute | solution.py:24
  33.2 8.0 %collective-permute-start.9 = (bf16[32,1536]{1,0:T(8,128)(2,1)S(1)}, bf16[32,1536]{1,0:T(8,128)(2,1)S(1)}, u32[]{:S(2)}, u32[]{:S(2)}) collective-permute-start(bf16[32,1536]{1,0:T(8,128)(2,1)S(1)} %collective-permute-done.8.refs_2_), channel_id=1, source_target_pairs={{16,0},{32,16},{48,32},{64,48},{80,64},{96,80},{112,96},{0,112},{1... | collective-permute-start | bytes 294920 | tf_op jit(solution)/shard_map/ppermute | solution.py:24
  36.7 13.5 %collective-permute-start.6 = (bf16[256,512]{1,0:T(8,128)(2,1)}, bf16[256,512]{1,0:T(8,128)(2,1)S(1)}, u32[]{:S(2)}, u32[]{:S(2)}) collective-permute-start(bf16[256,512]{1,0:T(8,128)(2,1)} %param.10), channel_id=1, source_target_pairs={{0,2},{2,0},{1,3},{3,1},{4,6},{6,4},{5,7},{7,5},{8,10},{10,8},{9,1... | collective-permute-start | bytes 786440 | tf_op jit(solution)/shard_map/ppermute | solution.py:28
  38.1 8.1 %collective-permute-start.12 = (bf16[32,1536]{1,0:T(8,128)(2,1)S(1)}, bf16[32,1536]{1,0:T(8,128)(2,1)S(1)}, u32[]{:S(2)}, u32[]{:S(2)}) collective-permute-start(bf16[32,1536]{1,0:T(8,128)(2,1)S(1)} %collective-permute-done.11.refs_6_), channel_id=1, source_target_pairs={{112,0},{0,16},{16,32},{32,48},{48,64},{64,80},{80,96},{96,112},{1... | collective-permute-start | bytes 294920 | tf_op jit(solution)/shard_map/ppermute | solution.py:24
  41.1 7.7 %collective-permute-start.10 = (bf16[32,1536]{1,0:T(8,128)(2,1)S(1)}, bf16[32,1536]{1,0:T(8,128)(2,1)S(1)}, u32[]{:S(2)}, u32[]{:S(2)}) collective-permute-start(bf16[32,1536]{1,0:T(8,128)(2,1)S(1)} %collective-permute-done.9.refs_3_), channel_id=1, source_target_pairs={{16,0},{32,16},{48,32},{64,48},{80,64},{96,80},{112,96},{0,112},{1... | collective-permute-start | bytes 294920 | tf_op jit(solution)/shard_map/ppermute | solution.py:24
  49.4 54.7 %copy-start.6 = (bf16[8,32,768]{2,1,0:T(8,128)(2,1)}, bf16[8,32,768]{2,1,0:T(8,128)(2,1)S(1)}, u32[]{:S(2)}) copy-start(bf16[8,32,768]{2,1,0:T(8,128)(2,1)S(1)} %get-tuple-element.53) | copy-start | bytes 1179652
  49.5 16.6 %collective-permute-start.13 = (bf16[256,1536]{1,0:T(8,128)(2,1)S(1)}, bf16[256,1536]{1,0:T(8,128)(2,1)}, u32[]{:S(2)}, u32[]{:S(2)}) collective-permute-start(bf16[256,1536]{1,0:T(8,128)(2,1)S(1)} %bitcast.30), channel_id=1, source_target_pairs={{0,128},{128,0},{1,129},{129,1},{2,130},{130,2},{3,131},{131,3},{4... | collective-permute-start | bytes 2359304 | tf_op jit(solution)/shard_map/ppermute | solution.py:28
  50.2 20.2 %copy-start.2 = (bf16[512,1536]{1,0:T(8,128)(2,1)S(1)}, bf16[512,1536]{1,0:T(8,128)(2,1)}, u32[]{:S(2)}) copy-start(bf16[512,1536]{1,0:T(8,128)(2,1)} %w_down.1) | copy-start | bytes 4718596
  50.6 3.4 %collective-permute-start.7 = (bf16[2,256,512]{2,1,0:T(8,128)(2,1)S(1)}, bf16[2,256,512]{2,1,0:T(8,128)(2,1)S(1)}, u32[]{:S(2)}, u32[]{:S(2)}) collective-permute-start(bf16[2,256,512]{2,1,0:T(8,128)(2,1)S(1)} %fusion.12.hidden), channel_id=1, source_target_pairs={{0,1},{1,0},{2,3},{3,2},{4,5},{5,4},{6,7},{7,6},{8,9},{9,8},{10,11... | collective-permute-start | bytes 1572872 | tf_op jit(solution)/shard_map/ppermute | solution.py:28
  50.7 11.6 %collective-permute-start.14 = (bf16[256,768]{1,0:T(8,128)(2,1)S(1)}, bf16[256,768]{1,0:T(8,128)(2,1)S(1)}, u32[]{:S(2)}, u32[]{:S(2)}) collective-permute-start(bf16[256,768]{1,0:T(8,128)(2,1)S(1)} %bitcast.26), channel_id=1, source_target_pairs={{4,0},{8,4},{12,8},{0,12},{5,1},{9,5},{13,9},{1,13},{6,2},{10,6},{... | collective-permute-start | bytes 1179656 | tf_op jit(solution)/shard_map/ppermute | solution.py:24
  52.9 12.4 %collective-permute-start.15 = (bf16[256,768]{1,0:T(8,128)(2,1)S(1)}, bf16[256,768]{1,0:T(8,128)(2,1)S(1)}, u32[]{:S(2)}, u32[]{:S(2)}) collective-permute-start(bf16[256,768]{1,0:T(8,128)(2,1)S(1)} %bitcast.27), channel_id=1, source_target_pairs={{12,0},{0,4},{4,8},{8,12},{13,1},{1,5},{5,9},{9,13},{14,2},{2,6},{... | collective-permute-start | bytes 1179656 | tf_op jit(solution)/shard_map/ppermute | solution.py:24
  62.3 3.0 %copy-start.9 = (bf16[256,768]{1,0:T(8,128)(2,1)}, bf16[256,768]{1,0:T(8,128)(2,1)S(1)}, u32[]{:S(2)}) copy-start(bf16[256,768]{1,0:T(8,128)(2,1)S(1)} %collective-permute-done.14.p1) | copy-start | bytes 1179652
  65.3 0.7 copy-start.10
  70.4 87.3 %reduce-scatter.2.cloned.1.call-start = ((), (), s32[]{:S(2)}) async-start(), calls=%async_computation.2 | async-start | bytes 3538944 | tf_op jit(solution)/shard_map/reduce_scatter | solution.py:318
  74.6 2.0 %collective-permute-start.16 = (bf16[2,256,512]{2,1,0:T(8,128)(2,1)S(1)}, bf16[2,256,512]{2,1,0:T(8,128)(2,1)S(1)}, u32[]{:S(2)}, u32[]{:S(2)}) collective-permute-start(bf16[2,256,512]{2,1,0:T(8,128)(2,1)S(1)} %get-tuple-element.57), channel_id=1, source_target_pairs={{0,1},{1,0},{2,3},{3,2},{4,5},{5,4},{6,7},{7,6},{8,9},{9,8},{10,11... | collective-permute-start | bytes 1572872 | tf_op jit(solution)/shard_map/ppermute | solution.py:28
  76.8 15.6 %copy-start.7 = (bf16[2,256,512]{2,1,0:T(8,128)(2,1)S(1)}, bf16[2,256,512]{2,1,0:T(8,128)(2,1)}, u32[]{:S(2)}) copy-start(bf16[2,256,512]{2,1,0:T(8,128)(2,1)} %get-tuple-element.63) | copy-start | bytes 1572868
  76.8 15.6 %copy-start.8 = (bf16[2,256,512]{2,1,0:T(8,128)(2,1)S(1)}, bf16[2,256,512]{2,1,0:T(8,128)(2,1)}, u32[]{:S(2)}) copy-start(bf16[2,256,512]{2,1,0:T(8,128)(2,1)} %get-tuple-element.62) | copy-start | bytes 1572868
  76.8 15.6 %collective-permute-start.17 = (bf16[2,256,512]{2,1,0:T(8,128)(2,1)S(1)}, bf16[2,256,512]{2,1,0:T(8,128)(2,1)S(1)}, u32[]{:S(2)}, u32[]{:S(2)}) collective-permute-start(bf16[2,256,512]{2,1,0:T(8,128)(2,1)S(1)} %get-tuple-element.86), channel_id=1, source_target_pairs={{0,2},{2,0},{1,3},{3,1},{4,6},{6,4},{5,7},{7,5},{8,10},{10,8},{9,1... | collective-permute-start | bytes 1572872 | tf_op jit(solution)/shard_map/ppermute | solution.py:28
  79.0 23.0 %collective-permute-start.20 = (bf16[256,1536]{1,0:T(8,128)(2,1)}, bf16[256,1536]{1,0:T(8,128)(2,1)}, u32[]{:S(2)}, u32[]{:S(2)}) collective-permute-start(bf16[256,1536]{1,0:T(8,128)(2,1)} %collective-permute-done.13.p0), channel_id=1, source_target_pairs={{4,0},{8,4},{12,8},{0,12},{5,1},{9,5},{13,9},{1,13},{6,2},{10,6},{... | collective-permute-start | bytes 2359304 | tf_op jit(solution)/shard_map/ppermute | solution.py:24
  80.6 21.3 %collective-permute-start.21 = (bf16[256,1536]{1,0:T(8,128)(2,1)}, bf16[256,1536]{1,0:T(8,128)(2,1)}, u32[]{:S(2)}, u32[]{:S(2)}) collective-permute-start(bf16[256,1536]{1,0:T(8,128)(2,1)} %collective-permute-done.13.p0), channel_id=1, source_target_pairs={{12,0},{0,4},{4,8},{8,12},{13,1},{1,5},{5,9},{9,13},{14,2},{2,6},{... | collective-permute-start | bytes 2359304 | tf_op jit(solution)/shard_map/ppermute | solution.py:24
  92.3 3.4 %copy-start.3 = (bf16[1536,512]{1,0:T(8,128)(2,1)S(1)}, bf16[1536,512]{1,0:T(8,128)(2,1)}, u32[]{:S(2)}) copy-start(bf16[1536,512]{1,0:T(8,128)(2,1)} %w_gate.1) | copy-start | bytes 4718596
  92.3 3.4 %copy-start.4 = (bf16[1536,512]{1,0:T(8,128)(2,1)S(1)}, bf16[1536,512]{1,0:T(8,128)(2,1)}, u32[]{:S(2)}) copy-start(bf16[1536,512]{1,0:T(8,128)(2,1)} %w_up.1) | copy-start | bytes 4718596
  93.0 2.0 %collective-permute-start.18 = (bf16[2,256,512]{2,1,0:T(8,128)(2,1)S(1)}, bf16[2,256,512]{2,1,0:T(8,128)(2,1)S(1)}, u32[]{:S(2)}, u32[]{:S(2)}) collective-permute-start(bf16[2,256,512]{2,1,0:T(8,128)(2,1)S(1)} %get-tuple-element.89.gg), channel_id=1, source_target_pairs={{0,1},{1,0},{2,3},{3,2},{4,5},{5,4},{6,7},{7,6},{8,9},{9,8},{10,11... | collective-permute-start | bytes 1572872 | tf_op jit(solution)/shard_map/ppermute | solution.py:28
  93.1 2.6 %collective-permute-start.19 = (bf16[2,256,512]{2,1,0:T(8,128)(2,1)S(1)}, bf16[2,256,512]{2,1,0:T(8,128)(2,1)S(1)}, u32[]{:S(2)}, u32[]{:S(2)}) collective-permute-start(bf16[2,256,512]{2,1,0:T(8,128)(2,1)S(1)} %get-tuple-element.88.gu), channel_id=1, source_target_pairs={{0,1},{1,0},{2,3},{3,2},{4,5},{5,4},{6,7},{7,6},{8,9},{9,8},{10,11... | collective-permute-start | bytes 1572872 | tf_op jit(solution)/shard_map/ppermute | solution.py:28
  101.2 0.8 copy-start
  102.0 15.7 %collective-permute-start.23 = (bf16[2,256,512]{2,1,0:T(8,128)(2,1)S(1)}, bf16[2,256,512]{2,1,0:T(8,128)(2,1)}, u32[]{:S(2)}, u32[]{:S(2)}) collective-permute-start(bf16[2,256,512]{2,1,0:T(8,128)(2,1)S(1)} %get-tuple-element.89.gg), channel_id=1, source_target_pairs={{0,128},{128,0},{1,129},{129,1},{2,130},{130,2},{3,131},{131,3},{4... | collective-permute-start | bytes 1572872 | tf_op jit(solution)/shard_map/ppermute | solution.py:28
  103.1 24.3 %collective-permute-start.24 = (bf16[2,256,512]{2,1,0:T(8,128)(2,1)S(1)}, bf16[2,256,512]{2,1,0:T(8,128)(2,1)}, u32[]{:S(2)}, u32[]{:S(2)}) collective-permute-start(bf16[2,256,512]{2,1,0:T(8,128)(2,1)S(1)} %get-tuple-element.88.gu), channel_id=1, source_target_pairs={{0,128},{128,0},{1,129},{129,1},{2,130},{130,2},{3,131},{131,3},{4... | collective-permute-start | bytes 1572872 | tf_op jit(solution)/shard_map/ppermute | solution.py:28
  104.1 13.5 %collective-permute-start.25 = (bf16[256,768]{1,0:T(8,128)(2,1)S(1)}, bf16[256,768]{1,0:T(8,128)(2,1)S(1)}, u32[]{:S(2)}, u32[]{:S(2)}) collective-permute-start(bf16[256,768]{1,0:T(8,128)(2,1)S(1)} %bitcast.28), channel_id=1, source_target_pairs={{8,0},{12,4},{0,8},{4,12},{9,1},{13,5},{1,9},{5,13},{10,2},{14,6},... | collective-permute-start | bytes 1179656 | tf_op jit(solution)/shard_map/ppermute | solution.py:24
  106.3 30.6 %collective-permute-start.22 = (bf16[256,1536]{1,0:T(8,128)(2,1)}, bf16[256,1536]{1,0:T(8,128)(2,1)}, u32[]{:S(2)}, u32[]{:S(2)}) collective-permute-start(bf16[256,1536]{1,0:T(8,128)(2,1)} %collective-permute-done.13.p0), channel_id=1, source_target_pairs={{8,0},{12,4},{0,8},{4,12},{9,1},{13,5},{1,9},{5,13},{10,2},{14,6},... | collective-permute-start | bytes 2359304 | tf_op jit(solution)/shard_map/ppermute | solution.py:24
  117.7 9.7 %copy-start.11 = (bf16[256,768]{1,0:T(8,128)(2,1)}, bf16[256,768]{1,0:T(8,128)(2,1)S(1)}, u32[]{:S(2)}) copy-start(bf16[256,768]{1,0:T(8,128)(2,1)S(1)} %collective-permute-done.25.p2) | copy-start | bytes 1179652
  127.4 43.0 %collective-permute-start.31 = (bf16[512,1536]{1,0:T(8,128)(2,1)S(1)}, bf16[512,1536]{1,0:T(8,128)(2,1)}, u32[]{:S(2)}, u32[]{:S(2)}) collective-permute-start(bf16[512,1536]{1,0:T(8,128)(2,1)S(1)} %shard_map.106.left), channel_id=1, source_target_pairs={{0,128},{128,0},{1,129},{129,1},{2,130},{130,2},{3,131},{131,3},{4... | collective-permute-start | bytes 4718600 | tf_op jit(solution)/shard_map/ppermute | solution.py:28
  128.4 8.5 %collective-permute-start.26 = (bf16[2,256,512]{2,1,0:T(8,128)(2,1)}, bf16[2,256,512]{2,1,0:T(8,128)(2,1)}, u32[]{:S(2)}, u32[]{:S(2)}) collective-permute-start(bf16[2,256,512]{2,1,0:T(8,128)(2,1)} %collective-permute-done.23.gg), channel_id=1, source_target_pairs={{0,1},{1,0},{2,3},{3,2},{4,5},{5,4},{6,7},{7,6},{8,9},{9,8},{10,11... | collective-permute-start | bytes 1572872 | tf_op jit(solution)/shard_map/ppermute | solution.py:28
  128.4 8.5 %collective-permute-start.27 = (bf16[2,256,512]{2,1,0:T(8,128)(2,1)}, bf16[2,256,512]{2,1,0:T(8,128)(2,1)}, u32[]{:S(2)}, u32[]{:S(2)}) collective-permute-start(bf16[2,256,512]{2,1,0:T(8,128)(2,1)} %collective-permute-done.24.gu), channel_id=1, source_target_pairs={{0,1},{1,0},{2,3},{3,2},{4,5},{5,4},{6,7},{7,6},{8,9},{9,8},{10,11... | collective-permute-start | bytes 1572872 | tf_op jit(solution)/shard_map/ppermute | solution.py:28
  129.0 1.0 copy-start.1
  158.7 5.2 %collective-permute-start.30 = (bf16[32,1536]{1,0:T(8,128)(2,1)S(1)}, bf16[32,1536]{1,0:T(8,128)(2,1)S(1)}, u32[]{:S(2)}, u32[]{:S(2)}) collective-permute-start(bf16[32,1536]{1,0:T(8,128)(2,1)S(1)} %get-tuple-element.95), channel_id=1, source_target_pairs={{4,0},{8,4},{12,8},{0,12},{5,1},{9,5},{13,9},{1,13},{6,2},{10,6},{... | collective-permute-start | bytes 294920 | tf_op jit(solution)/shard_map/ppermute | solution.py:24
  161.6 6.2 %collective-permute-start.29 = (bf16[32,1536]{1,0:T(8,128)(2,1)S(1)}, bf16[32,1536]{1,0:T(8,128)(2,1)S(1)}, u32[]{:S(2)}, u32[]{:S(2)}) collective-permute-start(bf16[32,1536]{1,0:T(8,128)(2,1)S(1)} %get-tuple-element.96), channel_id=1, source_target_pairs={{8,0},{12,4},{0,8},{4,12},{9,1},{13,5},{1,9},{5,13},{10,2},{14,6},... | collective-permute-start | bytes 294920 | tf_op jit(solution)/shard_map/ppermute | solution.py:24
  162.5 6.3 %collective-permute-start.28 = (bf16[32,1536]{1,0:T(8,128)(2,1)S(1)}, bf16[32,1536]{1,0:T(8,128)(2,1)S(1)}, u32[]{:S(2)}, u32[]{:S(2)}) collective-permute-start(bf16[32,1536]{1,0:T(8,128)(2,1)S(1)} %get-tuple-element.94), channel_id=1, source_target_pairs={{12,0},{0,4},{4,8},{8,12},{13,1},{1,5},{5,9},{9,13},{14,2},{2,6},{... | collective-permute-start | bytes 294920 | tf_op jit(solution)/shard_map/ppermute | solution.py:24
Sparse Core Ops, SparseCore 0:
  26.4 43.9 all-gather.2
  72.2 37.0 all-gather.4
  111.8 45.7 reduce-scatter.1

commit v5 on v4

v5 whole, which is shorter than its diff:
```python
import functools

import jax
import jax.numpy as jnp
from jax import lax
from jax.experimental import pallas as pl
from jax.experimental.pallas import tpu as pltpu
from jax.sharding import Mesh, PartitionSpec as P

F32, BF16 = jnp.float32, jnp.bfloat16
NZ, NY = 8, 4
FIRST = 64
VMEM = pl.BlockSpec(memory_space=pltpu.VMEM)
SMEM = pl.BlockSpec(memory_space=pltpu.SMEM)
HBM = pl.BlockSpec(memory_space=pltpu.HBM)


def dot(left, right, left_dim, right_dim):
    dims = (((left_dim,), (right_dim,)), ((), ()))
    return lax.dot_general(left, right, dims, preferred_element_type=F32)


def from_ahead(x, axis, n, k):
    return lax.ppermute(x, axis, [((d + k) % n, d) for d in range(n)])


def swap(x, axis):
    return lax.ppermute(x, axis, [(0, 1), (1, 0)])


def grant(mib):
    return pltpu.CompilerParams(vmem_limit_bytes=mib << 20)


def in_hbm(x):
    return pltpu.with_memory_space_constraint(x, pltpu.HBM)


def arrange_kernel(n, slot, place, *refs):
    for k in range(n):
        refs[n][(place[slot] + k) % n] = refs[k][...]


def arrange(place, slot, parts):
    n, (rows, cols) = len(parts), parts[0].shape
    out = pl.pallas_call(
        functools.partial(arrange_kernel, n, slot),
        out_shape=jax.ShapeDtypeStruct((n, rows, cols), BF16),
        in_specs=[SMEM] + [VMEM] * n,
        out_specs=VMEM,
        compiler_params=grant(6),
    )(place, in_hbm(parts[0]), *parts[1:])
    return out.reshape(n * rows, cols)


def hidden_grad_kernel(place, go, w_down, mine, send, rows, sems):
    copies = [
        pltpu.make_async_copy(go.at[pl.ds(512 * half, 512)], rows.at[half], sems.at[half])
        for half in range(2)
    ]
    for copy in copies:
        copy.start()
    for half, copy in enumerate(copies):
        copy.wait()
        part = dot(rows[half], w_down[...], 1, 1)
        for which in range(2):
            block = part[256 * which:256 * which + 256]

            @pl.when(place[3] == which)
            def _():
                mine[half] = block

            @pl.when(place[3] != which)
            def _():
                send[half] = block.astype(BF16)


def hidden_grad(place, go, w_down):
    return pl.pallas_call(
        hidden_grad_kernel,
        out_shape=(
            jax.ShapeDtypeStruct((2, 256, 512), F32),
            jax.ShapeDtypeStruct((2, 256, 512), BF16),
        ),
        in_specs=[SMEM, HBM, VMEM],
        out_specs=(VMEM,) * 2,
        scratch_shapes=[pltpu.VMEM((2, 512, 1536), BF16), pltpu.SemaphoreType.DMA((2,))],
        compiler_params=grant(16),
    )(place, in_hbm(go), w_down)


def input_grad_kernel(place, gg, gg_other, gu, gu_other, w_gate, w_up, out):
    def emit(gate_ref, up_ref, core):
        gate_rows, up_rows = gate_ref[...].reshape(512, 512), up_ref[...].reshape(512, 512)
        total = (dot(gate_rows, w_gate[...], 1, 1) + dot(up_rows, w_up[...], 1, 1)).astype(BF16)
        for half in range(2):
            start = pl.multiple_of(512 * half + 256 * core, 256)
            out[pl.ds(start, 256), :] = total[256 * half:256 * half + 256]

    emit(gg, gu, place[3])
    emit(gg_other, gu_other, 1 - place[3])


def input_grad(place, gg, gg_other, gu, gu_other, w_gate, w_up):
    weight = pl.BlockSpec((512, 512), lambda i: (i, 0))
    return pl.pallas_call(
        input_grad_kernel,
        grid=(3,),
        out_shape=jax.ShapeDtypeStruct((1024, 1536), BF16),
        in_specs=[SMEM] + [VMEM] * 4 + [weight] * 2,
        out_specs=pl.BlockSpec((1024, 512), lambda i: (0, i)),
        compiler_params=grant(16),
    )(place, gg, gg_other, gu, gu_other, w_gate, w_up)


def fill_natural(place, own, other, rows, col):
    for half in range(2):
        base = half * 512
        start = pl.multiple_of(base + place[3] * 256, 256)
        rows[pl.ds(start, 256), col:col + 512] = own[half]
        start = pl.multiple_of(base + (1 - place[3]) * 256, 256)
        rows[pl.ds(start, 256), col:col + 512] = other[half]


def down_kernel(place, hidden, hidden_other, go, first, rest, rows):
    @pl.when(pl.program_id(0) == 0)
    def _():
        fill_natural(place, hidden, hidden_other, rows, 0)

    total = dot(rows[...], go[...], 0, 0).astype(BF16)
    first[...] = total[:FIRST]
    rest[...] = total[FIRST:]


def down_grad(place, hidden, hidden_other, go):
    return pl.pallas_call(
        down_kernel,
        grid=(3,),
        out_shape=(
            jax.ShapeDtypeStruct((FIRST, 1536), BF16),
            jax.ShapeDtypeStruct((512 - FIRST, 1536), BF16),
        ),
        in_specs=[SMEM, VMEM, VMEM, pl.BlockSpec((1024, 512), lambda i: (0, i))],
        out_specs=(
            pl.BlockSpec((FIRST, 512), lambda i: (0, i)),
            pl.BlockSpec((512 - FIRST, 512), lambda i: (0, i)),
        ),
        scratch_shapes=[pltpu.VMEM((1024, 512), BF16)],
        compiler_params=grant(12),
    )(place, hidden, hidden_other, in_hbm(go))


def fill_rolled(place, own, other, rows, col):
    for half in range(2):
        for pair in range(2):
            for y in range(NY):
                k = (y - place[1] + NY) % NY
                lines = pl.ds(pair * 128 + y * 32, 32)
                z_own = 4 * half + 2 * place[3] + pair
                rows[k, z_own, :, col:col + 512] = own[half, lines, :]
                z_other = 4 * half + 2 * (1 - place[3]) + pair
                rows[k, z_other, :, col:col + 512] = other[half, lines, :]


def rolled_total(place, pieces, grads, rows):
    @pl.when(pl.program_id(0) == 0)
    def _():
        fill_rolled(place, *grads[:2], rows, 0)
        fill_rolled(place, *grads[2:], rows, 512)

    total = jnp.zeros((256, 1024), F32)
    for k, piece in enumerate(pieces):
        total = total + dot(piece[...], rows[k].reshape(256, 1024), 0, 0)
    return total.astype(BF16)


def own_kernel(place, *refs):
    total = rolled_total(place, refs[:4], refs[4:8], refs[10])
    refs[8][...] = total[:, :512]
    refs[9][...] = total[:, 512:]


def partner_kernel(place, *refs):
    total = rolled_total(place, refs[:4], refs[4:8], refs[12]).astype(F32)
    refs[10][...] = (total[:, :512] + refs[8][...].astype(F32)).astype(BF16)
    refs[11][...] = (total[:, 512:] + refs[9][...].astype(F32)).astype(BF16)


TILE = pl.BlockSpec((256, 512), lambda i: (i, 0))
WEIGHT = jax.ShapeDtypeStruct((1536, 512), BF16)
ROLLED = pltpu.VMEM((NY, NZ, 32, 1024), BF16)


def own_weight_grads(place, pieces, grads):
    every = pl.BlockSpec((256, 256), lambda i: (0, i))
    return pl.pallas_call(
        own_kernel,
        grid=(6,),
        out_shape=(WEIGHT, WEIGHT),
        in_specs=[SMEM] + [every] * 4 + [VMEM] * 4,
        out_specs=(TILE, TILE),
        scratch_shapes=[ROLLED],
        compiler_params=grant(16),
    )(place, *(in_hbm(x) for x in pieces), *grads)


def partner_weight_grads(place, pieces, grads, own_gate, own_up):
    every = pl.BlockSpec((256, 256), lambda i: (0, i))
    return pl.pallas_call(
        partner_kernel,
        grid=(6,),
        out_shape=(WEIGHT, WEIGHT),
        in_specs=[SMEM] + [every] * 4 + [VMEM] * 4 + [TILE] * 2,
        out_specs=(TILE, TILE),
        scratch_shapes=[ROLLED],
        compiler_params=grant(16),
    )(place, in_hbm(pieces[0]), *pieces[1:], *grads, own_gate, own_up)


def add_kernel(first, first_far, rest, rest_far, out):
    out[:FIRST] = (first[...].astype(F32) + first_far[...].astype(F32)).astype(BF16)
    out[FIRST:] = (rest[...].astype(F32) + rest_far[...].astype(F32)).astype(BF16)


def add(first, first_far, rest, rest_far):
    top = pl.BlockSpec((FIRST, 512), lambda i: (0, i))
    low = pl.BlockSpec((512 - FIRST, 512), lambda i: (0, i))
    return pl.pallas_call(
        add_kernel,
        grid=(3,),
        out_shape=jax.ShapeDtypeStruct((512, 1536), BF16),
        in_specs=[top, top, low, low],
        out_specs=pl.BlockSpec((512, 512), lambda i: (0, i)),
        compiler_params=grant(8),
    )(first, first_far, rest, rest_far)


def ring(x, up, down, axis, n):
    ahead, behind = [up], [down]
    for step in range(2, n // 2 + 1):
        up = from_ahead(up, axis, n, 1)
        ahead.append(up)
        if step < n // 2:
            down = from_ahead(down, axis, n, n - 1)
            behind.append(down)
    return [x] + ahead + behind[::-1]


def ordered(mine, other, index):
    low = jnp.where(index == 0, mine, other)
    high = jnp.where(index == 0, other, mine)
    return jnp.stack([low, high], axis=0)


def body(layer_input, grad_output, gate_saved, up_saved, w_gate, w_up, w_down):
    place = jnp.stack([lax.axis_index(name) for name in ("z", "y", "xh", "core")]).astype(jnp.int32)
    xh = place[2]

    go_parts = [grad_output] + [from_ahead(grad_output, "y", NY, k) for k in (1, 2, 3)]
    z_up, z_down = from_ahead(layer_input, "z", NZ, 1), from_ahead(layer_input, "z", NZ, NZ - 1)
    go_parts, z_up, z_down = lax.optimization_barrier((go_parts, z_up, z_down))
    go = lax.all_gather(arrange(place, 1, go_parts), "z", axis=0, tiled=True)
    own_z = arrange(place, 0, ring(layer_input, z_up, z_down, "z", NZ))
    partner_z = swap(own_z, "dp")
    own1, own3 = from_ahead(own_z, "y", NY, 1), from_ahead(own_z, "y", NY, 3)

    gate = ordered(gate_saved, swap(gate_saved, "xh"), xh)
    up = ordered(up_saved, swap(up_saved, "xh"), xh)
    gate_val, up_val = gate.astype(F32), up.astype(F32)
    hidden = (gate_val * jax.nn.sigmoid(gate_val) * up_val).astype(BF16)
    hidden_other = swap(hidden, "core")
    go, gate, up, hidden, hidden_other, own_z, partner_z, own1, own3 = lax.optimization_barrier(
        (go, gate, up, hidden, hidden_other, own_z, partner_z, own1, own3)
    )

    own2 = from_ahead(own_z, "y", NY, 2)
    mine, send = hidden_grad(place, go, w_down)
    chip = mine + swap(send, "core").astype(F32)
    chip_far = swap(chip.astype(BF16), "xh")
    down_first, down_rest = down_grad(place, hidden, hidden_other, go)

    chip, chip_far, down_first, down_rest = lax.optimization_barrier((chip, chip_far, down_first, down_rest))
    first_far = swap(down_first, "dp")

    grad_hidden = chip + chip_far.astype(F32)
    gate_val, up_val = gate.astype(F32), up.astype(F32)
    sigma = jax.nn.sigmoid(gate_val)
    gg = (grad_hidden * up_val * sigma * (1.0 + gate_val * (1.0 - sigma))).astype(BF16)
    gu = (grad_hidden * gate_val * sigma).astype(BF16)
    gg_other, gu_other = swap(gg, "core"), swap(gu, "core")
    partial_in = input_grad(place, gg, gg_other, gu, gu_other, w_gate, w_up)
    partial_in, own2, first_far = lax.optimization_barrier((partial_in, own2, first_far))
    in_z = lax.psum_scatter(partial_in, "z", scatter_dimension=0, tiled=True).reshape(NY, 32, 1536)

    gg_far, gu_far = swap(gg, "dp"), swap(gu, "dp")
    partner_pieces = [partner_z] + [from_ahead(partner_z, "y", NY, k) for k in (1, 2, 3)]
    own_gate, own_up = own_weight_grads(place, (own_z, own1, own2, own3), (gg, gg_other, gu, gu_other))
    gg_far, gu_far, down_rest, own_gate, own_up = lax.optimization_barrier(
        (gg_far, gu_far, down_rest, own_gate, own_up)
    )
    rest_far = swap(down_rest, "dp")
    far = (gg_far, swap(gg_far, "core"), gu_far, swap(gu_far, "core"))
    grad_gate, grad_up = partner_weight_grads(place, partner_pieces, far, own_gate, own_up)
    in_z, grad_gate, grad_up = lax.optimization_barrier((in_z, grad_gate, grad_up))

    y = place[1]
    total = lax.dynamic_index_in_dim(in_z, y, 0, keepdims=False).astype(F32)
    for k in range(1, NY):
        slab = lax.dynamic_index_in_dim(in_z, (y + k) % NY, 0, keepdims=False)
        total = total + from_ahead(slab, "y", NY, NY - k).astype(F32)
    grad_input = total.astype(BF16)
    grad_input, rest_far = lax.optimization_barrier((grad_input, rest_far))
    return grad_input, grad_gate, grad_up, add(down_first, first_far, down_rest, rest_far)


def solution(mesh):
    fine = Mesh(mesh.devices.reshape(2, NZ, NY, 2, 2), ("dp", "z", "y", "xh", "core"))
    tokens, col, row = ("dp", "z", "y"), ("xh", "core"), ("z", "y")
    in_specs = (
        P(tokens, col),
        P(tokens, col),
        P(("dp",) + col, row),
        P(("dp",) + col, row),
        P(col, row),
        P(col, row),
        P(row, col),
    )
    out_specs = (P(tokens, col), P(col, row), P(col, row), P(row, col))
    return jax.shard_map(body, mesh=fine, in_specs=in_specs, out_specs=out_specs, check_vma=False)
```

time: 181 us -> 177 us (0.978)
  starting transfers between devices: 43.4 us -> 36.9 us
  local copies, waits for them, and re-layouts: 3.64 us -> 9.71 us
  waiting for transfers between devices: 79.1 us -> 75 us
    reduce_scatter x1, waiting for transfers between devices: 12.4 us -> 0.01 us  [body(): lax.psum_scatter(partial_in, 'z', scatter_dimension=0, tiled=True)]
    ppermute x13 -> x14, waiting for transfers between devices: 21.1 us -> 30.8 us  [swap(): return lax.ppermute(x, axis, [(0, 1), (1, 0)])]
    ppermute x19, starting transfers between devices: 32.4 us -> 25.8 us  [from_ahead(): return lax.ppermute(x, axis, [((d + k) % n, d) for d in range(n)])]
    unnamed x26 -> x36, local copies, waits for them, and re-layouts: 2.63 us -> 8.71 us
    all_gather x2 -> x1, waiting for transfers between devices: 4.3 us -> 3.75 us  [body(): go = lax.all_gather(arrange(place, 1, go_parts), 'z', axis=0, tiled=True)]
    pallas_call x5 -> x4, Pallas kernels: 10.8 us -> 11.1 us  [the longest x1 5.03 us: down_grad(): pl.pallas_call(down_kernel, grid=(3,), out_shape=(jax.ShapeDtypeStruct((F...]
    ppermute x13 -> x14, starting transfers between devices: 11 us -> 11 us  [swap(): return lax.ppermute(x, axis, [(0, 1), (1, 0)])]
  transfers between devices with their start and end apart: 35 -> 35, of which waited for: 19 -> 23; matrix products, arithmetic and copies ran while one was open for 3% -> 3% of each run, Pallas kernels for 16% -> 15%
where the time goes in v5:
time: 177 us; the launch traced here: 176 us
  waiting for transfers between devices  75 us (42%)
  starting transfers between devices  36.9 us (21%)
  Pallas kernels  35 us (20%)
  between operations  14.2 us (8%)
  local copies, waits for them, and re-layouts  9.71 us (5%)
  other arithmetic  4.96 us (3%)
    ppermute x19, waiting for transfers between devices, from_ahead(): return lax.ppermute(x, axis, [((d + k) % n, d) for d in range(n)])  40.4 us
    ppermute x14, waiting for transfers between devices, swap(): return lax.ppermute(x, axis, [(0, 1), (1, 0)])  30.8 us
    ppermute x19, starting transfers between devices, from_ahead(): return lax.ppermute(x, axis, [((d + k) % n, d) for d in range(n)])  25.8 us
    ppermute x14, starting transfers between devices, swap(): return lax.ppermute(x, axis, [(0, 1), (1, 0)])  11 us
    unnamed x36, local copies, waits for them, and re-layouts  8.71 us
    pallas_call x1, Pallas kernels, partner_weight_grads(): pl.pallas_call(partner_kernel, grid=(6,), out_shape=(WEIGHT, WEIGHT), in_...  7.63 us
    pallas_call x1, Pallas kernels, own_weight_grads(): pl.pallas_call(own_kernel, grid=(6,), out_shape=(WEIGHT, WEIGHT), in_spec...  6.66 us
    pallas_call x1, Pallas kernels, input_grad(): pl.pallas_call(input_grad_kernel, grid=(3,), out_shape=jax.ShapeDtypeStru...  5.5 us
  transfers between devices with their start and end apart: 35, of which 23 were waited for; matrix products, arithmetic and copies ran while one was open for 3% of the time, Pallas kernels for 15%

profile of v5, /device:TPU:2, one launch (start us, length us, event | category | flops | bytes accessed | tf_op | source)
XLA Modules:
  0.0 175.9 jit_solution(4084830169117356911)
XLA Ops:
  7.2 3.1 %collective-permute-start = (bf16[32,1536]{1,0:T(8,128)(2,1)}, bf16[32,1536]{1,0:T(8,128)(2,1)S(1)}, u32[]{:S(2)}, u32[]{:S(2)}) collective-permute-start(bf16[32,1536]{1,0:T(8,128)(2,1)} %refs_0_.1), channel_id=1, source_target_pairs={{4,0},{8,4},{12,8},{0,12},{5,1},{9,5},{13,9},{1,13},{6,2},{10,6},{... | collective-permute-start | bytes 294920 | tf_op jit(solution)/shard_map/ppermute | solution.py:24
  10.9 1.0 collective-permute-start.2
  11.9 5.9 %collective-permute-start.3 = (bf16[32,1536]{1,0:T(8,128)(2,1)}, bf16[32,1536]{1,0:T(8,128)(2,1)S(1)}, u32[]{:S(2)}, u32[]{:S(2)}) collective-permute-start(bf16[32,1536]{1,0:T(8,128)(2,1)} %refs_0_.2), channel_id=1, source_target_pairs={{16,0},{32,16},{48,32},{64,48},{80,64},{96,80},{112,96},{0,112},{1... | collective-permute-start | bytes 294920 | tf_op jit(solution)/shard_map/ppermute | solution.py:24
  18.4 1.9 %collective-permute-done.3.refs_1_ = bf16[32,1536]{1,0:T(8,128)(2,1)S(1)} collective-permute-done((bf16[32,1536]{1,0:T(8,128)(2,1)}, bf16[32,1536]{1,0:T(8,128)(2,1)S(1)}, u32[]{:S(2)}, u32[]{:S(2)}) %collective-permute-start.3) | collective-permute-done | bytes 98336 | tf_op jit(solution)/shard_map/ppermute | solution.py:24
  20.3 3.5 %collective-permute-done.4.refs_7_ = bf16[32,1536]{1,0:T(8,128)(2,1)S(1)} collective-permute-done((bf16[32,1536]{1,0:T(8,128)(2,1)}, bf16[32,1536]{1,0:T(8,128)(2,1)S(1)}, u32[]{:S(2)}, u32[]{:S(2)}) %collective-permute-start.4) | collective-permute-done | bytes 98336 | tf_op jit(solution)/shard_map/ppermute | solution.py:24
  23.8 1.7 shard_map.102
  25.6 2.2 %collective-permute-start.5 = (bf16[256,512]{1,0:T(8,128)(2,1)}, bf16[256,512]{1,0:T(8,128)(2,1)S(1)}, u32[]{:S(2)}, u32[]{:S(2)}) collective-permute-start(bf16[256,512]{1,0:T(8,128)(2,1)} %param.9), channel_id=1, source_target_pairs={{0,2},{2,0},{1,3},{3,1},{4,6},{6,4},{5,7},{7,5},{8,10},{10,8},{9,1... | collective-permute-start | bytes 786440 | tf_op jit(solution)/shard_map/ppermute | solution.py:28
  28.2 1.6 collective-permute-start.11
  29.8 3.6 %collective-permute-done.8.refs_2_ = bf16[32,1536]{1,0:T(8,128)(2,1)S(1)} collective-permute-done((bf16[32,1536]{1,0:T(8,128)(2,1)S(1)}, bf16[32,1536]{1,0:T(8,128)(2,1)S(1)}, u32[]{:S(2)}, u32[]{:S(2)}) %collective-permute-start.8) | collective-permute-done | bytes 98336 | tf_op jit(solution)/shard_map/ppermute | solution.py:24
  34.0 1.4 collective-permute-start.6
  35.4 1.4 collective-permute-start.12
  36.8 4.2 %collective-permute-done.9.refs_3_ = bf16[32,1536]{1,0:T(8,128)(2,1)S(1)} collective-permute-done((bf16[32,1536]{1,0:T(8,128)(2,1)S(1)}, bf16[32,1536]{1,0:T(8,128)(2,1)S(1)}, u32[]{:S(2)}, u32[]{:S(2)}) %collective-permute-start.9) | collective-permute-done | bytes 98336 | tf_op jit(solution)/shard_map/ppermute | solution.py:24
  42.0 1.0 select_bitcast_fusion.3
  43.4 4.4 %collective-permute-done.10.refs_4_ = bf16[32,1536]{1,0:T(8,128)(2,1)S(1)} collective-permute-done((bf16[32,1536]{1,0:T(8,128)(2,1)S(1)}, bf16[32,1536]{1,0:T(8,128)(2,1)S(1)}, u32[]{:S(2)}, u32[]{:S(2)}) %collective-permute-start.10) | collective-permute-done | bytes 98336 | tf_op jit(solution)/shard_map/ppermute | solution.py:24
  47.8 1.0 shard_map.103
  48.7 1.1 collective-permute-start.13
  49.8 2.2 %collective-permute-start.14 = (bf16[256,1536]{1,0:T(8,128)(2,1)S(1)}, bf16[256,1536]{1,0:T(8,128)(2,1)S(1)}, u32[]{:S(2)}, u32[]{:S(2)}) collective-permute-start(bf16[256,1536]{1,0:T(8,128)(2,1)S(1)} %bitcast.25), channel_id=1, source_target_pairs={{4,0},{8,4},{12,8},{0,12},{5,1},{9,5},{13,9},{1,13},{6,2},{10,6},{... | collective-permute-start | bytes 2359304 | tf_op jit(solution)/shard_map/ppermute | solution.py:24
  52.7 1.1 pad_maximum_fusion
  54.6 7.8 %collective-permute-done.13.refs_0_ = bf16[256,1536]{1,0:T(8,128)(2,1)} collective-permute-done((bf16[256,1536]{1,0:T(8,128)(2,1)S(1)}, bf16[256,1536]{1,0:T(8,128)(2,1)}, u32[]{:S(2)}, u32[]{:S(2)}) %collective-permute-start.13) | collective-permute-done | bytes 786464 | tf_op jit(solution)/shard_map/ppermute | solution.py:28
  62.3 1.4 collective-permute-done.14.refs_1_
  65.3 3.8 %all-gather.2.cloned.1.call-done.go = bf16[1024,1536]{1,0:T(8,128)(2,1)} async-done(((bf16[128,1536]{1,0:T(8,128)(2,1)}), bf16[1024,1536]{1,0:T(8,128)(2,1)}) %all-gather.2.cloned.1.call-update) | async-done | bytes 3145744 | tf_op jit(solution)/shard_map/all_gather | solution.py:262
  69.0 4.1 %shard_map.104 = (f32[2,256,512]{2,1,0:T(8,128)S(1)}, bf16[2,256,512]{2,1,0:T(8,128)(2,1)S(1)}) custom-call(s32[4]{0:T(128)S(1)} %pad_add_fusion.place, bf16[1024,1536]{1,0:T(8,128)(2,1)} %all-gather.2.cloned.1.call-done.go, bf16[512,1536]{1,0:T(8,128)(2,1)S(1)} %copy-done.1), custom_call_target="tpu_custom_call" | custom-call | tf_op jit(solution)/shard_map/pallas_call | solution.py:79
  73.2 1.9 %collective-permute-done.16 = bf16[2,256,512]{2,1,0:T(8,128)(2,1)S(1)} collective-permute-done((bf16[2,256,512]{2,1,0:T(8,128)(2,1)S(1)}, bf16[2,256,512]{2,1,0:T(8,128)(2,1)S(1)}, u32[]{:S(2)}, u32[]{:S(2)}) %collective-permute-start.16) | collective-permute-done | bytes 524320 | tf_op jit(solution)/shard_map/ppermute | solution.py:28
  75.4 2.2 %collective-permute-start.17 = (bf16[2,256,512]{2,1,0:T(8,128)(2,1)S(1)}, bf16[2,256,512]{2,1,0:T(8,128)(2,1)S(1)}, u32[]{:S(2)}, u32[]{:S(2)}) collective-permute-start(bf16[2,256,512]{2,1,0:T(8,128)(2,1)S(1)} %get-tuple-element.84), channel_id=1, source_target_pairs={{0,2},{2,0},{1,3},{3,1},{4,6},{6,4},{5,7},{7,5},{8,10},{10,8},{9,1... | collective-permute-start | bytes 1572872 | tf_op jit(solution)/shard_map/ppermute | solution.py:28
  77.5 2.0 %collective-permute-start.20 = (bf16[256,1536]{1,0:T(8,128)(2,1)S(1)}, bf16[256,1536]{1,0:T(8,128)(2,1)}, u32[]{:S(2)}, u32[]{:S(2)}) collective-permute-start(bf16[256,1536]{1,0:T(8,128)(2,1)S(1)} %bitcast.27), channel_id=1, source_target_pairs={{8,0},{12,4},{0,8},{4,12},{9,1},{13,5},{1,9},{5,13},{10,2},{14,6},... | collective-permute-start | bytes 2359304 | tf_op jit(solution)/shard_map/ppermute | solution.py:24
  79.5 5.0 %shard_map.105 = (bf16[64,1536]{1,0:T(8,128)(2,1)S(1)}, bf16[448,1536]{1,0:T(8,128)(2,1)}) custom-call(s32[4]{0:T(128)S(1)} %pad_add_fusion.place, bf16[2,256,512]{2,1,0:T(8,128)(2,1)S(1)} %fusion.12.hidden, bf16[2,256,512]{2,1,0:T(8,128)(2,1)S(1)} %collective-permute-done.7.hidden_other, bf16[1024,1536]{1,0:T(8,128)(2,1)} %all-gather.2.cloned.1.call-done.go), custom_call_target="tpu_custom_call" | custom-call | tf_op jit(solution)/shard_map/pallas_call | solution.py:136
  84.5 6.4 %collective-permute-done.17 = bf16[2,256,512]{2,1,0:T(8,128)(2,1)S(1)} collective-permute-done((bf16[2,256,512]{2,1,0:T(8,128)(2,1)S(1)}, bf16[2,256,512]{2,1,0:T(8,128)(2,1)S(1)}, u32[]{:S(2)}, u32[]{:S(2)}) %collective-permute-start.17) | collective-permute-done | bytes 524320 | tf_op jit(solution)/shard_map/ppermute | solution.py:28
  94.3 5.5 %shard_map.106 = bf16[1024,1536]{1,0:T(8,128)(2,1)} custom-call(s32[4]{0:T(128)S(1)} %pad_add_fusion.place, bf16[2,256,512]{2,1,0:T(8,128)(2,1)S(1)} %get-tuple-element.87.gg.refs_4_, bf16[2,256,512]{2,1,0:T(8,128)(2,1)S(1)} %collective-permute-done.18.gg_other.refs_5_, bf16[2,256,512]{2,1,0:T(8,128)(2,1)S(1)} %get-tuple-element.86.gu.refs_6_, ...), custom_call_target="tpu_custom_call" | custom-call | tf_op jit(solution)/shard_map/pallas_call | solution.py:106
  100.5 2.0 %collective-permute-start.22 = (bf16[256,1536]{1,0:T(8,128)(2,1)}, bf16[256,1536]{1,0:T(8,128)(2,1)S(1)}, u32[]{:S(2)}, u32[]{:S(2)}) collective-permute-start(bf16[256,1536]{1,0:T(8,128)(2,1)} %collective-permute-done.13.refs_0_), channel_id=1, source_target_pairs={{4,0},{8,4},{12,8},{0,12},{5,1},{9,5},{13,9},{1,13},{6,2},{10,6},{... | collective-permute-start | bytes 2359304 | tf_op jit(solution)/shard_map/ppermute | solution.py:24
  103.1 1.4 collective-permute-start.26
  106.2 6.7 %shard_map.107 = (bf16[1536,512]{1,0:T(8,128)(2,1)S(1)}, bf16[1536,512]{1,0:T(8,128)(2,1)S(1)}) custom-call(s32[4]{0:T(128)S(1)} %pad_add_fusion.place, bf16[256,1536]{1,0:T(8,128)(2,1)} %bitcast.28, bf16[256,1536]{1,0:T(8,128)(2,1)} %copy-done.16, bf16[256,1536]{1,0:T(8,128)(2,1)} %collective-permute-done.20.refs_2_, ...), custom_call_target="tpu_custom_call" | custom-call | tf_op jit(solution)/shard_map/pallas_call | solution.py:196
  112.9 1.1 copy-done.4
  114.1 1.1 copy-done.6
  115.2 2.1 %collective-permute-done.25.refs_4_ = bf16[2,256,512]{2,1,0:T(8,128)(2,1)S(1)} collective-permute-done((bf16[2,256,512]{2,1,0:T(8,128)(2,1)S(1)}, bf16[2,256,512]{2,1,0:T(8,128)(2,1)S(1)}, u32[]{:S(2)}, u32[]{:S(2)}) %collective-permute-start.25) | collective-permute-done | bytes 524320 | tf_op jit(solution)/shard_map/ppermute | solution.py:28
  117.3 10.2 %collective-permute-done.26.refs_6_ = bf16[2,256,512]{2,1,0:T(8,128)(2,1)} collective-permute-done((bf16[2,256,512]{2,1,0:T(8,128)(2,1)S(1)}, bf16[2,256,512]{2,1,0:T(8,128)(2,1)}, u32[]{:S(2)}, u32[]{:S(2)}) %collective-permute-start.26) | collective-permute-done | bytes 524320 | tf_op jit(solution)/shard_map/ppermute | solution.py:28
  128.2 8.7 %collective-permute-done.22.refs_1_ = bf16[256,1536]{1,0:T(8,128)(2,1)S(1)} collective-permute-done((bf16[256,1536]{1,0:T(8,128)(2,1)}, bf16[256,1536]{1,0:T(8,128)(2,1)S(1)}, u32[]{:S(2)}, u32[]{:S(2)}) %collective-permute-start.22) | collective-permute-done | bytes 786464 | tf_op jit(solution)/shard_map/ppermute | solution.py:24
  137.7 4.3 %collective-permute-done.24.refs_3_ = bf16[256,1536]{1,0:T(8,128)(2,1)} collective-permute-done((bf16[256,1536]{1,0:T(8,128)(2,1)}, bf16[256,1536]{1,0:T(8,128)(2,1)}, u32[]{:S(2)}, u32[]{:S(2)}) %collective-permute-start.24) | collective-permute-done | bytes 786464 | tf_op jit(solution)/shard_map/ppermute | solution.py:24
  142.0 1.4 copy-done.5
  143.4 1.4 copy-done.7
  144.8 1.1 copy-done.9
  145.9 7.6 %shard_map.108 = (bf16[1536,512]{1,0:T(8,128)(2,1)}, bf16[1536,512]{1,0:T(8,128)(2,1)}) custom-call(s32[4]{0:T(128)S(1)} %pad_add_fusion.place, bf16[256,1536]{1,0:T(8,128)(2,1)} %collective-permute-done.13.refs_0_, bf16[256,1536]{1,0:T(8,128)(2,1)S(1)} %copy-done.9, bf16[256,1536]{1,0:T(8,128)(2,1)} %collective-permute-done.23.refs_2_, ...), custom_call_target="tpu_custom_call" | custom-call | tf_op jit(solution)/shard_map/pallas_call | solution.py:209
  153.6 1.0 dynamic-slice_bitcast_fusion.2
  154.6 1.5 collective-permute-start.31
  156.1 0.9 collective-permute-start.29
  157.1 3.3 %collective-permute-done.31 = bf16[32,1536]{1,0:T(8,128)(2,1)S(1)} collective-permute-done((bf16[32,1536]{1,0:T(8,128)(2,1)S(1)}, bf16[32,1536]{1,0:T(8,128)(2,1)S(1)}, u32[]{:S(2)}, u32[]{:S(2)}) %collective-permute-start.31) | collective-permute-done | bytes 98336 | tf_op jit(solution)/shard_map/ppermute | solution.py:24
  160.3 2.9 %collective-permute-done.30 = bf16[32,1536]{1,0:T(8,128)(2,1)S(1)} collective-permute-done((bf16[32,1536]{1,0:T(8,128)(2,1)S(1)}, bf16[32,1536]{1,0:T(8,128)(2,1)S(1)}, u32[]{:S(2)}, u32[]{:S(2)}) %collective-permute-start.30) | collective-permute-done | bytes 98336 | tf_op jit(solution)/shard_map/ppermute | solution.py:24
  163.9 1.6 fusion.15
  165.5 3.5 %shard_map.109 = bf16[512,1536]{1,0:T(8,128)(2,1)} custom-call(bf16[64,1536]{1,0:T(8,128)(2,1)S(1)} %copy-done.11, bf16[64,1536]{1,0:T(8,128)(2,1)S(1)} %copy-done.13, bf16[448,1536]{1,0:T(8,128)(2,1)} %get-tuple-element.78.rest, bf16[448,1536]{1,0:T(8,128)(2,1)S(1)} %collective-permute-done.32.rest_far), custom_call_target="tpu_custom_call" | custom-call | tf_op jit(solution)/shard_map/pallas_call | solution.py:228
  (77 shorter events, 15.7 us)
Async XLA Ops:
  7.2 61.9 %all-gather.2.cloned.1.call-start = ((), (), s32[]{:S(2)}) async-start(), calls=%async_computation.1 | async-start | bytes 3538944 | tf_op jit(solution)/shard_map/all_gather | solution.py:262
  7.2 10.6 %collective-permute-start = (bf16[32,1536]{1,0:T(8,128)(2,1)}, bf16[32,1536]{1,0:T(8,128)(2,1)S(1)}, u32[]{:S(2)}, u32[]{:S(2)}) collective-permute-start(bf16[32,1536]{1,0:T(8,128)(2,1)} %refs_0_.1), channel_id=1, source_target_pairs={{4,0},{8,4},{12,8},{0,12},{5,1},{9,5},{13,9},{1,13},{6,2},{10,6},{... | collective-permute-start | bytes 294920 | tf_op jit(solution)/shard_map/ppermute | solution.py:24
  10.3 7.5 %collective-permute-start.1 = (bf16[32,1536]{1,0:T(8,128)(2,1)}, bf16[32,1536]{1,0:T(8,128)(2,1)S(1)}, u32[]{:S(2)}, u32[]{:S(2)}) collective-permute-start(bf16[32,1536]{1,0:T(8,128)(2,1)} %refs_0_.1), channel_id=1, source_target_pairs={{8,0},{12,4},{0,8},{4,12},{9,1},{13,5},{1,9},{5,13},{10,2},{14,6},... | collective-permute-start | bytes 294920 | tf_op jit(solution)/shard_map/ppermute | solution.py:24
  10.9 7.4 %collective-permute-start.2 = (bf16[32,1536]{1,0:T(8,128)(2,1)}, bf16[32,1536]{1,0:T(8,128)(2,1)S(1)}, u32[]{:S(2)}, u32[]{:S(2)}) collective-permute-start(bf16[32,1536]{1,0:T(8,128)(2,1)} %refs_0_.1), channel_id=1, source_target_pairs={{12,0},{0,4},{4,8},{8,12},{13,1},{1,5},{5,9},{9,13},{14,2},{2,6},{... | collective-permute-start | bytes 294920 | tf_op jit(solution)/shard_map/ppermute | solution.py:24
  11.9 8.4 %collective-permute-start.3 = (bf16[32,1536]{1,0:T(8,128)(2,1)}, bf16[32,1536]{1,0:T(8,128)(2,1)S(1)}, u32[]{:S(2)}, u32[]{:S(2)}) collective-permute-start(bf16[32,1536]{1,0:T(8,128)(2,1)} %refs_0_.2), channel_id=1, source_target_pairs={{16,0},{32,16},{48,32},{64,48},{80,64},{96,80},{112,96},{0,112},{1... | collective-permute-start | bytes 294920 | tf_op jit(solution)/shard_map/ppermute | solution.py:24
  17.8 6.0 %collective-permute-start.4 = (bf16[32,1536]{1,0:T(8,128)(2,1)}, bf16[32,1536]{1,0:T(8,128)(2,1)S(1)}, u32[]{:S(2)}, u32[]{:S(2)}) collective-permute-start(bf16[32,1536]{1,0:T(8,128)(2,1)} %refs_0_.2), channel_id=1, source_target_pairs={{112,0},{0,16},{16,32},{32,48},{48,64},{64,80},{80,96},{96,112},{1... | collective-permute-start | bytes 294920 | tf_op jit(solution)/shard_map/ppermute | solution.py:24
  25.5 26.5 %copy-start.17 = (bf16[256,512]{1,0:T(8,128)(2,1)S(1)}, bf16[256,512]{1,0:T(8,128)(2,1)}, u32[]{:S(2)}) copy-start(bf16[256,512]{1,0:T(8,128)(2,1)} %param.10) | copy-start | bytes 786436
  25.5 128.1 %reduce-scatter.2.cloned.1.call-start = ((), (), s32[]{:S(2)}) async-start(), calls=%async_computation.2 | async-start | bytes 3538944 | tf_op jit(solution)/shard_map/reduce_scatter | solution.py:293
  25.6 16.4 %collective-permute-start.5 = (bf16[256,512]{1,0:T(8,128)(2,1)}, bf16[256,512]{1,0:T(8,128)(2,1)S(1)}, u32[]{:S(2)}, u32[]{:S(2)}) collective-permute-start(bf16[256,512]{1,0:T(8,128)(2,1)} %param.9), channel_id=1, source_target_pairs={{0,2},{2,0},{1,3},{3,1},{4,6},{6,4},{5,7},{7,5},{8,10},{10,8},{9,1... | collective-permute-start | bytes 786440 | tf_op jit(solution)/shard_map/ppermute | solution.py:28
  27.8 5.6 %collective-permute-start.8 = (bf16[32,1536]{1,0:T(8,128)(2,1)S(1)}, bf16[32,1536]{1,0:T(8,128)(2,1)S(1)}, u32[]{:S(2)}, u32[]{:S(2)}) collective-permute-start(bf16[32,1536]{1,0:T(8,128)(2,1)S(1)} %collective-permute-done.3.refs_1_), channel_id=1, source_target_pairs={{16,0},{32,16},{48,32},{64,48},{80,64},{96,80},{112,96},{0,112},{1... | collective-permute-start | bytes 294920 | tf_op jit(solution)/shard_map/ppermute | solution.py:24
  28.2 7.2 %collective-permute-start.11 = (bf16[32,1536]{1,0:T(8,128)(2,1)S(1)}, bf16[32,1536]{1,0:T(8,128)(2,1)S(1)}, u32[]{:S(2)}, u32[]{:S(2)}) collective-permute-start(bf16[32,1536]{1,0:T(8,128)(2,1)S(1)} %collective-permute-done.4.refs_7_), channel_id=1, source_target_pairs={{112,0},{0,16},{16,32},{32,48},{48,64},{64,80},{80,96},{96,112},{1... | collective-permute-start | bytes 294920 | tf_op jit(solution)/shard_map/ppermute | solution.py:24
  33.4 7.7 %collective-permute-start.9 = (bf16[32,1536]{1,0:T(8,128)(2,1)S(1)}, bf16[32,1536]{1,0:T(8,128)(2,1)S(1)}, u32[]{:S(2)}, u32[]{:S(2)}) collective-permute-start(bf16[32,1536]{1,0:T(8,128)(2,1)S(1)} %collective-permute-done.8.refs_2_), channel_id=1, source_target_pairs={{16,0},{32,16},{48,32},{64,48},{80,64},{96,80},{112,96},{0,112},{1... | collective-permute-start | bytes 294920 | tf_op jit(solution)/shard_map/ppermute | solution.py:24
  34.0 17.9 %collective-permute-start.6 = (bf16[256,512]{1,0:T(8,128)(2,1)}, bf16[256,512]{1,0:T(8,128)(2,1)S(1)}, u32[]{:S(2)}, u32[]{:S(2)}) collective-permute-start(bf16[256,512]{1,0:T(8,128)(2,1)} %param.10), channel_id=1, source_target_pairs={{0,2},{2,0},{1,3},{3,1},{4,6},{6,4},{5,7},{7,5},{8,10},{10,8},{9,1... | collective-permute-start | bytes 786440 | tf_op jit(solution)/shard_map/ppermute | solution.py:28
  35.4 7.9 %collective-permute-start.12 = (bf16[32,1536]{1,0:T(8,128)(2,1)S(1)}, bf16[32,1536]{1,0:T(8,128)(2,1)S(1)}, u32[]{:S(2)}, u32[]{:S(2)}) collective-permute-start(bf16[32,1536]{1,0:T(8,128)(2,1)S(1)} %collective-permute-done.11.refs_6_), channel_id=1, source_target_pairs={{112,0},{0,16},{16,32},{32,48},{48,64},{64,80},{80,96},{96,112},{1... | collective-permute-start | bytes 294920 | tf_op jit(solution)/shard_map/ppermute | solution.py:24
  41.1 6.7 %collective-permute-start.10 = (bf16[32,1536]{1,0:T(8,128)(2,1)S(1)}, bf16[32,1536]{1,0:T(8,128)(2,1)S(1)}, u32[]{:S(2)}, u32[]{:S(2)}) collective-permute-start(bf16[32,1536]{1,0:T(8,128)(2,1)S(1)} %collective-permute-done.9.refs_3_), channel_id=1, source_target_pairs={{16,0},{32,16},{48,32},{64,48},{80,64},{96,80},{112,96},{0,112},{1... | collective-permute-start | bytes 294920 | tf_op jit(solution)/shard_map/ppermute | solution.py:24
  48.7 28.8 %copy-start = (bf16[8,32,1536]{2,1,0:T(8,128)(2,1)}, bf16[8,32,1536]{2,1,0:T(8,128)(2,1)S(1)}, u32[]{:S(2)}) copy-start(bf16[8,32,1536]{2,1,0:T(8,128)(2,1)S(1)} %shard_map.103) | copy-start | bytes 2359300
  48.7 13.6 %collective-permute-start.13 = (bf16[256,1536]{1,0:T(8,128)(2,1)S(1)}, bf16[256,1536]{1,0:T(8,128)(2,1)}, u32[]{:S(2)}, u32[]{:S(2)}) collective-permute-start(bf16[256,1536]{1,0:T(8,128)(2,1)S(1)} %bitcast.24), channel_id=1, source_target_pairs={{0,128},{128,0},{1,129},{129,1},{2,130},{130,2},{3,131},{131,3},{4... | collective-permute-start | bytes 2359304 | tf_op jit(solution)/shard_map/ppermute | solution.py:28
  49.8 13.8 %collective-permute-start.14 = (bf16[256,1536]{1,0:T(8,128)(2,1)S(1)}, bf16[256,1536]{1,0:T(8,128)(2,1)S(1)}, u32[]{:S(2)}, u32[]{:S(2)}) collective-permute-start(bf16[256,1536]{1,0:T(8,128)(2,1)S(1)} %bitcast.25), channel_id=1, source_target_pairs={{4,0},{8,4},{12,8},{0,12},{5,1},{9,5},{13,9},{1,13},{6,2},{10,6},{... | collective-permute-start | bytes 2359304 | tf_op jit(solution)/shard_map/ppermute | solution.py:24
  52.0 13.3 %collective-permute-start.15 = (bf16[256,1536]{1,0:T(8,128)(2,1)S(1)}, bf16[256,1536]{1,0:T(8,128)(2,1)}, u32[]{:S(2)}, u32[]{:S(2)}) collective-permute-start(bf16[256,1536]{1,0:T(8,128)(2,1)S(1)} %bitcast.26), channel_id=1, source_target_pairs={{12,0},{0,4},{4,8},{8,12},{13,1},{1,5},{5,9},{9,13},{14,2},{2,6},{... | collective-permute-start | bytes 2359304 | tf_op jit(solution)/shard_map/ppermute | solution.py:24
  52.0 17.0 %copy-start.1 = (bf16[512,1536]{1,0:T(8,128)(2,1)S(1)}, bf16[512,1536]{1,0:T(8,128)(2,1)}, u32[]{:S(2)}) copy-start(bf16[512,1536]{1,0:T(8,128)(2,1)} %w_down.1) | copy-start | bytes 4718596
  52.4 2.2 %collective-permute-start.7 = (bf16[2,256,512]{2,1,0:T(8,128)(2,1)S(1)}, bf16[2,256,512]{2,1,0:T(8,128)(2,1)S(1)}, u32[]{:S(2)}, u32[]{:S(2)}) collective-permute-start(bf16[2,256,512]{2,1,0:T(8,128)(2,1)S(1)} %fusion.12.hidden), channel_id=1, source_target_pairs={{0,1},{1,0},{2,3},{3,2},{4,5},{5,4},{6,7},{7,6},{8,9},{9,8},{10,11... | collective-permute-start | bytes 1572872 | tf_op jit(solution)/shard_map/ppermute | solution.py:28
  73.1 2.0 %collective-permute-start.16 = (bf16[2,256,512]{2,1,0:T(8,128)(2,1)S(1)}, bf16[2,256,512]{2,1,0:T(8,128)(2,1)S(1)}, u32[]{:S(2)}, u32[]{:S(2)}) collective-permute-start(bf16[2,256,512]{2,1,0:T(8,128)(2,1)S(1)} %get-tuple-element.52), channel_id=1, source_target_pairs={{0,1},{1,0},{2,3},{3,2},{4,5},{5,4},{6,7},{7,6},{8,9},{9,8},{10,11... | collective-permute-start | bytes 1572872 | tf_op jit(solution)/shard_map/ppermute | solution.py:28
  75.3 15.6 %copy-start.14 = (bf16[2,256,512]{2,1,0:T(8,128)(2,1)S(1)}, bf16[2,256,512]{2,1,0:T(8,128)(2,1)}, u32[]{:S(2)}) copy-start(bf16[2,256,512]{2,1,0:T(8,128)(2,1)} %get-tuple-element.60) | copy-start | bytes 1572868
  75.4 15.6 %copy-start.15 = (bf16[2,256,512]{2,1,0:T(8,128)(2,1)S(1)}, bf16[2,256,512]{2,1,0:T(8,128)(2,1)}, u32[]{:S(2)}) copy-start(bf16[2,256,512]{2,1,0:T(8,128)(2,1)} %get-tuple-element.59) | copy-start | bytes 1572868
  75.4 15.6 %collective-permute-start.17 = (bf16[2,256,512]{2,1,0:T(8,128)(2,1)S(1)}, bf16[2,256,512]{2,1,0:T(8,128)(2,1)S(1)}, u32[]{:S(2)}, u32[]{:S(2)}) collective-permute-start(bf16[2,256,512]{2,1,0:T(8,128)(2,1)S(1)} %get-tuple-element.84), channel_id=1, source_target_pairs={{0,2},{2,0},{1,3},{3,1},{4,6},{6,4},{5,7},{7,5},{8,10},{10,8},{9,1... | collective-permute-start | bytes 1572872 | tf_op jit(solution)/shard_map/ppermute | solution.py:28
  77.5 22.3 %collective-permute-start.20 = (bf16[256,1536]{1,0:T(8,128)(2,1)S(1)}, bf16[256,1536]{1,0:T(8,128)(2,1)}, u32[]{:S(2)}, u32[]{:S(2)}) collective-permute-start(bf16[256,1536]{1,0:T(8,128)(2,1)S(1)} %bitcast.27), channel_id=1, source_target_pairs={{8,0},{12,4},{0,8},{4,12},{9,1},{13,5},{1,9},{5,13},{10,2},{14,6},... | collective-permute-start | bytes 2359304 | tf_op jit(solution)/shard_map/ppermute | solution.py:24
  84.5 7.6 %copy-start.10 = (bf16[64,1536]{1,0:T(8,128)(2,1)}, bf16[64,1536]{1,0:T(8,128)(2,1)S(1)}, u32[]{:S(2)}) copy-start(bf16[64,1536]{1,0:T(8,128)(2,1)S(1)} %get-tuple-element.62.first) | copy-start | bytes 589828
  90.9 3.4 %copy-start.2 = (bf16[1536,512]{1,0:T(8,128)(2,1)S(1)}, bf16[1536,512]{1,0:T(8,128)(2,1)}, u32[]{:S(2)}) copy-start(bf16[1536,512]{1,0:T(8,128)(2,1)} %w_gate.1) | copy-start | bytes 4718596
  90.9 3.4 %copy-start.3 = (bf16[1536,512]{1,0:T(8,128)(2,1)S(1)}, bf16[1536,512]{1,0:T(8,128)(2,1)}, u32[]{:S(2)}) copy-start(bf16[1536,512]{1,0:T(8,128)(2,1)} %w_up.1) | copy-start | bytes 4718596
  91.6 2.0 %collective-permute-start.18 = (bf16[2,256,512]{2,1,0:T(8,128)(2,1)S(1)}, bf16[2,256,512]{2,1,0:T(8,128)(2,1)S(1)}, u32[]{:S(2)}, u32[]{:S(2)}) collective-permute-start(bf16[2,256,512]{2,1,0:T(8,128)(2,1)S(1)} %get-tuple-element.87.gg.refs_4_), channel_id=1, source_target_pairs={{0,1},{1,0},{2,3},{3,2},{4,5},{5,4},{6,7},{7,6},{8,9},{9,8},{10,11... | collective-permute-start | bytes 1572872 | tf_op jit(solution)/shard_map/ppermute | solution.py:28
  91.7 2.6 %collective-permute-start.19 = (bf16[2,256,512]{2,1,0:T(8,128)(2,1)S(1)}, bf16[2,256,512]{2,1,0:T(8,128)(2,1)S(1)}, u32[]{:S(2)}, u32[]{:S(2)}) collective-permute-start(bf16[2,256,512]{2,1,0:T(8,128)(2,1)S(1)} %get-tuple-element.86.gu.refs_6_), channel_id=1, source_target_pairs={{0,1},{1,0},{2,3},{3,2},{4,5},{5,4},{6,7},{7,6},{8,9},{9,8},{10,11... | collective-permute-start | bytes 1572872 | tf_op jit(solution)/shard_map/ppermute | solution.py:28
  92.2 7.7 %collective-permute-start.21 = (bf16[64,1536]{1,0:T(8,128)(2,1)S(1)}, bf16[64,1536]{1,0:T(8,128)(2,1)S(1)}, u32[]{:S(2)}, u32[]{:S(2)}) collective-permute-start(bf16[64,1536]{1,0:T(8,128)(2,1)S(1)} %get-tuple-element.62.first), channel_id=1, source_target_pairs={{0,128},{128,0},{1,129},{129,1},{2,130},{130,2},{3,131},{131,3},{4... | collective-permute-start | bytes 589832 | tf_op jit(solution)/shard_map/ppermute | solution.py:28
  100.5 36.3 %collective-permute-start.22 = (bf16[256,1536]{1,0:T(8,128)(2,1)}, bf16[256,1536]{1,0:T(8,128)(2,1)S(1)}, u32[]{:S(2)}, u32[]{:S(2)}) collective-permute-start(bf16[256,1536]{1,0:T(8,128)(2,1)} %collective-permute-done.13.refs_0_), channel_id=1, source_target_pairs={{4,0},{8,4},{12,8},{0,12},{5,1},{9,5},{13,9},{1,13},{6,2},{10,6},{... | collective-permute-start | bytes 2359304 | tf_op jit(solution)/shard_map/ppermute | solution.py:24
  102.5 14.8 %collective-permute-start.25 = (bf16[2,256,512]{2,1,0:T(8,128)(2,1)S(1)}, bf16[2,256,512]{2,1,0:T(8,128)(2,1)S(1)}, u32[]{:S(2)}, u32[]{:S(2)}) collective-permute-start(bf16[2,256,512]{2,1,0:T(8,128)(2,1)S(1)} %get-tuple-element.87.gg.refs_4_), channel_id=1, source_target_pairs={{0,128},{128,0},{1,129},{129,1},{2,130},{130,2},{3,131},{131,3},{4... | collective-permute-start | bytes 1572872 | tf_op jit(solution)/shard_map/ppermute | solution.py:28
  103.1 24.4 %collective-permute-start.26 = (bf16[2,256,512]{2,1,0:T(8,128)(2,1)S(1)}, bf16[2,256,512]{2,1,0:T(8,128)(2,1)}, u32[]{:S(2)}, u32[]{:S(2)}) collective-permute-start(bf16[2,256,512]{2,1,0:T(8,128)(2,1)S(1)} %get-tuple-element.86.gu.refs_6_), channel_id=1, source_target_pairs={{0,128},{128,0},{1,129},{129,1},{2,130},{130,2},{3,131},{131,3},{4... | collective-permute-start | bytes 1572872 | tf_op jit(solution)/shard_map/ppermute | solution.py:28
  104.5 33.2 %collective-permute-start.23 = (bf16[256,1536]{1,0:T(8,128)(2,1)}, bf16[256,1536]{1,0:T(8,128)(2,1)}, u32[]{:S(2)}, u32[]{:S(2)}) collective-permute-start(bf16[256,1536]{1,0:T(8,128)(2,1)} %collective-permute-done.13.refs_0_), channel_id=1, source_target_pairs={{8,0},{12,4},{0,8},{4,12},{9,1},{13,5},{1,9},{5,13},{10,2},{14,6},... | collective-permute-start | bytes 2359304 | tf_op jit(solution)/shard_map/ppermute | solution.py:24
  105.3 36.6 %collective-permute-start.24 = (bf16[256,1536]{1,0:T(8,128)(2,1)}, bf16[256,1536]{1,0:T(8,128)(2,1)}, u32[]{:S(2)}, u32[]{:S(2)}) collective-permute-start(bf16[256,1536]{1,0:T(8,128)(2,1)} %collective-permute-done.13.refs_0_), channel_id=1, source_target_pairs={{12,0},{0,4},{4,8},{8,12},{13,1},{1,5},{5,9},{9,13},{14,2},{2,6},{... | collective-permute-start | bytes 2359304 | tf_op jit(solution)/shard_map/ppermute | solution.py:24
  112.9 1.1 copy-start.4
  127.5 38.0 %collective-permute-start.32 = (bf16[448,1536]{1,0:T(8,128)(2,1)}, bf16[448,1536]{1,0:T(8,128)(2,1)S(1)}, u32[]{:S(2)}, u32[]{:S(2)}) collective-permute-start(bf16[448,1536]{1,0:T(8,128)(2,1)} %get-tuple-element.78.rest), channel_id=1, source_target_pairs={{0,128},{128,0},{1,129},{129,1},{2,130},{130,2},{3,131},{131,3},{4... | collective-permute-start | bytes 4128776 | tf_op jit(solution)/shard_map/ppermute | solution.py:28
  128.2 13.8 %collective-permute-start.27 = (bf16[2,256,512]{2,1,0:T(8,128)(2,1)S(1)}, bf16[2,256,512]{2,1,0:T(8,128)(2,1)S(1)}, u32[]{:S(2)}, u32[]{:S(2)}) collective-permute-start(bf16[2,256,512]{2,1,0:T(8,128)(2,1)S(1)} %collective-permute-done.25.refs_4_), channel_id=1, source_target_pairs={{0,1},{1,0},{2,3},{3,2},{4,5},{5,4},{6,7},{7,6},{8,9},{9,8},{10,11... | collective-permute-start | bytes 1572872 | tf_op jit(solution)/shard_map/ppermute | solution.py:28
  137.7 4.3 %collective-permute-start.28 = (bf16[2,256,512]{2,1,0:T(8,128)(2,1)}, bf16[2,256,512]{2,1,0:T(8,128)(2,1)S(1)}, u32[]{:S(2)}, u32[]{:S(2)}) collective-permute-start(bf16[2,256,512]{2,1,0:T(8,128)(2,1)} %collective-permute-done.26.refs_6_), channel_id=1, source_target_pairs={{0,1},{1,0},{2,3},{3,2},{4,5},{5,4},{6,7},{7,6},{8,9},{9,8},{10,11... | collective-permute-start | bytes 1572872 | tf_op jit(solution)/shard_map/ppermute | solution.py:28
  142.0 1.4 copy-start.5
  143.4 1.4 copy-start.7
  145.9 19.6 %copy-start.11 = (bf16[64,1536]{1,0:T(8,128)(2,1)S(1)}, bf16[64,1536]{1,0:T(8,128)(2,1)}, u32[]{:S(2)}) copy-start(bf16[64,1536]{1,0:T(8,128)(2,1)} %copy-done.10) | copy-start | bytes 589828
  145.9 19.6 %copy-start.13 = (bf16[64,1536]{1,0:T(8,128)(2,1)S(1)}, bf16[64,1536]{1,0:T(8,128)(2,1)}, u32[]{:S(2)}) copy-start(bf16[64,1536]{1,0:T(8,128)(2,1)} %copy-done.12) | copy-start | bytes 589828
  154.6 5.7 %collective-permute-start.31 = (bf16[32,1536]{1,0:T(8,128)(2,1)S(1)}, bf16[32,1536]{1,0:T(8,128)(2,1)S(1)}, u32[]{:S(2)}, u32[]{:S(2)}) collective-permute-start(bf16[32,1536]{1,0:T(8,128)(2,1)S(1)} %get-tuple-element.93), channel_id=1, source_target_pairs={{4,0},{8,4},{12,8},{0,12},{5,1},{9,5},{13,9},{1,13},{6,2},{10,6},{... | collective-permute-start | bytes 294920 | tf_op jit(solution)/shard_map/ppermute | solution.py:24
  156.1 7.1 %collective-permute-start.30 = (bf16[32,1536]{1,0:T(8,128)(2,1)S(1)}, bf16[32,1536]{1,0:T(8,128)(2,1)S(1)}, u32[]{:S(2)}, u32[]{:S(2)}) collective-permute-start(bf16[32,1536]{1,0:T(8,128)(2,1)S(1)} %get-tuple-element.94), channel_id=1, source_target_pairs={{8,0},{12,4},{0,8},{4,12},{9,1},{13,5},{1,9},{5,13},{10,2},{14,6},... | collective-permute-start | bytes 294920 | tf_op jit(solution)/shard_map/ppermute | solution.py:24
  156.1 7.8 %collective-permute-start.29 = (bf16[32,1536]{1,0:T(8,128)(2,1)S(1)}, bf16[32,1536]{1,0:T(8,128)(2,1)S(1)}, u32[]{:S(2)}, u32[]{:S(2)}) collective-permute-start(bf16[32,1536]{1,0:T(8,128)(2,1)S(1)} %get-tuple-element.92), channel_id=1, source_target_pairs={{12,0},{0,4},{4,8},{8,12},{13,1},{1,5},{5,9},{9,13},{14,2},{2,6},{... | collective-permute-start | bytes 294920 | tf_op jit(solution)/shard_map/ppermute | solution.py:24
  (5 other events, 4.7 us)
Sparse Core Ops, SparseCore 0:
  25.6 43.3 all-gather.1
  100.0 44.3 reduce-scatter.1

commit v6 on v5

--- a/solution.py
+++ b/solution.py
@@ -89,19 +89,40 @@
     )(place, in_hbm(go), w_down)
 
 
-def input_grad_kernel(place, gg, gg_other, gu, gu_other, w_gate, w_up, out):
-    def emit(gate_ref, up_ref, core):
-        gate_rows, up_rows = gate_ref[...].reshape(512, 512), up_ref[...].reshape(512, 512)
-        total = (dot(gate_rows, w_gate[...], 1, 1) + dot(up_rows, w_up[...], 1, 1)).astype(BF16)
-        for half in range(2):
+def act_kernel(chip, chip_far, gate, up, out0, out1):
+    def rows(i, carry):
+        lines = pl.ds(pl.multiple_of(i * 32, 32), 32)
+        for half, out in enumerate((out0, out1)):
+            grad_hidden = chip[half, lines, :] + chip_far[half, lines, :].astype(F32)
+            gate_val, up_val = gate[half, lines, :].astype(F32), up[half, lines, :].astype(F32)
+            sigma = jax.nn.sigmoid(gate_val)
+            out[0, lines, :] = (grad_hidden * up_val * sigma * (1.0 + gate_val * (1.0 - sigma))).astype(BF16)
+            out[1, lines, :] = (grad_hidden * gate_val * sigma).astype(BF16)
+        return carry
+
+    lax.fori_loop(0, 8, rows, 0)
+
+
+def act_grad(chip, chip_far, gate, up):
+    shape = jax.ShapeDtypeStruct((2, 256, 512), BF16)
+    return pl.pallas_call(
+        act_kernel,
+        out_shape=(shape, shape),
+        in_specs=[VMEM] * 4,
+        out_specs=(VMEM,) * 2,
+        compiler_params=grant(8),
+    )(chip, chip_far, gate, up)
+
+
+def input_grad_kernel(place, near0, near1, other0, other1, w_gate, w_up, out):
+    for refs, core in (((near0, near1), place[3]), ((other0, other1), 1 - place[3])):
+        for half, ref in enumerate(refs):
+            total = dot(ref[0], w_gate[...], 1, 1) + dot(ref[1], w_up[...], 1, 1)
             start = pl.multiple_of(512 * half + 256 * core, 256)
-            out[pl.ds(start, 256), :] = total[256 * half:256 * half + 256]
-
-    emit(gg, gu, place[3])
-    emit(gg_other, gu_other, 1 - place[3])
-
-
-def input_grad(place, gg, gg_other, gu, gu_other, w_gate, w_up):
+            out[pl.ds(start, 256), :] = total.astype(BF16)
+
+
+def input_grad(place, near, other, w_gate, w_up):
     weight = pl.BlockSpec((512, 512), lambda i: (i, 0))
     return pl.pallas_call(
         input_grad_kernel,
@@ -110,7 +131,7 @@
         in_specs=[SMEM] + [VMEM] * 4 + [weight] * 2,
         out_specs=pl.BlockSpec((1024, 512), lambda i: (0, i)),
         compiler_params=grant(16),
-    )(place, gg, gg_other, gu, gu_other, w_gate, w_up)
+    )(place, *near, *other, w_gate, w_up)
 
 
 def fill_natural(place, own, other, rows, col):
@@ -150,23 +171,22 @@
     )(place, hidden, hidden_other, in_hbm(go))
 
 
-def fill_rolled(place, own, other, rows, col):
-    for half in range(2):
-        for pair in range(2):
-            for y in range(NY):
-                k = (y - place[1] + NY) % NY
-                lines = pl.ds(pair * 128 + y * 32, 32)
-                z_own = 4 * half + 2 * place[3] + pair
-                rows[k, z_own, :, col:col + 512] = own[half, lines, :]
-                z_other = 4 * half + 2 * (1 - place[3]) + pair
-                rows[k, z_other, :, col:col + 512] = other[half, lines, :]
+def fill_rolled(place, near, other, rows):
+    for refs, core in ((near, place[3]), (other, 1 - place[3])):
+        for half, ref in enumerate(refs):
+            for pair in range(2):
+                z = 4 * half + 2 * core + pair
+                for y in range(NY):
+                    k = (y - place[1] + NY) % NY
+                    lines = slice(pair * 128 + y * 32, pair * 128 + y * 32 + 32)
+                    rows[k, z, :, :512] = ref[0, lines, :]
+                    rows[k, z, :, 512:] = ref[1, lines, :]
 
 
 def rolled_total(place, pieces, grads, rows):
     @pl.when(pl.program_id(0) == 0)
     def _():
-        fill_rolled(place, *grads[:2], rows, 0)
-        fill_rolled(place, *grads[2:], rows, 512)
+        fill_rolled(place, grads[:2], grads[2:], rows)
 
     total = jnp.zeros((256, 1024), F32)
     for k, piece in enumerate(pieces):
@@ -196,7 +216,7 @@
     return pl.pallas_call(
         own_kernel,
         grid=(6,),
-        out_shape=(WEIGHT, WEIGHT),
+        out_shape=(pltpu.HBM((1536, 512), BF16),) * 2,
         in_specs=[SMEM] + [every] * 4 + [VMEM] * 4,
         out_specs=(TILE, TILE),
         scratch_shapes=[ROLLED],
@@ -214,7 +234,7 @@
         out_specs=(TILE, TILE),
         scratch_shapes=[ROLLED],
         compiler_params=grant(16),
-    )(place, in_hbm(pieces[0]), *pieces[1:], *grads, own_gate, own_up)
+    )(place, *(in_hbm(x) for x in pieces), *grads, in_hbm(own_gate), in_hbm(own_up))
 
 
 def add_kernel(first, first_far, rest, rest_far, out):
@@ -282,34 +302,31 @@
     chip, chip_far, down_first, down_rest = lax.optimization_barrier((chip, chip_far, down_first, down_rest))
     first_far = swap(down_first, "dp")
 
-    grad_hidden = chip + chip_far.astype(F32)
-    gate_val, up_val = gate.astype(F32), up.astype(F32)
-    sigma = jax.nn.sigmoid(gate_val)
-    gg = (grad_hidden * up_val * sigma * (1.0 + gate_val * (1.0 - sigma))).astype(BF16)
-    gu = (grad_hidden * gate_val * sigma).astype(BF16)
-    gg_other, gu_other = swap(gg, "core"), swap(gu, "core")
-    partial_in = input_grad(place, gg, gg_other, gu, gu_other, w_gate, w_up)
+    near = act_grad(chip, chip_far, gate, up)
+    other = [swap(half, "core") for half in near]
+    partial_in = input_grad(place, near, other, w_gate, w_up)
     partial_in, own2, first_far = lax.optimization_barrier((partial_in, own2, first_far))
     in_z = lax.psum_scatter(partial_in, "z", scatter_dimension=0, tiled=True).reshape(NY, 32, 1536)
 
-    gg_far, gu_far = swap(gg, "dp"), swap(gu, "dp")
-    partner_pieces = [partner_z] + [from_ahead(partner_z, "y", NY, k) for k in (1, 2, 3)]
-    own_gate, own_up = own_weight_grads(place, (own_z, own1, own2, own3), (gg, gg_other, gu, gu_other))
-    gg_far, gu_far, down_rest, own_gate, own_up = lax.optimization_barrier(
-        (gg_far, gu_far, down_rest, own_gate, own_up)
+    far = [swap(near[0], "dp"), lax.ppermute(near[1], ("dp", "xh"), [(0, 3), (3, 0), (1, 2), (2, 1)])]
+    partner1, partner2, partner3 = (from_ahead(partner_z, "y", NY, k) for k in (1, 2, 3))
+    own_gate, own_up = own_weight_grads(place, (own_z, own1, own2, own3), (*near, *other))
+    far, down_rest, own_gate, own_up, partner1, partner3 = lax.optimization_barrier(
+        (far, down_rest, own_gate, own_up, partner1, partner3)
     )
     rest_far = swap(down_rest, "dp")
-    far = (gg_far, swap(gg_far, "core"), gu_far, swap(gu_far, "core"))
-    grad_gate, grad_up = partner_weight_grads(place, partner_pieces, far, own_gate, own_up)
-    in_z, grad_gate, grad_up = lax.optimization_barrier((in_z, grad_gate, grad_up))
+    far_other = [swap(half, "core") for half in far]
 
     y = place[1]
-    total = lax.dynamic_index_in_dim(in_z, y, 0, keepdims=False).astype(F32)
+    slabs = [lax.dynamic_index_in_dim(in_z, (y + k) % NY, 0, keepdims=False) for k in range(NY)]
+    partner = [partner_z, partner1, partner2, partner3]
+    slabs, partner, far, far_other = lax.optimization_barrier((slabs, partner, far, far_other))
+    total = slabs[0].astype(F32)
     for k in range(1, NY):
-        slab = lax.dynamic_index_in_dim(in_z, (y + k) % NY, 0, keepdims=False)
-        total = total + from_ahead(slab, "y", NY, NY - k).astype(F32)
+        total = total + from_ahead(slabs[k], "y", NY, NY - k).astype(F32)
     grad_input = total.astype(BF16)
-    grad_input, rest_far = lax.optimization_barrier((grad_input, rest_far))
+    grad_gate, grad_up = partner_weight_grads(place, partner, (*far, *far_other), own_gate, own_up)
+    grad_input, grad_gate, grad_up, rest_far = lax.optimization_barrier((grad_input, grad_gate, grad_up, rest_far))
     return grad_input, grad_gate, grad_up, add(down_first, first_far, down_rest, rest_far)
 
 

time: 177 us -> 172 us (0.972)
  local copies, waits for them, and re-layouts: 9.71 us -> 4.18 us
  other arithmetic: 4.96 us -> 2.42 us
  Pallas kernels: 35 us -> 37.2 us
    reduce_scatter x1, waiting for transfers between devices: 0.01 us -> 19.9 us  [body(): lax.psum_scatter(partial_in, 'z', scatter_dimension=0, tiled=True)]
    ppermute x14 -> x13, waiting for transfers between devices: 30.8 us -> 19.4 us  [swap(): return lax.ppermute(x, axis, [(0, 1), (1, 0)])]
    ppermute x19, waiting for transfers between devices: 40.4 us -> 31.2 us  [from_ahead(): return lax.ppermute(x, axis, [((d + k) % n, d) for d in range(n)])]
    unnamed x36 -> x24, local copies, waits for them, and re-layouts: 8.71 us -> 3.12 us
    ppermute x0 -> x1, starting transfers between devices: none -> 2.05 us  [body(): lax.ppermute(near[1], ('dp', 'xh'), [(0, 3), (3, 0), (1, 2), (2, 1)])]
    pallas_call x1 -> x2, Pallas kernels: 6.66 us -> 8.06 us  [the longest x1 7.5 us: own_weight_grads(): pl.pallas_call(own_kernel, grid=(6,), out_shape=(pltpu.HBM((1536, 512), B...]
    ppermute x14 -> x13, starting transfers between devices: 11 us -> 10 us  [swap(): return lax.ppermute(x, axis, [(0, 1), (1, 0)])]
  transfers between devices with their start and end apart: 35 -> 35, of which waited for: 23 -> 19; matrix products, arithmetic and copies ran while one was open for 3% -> 2% of each run, Pallas kernels for 15% -> 16%
where the time goes in v6:
time: 172 us; the launch traced here: 171 us
  waiting for transfers between devices  74.3 us (43%)
  starting transfers between devices  38.3 us (22%)
  Pallas kernels  37.2 us (22%)
  between operations  14.3 us (8%)
  local copies, waits for them, and re-layouts  4.18 us (2%)
  other arithmetic  2.42 us (1%)
    ppermute x19, waiting for transfers between devices, from_ahead(): return lax.ppermute(x, axis, [((d + k) % n, d) for d in range(n)])  31.2 us
    ppermute x19, starting transfers between devices, from_ahead(): return lax.ppermute(x, axis, [((d + k) % n, d) for d in range(n)])  26.2 us
    reduce_scatter x1, waiting for transfers between devices, body(): lax.psum_scatter(partial_in, 'z', scatter_dimension=0, tiled=True)  19.9 us
    ppermute x13, waiting for transfers between devices, swap(): return lax.ppermute(x, axis, [(0, 1), (1, 0)])  19.4 us
    ppermute x13, starting transfers between devices, swap(): return lax.ppermute(x, axis, [(0, 1), (1, 0)])  10 us
    pallas_call x1, Pallas kernels, partner_weight_grads(): pl.pallas_call(partner_kernel, grid=(6,), out_shape=(WEIGHT, WEIGHT), in_...  8.31 us
    pallas_call x1, Pallas kernels, own_weight_grads(): pl.pallas_call(own_kernel, grid=(6,), out_shape=(pltpu.HBM((1536, 512), B...  7.5 us
    pallas_call x1, Pallas kernels, input_grad(): pl.pallas_call(input_grad_kernel, grid=(3,), out_shape=jax.ShapeDtypeStru...  5.5 us
  transfers between devices with their start and end apart: 35, of which 19 were waited for; matrix products, arithmetic and copies ran while one was open for 2% of the time, Pallas kernels for 16%

profile of v6, /device:TPU:2, one launch (start us, length us, event | category | flops | bytes accessed | tf_op | source)
XLA Modules:
  0.0 170.7 jit_solution(11982989312584288948)
XLA Ops:
  7.2 3.1 %collective-permute-start = (bf16[32,1536]{1,0:T(8,128)(2,1)}, bf16[32,1536]{1,0:T(8,128)(2,1)S(1)}, u32[]{:S(2)}, u32[]{:S(2)}) collective-permute-start(bf16[32,1536]{1,0:T(8,128)(2,1)} %refs_0_.1), channel_id=1, source_target_pairs={{4,0},{8,4},{12,8},{0,12},{5,1},{9,5},{13,9},{1,13},{6,2},{10,6},{... | collective-permute-start | bytes 294920 | tf_op jit(solution)/shard_map/ppermute | solution.py:24
  10.9 1.0 collective-permute-start.2
  11.9 5.9 %collective-permute-start.3 = (bf16[32,1536]{1,0:T(8,128)(2,1)}, bf16[32,1536]{1,0:T(8,128)(2,1)S(1)}, u32[]{:S(2)}, u32[]{:S(2)}) collective-permute-start(bf16[32,1536]{1,0:T(8,128)(2,1)} %refs_0_.2), channel_id=1, source_target_pairs={{16,0},{32,16},{48,32},{64,48},{80,64},{96,80},{112,96},{0,112},{1... | collective-permute-start | bytes 294920 | tf_op jit(solution)/shard_map/ppermute | solution.py:24
  18.4 1.9 %collective-permute-done.3.refs_1_ = bf16[32,1536]{1,0:T(8,128)(2,1)S(1)} collective-permute-done((bf16[32,1536]{1,0:T(8,128)(2,1)}, bf16[32,1536]{1,0:T(8,128)(2,1)S(1)}, u32[]{:S(2)}, u32[]{:S(2)}) %collective-permute-start.3) | collective-permute-done | bytes 98336 | tf_op jit(solution)/shard_map/ppermute | solution.py:24
  20.3 3.5 %collective-permute-done.4.refs_7_ = bf16[32,1536]{1,0:T(8,128)(2,1)S(1)} collective-permute-done((bf16[32,1536]{1,0:T(8,128)(2,1)}, bf16[32,1536]{1,0:T(8,128)(2,1)S(1)}, u32[]{:S(2)}, u32[]{:S(2)}) %collective-permute-start.4) | collective-permute-done | bytes 98336 | tf_op jit(solution)/shard_map/ppermute | solution.py:24
  23.8 1.7 shard_map.102
  25.6 2.2 %collective-permute-start.5 = (bf16[256,512]{1,0:T(8,128)(2,1)}, bf16[256,512]{1,0:T(8,128)(2,1)S(1)}, u32[]{:S(2)}, u32[]{:S(2)}) collective-permute-start(bf16[256,512]{1,0:T(8,128)(2,1)} %param.9), channel_id=1, source_target_pairs={{0,2},{2,0},{1,3},{3,1},{4,6},{6,4},{5,7},{7,5},{8,10},{10,8},{9,1... | collective-permute-start | bytes 786440 | tf_op jit(solution)/shard_map/ppermute | solution.py:28
  28.2 1.6 collective-permute-start.11
  29.8 3.6 %collective-permute-done.8.refs_2_ = bf16[32,1536]{1,0:T(8,128)(2,1)S(1)} collective-permute-done((bf16[32,1536]{1,0:T(8,128)(2,1)S(1)}, bf16[32,1536]{1,0:T(8,128)(2,1)S(1)}, u32[]{:S(2)}, u32[]{:S(2)}) %collective-permute-start.8) | collective-permute-done | bytes 98336 | tf_op jit(solution)/shard_map/ppermute | solution.py:24
  34.0 1.4 collective-permute-start.6
  35.4 1.4 collective-permute-start.12
  36.8 4.2 %collective-permute-done.9.refs_3_ = bf16[32,1536]{1,0:T(8,128)(2,1)S(1)} collective-permute-done((bf16[32,1536]{1,0:T(8,128)(2,1)S(1)}, bf16[32,1536]{1,0:T(8,128)(2,1)S(1)}, u32[]{:S(2)}, u32[]{:S(2)}) %collective-permute-start.9) | collective-permute-done | bytes 98336 | tf_op jit(solution)/shard_map/ppermute | solution.py:24
  41.1 0.9 collective-permute-start.10
  42.0 1.0 select_bitcast_fusion.3
  43.4 4.4 %collective-permute-done.10.refs_4_ = bf16[32,1536]{1,0:T(8,128)(2,1)S(1)} collective-permute-done((bf16[32,1536]{1,0:T(8,128)(2,1)S(1)}, bf16[32,1536]{1,0:T(8,128)(2,1)S(1)}, u32[]{:S(2)}, u32[]{:S(2)}) %collective-permute-start.10) | collective-permute-done | bytes 98336 | tf_op jit(solution)/shard_map/ppermute | solution.py:24
  47.7 1.0 shard_map.103
  48.7 1.1 collective-permute-start.13
  49.8 2.2 %collective-permute-start.14 = (bf16[256,1536]{1,0:T(8,128)(2,1)S(1)}, bf16[256,1536]{1,0:T(8,128)(2,1)S(1)}, u32[]{:S(2)}, u32[]{:S(2)}) collective-permute-start(bf16[256,1536]{1,0:T(8,128)(2,1)S(1)} %bitcast.24), channel_id=1, source_target_pairs={{4,0},{8,4},{12,8},{0,12},{5,1},{9,5},{13,9},{1,13},{6,2},{10,6},{... | collective-permute-start | bytes 2359304 | tf_op jit(solution)/shard_map/ppermute | solution.py:24
  52.8 1.8 %collective-permute-done.7.hidden_other = bf16[2,256,512]{2,1,0:T(8,128)(2,1)S(1)} collective-permute-done((bf16[2,256,512]{2,1,0:T(8,128)(2,1)S(1)}, bf16[2,256,512]{2,1,0:T(8,128)(2,1)S(1)}, u32[]{:S(2)}, u32[]{:S(2)}) %collective-permute-start.7) | collective-permute-done | bytes 524320 | tf_op jit(solution)/shard_map/ppermute | solution.py:28
  54.5 7.8 %collective-permute-done.13.refs_0_ = bf16[256,1536]{1,0:T(8,128)(2,1)} collective-permute-done((bf16[256,1536]{1,0:T(8,128)(2,1)S(1)}, bf16[256,1536]{1,0:T(8,128)(2,1)}, u32[]{:S(2)}, u32[]{:S(2)}) %collective-permute-start.13) | collective-permute-done | bytes 786464 | tf_op jit(solution)/shard_map/ppermute | solution.py:28
  62.3 1.4 collective-permute-done.14.refs_1_
  63.7 0.9 copy-done.10
  64.5 0.7 collective-permute-done.15.refs_3_
  65.3 3.8 %all-gather.2.cloned.1.call-done.go = bf16[1024,1536]{1,0:T(8,128)(2,1)} async-done(((bf16[128,1536]{1,0:T(8,128)(2,1)}), bf16[1024,1536]{1,0:T(8,128)(2,1)}) %all-gather.2.cloned.1.call-update) | async-done | bytes 3145744 | tf_op jit(solution)/shard_map/all_gather | solution.py:282
  69.0 1.4 copy-done.1
  70.4 4.1 %shard_map.104 = (f32[2,256,512]{2,1,0:T(8,128)S(1)}, bf16[2,256,512]{2,1,0:T(8,128)(2,1)S(1)}) custom-call(s32[4]{0:T(128)S(1)} %pad_add_fusion.place, bf16[1024,1536]{1,0:T(8,128)(2,1)} %all-gather.2.cloned.1.call-done.go, bf16[512,1536]{1,0:T(8,128)(2,1)S(1)} %copy-done.1), custom_call_target="tpu_custom_call" | custom-call | tf_op jit(solution)/shard_map/pallas_call | solution.py:79
  74.6 1.9 %collective-permute-done.16 = bf16[2,256,512]{2,1,0:T(8,128)(2,1)S(1)} collective-permute-done((bf16[2,256,512]{2,1,0:T(8,128)(2,1)S(1)}, bf16[2,256,512]{2,1,0:T(8,128)(2,1)S(1)}, u32[]{:S(2)}, u32[]{:S(2)}) %collective-permute-start.16) | collective-permute-done | bytes 524320 | tf_op jit(solution)/shard_map/ppermute | solution.py:28
  76.7 2.2 %collective-permute-start.17 = (bf16[2,256,512]{2,1,0:T(8,128)(2,1)S(1)}, bf16[2,256,512]{2,1,0:T(8,128)(2,1)S(1)}, u32[]{:S(2)}, u32[]{:S(2)}) collective-permute-start(bf16[2,256,512]{2,1,0:T(8,128)(2,1)S(1)} %get-tuple-element.114), channel_id=1, source_target_pairs={{0,2},{2,0},{1,3},{3,1},{4,6},{6,4},{5,7},{7,5},{8,10},{10,8},{9,1... | collective-permute-start | bytes 1572872 | tf_op jit(solution)/shard_map/ppermute | solution.py:28
  78.9 2.0 %collective-permute-start.20 = (bf16[256,1536]{1,0:T(8,128)(2,1)S(1)}, bf16[256,1536]{1,0:T(8,128)(2,1)}, u32[]{:S(2)}, u32[]{:S(2)}) collective-permute-start(bf16[256,1536]{1,0:T(8,128)(2,1)S(1)} %bitcast.26), channel_id=1, source_target_pairs={{8,0},{12,4},{0,8},{4,12},{9,1},{13,5},{1,9},{5,13},{10,2},{14,6},... | collective-permute-start | bytes 2359304 | tf_op jit(solution)/shard_map/ppermute | solution.py:24
  80.9 5.1 %shard_map.105 = (bf16[64,1536]{1,0:T(8,128)(2,1)S(1)}, bf16[448,1536]{1,0:T(8,128)(2,1)}) custom-call(s32[4]{0:T(128)S(1)} %pad_add_fusion.place, bf16[2,256,512]{2,1,0:T(8,128)(2,1)S(1)} %fusion.4.hidden, bf16[2,256,512]{2,1,0:T(8,128)(2,1)S(1)} %collective-permute-done.7.hidden_other, bf16[1024,1536]{1,0:T(8,128)(2,1)} %all-gather.2.cloned.1.call-done.go), custom_call_target="tpu_custom_call" | custom-call | tf_op jit(solution)/shard_map/pallas_call | solution.py:157
  86.0 6.3 %collective-permute-done.17.chip_far = bf16[2,256,512]{2,1,0:T(8,128)(2,1)S(1)} collective-permute-done((bf16[2,256,512]{2,1,0:T(8,128)(2,1)S(1)}, bf16[2,256,512]{2,1,0:T(8,128)(2,1)S(1)}, u32[]{:S(2)}, u32[]{:S(2)}) %collective-permute-start.17) | collective-permute-done | bytes 524320 | tf_op jit(solution)/shard_map/ppermute | solution.py:28
  94.0 0.8 collective-permute-done.18.other0.refs_6_
  94.9 0.7 collective-permute-done.19.other1.refs_7_
  95.6 5.5 %shard_map.107 = bf16[1024,1536]{1,0:T(8,128)(2,1)} custom-call(s32[4]{0:T(128)S(1)} %pad_add_fusion.place, bf16[2,256,512]{2,1,0:T(8,128)(2,1)S(1)} %get-tuple-element.76.near0.refs_4_, bf16[2,256,512]{2,1,0:T(8,128)(2,1)S(1)} %get-tuple-element.77.near1.refs_5_, bf16[2,256,512]{2,1,0:T(8,128)(2,1)S(1)} %collective-permute-done.18.other0.refs_6_, ...), custom_call_target="tpu_custom_call" | custom-call | tf_op jit(solution)/shard_map/pallas_call | solution.py:127
  101.8 2.0 %collective-permute-start.24 = (bf16[256,1536]{1,0:T(8,128)(2,1)}, bf16[256,1536]{1,0:T(8,128)(2,1)S(1)}, u32[]{:S(2)}, u32[]{:S(2)}) collective-permute-start(bf16[256,1536]{1,0:T(8,128)(2,1)} %collective-permute-done.13.refs_0_), channel_id=1, source_target_pairs={{4,0},{8,4},{12,8},{0,12},{5,1},{9,5},{13,9},{1,13},{6,2},{10,6},{... | collective-permute-start | bytes 2359304 | tf_op jit(solution)/shard_map/ppermute | solution.py:24
  104.4 2.0 %collective-permute-start.23 = (bf16[2,256,512]{2,1,0:T(8,128)(2,1)S(1)}, bf16[2,256,512]{2,1,0:T(8,128)(2,1)}, u32[]{:S(2)}, u32[]{:S(2)}) collective-permute-start(bf16[2,256,512]{2,1,0:T(8,128)(2,1)S(1)} %get-tuple-element.77.near1.refs_5_), channel_id=1, source_target_pairs={{0,130},{130,0},{2,128},{128,2},{1,131},{131,1},{3,129},{129,3},{4... | collective-permute-start | bytes 1572872 | tf_op jit(solution)/shard_map/ppermute | solution.py:311
  106.5 7.5 %shard_map.108 = (bf16[1536,512]{1,0:T(8,128)(2,1)}, bf16[1536,512]{1,0:T(8,128)(2,1)}) custom-call(s32[4]{0:T(128)S(1)} %pad_add_fusion.place, bf16[256,1536]{1,0:T(8,128)(2,1)} %bitcast.27, bf16[256,1536]{1,0:T(8,128)(2,1)} %copy-done.10, bf16[256,1536]{1,0:T(8,128)(2,1)} %collective-permute-done.20.refs_2_, ...), custom_call_target="tpu_custom_call" | custom-call | tf_op jit(solution)/shard_map/pallas_call | solution.py:216
  114.0 7.6 %collective-permute-done.24.refs_1_ = bf16[256,1536]{1,0:T(8,128)(2,1)S(1)} collective-permute-done((bf16[256,1536]{1,0:T(8,128)(2,1)}, bf16[256,1536]{1,0:T(8,128)(2,1)S(1)}, u32[]{:S(2)}, u32[]{:S(2)}) %collective-permute-start.24) | collective-permute-done | bytes 786464 | tf_op jit(solution)/shard_map/ppermute | solution.py:24
  121.6 2.9 %collective-permute-done.25.refs_3_ = bf16[256,1536]{1,0:T(8,128)(2,1)S(1)} collective-permute-done((bf16[256,1536]{1,0:T(8,128)(2,1)}, bf16[256,1536]{1,0:T(8,128)(2,1)S(1)}, u32[]{:S(2)}, u32[]{:S(2)}) %collective-permute-start.25) | collective-permute-done | bytes 786464 | tf_op jit(solution)/shard_map/ppermute | solution.py:24
  124.5 0.7 collective-permute-start.32
  125.8 19.9 %reduce-scatter.2.cloned.1.call-done = bf16[128,1536]{1,0:T(8,128)(2,1)} async-done(((bf16[1024,1536]{1,0:T(8,128)(2,1)}), bf16[128,1536]{1,0:T(8,128)(2,1)}) %reduce-scatter.2.cloned.1.call-update) | async-done | bytes 393232 | tf_op jit(solution)/shard_map/reduce_scatter | solution.py:309
  145.7 1.1 dynamic-slice_bitcast_fusion
  146.8 2.6 %collective-permute-start.31 = (bf16[32,1536]{1,0:T(8,128)(2,1)S(1)}, bf16[32,1536]{1,0:T(8,128)(2,1)S(1)}, u32[]{:S(2)}, u32[]{:S(2)}) collective-permute-start(bf16[32,1536]{1,0:T(8,128)(2,1)S(1)} %get-tuple-element.95), channel_id=1, source_target_pairs={{4,0},{8,4},{12,8},{0,12},{5,1},{9,5},{13,9},{1,13},{6,2},{10,6},{... | collective-permute-start | bytes 294920 | tf_op jit(solution)/shard_map/ppermute | solution.py:24
  149.4 0.9 collective-permute-start.30
  150.3 1.0 collective-permute-start.29
  151.3 8.3 %shard_map.109 = (bf16[1536,512]{1,0:T(8,128)(2,1)}, bf16[1536,512]{1,0:T(8,128)(2,1)}) custom-call(s32[4]{0:T(128)S(1)} %pad_add_fusion.place, bf16[256,1536]{1,0:T(8,128)(2,1)} %collective-permute-done.13.refs_0_, bf16[256,1536]{1,0:T(8,128)(2,1)} %copy-done.8, bf16[256,1536]{1,0:T(8,128)(2,1)} %collective-permute-done.26.refs_2_, ...), custom_call_target="tpu_custom_call" | custom-call | tf_op jit(solution)/shard_map/pallas_call | solution.py:229
  159.7 0.7 add_convert_fusion
  160.4 3.5 %shard_map.110 = bf16[512,1536]{1,0:T(8,128)(2,1)} custom-call(bf16[64,1536]{1,0:T(8,128)(2,1)S(1)} %copy-done.5, bf16[64,1536]{1,0:T(8,128)(2,1)S(1)} %copy-done.7, bf16[448,1536]{1,0:T(8,128)(2,1)} %get-tuple-element.108.rest, bf16[448,1536]{1,0:T(8,128)(2,1)S(1)} %collective-permute-done.32.rest_far), custom_call_target="tpu_custom_call" | custom-call | tf_op jit(solution)/shard_map/pallas_call | solution.py:248
  (65 shorter events, 7.4 us)
Async XLA Ops:
  7.2 61.9 %all-gather.2.cloned.1.call-start = ((), (), s32[]{:S(2)}) async-start(), calls=%async_computation.1 | async-start | bytes 3538944 | tf_op jit(solution)/shard_map/all_gather | solution.py:282
  7.2 10.6 %collective-permute-start = (bf16[32,1536]{1,0:T(8,128)(2,1)}, bf16[32,1536]{1,0:T(8,128)(2,1)S(1)}, u32[]{:S(2)}, u32[]{:S(2)}) collective-permute-start(bf16[32,1536]{1,0:T(8,128)(2,1)} %refs_0_.1), channel_id=1, source_target_pairs={{4,0},{8,4},{12,8},{0,12},{5,1},{9,5},{13,9},{1,13},{6,2},{10,6},{... | collective-permute-start | bytes 294920 | tf_op jit(solution)/shard_map/ppermute | solution.py:24
  10.3 7.5 %collective-permute-start.1 = (bf16[32,1536]{1,0:T(8,128)(2,1)}, bf16[32,1536]{1,0:T(8,128)(2,1)S(1)}, u32[]{:S(2)}, u32[]{:S(2)}) collective-permute-start(bf16[32,1536]{1,0:T(8,128)(2,1)} %refs_0_.1), channel_id=1, source_target_pairs={{8,0},{12,4},{0,8},{4,12},{9,1},{13,5},{1,9},{5,13},{10,2},{14,6},... | collective-permute-start | bytes 294920 | tf_op jit(solution)/shard_map/ppermute | solution.py:24
  10.9 7.4 %collective-permute-start.2 = (bf16[32,1536]{1,0:T(8,128)(2,1)}, bf16[32,1536]{1,0:T(8,128)(2,1)S(1)}, u32[]{:S(2)}, u32[]{:S(2)}) collective-permute-start(bf16[32,1536]{1,0:T(8,128)(2,1)} %refs_0_.1), channel_id=1, source_target_pairs={{12,0},{0,4},{4,8},{8,12},{13,1},{1,5},{5,9},{9,13},{14,2},{2,6},{... | collective-permute-start | bytes 294920 | tf_op jit(solution)/shard_map/ppermute | solution.py:24
  11.9 8.4 %collective-permute-start.3 = (bf16[32,1536]{1,0:T(8,128)(2,1)}, bf16[32,1536]{1,0:T(8,128)(2,1)S(1)}, u32[]{:S(2)}, u32[]{:S(2)}) collective-permute-start(bf16[32,1536]{1,0:T(8,128)(2,1)} %refs_0_.2), channel_id=1, source_target_pairs={{16,0},{32,16},{48,32},{64,48},{80,64},{96,80},{112,96},{0,112},{1... | collective-permute-start | bytes 294920 | tf_op jit(solution)/shard_map/ppermute | solution.py:24
  17.8 6.0 %collective-permute-start.4 = (bf16[32,1536]{1,0:T(8,128)(2,1)}, bf16[32,1536]{1,0:T(8,128)(2,1)S(1)}, u32[]{:S(2)}, u32[]{:S(2)}) collective-permute-start(bf16[32,1536]{1,0:T(8,128)(2,1)} %refs_0_.2), channel_id=1, source_target_pairs={{112,0},{0,16},{16,32},{32,48},{48,64},{64,80},{80,96},{96,112},{1... | collective-permute-start | bytes 294920 | tf_op jit(solution)/shard_map/ppermute | solution.py:24
  25.5 26.5 %copy-start.11 = (bf16[256,512]{1,0:T(8,128)(2,1)S(1)}, bf16[256,512]{1,0:T(8,128)(2,1)}, u32[]{:S(2)}) copy-start(bf16[256,512]{1,0:T(8,128)(2,1)} %param.10) | copy-start | bytes 786436
  25.5 120.2 %reduce-scatter.2.cloned.1.call-start = ((), (), s32[]{:S(2)}) async-start(), calls=%async_computation.2 | async-start | bytes 3538944 | tf_op jit(solution)/shard_map/reduce_scatter | solution.py:309
  25.6 16.4 %collective-permute-start.5 = (bf16[256,512]{1,0:T(8,128)(2,1)}, bf16[256,512]{1,0:T(8,128)(2,1)S(1)}, u32[]{:S(2)}, u32[]{:S(2)}) collective-permute-start(bf16[256,512]{1,0:T(8,128)(2,1)} %param.9), channel_id=1, source_target_pairs={{0,2},{2,0},{1,3},{3,1},{4,6},{6,4},{5,7},{7,5},{8,10},{10,8},{9,1... | collective-permute-start | bytes 786440 | tf_op jit(solution)/shard_map/ppermute | solution.py:28
  27.8 5.6 %collective-permute-start.8 = (bf16[32,1536]{1,0:T(8,128)(2,1)S(1)}, bf16[32,1536]{1,0:T(8,128)(2,1)S(1)}, u32[]{:S(2)}, u32[]{:S(2)}) collective-permute-start(bf16[32,1536]{1,0:T(8,128)(2,1)S(1)} %collective-permute-done.3.refs_1_), channel_id=1, source_target_pairs={{16,0},{32,16},{48,32},{64,48},{80,64},{96,80},{112,96},{0,112},{1... | collective-permute-start | bytes 294920 | tf_op jit(solution)/shard_map/ppermute | solution.py:24
  28.2 7.2 %collective-permute-start.11 = (bf16[32,1536]{1,0:T(8,128)(2,1)S(1)}, bf16[32,1536]{1,0:T(8,128)(2,1)S(1)}, u32[]{:S(2)}, u32[]{:S(2)}) collective-permute-start(bf16[32,1536]{1,0:T(8,128)(2,1)S(1)} %collective-permute-done.4.refs_7_), channel_id=1, source_target_pairs={{112,0},{0,16},{16,32},{32,48},{48,64},{64,80},{80,96},{96,112},{1... | collective-permute-start | bytes 294920 | tf_op jit(solution)/shard_map/ppermute | solution.py:24
  33.4 7.7 %collective-permute-start.9 = (bf16[32,1536]{1,0:T(8,128)(2,1)S(1)}, bf16[32,1536]{1,0:T(8,128)(2,1)S(1)}, u32[]{:S(2)}, u32[]{:S(2)}) collective-permute-start(bf16[32,1536]{1,0:T(8,128)(2,1)S(1)} %collective-permute-done.8.refs_2_), channel_id=1, source_target_pairs={{16,0},{32,16},{48,32},{64,48},{80,64},{96,80},{112,96},{0,112},{1... | collective-permute-start | bytes 294920 | tf_op jit(solution)/shard_map/ppermute | solution.py:24
  34.0 17.9 %collective-permute-start.6 = (bf16[256,512]{1,0:T(8,128)(2,1)}, bf16[256,512]{1,0:T(8,128)(2,1)S(1)}, u32[]{:S(2)}, u32[]{:S(2)}) collective-permute-start(bf16[256,512]{1,0:T(8,128)(2,1)} %param.10), channel_id=1, source_target_pairs={{0,2},{2,0},{1,3},{3,1},{4,6},{6,4},{5,7},{7,5},{8,10},{10,8},{9,1... | collective-permute-start | bytes 786440 | tf_op jit(solution)/shard_map/ppermute | solution.py:28
  35.4 7.9 %collective-permute-start.12 = (bf16[32,1536]{1,0:T(8,128)(2,1)S(1)}, bf16[32,1536]{1,0:T(8,128)(2,1)S(1)}, u32[]{:S(2)}, u32[]{:S(2)}) collective-permute-start(bf16[32,1536]{1,0:T(8,128)(2,1)S(1)} %collective-permute-done.11.refs_6_), channel_id=1, source_target_pairs={{112,0},{0,16},{16,32},{32,48},{48,64},{64,80},{80,96},{96,112},{1... | collective-permute-start | bytes 294920 | tf_op jit(solution)/shard_map/ppermute | solution.py:24
  41.1 6.7 %collective-permute-start.10 = (bf16[32,1536]{1,0:T(8,128)(2,1)S(1)}, bf16[32,1536]{1,0:T(8,128)(2,1)S(1)}, u32[]{:S(2)}, u32[]{:S(2)}) collective-permute-start(bf16[32,1536]{1,0:T(8,128)(2,1)S(1)} %collective-permute-done.9.refs_3_), channel_id=1, source_target_pairs={{16,0},{32,16},{48,32},{64,48},{80,64},{96,80},{112,96},{0,112},{1... | collective-permute-start | bytes 294920 | tf_op jit(solution)/shard_map/ppermute | solution.py:24
  48.7 30.2 %copy-start = (bf16[8,32,1536]{2,1,0:T(8,128)(2,1)}, bf16[8,32,1536]{2,1,0:T(8,128)(2,1)S(1)}, u32[]{:S(2)}) copy-start(bf16[8,32,1536]{2,1,0:T(8,128)(2,1)S(1)} %shard_map.103) | copy-start | bytes 2359300
  48.7 13.6 %collective-permute-start.13 = (bf16[256,1536]{1,0:T(8,128)(2,1)S(1)}, bf16[256,1536]{1,0:T(8,128)(2,1)}, u32[]{:S(2)}, u32[]{:S(2)}) collective-permute-start(bf16[256,1536]{1,0:T(8,128)(2,1)S(1)} %bitcast.23), channel_id=1, source_target_pairs={{0,128},{128,0},{1,129},{129,1},{2,130},{130,2},{3,131},{131,3},{4... | collective-permute-start | bytes 2359304 | tf_op jit(solution)/shard_map/ppermute | solution.py:28
  49.8 13.8 %collective-permute-start.14 = (bf16[256,1536]{1,0:T(8,128)(2,1)S(1)}, bf16[256,1536]{1,0:T(8,128)(2,1)S(1)}, u32[]{:S(2)}, u32[]{:S(2)}) collective-permute-start(bf16[256,1536]{1,0:T(8,128)(2,1)S(1)} %bitcast.24), channel_id=1, source_target_pairs={{4,0},{8,4},{12,8},{0,12},{5,1},{9,5},{13,9},{1,13},{6,2},{10,6},{... | collective-permute-start | bytes 2359304 | tf_op jit(solution)/shard_map/ppermute | solution.py:24
  52.0 13.3 %collective-permute-start.15 = (bf16[256,1536]{1,0:T(8,128)(2,1)S(1)}, bf16[256,1536]{1,0:T(8,128)(2,1)}, u32[]{:S(2)}, u32[]{:S(2)}) collective-permute-start(bf16[256,1536]{1,0:T(8,128)(2,1)S(1)} %bitcast.25), channel_id=1, source_target_pairs={{12,0},{0,4},{4,8},{8,12},{13,1},{1,5},{5,9},{9,13},{14,2},{2,6},{... | collective-permute-start | bytes 2359304 | tf_op jit(solution)/shard_map/ppermute | solution.py:24
  52.4 2.2 %collective-permute-start.7 = (bf16[2,256,512]{2,1,0:T(8,128)(2,1)S(1)}, bf16[2,256,512]{2,1,0:T(8,128)(2,1)S(1)}, u32[]{:S(2)}, u32[]{:S(2)}) collective-permute-start(bf16[2,256,512]{2,1,0:T(8,128)(2,1)S(1)} %fusion.4.hidden), channel_id=1, source_target_pairs={{0,1},{1,0},{2,3},{3,2},{4,5},{5,4},{6,7},{7,6},{8,9},{9,8},{10,11... | collective-permute-start | bytes 1572872 | tf_op jit(solution)/shard_map/ppermute | solution.py:28
  63.7 0.9 copy-start.10
  69.0 1.4 copy-start.1
  74.5 2.0 %collective-permute-start.16 = (bf16[2,256,512]{2,1,0:T(8,128)(2,1)S(1)}, bf16[2,256,512]{2,1,0:T(8,128)(2,1)S(1)}, u32[]{:S(2)}, u32[]{:S(2)}) collective-permute-start(bf16[2,256,512]{2,1,0:T(8,128)(2,1)S(1)} %get-tuple-element.67), channel_id=1, source_target_pairs={{0,1},{1,0},{2,3},{3,2},{4,5},{5,4},{6,7},{7,6},{8,9},{9,8},{10,11... | collective-permute-start | bytes 1572872 | tf_op jit(solution)/shard_map/ppermute | solution.py:28
  76.7 15.6 %collective-permute-start.17 = (bf16[2,256,512]{2,1,0:T(8,128)(2,1)S(1)}, bf16[2,256,512]{2,1,0:T(8,128)(2,1)S(1)}, u32[]{:S(2)}, u32[]{:S(2)}) collective-permute-start(bf16[2,256,512]{2,1,0:T(8,128)(2,1)S(1)} %get-tuple-element.114), channel_id=1, source_target_pairs={{0,2},{2,0},{1,3},{3,1},{4,6},{6,4},{5,7},{7,5},{8,10},{10,8},{9,1... | collective-permute-start | bytes 1572872 | tf_op jit(solution)/shard_map/ppermute | solution.py:28
  78.9 22.2 %collective-permute-start.20 = (bf16[256,1536]{1,0:T(8,128)(2,1)S(1)}, bf16[256,1536]{1,0:T(8,128)(2,1)}, u32[]{:S(2)}, u32[]{:S(2)}) collective-permute-start(bf16[256,1536]{1,0:T(8,128)(2,1)S(1)} %bitcast.26), channel_id=1, source_target_pairs={{8,0},{12,4},{0,8},{4,12},{9,1},{13,5},{1,9},{5,13},{10,2},{14,6},... | collective-permute-start | bytes 2359304 | tf_op jit(solution)/shard_map/ppermute | solution.py:24
  80.9 14.8 %copy-start.3 = (bf16[1536,512]{1,0:T(8,128)(2,1)S(1)}, bf16[1536,512]{1,0:T(8,128)(2,1)}, u32[]{:S(2)}) copy-start(bf16[1536,512]{1,0:T(8,128)(2,1)} %w_up.1) | copy-start | bytes 4718596
  86.0 15.1 %copy-start.4 = (bf16[64,1536]{1,0:T(8,128)(2,1)}, bf16[64,1536]{1,0:T(8,128)(2,1)S(1)}, u32[]{:S(2)}) copy-start(bf16[64,1536]{1,0:T(8,128)(2,1)S(1)} %get-tuple-element.79.first) | copy-start | bytes 589828
  86.0 9.6 %copy-start.2 = (bf16[1536,512]{1,0:T(8,128)(2,1)S(1)}, bf16[1536,512]{1,0:T(8,128)(2,1)}, u32[]{:S(2)}) copy-start(bf16[1536,512]{1,0:T(8,128)(2,1)} %w_gate.1) | copy-start | bytes 4718596
  92.9 2.0 %collective-permute-start.18 = (bf16[2,256,512]{2,1,0:T(8,128)(2,1)S(1)}, bf16[2,256,512]{2,1,0:T(8,128)(2,1)S(1)}, u32[]{:S(2)}, u32[]{:S(2)}) collective-permute-start(bf16[2,256,512]{2,1,0:T(8,128)(2,1)S(1)} %get-tuple-element.76.near0.refs_4_), channel_id=1, source_target_pairs={{0,1},{1,0},{2,3},{3,2},{4,5},{5,4},{6,7},{7,6},{8,9},{9,8},{10,11... | collective-permute-start | bytes 1572872 | tf_op jit(solution)/shard_map/ppermute | solution.py:28
  93.0 2.6 %collective-permute-start.19 = (bf16[2,256,512]{2,1,0:T(8,128)(2,1)S(1)}, bf16[2,256,512]{2,1,0:T(8,128)(2,1)S(1)}, u32[]{:S(2)}, u32[]{:S(2)}) collective-permute-start(bf16[2,256,512]{2,1,0:T(8,128)(2,1)S(1)} %get-tuple-element.77.near1.refs_5_), channel_id=1, source_target_pairs={{0,1},{1,0},{2,3},{3,2},{4,5},{5,4},{6,7},{7,6},{8,9},{9,8},{10,11... | collective-permute-start | bytes 1572872 | tf_op jit(solution)/shard_map/ppermute | solution.py:28
  93.5 7.7 %collective-permute-start.21 = (bf16[64,1536]{1,0:T(8,128)(2,1)S(1)}, bf16[64,1536]{1,0:T(8,128)(2,1)S(1)}, u32[]{:S(2)}, u32[]{:S(2)}) collective-permute-start(bf16[64,1536]{1,0:T(8,128)(2,1)S(1)} %get-tuple-element.79.first), channel_id=1, source_target_pairs={{0,128},{128,0},{1,129},{129,1},{2,130},{130,2},{3,131},{131,3},{4... | collective-permute-start | bytes 589832 | tf_op jit(solution)/shard_map/ppermute | solution.py:28
  101.1 0.7 copy-start.6
  101.8 19.8 %collective-permute-start.24 = (bf16[256,1536]{1,0:T(8,128)(2,1)}, bf16[256,1536]{1,0:T(8,128)(2,1)S(1)}, u32[]{:S(2)}, u32[]{:S(2)}) collective-permute-start(bf16[256,1536]{1,0:T(8,128)(2,1)} %collective-permute-done.13.refs_0_), channel_id=1, source_target_pairs={{4,0},{8,4},{12,8},{0,12},{5,1},{9,5},{13,9},{1,13},{6,2},{10,6},{... | collective-permute-start | bytes 2359304 | tf_op jit(solution)/shard_map/ppermute | solution.py:24
  103.8 20.7 %collective-permute-start.25 = (bf16[256,1536]{1,0:T(8,128)(2,1)}, bf16[256,1536]{1,0:T(8,128)(2,1)S(1)}, u32[]{:S(2)}, u32[]{:S(2)}) collective-permute-start(bf16[256,1536]{1,0:T(8,128)(2,1)} %collective-permute-done.13.refs_0_), channel_id=1, source_target_pairs={{12,0},{0,4},{4,8},{8,12},{13,1},{1,5},{5,9},{9,13},{14,2},{2,6},{... | collective-permute-start | bytes 2359304 | tf_op jit(solution)/shard_map/ppermute | solution.py:24
  103.8 20.7 %collective-permute-start.22 = (bf16[2,256,512]{2,1,0:T(8,128)(2,1)S(1)}, bf16[2,256,512]{2,1,0:T(8,128)(2,1)S(1)}, u32[]{:S(2)}, u32[]{:S(2)}) collective-permute-start(bf16[2,256,512]{2,1,0:T(8,128)(2,1)S(1)} %get-tuple-element.76.near0.refs_4_), channel_id=1, source_target_pairs={{0,128},{128,0},{1,129},{129,1},{2,130},{130,2},{3,131},{131,3},{4... | collective-permute-start | bytes 1572872 | tf_op jit(solution)/shard_map/ppermute | solution.py:28
  104.4 20.1 %collective-permute-start.23 = (bf16[2,256,512]{2,1,0:T(8,128)(2,1)S(1)}, bf16[2,256,512]{2,1,0:T(8,128)(2,1)}, u32[]{:S(2)}, u32[]{:S(2)}) collective-permute-start(bf16[2,256,512]{2,1,0:T(8,128)(2,1)S(1)} %get-tuple-element.77.near1.refs_5_), channel_id=1, source_target_pairs={{0,130},{130,0},{2,128},{128,2},{1,131},{131,1},{3,129},{129,3},{4... | collective-permute-start | bytes 1572872 | tf_op jit(solution)/shard_map/ppermute | solution.py:311
  121.6 3.7 %copy-start.8 = (bf16[256,1536]{1,0:T(8,128)(2,1)}, bf16[256,1536]{1,0:T(8,128)(2,1)S(1)}, u32[]{:S(2)}) copy-start(bf16[256,1536]{1,0:T(8,128)(2,1)S(1)} %collective-permute-done.24.refs_1_) | copy-start | bytes 2359300
  124.5 0.9 copy-start.9
  124.5 35.8 %collective-permute-start.32 = (bf16[448,1536]{1,0:T(8,128)(2,1)}, bf16[448,1536]{1,0:T(8,128)(2,1)S(1)}, u32[]{:S(2)}, u32[]{:S(2)}) collective-permute-start(bf16[448,1536]{1,0:T(8,128)(2,1)} %get-tuple-element.108.rest), channel_id=1, source_target_pairs={{0,128},{128,0},{1,129},{129,1},{2,130},{130,2},{3,131},{131,3},{4... | collective-permute-start | bytes 4128776 | tf_op jit(solution)/shard_map/ppermute | solution.py:28
  125.2 21.5 %collective-permute-start.26 = (bf16[256,1536]{1,0:T(8,128)(2,1)}, bf16[256,1536]{1,0:T(8,128)(2,1)}, u32[]{:S(2)}, u32[]{:S(2)}) collective-permute-start(bf16[256,1536]{1,0:T(8,128)(2,1)} %collective-permute-done.13.refs_0_), channel_id=1, source_target_pairs={{8,0},{12,4},{0,8},{4,12},{9,1},{13,5},{1,9},{5,13},{10,2},{14,6},... | collective-permute-start | bytes 2359304 | tf_op jit(solution)/shard_map/ppermute | solution.py:24
  125.3 21.5 %collective-permute-start.27 = (bf16[2,256,512]{2,1,0:T(8,128)(2,1)S(1)}, bf16[2,256,512]{2,1,0:T(8,128)(2,1)S(1)}, u32[]{:S(2)}, u32[]{:S(2)}) collective-permute-start(bf16[2,256,512]{2,1,0:T(8,128)(2,1)S(1)} %collective-permute-done.22.refs_4_), channel_id=1, source_target_pairs={{0,1},{1,0},{2,3},{3,2},{4,5},{5,4},{6,7},{7,6},{8,9},{9,8},{10,11... | collective-permute-start | bytes 1572872 | tf_op jit(solution)/shard_map/ppermute | solution.py:28
  125.4 21.4 %collective-permute-start.28 = (bf16[2,256,512]{2,1,0:T(8,128)(2,1)}, bf16[2,256,512]{2,1,0:T(8,128)(2,1)S(1)}, u32[]{:S(2)}, u32[]{:S(2)}) collective-permute-start(bf16[2,256,512]{2,1,0:T(8,128)(2,1)} %collective-permute-done.23.refs_5_), channel_id=1, source_target_pairs={{0,1},{1,0},{2,3},{3,2},{4,5},{5,4},{6,7},{7,6},{8,9},{9,8},{10,11... | collective-permute-start | bytes 1572872 | tf_op jit(solution)/shard_map/ppermute | solution.py:28
  146.8 13.6 %copy-start.5 = (bf16[64,1536]{1,0:T(8,128)(2,1)S(1)}, bf16[64,1536]{1,0:T(8,128)(2,1)}, u32[]{:S(2)}) copy-start(bf16[64,1536]{1,0:T(8,128)(2,1)} %copy-done.4) | copy-start | bytes 589828
  146.8 13.6 %copy-start.7 = (bf16[64,1536]{1,0:T(8,128)(2,1)S(1)}, bf16[64,1536]{1,0:T(8,128)(2,1)}, u32[]{:S(2)}) copy-start(bf16[64,1536]{1,0:T(8,128)(2,1)} %copy-done.6) | copy-start | bytes 589828
  146.8 12.8 %collective-permute-start.31 = (bf16[32,1536]{1,0:T(8,128)(2,1)S(1)}, bf16[32,1536]{1,0:T(8,128)(2,1)S(1)}, u32[]{:S(2)}, u32[]{:S(2)}) collective-permute-start(bf16[32,1536]{1,0:T(8,128)(2,1)S(1)} %get-tuple-element.95), channel_id=1, source_target_pairs={{4,0},{8,4},{12,8},{0,12},{5,1},{9,5},{13,9},{1,13},{6,2},{10,6},{... | collective-permute-start | bytes 294920 | tf_op jit(solution)/shard_map/ppermute | solution.py:24
  149.4 10.2 %collective-permute-start.30 = (bf16[32,1536]{1,0:T(8,128)(2,1)S(1)}, bf16[32,1536]{1,0:T(8,128)(2,1)S(1)}, u32[]{:S(2)}, u32[]{:S(2)}) collective-permute-start(bf16[32,1536]{1,0:T(8,128)(2,1)S(1)} %get-tuple-element.94), channel_id=1, source_target_pairs={{8,0},{12,4},{0,8},{4,12},{9,1},{13,5},{1,9},{5,13},{10,2},{14,6},... | collective-permute-start | bytes 294920 | tf_op jit(solution)/shard_map/ppermute | solution.py:24
  150.3 9.3 %collective-permute-start.29 = (bf16[32,1536]{1,0:T(8,128)(2,1)S(1)}, bf16[32,1536]{1,0:T(8,128)(2,1)S(1)}, u32[]{:S(2)}, u32[]{:S(2)}) collective-permute-start(bf16[32,1536]{1,0:T(8,128)(2,1)S(1)} %get-tuple-element.93), channel_id=1, source_target_pairs={{12,0},{0,4},{4,8},{8,12},{13,1},{1,5},{5,9},{9,13},{14,2},{2,6},{... | collective-permute-start | bytes 294920 | tf_op jit(solution)/shard_map/ppermute | solution.py:24
Sparse Core Ops, SparseCore 0:
  25.6 43.3 all-gather.1
  101.3 44.3 reduce-scatter.1

commit v7 on v6

--- a/solution.py
+++ b/solution.py
@@ -53,40 +53,33 @@
     return out.reshape(n * rows, cols)
 
 
-def hidden_grad_kernel(place, go, w_down, mine, send, rows, sems):
-    copies = [
-        pltpu.make_async_copy(go.at[pl.ds(512 * half, 512)], rows.at[half], sems.at[half])
-        for half in range(2)
-    ]
+def hidden_grad_kernel(far, place, go, w_down, out, rows, weight, sems):
+    core = 1 - place[3] if far else place[3]
+    copies = [pltpu.make_async_copy(w_down, weight, sems.at[2])]
+    for half in range(2):
+        start = pl.multiple_of(512 * half + 256 * core, 256)
+        copies.append(pltpu.make_async_copy(go.at[pl.ds(start, 256)], rows.at[half], sems.at[half]))
     for copy in copies:
         copy.start()
-    for half, copy in enumerate(copies):
-        copy.wait()
-        part = dot(rows[half], w_down[...], 1, 1)
-        for which in range(2):
-            block = part[256 * which:256 * which + 256]
-
-            @pl.when(place[3] == which)
-            def _():
-                mine[half] = block
-
-            @pl.when(place[3] != which)
-            def _():
-                send[half] = block.astype(BF16)
-
-
-def hidden_grad(place, go, w_down):
-    return pl.pallas_call(
-        hidden_grad_kernel,
-        out_shape=(
-            jax.ShapeDtypeStruct((2, 256, 512), F32),
-            jax.ShapeDtypeStruct((2, 256, 512), BF16),
-        ),
-        in_specs=[SMEM, HBM, VMEM],
-        out_specs=(VMEM,) * 2,
-        scratch_shapes=[pltpu.VMEM((2, 512, 1536), BF16), pltpu.SemaphoreType.DMA((2,))],
-        compiler_params=grant(16),
-    )(place, in_hbm(go), w_down)
+    copies[0].wait()
+    for half in range(2):
+        copies[1 + half].wait()
+        out[half] = dot(rows[half], weight[...], 1, 1).astype(out.dtype)
+
+
+def hidden_grad(place, go, w_down, far):
+    return pl.pallas_call(
+        functools.partial(hidden_grad_kernel, far),
+        out_shape=jax.ShapeDtypeStruct((2, 256, 512), BF16 if far else F32),
+        in_specs=[SMEM, HBM, HBM],
+        out_specs=VMEM,
+        scratch_shapes=[
+            pltpu.VMEM((2, 256, 1536), BF16),
+            pltpu.VMEM((512, 1536), BF16),
+            pltpu.SemaphoreType.DMA((3,)),
+        ],
+        compiler_params=grant(12),
+    )(place, in_hbm(go), in_hbm(w_down))
 
 
 def act_kernel(chip, chip_far, gate, up, out0, out1):
@@ -114,12 +107,31 @@
     )(chip, chip_far, gate, up)
 
 
-def input_grad_kernel(place, near0, near1, other0, other1, w_gate, w_up, out):
-    for refs, core in (((near0, near1), place[3]), ((other0, other1), 1 - place[3])):
-        for half, ref in enumerate(refs):
-            total = dot(ref[0], w_gate[...], 1, 1) + dot(ref[1], w_up[...], 1, 1)
-            start = pl.multiple_of(512 * half + 256 * core, 256)
-            out[pl.ds(start, 256), :] = total.astype(BF16)
+def near_input_kernel(near0, near1, w_gate, w_up, out):
+    for half, ref in enumerate((near0, near1)):
+        total = dot(ref[0], w_gate[...], 1, 1) + dot(ref[1], w_up[...], 1, 1)
+        out[256 * half:256 * half + 256, :] = total.astype(BF16)
+
+
+def near_input_grad(near, w_gate, w_up):
+    weight = pl.BlockSpec((512, 512), lambda i: (i, 0))
+    return pl.pallas_call(
+        near_input_kernel,
+        grid=(3,),
+        out_shape=jax.ShapeDtypeStruct((512, 1536), BF16),
+        in_specs=[VMEM] * 2 + [weight] * 2,
+        out_specs=pl.BlockSpec((512, 512), lambda i: (0, i)),
+        compiler_params=grant(12),
+    )(*near, w_gate, w_up)
+
+
+def input_grad_kernel(place, near, other0, other1, w_gate, w_up, out):
+    for half, ref in enumerate((other0, other1)):
+        start = pl.multiple_of(512 * half + 256 * place[3], 256)
+        out[pl.ds(start, 256), :] = near[256 * half:256 * half + 256, :]
+        total = dot(ref[0], w_gate[...], 1, 1) + dot(ref[1], w_up[...], 1, 1)
+        start = pl.multiple_of(512 * half + 256 * (1 - place[3]), 256)
+        out[pl.ds(start, 256), :] = total.astype(BF16)
 
 
 def input_grad(place, near, other, w_gate, w_up):
@@ -128,10 +140,10 @@
         input_grad_kernel,
         grid=(3,),
         out_shape=jax.ShapeDtypeStruct((1024, 1536), BF16),
-        in_specs=[SMEM] + [VMEM] * 4 + [weight] * 2,
+        in_specs=[SMEM, pl.BlockSpec((512, 512), lambda i: (0, i))] + [VMEM] * 2 + [weight] * 2,
         out_specs=pl.BlockSpec((1024, 512), lambda i: (0, i)),
-        compiler_params=grant(16),
-    )(place, *near, *other, w_gate, w_up)
+        compiler_params=grant(14),
+    )(place, near, *other, w_gate, w_up)
 
 
 def fill_natural(place, own, other, rows, col):
@@ -171,86 +183,68 @@
     )(place, hidden, hidden_other, in_hbm(go))
 
 
-def fill_rolled(place, near, other, rows):
-    for refs, core in ((near, place[3]), (other, 1 - place[3])):
-        for half, ref in enumerate(refs):
-            for pair in range(2):
-                z = 4 * half + 2 * core + pair
-                for y in range(NY):
-                    k = (y - place[1] + NY) % NY
-                    lines = slice(pair * 128 + y * 32, pair * 128 + y * 32 + 32)
-                    rows[k, z, :, :512] = ref[0, lines, :]
-                    rows[k, z, :, 512:] = ref[1, lines, :]
-
-
-def rolled_total(place, pieces, grads, rows):
+def weight_kernel(slots, based, place, *refs):
+    count = len(slots)
+    pieces, grads, base = refs[:count], refs[count:count + 4], refs[count + 4:-3]
+    d_gate, d_up, rows = refs[-3:]
+
     @pl.when(pl.program_id(0) == 0)
     def _():
-        fill_rolled(place, grads[:2], grads[2:], rows)
+        for half in range(4):
+            core = place[3] if half < 2 else 1 - place[3]
+            for pair in range(2):
+                z = 4 * (half % 2) + 2 * core + pair
+                for index, k in enumerate(slots):
+                    start = pair * 128 + (place[1] + k) % NY * 32
+                    lines = pl.ds(pl.multiple_of(start, 32), 32)
+                    rows[index, z, :, :512] = grads[half][0, lines, :]
+                    rows[index, z, :, 512:] = grads[half][1, lines, :]
 
     total = jnp.zeros((256, 1024), F32)
-    for k, piece in enumerate(pieces):
-        total = total + dot(piece[...], rows[k].reshape(256, 1024), 0, 0)
-    return total.astype(BF16)
-
-
-def own_kernel(place, *refs):
-    total = rolled_total(place, refs[:4], refs[4:8], refs[10])
-    refs[8][...] = total[:, :512]
-    refs[9][...] = total[:, 512:]
-
-
-def partner_kernel(place, *refs):
-    total = rolled_total(place, refs[:4], refs[4:8], refs[12]).astype(F32)
-    refs[10][...] = (total[:, :512] + refs[8][...].astype(F32)).astype(BF16)
-    refs[11][...] = (total[:, 512:] + refs[9][...].astype(F32)).astype(BF16)
-
-
-TILE = pl.BlockSpec((256, 512), lambda i: (i, 0))
-WEIGHT = jax.ShapeDtypeStruct((1536, 512), BF16)
-ROLLED = pltpu.VMEM((NY, NZ, 32, 1024), BF16)
-
-
-def own_weight_grads(place, pieces, grads):
-    every = pl.BlockSpec((256, 256), lambda i: (0, i))
-    return pl.pallas_call(
-        own_kernel,
+    for index, piece in enumerate(pieces):
+        total = total + dot(piece[...], rows[index].reshape(256, 1024), 0, 0)
+    gate, up = total[:, :512], total[:, 512:]
+    if based:
+        gate = gate + base[0][...].astype(F32)
+        up = up + base[1][...].astype(F32)
+    d_gate[...] = gate.astype(BF16)
+    d_up[...] = up.astype(BF16)
+
+
+def weight_grads(place, slots, pieces, grads, base=(), last=False):
+    piece = pl.BlockSpec((256, 256), lambda i: (0, i))
+    tile = pl.BlockSpec((256, 512), lambda i: (i, 0))
+    shape = jax.ShapeDtypeStruct((1536, 512), BF16) if last else pltpu.HBM((1536, 512), BF16)
+    return pl.pallas_call(
+        functools.partial(weight_kernel, slots, bool(base)),
         grid=(6,),
-        out_shape=(pltpu.HBM((1536, 512), BF16),) * 2,
-        in_specs=[SMEM] + [every] * 4 + [VMEM] * 4,
-        out_specs=(TILE, TILE),
-        scratch_shapes=[ROLLED],
+        out_shape=(shape, shape),
+        in_specs=[SMEM] + [piece] * len(slots) + [VMEM] * 4 + [tile] * len(base),
+        out_specs=(tile, tile),
+        scratch_shapes=[pltpu.VMEM((len(slots), NZ, 32, 1024), BF16)],
         compiler_params=grant(16),
-    )(place, *(in_hbm(x) for x in pieces), *grads)
-
-
-def partner_weight_grads(place, pieces, grads, own_gate, own_up):
-    every = pl.BlockSpec((256, 256), lambda i: (0, i))
-    return pl.pallas_call(
-        partner_kernel,
-        grid=(6,),
-        out_shape=(WEIGHT, WEIGHT),
-        in_specs=[SMEM] + [every] * 4 + [VMEM] * 4 + [TILE] * 2,
-        out_specs=(TILE, TILE),
-        scratch_shapes=[ROLLED],
-        compiler_params=grant(16),
-    )(place, *(in_hbm(x) for x in pieces), *grads, in_hbm(own_gate), in_hbm(own_up))
+    )(place, *(x if last else in_hbm(x) for x in pieces), *grads, *(in_hbm(x) for x in base))
 
 
 def add_kernel(first, first_far, rest, rest_far, out):
-    out[:FIRST] = (first[...].astype(F32) + first_far[...].astype(F32)).astype(BF16)
-    out[FIRST:] = (rest[...].astype(F32) + rest_far[...].astype(F32)).astype(BF16)
+    @pl.when(pl.program_id(0) == 0)
+    def _():
+        out[...] = (first[...].astype(F32) + first_far[...].astype(F32)).astype(BF16)
+
+    @pl.when(pl.program_id(0) > 0)
+    def _():
+        out[...] = (rest[...].astype(F32) + rest_far[...].astype(F32)).astype(BF16)
 
 
 def add(first, first_far, rest, rest_far):
-    top = pl.BlockSpec((FIRST, 512), lambda i: (0, i))
-    low = pl.BlockSpec((512 - FIRST, 512), lambda i: (0, i))
+    top = pl.BlockSpec((FIRST, 1536), lambda i: (0, 0))
+    low = pl.BlockSpec((FIRST, 1536), lambda i: (jnp.maximum(i - 1, 0), 0))
     return pl.pallas_call(
         add_kernel,
-        grid=(3,),
+        grid=(512 // FIRST,),
         out_shape=jax.ShapeDtypeStruct((512, 1536), BF16),
         in_specs=[top, top, low, low],
-        out_specs=pl.BlockSpec((512, 512), lambda i: (0, i)),
+        out_specs=pl.BlockSpec((FIRST, 1536), lambda i: (i, 0)),
         compiler_params=grant(8),
     )(first, first_far, rest, rest_far)
 
@@ -294,8 +288,8 @@
     )
 
     own2 = from_ahead(own_z, "y", NY, 2)
-    mine, send = hidden_grad(place, go, w_down)
-    chip = mine + swap(send, "core").astype(F32)
+    from_other = swap(hidden_grad(place, go, w_down, True), "core")
+    chip = hidden_grad(place, go, w_down, False) + from_other.astype(F32)
     chip_far = swap(chip.astype(BF16), "xh")
     down_first, down_rest = down_grad(place, hidden, hidden_other, go)
 
@@ -304,13 +298,13 @@
 
     near = act_grad(chip, chip_far, gate, up)
     other = [swap(half, "core") for half in near]
-    partial_in = input_grad(place, near, other, w_gate, w_up)
+    partial_in = input_grad(place, near_input_grad(near, w_gate, w_up), other, w_gate, w_up)
     partial_in, own2, first_far = lax.optimization_barrier((partial_in, own2, first_far))
     in_z = lax.psum_scatter(partial_in, "z", scatter_dimension=0, tiled=True).reshape(NY, 32, 1536)
 
     far = [swap(near[0], "dp"), lax.ppermute(near[1], ("dp", "xh"), [(0, 3), (3, 0), (1, 2), (2, 1)])]
     partner1, partner2, partner3 = (from_ahead(partner_z, "y", NY, k) for k in (1, 2, 3))
-    own_gate, own_up = own_weight_grads(place, (own_z, own1, own2, own3), (*near, *other))
+    own_gate, own_up = weight_grads(place, (0, 1, 2, 3), (own_z, own1, own2, own3), (*near, *other))
     far, down_rest, own_gate, own_up, partner1, partner3 = lax.optimization_barrier(
         (far, down_rest, own_gate, own_up, partner1, partner3)
     )
@@ -319,13 +313,14 @@
 
     y = place[1]
     slabs = [lax.dynamic_index_in_dim(in_z, (y + k) % NY, 0, keepdims=False) for k in range(NY)]
-    partner = [partner_z, partner1, partner2, partner3]
-    slabs, partner, far, far_other = lax.optimization_barrier((slabs, partner, far, far_other))
+    grads = (*far, *far_other)
+    most = weight_grads(place, (0, 1, 3), (partner_z, partner1, partner3), grads, (own_gate, own_up))
+    slabs, partner2, most = lax.optimization_barrier((slabs, partner2, most))
     total = slabs[0].astype(F32)
     for k in range(1, NY):
         total = total + from_ahead(slabs[k], "y", NY, NY - k).astype(F32)
     grad_input = total.astype(BF16)
-    grad_gate, grad_up = partner_weight_grads(place, partner, (*far, *far_other), own_gate, own_up)
+    grad_gate, grad_up = weight_grads(place, (2,), (partner2,), grads, most, True)
     grad_input, grad_gate, grad_up, rest_far = lax.optimization_barrier((grad_input, grad_gate, grad_up, rest_far))
     return grad_input, grad_gate, grad_up, add(down_first, first_far, down_rest, rest_far)
 

time: 172 us -> 171 us (level)
  Pallas kernels: 37.2 us -> 48.3 us
  waiting for transfers between devices: 74.3 us -> 63.3 us
    pallas_call x4 -> x7, Pallas kernels: 23.4 us -> 35.7 us  [the longest x3 20.5 us: weight_grads(): pl.pallas_call(functools.partial(weight_kernel, slots, bool(base)), grid=...]
    reduce_scatter x1, waiting for transfers between devices: 19.9 us -> 10.5 us  [body(): lax.psum_scatter(partial_in, 'z', scatter_dimension=0, tiled=True)]
    ppermute x13, starting transfers between devices: 10 us -> 11.8 us  [swap(): return lax.ppermute(x, axis, [(0, 1), (1, 0)])]
  transfers between devices with their start and end apart: 35 -> 35, of which waited for: 19 -> 18; matrix products, arithmetic and copies ran while one was open for 2% -> 2% of each run, Pallas kernels for 16% -> 22%
where the time goes in v7:
time: 171 us
  waiting for transfers between devices  63.3 us (37%)
  Pallas kernels  48.3 us (28%)
  starting transfers between devices  39.5 us (23%)
  between operations  14.3 us (8%)
  local copies, waits for them, and re-layouts  2.69 us (2%)
  other arithmetic  2.45 us (1%)
    ppermute x19, waiting for transfers between devices, from_ahead(): return lax.ppermute(x, axis, [((d + k) % n, d) for d in range(n)])  30.6 us
    ppermute x19, starting transfers between devices, from_ahead(): return lax.ppermute(x, axis, [((d + k) % n, d) for d in range(n)])  26.2 us
    pallas_call x3, Pallas kernels, weight_grads(): pl.pallas_call(functools.partial(weight_kernel, slots, bool(base)), grid=...  20.5 us
    ppermute x13, waiting for transfers between devices, swap(): return lax.ppermute(x, axis, [(0, 1), (1, 0)])  18.3 us
    ppermute x13, starting transfers between devices, swap(): return lax.ppermute(x, axis, [(0, 1), (1, 0)])  11.8 us
    reduce_scatter x1, waiting for transfers between devices, body(): lax.psum_scatter(partial_in, 'z', scatter_dimension=0, tiled=True)  10.5 us
    pallas_call x2, Pallas kernels, hidden_grad(): pl.pallas_call(functools.partial(hidden_grad_kernel, far), out_shape=jax....  6.76 us
    pallas_call x1, Pallas kernels, add(): pl.pallas_call(add_kernel, grid=(512 // FIRST,), out_shape=jax.ShapeDtype...  6.09 us
  transfers between devices with their start and end apart: 35, of which 18 were waited for; matrix products, arithmetic and copies ran while one was open for 2% of the time, Pallas kernels for 22%

profile of v7, /device:TPU:2, one launch (start us, length us, event | category | flops | bytes accessed | tf_op | source)
XLA Modules:
  0.0 170.5 jit_solution(18412855832610680259)
XLA Ops:
  7.2 3.1 %collective-permute-start = (bf16[32,1536]{1,0:T(8,128)(2,1)}, bf16[32,1536]{1,0:T(8,128)(2,1)S(1)}, u32[]{:S(2)}, u32[]{:S(2)}) collective-permute-start(bf16[32,1536]{1,0:T(8,128)(2,1)} %refs_0_.1), channel_id=1, source_target_pairs={{4,0},{8,4},{12,8},{0,12},{5,1},{9,5},{13,9},{1,13},{6,2},{10,6},{... | collective-permute-start | bytes 294920 | tf_op jit(solution)/shard_map/ppermute | solution.py:24
  10.9 1.0 collective-permute-start.2
  11.9 5.9 %collective-permute-start.3 = (bf16[32,1536]{1,0:T(8,128)(2,1)}, bf16[32,1536]{1,0:T(8,128)(2,1)S(1)}, u32[]{:S(2)}, u32[]{:S(2)}) collective-permute-start(bf16[32,1536]{1,0:T(8,128)(2,1)} %refs_0_.2), channel_id=1, source_target_pairs={{16,0},{32,16},{48,32},{64,48},{80,64},{96,80},{112,96},{0,112},{1... | collective-permute-start | bytes 294920 | tf_op jit(solution)/shard_map/ppermute | solution.py:24
  18.4 1.9 %collective-permute-done.3.refs_1_ = bf16[32,1536]{1,0:T(8,128)(2,1)S(1)} collective-permute-done((bf16[32,1536]{1,0:T(8,128)(2,1)}, bf16[32,1536]{1,0:T(8,128)(2,1)S(1)}, u32[]{:S(2)}, u32[]{:S(2)}) %collective-permute-start.3) | collective-permute-done | bytes 98336 | tf_op jit(solution)/shard_map/ppermute | solution.py:24
  20.3 3.5 %collective-permute-done.4.refs_7_ = bf16[32,1536]{1,0:T(8,128)(2,1)S(1)} collective-permute-done((bf16[32,1536]{1,0:T(8,128)(2,1)}, bf16[32,1536]{1,0:T(8,128)(2,1)S(1)}, u32[]{:S(2)}, u32[]{:S(2)}) %collective-permute-start.4) | collective-permute-done | bytes 98336 | tf_op jit(solution)/shard_map/ppermute | solution.py:24
  23.8 1.7 shard_map.102
  25.6 2.2 %collective-permute-start.5 = (bf16[256,512]{1,0:T(8,128)(2,1)}, bf16[256,512]{1,0:T(8,128)(2,1)S(1)}, u32[]{:S(2)}, u32[]{:S(2)}) collective-permute-start(bf16[256,512]{1,0:T(8,128)(2,1)} %param.9), channel_id=1, source_target_pairs={{0,2},{2,0},{1,3},{3,1},{4,6},{6,4},{5,7},{7,5},{8,10},{10,8},{9,1... | collective-permute-start | bytes 786440 | tf_op jit(solution)/shard_map/ppermute | solution.py:28
  28.2 1.6 collective-permute-start.11
  29.8 3.6 %collective-permute-done.8.refs_2_ = bf16[32,1536]{1,0:T(8,128)(2,1)S(1)} collective-permute-done((bf16[32,1536]{1,0:T(8,128)(2,1)S(1)}, bf16[32,1536]{1,0:T(8,128)(2,1)S(1)}, u32[]{:S(2)}, u32[]{:S(2)}) %collective-permute-start.8) | collective-permute-done | bytes 98336 | tf_op jit(solution)/shard_map/ppermute | solution.py:24
  34.0 1.4 collective-permute-start.6
  35.4 1.4 collective-permute-start.12
  36.8 4.2 %collective-permute-done.9.refs_3_ = bf16[32,1536]{1,0:T(8,128)(2,1)S(1)} collective-permute-done((bf16[32,1536]{1,0:T(8,128)(2,1)S(1)}, bf16[32,1536]{1,0:T(8,128)(2,1)S(1)}, u32[]{:S(2)}, u32[]{:S(2)}) %collective-permute-start.9) | collective-permute-done | bytes 98336 | tf_op jit(solution)/shard_map/ppermute | solution.py:24
  41.1 0.9 collective-permute-start.10
  42.0 1.0 select_bitcast_fusion.3
  43.4 4.4 %collective-permute-done.10.refs_4_ = bf16[32,1536]{1,0:T(8,128)(2,1)S(1)} collective-permute-done((bf16[32,1536]{1,0:T(8,128)(2,1)S(1)}, bf16[32,1536]{1,0:T(8,128)(2,1)S(1)}, u32[]{:S(2)}, u32[]{:S(2)}) %collective-permute-start.10) | collective-permute-done | bytes 98336 | tf_op jit(solution)/shard_map/ppermute | solution.py:24
  47.7 1.0 shard_map.103
  48.7 1.1 collective-permute-start.13
  49.8 2.2 %collective-permute-start.14 = (bf16[256,1536]{1,0:T(8,128)(2,1)S(1)}, bf16[256,1536]{1,0:T(8,128)(2,1)S(1)}, u32[]{:S(2)}, u32[]{:S(2)}) collective-permute-start(bf16[256,1536]{1,0:T(8,128)(2,1)S(1)} %bitcast.24), channel_id=1, source_target_pairs={{4,0},{8,4},{12,8},{0,12},{5,1},{9,5},{13,9},{1,13},{6,2},{10,6},{... | collective-permute-start | bytes 2359304 | tf_op jit(solution)/shard_map/ppermute | solution.py:24
  52.8 1.8 %collective-permute-done.7.hidden_other = bf16[2,256,512]{2,1,0:T(8,128)(2,1)S(1)} collective-permute-done((bf16[2,256,512]{2,1,0:T(8,128)(2,1)S(1)}, bf16[2,256,512]{2,1,0:T(8,128)(2,1)S(1)}, u32[]{:S(2)}, u32[]{:S(2)}) %collective-permute-start.7) | collective-permute-done | bytes 524320 | tf_op jit(solution)/shard_map/ppermute | solution.py:28
  54.5 7.8 %collective-permute-done.13.refs_0_ = bf16[256,1536]{1,0:T(8,128)(2,1)} collective-permute-done((bf16[256,1536]{1,0:T(8,128)(2,1)S(1)}, bf16[256,1536]{1,0:T(8,128)(2,1)}, u32[]{:S(2)}, u32[]{:S(2)}) %collective-permute-start.13) | collective-permute-done | bytes 786464 | tf_op jit(solution)/shard_map/ppermute | solution.py:28
  62.3 1.4 collective-permute-done.14.refs_1_
  63.7 1.0 copy-done.7
  65.3 3.8 %all-gather.2.cloned.1.call-done.go = bf16[1024,1536]{1,0:T(8,128)(2,1)} async-done(((bf16[128,1536]{1,0:T(8,128)(2,1)}), bf16[1024,1536]{1,0:T(8,128)(2,1)}) %all-gather.2.cloned.1.call-update) | async-done | bytes 3145744 | tf_op jit(solution)/shard_map/all_gather | solution.py:276
  69.0 3.4 %shard_map.105 = bf16[2,256,512]{2,1,0:T(8,128)(2,1)S(1)} custom-call(s32[4]{0:T(128)S(1)} %pad_add_fusion.place, bf16[1024,1536]{1,0:T(8,128)(2,1)} %all-gather.2.cloned.1.call-done.go, bf16[512,1536]{1,0:T(8,128)(2,1)} %w_down.3), custom_call_target="tpu_custom_call" | custom-call | tf_op jit(solution)/shard_map/pallas_call | solution.py:71
  72.5 3.4 %shard_map.104 = f32[2,256,512]{2,1,0:T(8,128)S(1)} custom-call(s32[4]{0:T(128)S(1)} %pad_add_fusion.place, bf16[1024,1536]{1,0:T(8,128)(2,1)} %all-gather.2.cloned.1.call-done.go, bf16[512,1536]{1,0:T(8,128)(2,1)} %w_down.3), custom_call_target="tpu_custom_call" | custom-call | tf_op jit(solution)/shard_map/pallas_call | solution.py:71
  76.1 2.2 %collective-permute-start.17 = (bf16[2,256,512]{2,1,0:T(8,128)(2,1)S(1)}, bf16[2,256,512]{2,1,0:T(8,128)(2,1)S(1)}, u32[]{:S(2)}, u32[]{:S(2)}) collective-permute-start(bf16[2,256,512]{2,1,0:T(8,128)(2,1)S(1)} %get-tuple-element.104), channel_id=1, source_target_pairs={{0,2},{2,0},{1,3},{3,1},{4,6},{6,4},{5,7},{7,5},{8,10},{10,8},{9,1... | collective-permute-start | bytes 1572872 | tf_op jit(solution)/shard_map/ppermute | solution.py:28
  78.3 1.9 %collective-permute-start.20 = (bf16[256,1536]{1,0:T(8,128)(2,1)S(1)}, bf16[256,1536]{1,0:T(8,128)(2,1)}, u32[]{:S(2)}, u32[]{:S(2)}) collective-permute-start(bf16[256,1536]{1,0:T(8,128)(2,1)S(1)} %bitcast.26), channel_id=1, source_target_pairs={{8,0},{12,4},{0,8},{4,12},{9,1},{13,5},{1,9},{5,13},{10,2},{14,6},... | collective-permute-start | bytes 2359304 | tf_op jit(solution)/shard_map/ppermute | solution.py:24
  80.3 5.2 %shard_map.106 = (bf16[64,1536]{1,0:T(8,128)(2,1)}, bf16[448,1536]{1,0:T(8,128)(2,1)}) custom-call(s32[4]{0:T(128)S(1)} %pad_add_fusion.place, bf16[2,256,512]{2,1,0:T(8,128)(2,1)S(1)} %fusion.4.hidden, bf16[2,256,512]{2,1,0:T(8,128)(2,1)S(1)} %collective-permute-done.7.hidden_other, bf16[1024,1536]{1,0:T(8,128)(2,1)} %all-gather.2.cloned.1.call-done.go), custom_call_target="tpu_custom_call" | custom-call | tf_op jit(solution)/shard_map/pallas_call | solution.py:169
  85.4 6.6 %collective-permute-done.17.chip_far = bf16[2,256,512]{2,1,0:T(8,128)(2,1)S(1)} collective-permute-done((bf16[2,256,512]{2,1,0:T(8,128)(2,1)S(1)}, bf16[2,256,512]{2,1,0:T(8,128)(2,1)S(1)}, u32[]{:S(2)}, u32[]{:S(2)}) %collective-permute-start.17) | collective-permute-done | bytes 524320 | tf_op jit(solution)/shard_map/ppermute | solution.py:28
  93.8 2.3 %shard_map.108.near = bf16[512,1536]{1,0:T(8,128)(2,1)S(1)} custom-call(bf16[2,256,512]{2,1,0:T(8,128)(2,1)S(1)} %get-tuple-element.69.near0.refs_4_, bf16[2,256,512]{2,1,0:T(8,128)(2,1)S(1)} %get-tuple-element.70.near1.refs_5_, bf16[1536,512]{1,0:T(8,128)(2,1)S(1)} %copy-done, bf16[1536,512]{1,0:T(8,128)(2,1)S(1)} %copy-done.1), custom_call_target="tpu_custom_call" | custom-call | tf_op jit(solution)/shard_map/pallas_call | solution.py:118
  96.1 4.2 %shard_map.109 = bf16[1024,1536]{1,0:T(8,128)(2,1)} custom-call(s32[4]{0:T(128)S(1)} %pad_add_fusion.place, bf16[512,1536]{1,0:T(8,128)(2,1)S(1)} %shard_map.108.near, bf16[2,256,512]{2,1,0:T(8,128)(2,1)S(1)} %collective-permute-done.18.other0.refs_6_, bf16[2,256,512]{2,1,0:T(8,128)(2,1)S(1)} %collective-permute-done.19.other1.refs_7_, ...), custom_call_target="tpu_custom_call" | custom-call | tf_op jit(solution)/shard_map/pallas_call | solution.py:139
  101.0 2.1 %collective-permute-start.25 = (bf16[256,1536]{1,0:T(8,128)(2,1)}, bf16[256,1536]{1,0:T(8,128)(2,1)S(1)}, u32[]{:S(2)}, u32[]{:S(2)}) collective-permute-start(bf16[256,1536]{1,0:T(8,128)(2,1)} %collective-permute-done.13.refs_0_), channel_id=1, source_target_pairs={{4,0},{8,4},{12,8},{0,12},{5,1},{9,5},{13,9},{1,13},{6,2},{10,6},{... | collective-permute-start | bytes 2359304 | tf_op jit(solution)/shard_map/ppermute | solution.py:24
  103.1 1.4 collective-permute-start.23
  104.5 1.5 collective-permute-start.24
  106.0 7.4 %shard_map.110 = (bf16[1536,512]{1,0:T(8,128)(2,1)}, bf16[1536,512]{1,0:T(8,128)(2,1)}) custom-call(s32[4]{0:T(128)S(1)} %pad_add_fusion.place, bf16[256,1536]{1,0:T(8,128)(2,1)} %bitcast.27, bf16[256,1536]{1,0:T(8,128)(2,1)} %copy-done.7, bf16[256,1536]{1,0:T(8,128)(2,1)} %collective-permute-done.20.refs_2_, ...), custom_call_target="tpu_custom_call" | custom-call | tf_op jit(solution)/shard_map/pallas_call | solution.py:218
  113.4 7.1 %collective-permute-done.25.refs_1_ = bf16[256,1536]{1,0:T(8,128)(2,1)S(1)} collective-permute-done((bf16[256,1536]{1,0:T(8,128)(2,1)}, bf16[256,1536]{1,0:T(8,128)(2,1)S(1)}, u32[]{:S(2)}, u32[]{:S(2)}) %collective-permute-start.25) | collective-permute-done | bytes 786464 | tf_op jit(solution)/shard_map/ppermute | solution.py:24
  120.5 3.0 %collective-permute-done.26.refs_2_ = bf16[256,1536]{1,0:T(8,128)(2,1)S(1)} collective-permute-done((bf16[256,1536]{1,0:T(8,128)(2,1)}, bf16[256,1536]{1,0:T(8,128)(2,1)S(1)}, u32[]{:S(2)}, u32[]{:S(2)}) %collective-permute-start.26) | collective-permute-done | bytes 786464 | tf_op jit(solution)/shard_map/ppermute | solution.py:24
  123.5 1.5 collective-permute-start.32
  125.5 1.4 collective-permute-done.27.refs_5_.refs_3_
  126.9 0.7 collective-permute-done.28.refs_6_.refs_4_
  127.7 7.3 %shard_map.111 = (bf16[1536,512]{1,0:T(8,128)(2,1)}, bf16[1536,512]{1,0:T(8,128)(2,1)}) custom-call(s32[4]{0:T(128)S(1)} %pad_add_fusion.place, bf16[256,1536]{1,0:T(8,128)(2,1)} %collective-permute-done.13.refs_0_, bf16[256,1536]{1,0:T(8,128)(2,1)} %copy-done.5, bf16[256,1536]{1,0:T(8,128)(2,1)} %copy-done.6, ...), custom_call_target="tpu_custom_call" | custom-call | tf_op jit(solution)/shard_map/pallas_call | solution.py:218
  134.9 10.5 %reduce-scatter.2.cloned.1.call-done = bf16[128,1536]{1,0:T(8,128)(2,1)} async-done(((bf16[1024,1536]{1,0:T(8,128)(2,1)}), bf16[128,1536]{1,0:T(8,128)(2,1)}) %reduce-scatter.2.cloned.1.call-update) | async-done | bytes 393232 | tf_op jit(solution)/shard_map/reduce_scatter | solution.py:303
  145.5 1.1 dynamic-slice_bitcast_fusion
  146.6 2.7 %collective-permute-start.31 = (bf16[32,1536]{1,0:T(8,128)(2,1)S(1)}, bf16[32,1536]{1,0:T(8,128)(2,1)S(1)}, u32[]{:S(2)}, u32[]{:S(2)}) collective-permute-start(bf16[32,1536]{1,0:T(8,128)(2,1)S(1)} %get-tuple-element.92), channel_id=1, source_target_pairs={{4,0},{8,4},{12,8},{0,12},{5,1},{9,5},{13,9},{1,13},{6,2},{10,6},{... | collective-permute-start | bytes 294920 | tf_op jit(solution)/shard_map/ppermute | solution.py:24
  149.2 1.1 collective-permute-start.30
  150.3 0.8 collective-permute-start.29
  151.1 5.8 %shard_map.112 = (bf16[1536,512]{1,0:T(8,128)(2,1)}, bf16[1536,512]{1,0:T(8,128)(2,1)}) custom-call(s32[4]{0:T(128)S(1)} %pad_add_fusion.place, bf16[256,1536]{1,0:T(8,128)(2,1)S(1)} %collective-permute-done.22.refs_0_, bf16[2,256,512]{2,1,0:T(8,128)(2,1)S(1)} %collective-permute-done.23.refs_3_.refs_1_, ...), custom_call_target="tpu_custom_call" | custom-call | tf_op jit(solution)/shard_map/pallas_call | solution.py:218
  157.6 6.1 %shard_map.113 = bf16[512,1536]{1,0:T(8,128)(2,1)} custom-call(bf16[64,1536]{1,0:T(8,128)(2,1)} %get-tuple-element.72.first, bf16[64,1536]{1,0:T(8,128)(2,1)S(1)} %copy-done.4, bf16[448,1536]{1,0:T(8,128)(2,1)} %get-tuple-element.98.rest, bf16[448,1536]{1,0:T(8,128)(2,1)} %collective-permute-done.32.rest_far), custom_call_target="tpu_custom_call" | custom-call | tf_op jit(solution)/shard_map/pallas_call | solution.py:242
  (62 shorter events, 8.2 us)
Async XLA Ops:
  7.2 61.9 %all-gather.2.cloned.1.call-start = ((), (), s32[]{:S(2)}) async-start(), calls=%async_computation.1 | async-start | bytes 3538944 | tf_op jit(solution)/shard_map/all_gather | solution.py:276
  7.2 10.6 %collective-permute-start = (bf16[32,1536]{1,0:T(8,128)(2,1)}, bf16[32,1536]{1,0:T(8,128)(2,1)S(1)}, u32[]{:S(2)}, u32[]{:S(2)}) collective-permute-start(bf16[32,1536]{1,0:T(8,128)(2,1)} %refs_0_.1), channel_id=1, source_target_pairs={{4,0},{8,4},{12,8},{0,12},{5,1},{9,5},{13,9},{1,13},{6,2},{10,6},{... | collective-permute-start | bytes 294920 | tf_op jit(solution)/shard_map/ppermute | solution.py:24
  10.3 7.5 %collective-permute-start.1 = (bf16[32,1536]{1,0:T(8,128)(2,1)}, bf16[32,1536]{1,0:T(8,128)(2,1)S(1)}, u32[]{:S(2)}, u32[]{:S(2)}) collective-permute-start(bf16[32,1536]{1,0:T(8,128)(2,1)} %refs_0_.1), channel_id=1, source_target_pairs={{8,0},{12,4},{0,8},{4,12},{9,1},{13,5},{1,9},{5,13},{10,2},{14,6},... | collective-permute-start | bytes 294920 | tf_op jit(solution)/shard_map/ppermute | solution.py:24
  10.9 7.4 %collective-permute-start.2 = (bf16[32,1536]{1,0:T(8,128)(2,1)}, bf16[32,1536]{1,0:T(8,128)(2,1)S(1)}, u32[]{:S(2)}, u32[]{:S(2)}) collective-permute-start(bf16[32,1536]{1,0:T(8,128)(2,1)} %refs_0_.1), channel_id=1, source_target_pairs={{12,0},{0,4},{4,8},{8,12},{13,1},{1,5},{5,9},{9,13},{14,2},{2,6},{... | collective-permute-start | bytes 294920 | tf_op jit(solution)/shard_map/ppermute | solution.py:24
  11.9 8.4 %collective-permute-start.3 = (bf16[32,1536]{1,0:T(8,128)(2,1)}, bf16[32,1536]{1,0:T(8,128)(2,1)S(1)}, u32[]{:S(2)}, u32[]{:S(2)}) collective-permute-start(bf16[32,1536]{1,0:T(8,128)(2,1)} %refs_0_.2), channel_id=1, source_target_pairs={{16,0},{32,16},{48,32},{64,48},{80,64},{96,80},{112,96},{0,112},{1... | collective-permute-start | bytes 294920 | tf_op jit(solution)/shard_map/ppermute | solution.py:24
  17.8 6.0 %collective-permute-start.4 = (bf16[32,1536]{1,0:T(8,128)(2,1)}, bf16[32,1536]{1,0:T(8,128)(2,1)S(1)}, u32[]{:S(2)}, u32[]{:S(2)}) collective-permute-start(bf16[32,1536]{1,0:T(8,128)(2,1)} %refs_0_.2), channel_id=1, source_target_pairs={{112,0},{0,16},{16,32},{32,48},{48,64},{64,80},{80,96},{96,112},{1... | collective-permute-start | bytes 294920 | tf_op jit(solution)/shard_map/ppermute | solution.py:24
  25.5 26.5 %copy-start.8 = (bf16[256,512]{1,0:T(8,128)(2,1)S(1)}, bf16[256,512]{1,0:T(8,128)(2,1)}, u32[]{:S(2)}) copy-start(bf16[256,512]{1,0:T(8,128)(2,1)} %param.10) | copy-start | bytes 786436
  25.5 120.0 %reduce-scatter.2.cloned.1.call-start = ((), (), s32[]{:S(2)}) async-start(), calls=%async_computation.2 | async-start | bytes 3538944 | tf_op jit(solution)/shard_map/reduce_scatter | solution.py:303
  25.6 16.4 %collective-permute-start.5 = (bf16[256,512]{1,0:T(8,128)(2,1)}, bf16[256,512]{1,0:T(8,128)(2,1)S(1)}, u32[]{:S(2)}, u32[]{:S(2)}) collective-permute-start(bf16[256,512]{1,0:T(8,128)(2,1)} %param.9), channel_id=1, source_target_pairs={{0,2},{2,0},{1,3},{3,1},{4,6},{6,4},{5,7},{7,5},{8,10},{10,8},{9,1... | collective-permute-start | bytes 786440 | tf_op jit(solution)/shard_map/ppermute | solution.py:28
  27.8 5.6 %collective-permute-start.8 = (bf16[32,1536]{1,0:T(8,128)(2,1)S(1)}, bf16[32,1536]{1,0:T(8,128)(2,1)S(1)}, u32[]{:S(2)}, u32[]{:S(2)}) collective-permute-start(bf16[32,1536]{1,0:T(8,128)(2,1)S(1)} %collective-permute-done.3.refs_1_), channel_id=1, source_target_pairs={{16,0},{32,16},{48,32},{64,48},{80,64},{96,80},{112,96},{0,112},{1... | collective-permute-start | bytes 294920 | tf_op jit(solution)/shard_map/ppermute | solution.py:24
  28.2 7.2 %collective-permute-start.11 = (bf16[32,1536]{1,0:T(8,128)(2,1)S(1)}, bf16[32,1536]{1,0:T(8,128)(2,1)S(1)}, u32[]{:S(2)}, u32[]{:S(2)}) collective-permute-start(bf16[32,1536]{1,0:T(8,128)(2,1)S(1)} %collective-permute-done.4.refs_7_), channel_id=1, source_target_pairs={{112,0},{0,16},{16,32},{32,48},{48,64},{64,80},{80,96},{96,112},{1... | collective-permute-start | bytes 294920 | tf_op jit(solution)/shard_map/ppermute | solution.py:24
  33.4 7.7 %collective-permute-start.9 = (bf16[32,1536]{1,0:T(8,128)(2,1)S(1)}, bf16[32,1536]{1,0:T(8,128)(2,1)S(1)}, u32[]{:S(2)}, u32[]{:S(2)}) collective-permute-start(bf16[32,1536]{1,0:T(8,128)(2,1)S(1)} %collective-permute-done.8.refs_2_), channel_id=1, source_target_pairs={{16,0},{32,16},{48,32},{64,48},{80,64},{96,80},{112,96},{0,112},{1... | collective-permute-start | bytes 294920 | tf_op jit(solution)/shard_map/ppermute | solution.py:24
  34.0 17.9 %collective-permute-start.6 = (bf16[256,512]{1,0:T(8,128)(2,1)}, bf16[256,512]{1,0:T(8,128)(2,1)S(1)}, u32[]{:S(2)}, u32[]{:S(2)}) collective-permute-start(bf16[256,512]{1,0:T(8,128)(2,1)} %param.10), channel_id=1, source_target_pairs={{0,2},{2,0},{1,3},{3,1},{4,6},{6,4},{5,7},{7,5},{8,10},{10,8},{9,1... | collective-permute-start | bytes 786440 | tf_op jit(solution)/shard_map/ppermute | solution.py:28
  35.4 7.9 %collective-permute-start.12 = (bf16[32,1536]{1,0:T(8,128)(2,1)S(1)}, bf16[32,1536]{1,0:T(8,128)(2,1)S(1)}, u32[]{:S(2)}, u32[]{:S(2)}) collective-permute-start(bf16[32,1536]{1,0:T(8,128)(2,1)S(1)} %collective-permute-done.11.refs_6_), channel_id=1, source_target_pairs={{112,0},{0,16},{16,32},{32,48},{48,64},{64,80},{80,96},{96,112},{1... | collective-permute-start | bytes 294920 | tf_op jit(solution)/shard_map/ppermute | solution.py:24
  41.1 6.7 %collective-permute-start.10 = (bf16[32,1536]{1,0:T(8,128)(2,1)S(1)}, bf16[32,1536]{1,0:T(8,128)(2,1)S(1)}, u32[]{:S(2)}, u32[]{:S(2)}) collective-permute-start(bf16[32,1536]{1,0:T(8,128)(2,1)S(1)} %collective-permute-done.9.refs_3_), channel_id=1, source_target_pairs={{16,0},{32,16},{48,32},{64,48},{80,64},{96,80},{112,96},{0,112},{1... | collective-permute-start | bytes 294920 | tf_op jit(solution)/shard_map/ppermute | solution.py:24
  48.7 29.6 %copy-start.2 = (bf16[8,32,1536]{2,1,0:T(8,128)(2,1)}, bf16[8,32,1536]{2,1,0:T(8,128)(2,1)S(1)}, u32[]{:S(2)}) copy-start(bf16[8,32,1536]{2,1,0:T(8,128)(2,1)S(1)} %shard_map.103) | copy-start | bytes 2359300
  48.7 13.6 %collective-permute-start.13 = (bf16[256,1536]{1,0:T(8,128)(2,1)S(1)}, bf16[256,1536]{1,0:T(8,128)(2,1)}, u32[]{:S(2)}, u32[]{:S(2)}) collective-permute-start(bf16[256,1536]{1,0:T(8,128)(2,1)S(1)} %bitcast.23), channel_id=1, source_target_pairs={{0,128},{128,0},{1,129},{129,1},{2,130},{130,2},{3,131},{131,3},{4... | collective-permute-start | bytes 2359304 | tf_op jit(solution)/shard_map/ppermute | solution.py:28
  49.8 13.8 %collective-permute-start.14 = (bf16[256,1536]{1,0:T(8,128)(2,1)S(1)}, bf16[256,1536]{1,0:T(8,128)(2,1)S(1)}, u32[]{:S(2)}, u32[]{:S(2)}) collective-permute-start(bf16[256,1536]{1,0:T(8,128)(2,1)S(1)} %bitcast.24), channel_id=1, source_target_pairs={{4,0},{8,4},{12,8},{0,12},{5,1},{9,5},{13,9},{1,13},{6,2},{10,6},{... | collective-permute-start | bytes 2359304 | tf_op jit(solution)/shard_map/ppermute | solution.py:24
  52.0 13.3 %collective-permute-start.15 = (bf16[256,1536]{1,0:T(8,128)(2,1)S(1)}, bf16[256,1536]{1,0:T(8,128)(2,1)}, u32[]{:S(2)}, u32[]{:S(2)}) collective-permute-start(bf16[256,1536]{1,0:T(8,128)(2,1)S(1)} %bitcast.25), channel_id=1, source_target_pairs={{12,0},{0,4},{4,8},{8,12},{13,1},{1,5},{5,9},{9,13},{14,2},{2,6},{... | collective-permute-start | bytes 2359304 | tf_op jit(solution)/shard_map/ppermute | solution.py:24
  52.4 2.2 %collective-permute-start.7 = (bf16[2,256,512]{2,1,0:T(8,128)(2,1)S(1)}, bf16[2,256,512]{2,1,0:T(8,128)(2,1)S(1)}, u32[]{:S(2)}, u32[]{:S(2)}) collective-permute-start(bf16[2,256,512]{2,1,0:T(8,128)(2,1)S(1)} %fusion.4.hidden), channel_id=1, source_target_pairs={{0,1},{1,0},{2,3},{3,2},{4,5},{5,4},{6,7},{7,6},{8,9},{9,8},{10,11... | collective-permute-start | bytes 1572872 | tf_op jit(solution)/shard_map/ppermute | solution.py:28
  63.7 1.0 copy-start.7
  72.4 3.5 %collective-permute-start.16 = (bf16[2,256,512]{2,1,0:T(8,128)(2,1)S(1)}, bf16[2,256,512]{2,1,0:T(8,128)(2,1)S(1)}, u32[]{:S(2)}, u32[]{:S(2)}) collective-permute-start(bf16[2,256,512]{2,1,0:T(8,128)(2,1)S(1)} %shard_map.105), channel_id=1, source_target_pairs={{0,1},{1,0},{2,3},{3,2},{4,5},{5,4},{6,7},{7,6},{8,9},{9,8},{10,11... | collective-permute-start | bytes 1572872 | tf_op jit(solution)/shard_map/ppermute | solution.py:28
  76.1 15.9 %collective-permute-start.17 = (bf16[2,256,512]{2,1,0:T(8,128)(2,1)S(1)}, bf16[2,256,512]{2,1,0:T(8,128)(2,1)S(1)}, u32[]{:S(2)}, u32[]{:S(2)}) collective-permute-start(bf16[2,256,512]{2,1,0:T(8,128)(2,1)S(1)} %get-tuple-element.104), channel_id=1, source_target_pairs={{0,2},{2,0},{1,3},{3,1},{4,6},{6,4},{5,7},{7,5},{8,10},{10,8},{9,1... | collective-permute-start | bytes 1572872 | tf_op jit(solution)/shard_map/ppermute | solution.py:28
  78.3 22.0 %collective-permute-start.20 = (bf16[256,1536]{1,0:T(8,128)(2,1)S(1)}, bf16[256,1536]{1,0:T(8,128)(2,1)}, u32[]{:S(2)}, u32[]{:S(2)}) collective-permute-start(bf16[256,1536]{1,0:T(8,128)(2,1)S(1)} %bitcast.26), channel_id=1, source_target_pairs={{8,0},{12,4},{0,8},{4,12},{9,1},{13,5},{1,9},{5,13},{10,2},{14,6},... | collective-permute-start | bytes 2359304 | tf_op jit(solution)/shard_map/ppermute | solution.py:24
  80.3 13.5 %copy-start.1 = (bf16[1536,512]{1,0:T(8,128)(2,1)S(1)}, bf16[1536,512]{1,0:T(8,128)(2,1)}, u32[]{:S(2)}) copy-start(bf16[1536,512]{1,0:T(8,128)(2,1)} %w_up.3) | copy-start | bytes 4718596
  85.4 8.4 %copy-start = (bf16[1536,512]{1,0:T(8,128)(2,1)S(1)}, bf16[1536,512]{1,0:T(8,128)(2,1)}, u32[]{:S(2)}) copy-start(bf16[1536,512]{1,0:T(8,128)(2,1)} %w_gate.3) | copy-start | bytes 4718596
  92.6 3.5 %collective-permute-start.18 = (bf16[2,256,512]{2,1,0:T(8,128)(2,1)S(1)}, bf16[2,256,512]{2,1,0:T(8,128)(2,1)S(1)}, u32[]{:S(2)}, u32[]{:S(2)}) collective-permute-start(bf16[2,256,512]{2,1,0:T(8,128)(2,1)S(1)} %get-tuple-element.69.near0.refs_4_), channel_id=1, source_target_pairs={{0,1},{1,0},{2,3},{3,2},{4,5},{5,4},{6,7},{7,6},{8,9},{9,8},{10,11... | collective-permute-start | bytes 1572872 | tf_op jit(solution)/shard_map/ppermute | solution.py:28
  92.7 3.4 %collective-permute-start.19 = (bf16[2,256,512]{2,1,0:T(8,128)(2,1)S(1)}, bf16[2,256,512]{2,1,0:T(8,128)(2,1)S(1)}, u32[]{:S(2)}, u32[]{:S(2)}) collective-permute-start(bf16[2,256,512]{2,1,0:T(8,128)(2,1)S(1)} %get-tuple-element.70.near1.refs_5_), channel_id=1, source_target_pairs={{0,1},{1,0},{2,3},{3,2},{4,5},{5,4},{6,7},{7,6},{8,9},{9,8},{10,11... | collective-permute-start | bytes 1572872 | tf_op jit(solution)/shard_map/ppermute | solution.py:28
  93.2 7.1 %collective-permute-start.21 = (bf16[64,1536]{1,0:T(8,128)(2,1)}, bf16[64,1536]{1,0:T(8,128)(2,1)S(1)}, u32[]{:S(2)}, u32[]{:S(2)}) collective-permute-start(bf16[64,1536]{1,0:T(8,128)(2,1)} %get-tuple-element.72.first), channel_id=1, source_target_pairs={{0,128},{128,0},{1,129},{129,1},{2,130},{130,2},{3,131},{131,3},{4... | collective-permute-start | bytes 589832 | tf_op jit(solution)/shard_map/ppermute | solution.py:28
  100.3 0.7 copy-start.3
  101.0 19.5 %collective-permute-start.25 = (bf16[256,1536]{1,0:T(8,128)(2,1)}, bf16[256,1536]{1,0:T(8,128)(2,1)S(1)}, u32[]{:S(2)}, u32[]{:S(2)}) collective-permute-start(bf16[256,1536]{1,0:T(8,128)(2,1)} %collective-permute-done.13.refs_0_), channel_id=1, source_target_pairs={{4,0},{8,4},{12,8},{0,12},{5,1},{9,5},{13,9},{1,13},{6,2},{10,6},{... | collective-permute-start | bytes 2359304 | tf_op jit(solution)/shard_map/ppermute | solution.py:24
  103.1 20.4 %collective-permute-start.26 = (bf16[256,1536]{1,0:T(8,128)(2,1)}, bf16[256,1536]{1,0:T(8,128)(2,1)S(1)}, u32[]{:S(2)}, u32[]{:S(2)}) collective-permute-start(bf16[256,1536]{1,0:T(8,128)(2,1)} %collective-permute-done.13.refs_0_), channel_id=1, source_target_pairs={{12,0},{0,4},{4,8},{8,12},{13,1},{1,5},{5,9},{9,13},{14,2},{2,6},{... | collective-permute-start | bytes 2359304 | tf_op jit(solution)/shard_map/ppermute | solution.py:24
  103.1 20.4 %collective-permute-start.23 = (bf16[2,256,512]{2,1,0:T(8,128)(2,1)S(1)}, bf16[2,256,512]{2,1,0:T(8,128)(2,1)S(1)}, u32[]{:S(2)}, u32[]{:S(2)}) collective-permute-start(bf16[2,256,512]{2,1,0:T(8,128)(2,1)S(1)} %get-tuple-element.69.near0.refs_4_), channel_id=1, source_target_pairs={{0,128},{128,0},{1,129},{129,1},{2,130},{130,2},{3,131},{131,3},{4... | collective-permute-start | bytes 1572872 | tf_op jit(solution)/shard_map/ppermute | solution.py:28
  104.5 19.0 %collective-permute-start.24 = (bf16[2,256,512]{2,1,0:T(8,128)(2,1)S(1)}, bf16[2,256,512]{2,1,0:T(8,128)(2,1)S(1)}, u32[]{:S(2)}, u32[]{:S(2)}) collective-permute-start(bf16[2,256,512]{2,1,0:T(8,128)(2,1)S(1)} %get-tuple-element.70.near1.refs_5_), channel_id=1, source_target_pairs={{0,130},{130,0},{2,128},{128,2},{1,131},{131,1},{3,129},{129,3},{4... | collective-permute-start | bytes 1572872 | tf_op jit(solution)/shard_map/ppermute | solution.py:305
  120.5 4.5 %copy-start.5 = (bf16[256,1536]{1,0:T(8,128)(2,1)}, bf16[256,1536]{1,0:T(8,128)(2,1)S(1)}, u32[]{:S(2)}) copy-start(bf16[256,1536]{1,0:T(8,128)(2,1)S(1)} %collective-permute-done.25.refs_1_) | copy-start | bytes 2359300
  123.5 1.5 copy-start.6
  123.5 34.1 %collective-permute-start.32 = (bf16[448,1536]{1,0:T(8,128)(2,1)}, bf16[448,1536]{1,0:T(8,128)(2,1)}, u32[]{:S(2)}, u32[]{:S(2)}) collective-permute-start(bf16[448,1536]{1,0:T(8,128)(2,1)} %get-tuple-element.98.rest), channel_id=1, source_target_pairs={{0,128},{128,0},{1,129},{129,1},{2,130},{130,2},{3,131},{131,3},{4... | collective-permute-start | bytes 4128776 | tf_op jit(solution)/shard_map/ppermute | solution.py:28
  125.0 21.6 %collective-permute-start.22 = (bf16[256,1536]{1,0:T(8,128)(2,1)}, bf16[256,1536]{1,0:T(8,128)(2,1)S(1)}, u32[]{:S(2)}, u32[]{:S(2)}) collective-permute-start(bf16[256,1536]{1,0:T(8,128)(2,1)} %collective-permute-done.13.refs_0_), channel_id=1, source_target_pairs={{8,0},{12,4},{0,8},{4,12},{9,1},{13,5},{1,9},{5,13},{10,2},{14,6},... | collective-permute-start | bytes 2359304 | tf_op jit(solution)/shard_map/ppermute | solution.py:24
  125.0 1.9 %collective-permute-start.27 = (bf16[2,256,512]{2,1,0:T(8,128)(2,1)S(1)}, bf16[2,256,512]{2,1,0:T(8,128)(2,1)S(1)}, u32[]{:S(2)}, u32[]{:S(2)}) collective-permute-start(bf16[2,256,512]{2,1,0:T(8,128)(2,1)S(1)} %collective-permute-done.23.refs_3_.refs_1_), channel_id=1, source_target_pairs={{0,1},{1,0},{2,3},{3,2},{4,5},{5,4},{6,7},{7,6},{8,9},{9,8},{10,11... | collective-permute-start | bytes 1572872 | tf_op jit(solution)/shard_map/ppermute | solution.py:28
  125.0 2.6 %collective-permute-start.28 = (bf16[2,256,512]{2,1,0:T(8,128)(2,1)S(1)}, bf16[2,256,512]{2,1,0:T(8,128)(2,1)S(1)}, u32[]{:S(2)}, u32[]{:S(2)}) collective-permute-start(bf16[2,256,512]{2,1,0:T(8,128)(2,1)S(1)} %collective-permute-done.24.refs_4_.refs_2_), channel_id=1, source_target_pairs={{0,1},{1,0},{2,3},{3,2},{4,5},{5,4},{6,7},{7,6},{8,9},{9,8},{10,11... | collective-permute-start | bytes 1572872 | tf_op jit(solution)/shard_map/ppermute | solution.py:28
  146.6 11.0 %copy-start.4 = (bf16[64,1536]{1,0:T(8,128)(2,1)S(1)}, bf16[64,1536]{1,0:T(8,128)(2,1)}, u32[]{:S(2)}) copy-start(bf16[64,1536]{1,0:T(8,128)(2,1)} %copy-done.3) | copy-start | bytes 589828
  146.6 10.3 %collective-permute-start.31 = (bf16[32,1536]{1,0:T(8,128)(2,1)S(1)}, bf16[32,1536]{1,0:T(8,128)(2,1)S(1)}, u32[]{:S(2)}, u32[]{:S(2)}) collective-permute-start(bf16[32,1536]{1,0:T(8,128)(2,1)S(1)} %get-tuple-element.92), channel_id=1, source_target_pairs={{4,0},{8,4},{12,8},{0,12},{5,1},{9,5},{13,9},{1,13},{6,2},{10,6},{... | collective-permute-start | bytes 294920 | tf_op jit(solution)/shard_map/ppermute | solution.py:24
  149.2 7.6 %collective-permute-start.30 = (bf16[32,1536]{1,0:T(8,128)(2,1)S(1)}, bf16[32,1536]{1,0:T(8,128)(2,1)S(1)}, u32[]{:S(2)}, u32[]{:S(2)}) collective-permute-start(bf16[32,1536]{1,0:T(8,128)(2,1)S(1)} %get-tuple-element.91), channel_id=1, source_target_pairs={{8,0},{12,4},{0,8},{4,12},{9,1},{13,5},{1,9},{5,13},{10,2},{14,6},... | collective-permute-start | bytes 294920 | tf_op jit(solution)/shard_map/ppermute | solution.py:24
  150.3 6.6 %collective-permute-start.29 = (bf16[32,1536]{1,0:T(8,128)(2,1)S(1)}, bf16[32,1536]{1,0:T(8,128)(2,1)S(1)}, u32[]{:S(2)}, u32[]{:S(2)}) collective-permute-start(bf16[32,1536]{1,0:T(8,128)(2,1)S(1)} %get-tuple-element.90), channel_id=1, source_target_pairs={{12,0},{0,4},{4,8},{8,12},{13,1},{1,5},{5,9},{9,13},{14,2},{2,6},{... | collective-permute-start | bytes 294920 | tf_op jit(solution)/shard_map/ppermute | solution.py:24
Sparse Core Ops, SparseCore 0:
  25.6 43.3 all-gather.1
  100.5 44.9 reduce-scatter.1

commit v8 on v7

--- a/solution.py
+++ b/solution.py
@@ -34,6 +34,10 @@
 
 def in_hbm(x):
     return pltpu.with_memory_space_constraint(x, pltpu.HBM)
+
+
+def in_vmem(x):
+    return pltpu.with_memory_space_constraint(x, pltpu.VMEM)
 
 
 def arrange_kernel(n, slot, place, *refs):
@@ -53,32 +57,43 @@
     return out.reshape(n * rows, cols)
 
 
-def hidden_grad_kernel(far, place, go, w_down, out, rows, weight, sems):
-    core = 1 - place[3] if far else place[3]
+def hidden_grad_kernel(place, go, w_down, mine, send, rows, weight, sems):
     copies = [pltpu.make_async_copy(w_down, weight, sems.at[2])]
     for half in range(2):
-        start = pl.multiple_of(512 * half + 256 * core, 256)
-        copies.append(pltpu.make_async_copy(go.at[pl.ds(start, 256)], rows.at[half], sems.at[half]))
+        copies.append(pltpu.make_async_copy(go.at[pl.ds(512 * half, 512)], rows.at[half], sems.at[half]))
     for copy in copies:
         copy.start()
     copies[0].wait()
     for half in range(2):
         copies[1 + half].wait()
-        out[half] = dot(rows[half], weight[...], 1, 1).astype(out.dtype)
-
-
-def hidden_grad(place, go, w_down, far):
-    return pl.pallas_call(
-        functools.partial(hidden_grad_kernel, far),
-        out_shape=jax.ShapeDtypeStruct((2, 256, 512), BF16 if far else F32),
+        part = dot(rows[half], weight[...], 1, 1)
+        for which in range(2):
+            block = part[256 * which:256 * which + 256]
+
+            @pl.when(place[3] == which)
+            def _():
+                mine[half] = block
+
+            @pl.when(place[3] != which)
+            def _():
+                send[half] = block.astype(BF16)
+
+
+def hidden_grad(place, go, w_down):
+    return pl.pallas_call(
+        hidden_grad_kernel,
+        out_shape=(
+            jax.ShapeDtypeStruct((2, 256, 512), F32),
+            jax.ShapeDtypeStruct((2, 256, 512), BF16),
+        ),
         in_specs=[SMEM, HBM, HBM],
-        out_specs=VMEM,
+        out_specs=(VMEM,) * 2,
         scratch_shapes=[
-            pltpu.VMEM((2, 256, 1536), BF16),
+            pltpu.VMEM((2, 512, 1536), BF16),
             pltpu.VMEM((512, 1536), BF16),
             pltpu.SemaphoreType.DMA((3,)),
         ],
-        compiler_params=grant(12),
+        compiler_params=grant(16),
     )(place, in_hbm(go), in_hbm(w_down))
 
 
@@ -107,31 +122,12 @@
     )(chip, chip_far, gate, up)
 
 
-def near_input_kernel(near0, near1, w_gate, w_up, out):
-    for half, ref in enumerate((near0, near1)):
-        total = dot(ref[0], w_gate[...], 1, 1) + dot(ref[1], w_up[...], 1, 1)
-        out[256 * half:256 * half + 256, :] = total.astype(BF16)
-
-
-def near_input_grad(near, w_gate, w_up):
-    weight = pl.BlockSpec((512, 512), lambda i: (i, 0))
-    return pl.pallas_call(
-        near_input_kernel,
-        grid=(3,),
-        out_shape=jax.ShapeDtypeStruct((512, 1536), BF16),
-        in_specs=[VMEM] * 2 + [weight] * 2,
-        out_specs=pl.BlockSpec((512, 512), lambda i: (0, i)),
-        compiler_params=grant(12),
-    )(*near, w_gate, w_up)
-
-
-def input_grad_kernel(place, near, other0, other1, w_gate, w_up, out):
-    for half, ref in enumerate((other0, other1)):
-        start = pl.multiple_of(512 * half + 256 * place[3], 256)
-        out[pl.ds(start, 256), :] = near[256 * half:256 * half + 256, :]
-        total = dot(ref[0], w_gate[...], 1, 1) + dot(ref[1], w_up[...], 1, 1)
-        start = pl.multiple_of(512 * half + 256 * (1 - place[3]), 256)
-        out[pl.ds(start, 256), :] = total.astype(BF16)
+def input_grad_kernel(place, near0, near1, other0, other1, w_gate, w_up, out):
+    for refs, core in (((near0, near1), place[3]), ((other0, other1), 1 - place[3])):
+        for half, ref in enumerate(refs):
+            total = dot(ref[0], w_gate[...], 1, 1) + dot(ref[1], w_up[...], 1, 1)
+            start = pl.multiple_of(512 * half + 256 * core, 256)
+            out[pl.ds(start, 256), :] = total.astype(BF16)
 
 
 def input_grad(place, near, other, w_gate, w_up):
@@ -140,10 +136,10 @@
         input_grad_kernel,
         grid=(3,),
         out_shape=jax.ShapeDtypeStruct((1024, 1536), BF16),
-        in_specs=[SMEM, pl.BlockSpec((512, 512), lambda i: (0, i))] + [VMEM] * 2 + [weight] * 2,
+        in_specs=[SMEM] + [VMEM] * 4 + [weight] * 2,
         out_specs=pl.BlockSpec((1024, 512), lambda i: (0, i)),
-        compiler_params=grant(14),
-    )(place, near, *other, w_gate, w_up)
+        compiler_params=grant(16),
+    )(place, *near, *other, w_gate, w_up)
 
 
 def fill_natural(place, own, other, rows, col):
@@ -211,10 +207,12 @@
     d_up[...] = up.astype(BF16)
 
 
-def weight_grads(place, slots, pieces, grads, base=(), last=False):
+def weight_grads(place, slots, pieces, grads, base=(), last=False, held=False):
     piece = pl.BlockSpec((256, 256), lambda i: (0, i))
     tile = pl.BlockSpec((256, 512), lambda i: (i, 0))
-    shape = jax.ShapeDtypeStruct((1536, 512), BF16) if last else pltpu.HBM((1536, 512), BF16)
+    space = pltpu.VMEM if held else pltpu.HBM
+    shape = jax.ShapeDtypeStruct((1536, 512), BF16) if last else space((1536, 512), BF16)
+    hold = in_vmem if last else in_hbm
     return pl.pallas_call(
         functools.partial(weight_kernel, slots, bool(base)),
         grid=(6,),
@@ -223,30 +221,25 @@
         out_specs=(tile, tile),
         scratch_shapes=[pltpu.VMEM((len(slots), NZ, 32, 1024), BF16)],
         compiler_params=grant(16),
-    )(place, *(x if last else in_hbm(x) for x in pieces), *grads, *(in_hbm(x) for x in base))
+    )(place, *(x if last else in_hbm(x) for x in pieces), *grads, *(hold(x) for x in base))
 
 
 def add_kernel(first, first_far, rest, rest_far, out):
-    @pl.when(pl.program_id(0) == 0)
-    def _():
-        out[...] = (first[...].astype(F32) + first_far[...].astype(F32)).astype(BF16)
-
-    @pl.when(pl.program_id(0) > 0)
-    def _():
-        out[...] = (rest[...].astype(F32) + rest_far[...].astype(F32)).astype(BF16)
-
-
-def add(first, first_far, rest, rest_far):
-    top = pl.BlockSpec((FIRST, 1536), lambda i: (0, 0))
-    low = pl.BlockSpec((FIRST, 1536), lambda i: (jnp.maximum(i - 1, 0), 0))
+    out[:FIRST] = (first[...].astype(F32) + first_far[...].astype(F32)).astype(BF16)
+    out[FIRST:] = (rest[...].astype(F32) + rest_far[...].astype(F32)).astype(BF16)
+
+
+def add(*parts):
+    top = pl.BlockSpec((FIRST, 512), lambda i: (0, i))
+    low = pl.BlockSpec((512 - FIRST, 512), lambda i: (0, i))
     return pl.pallas_call(
         add_kernel,
-        grid=(512 // FIRST,),
+        grid=(3,),
         out_shape=jax.ShapeDtypeStruct((512, 1536), BF16),
         in_specs=[top, top, low, low],
-        out_specs=pl.BlockSpec((FIRST, 1536), lambda i: (i, 0)),
+        out_specs=pl.BlockSpec((512, 512), lambda i: (0, i)),
         compiler_params=grant(8),
-    )(first, first_far, rest, rest_far)
+    )(*(in_vmem(x) for x in parts))
 
 
 def ring(x, up, down, axis, n):
@@ -288,8 +281,8 @@
     )
 
     own2 = from_ahead(own_z, "y", NY, 2)
-    from_other = swap(hidden_grad(place, go, w_down, True), "core")
-    chip = hidden_grad(place, go, w_down, False) + from_other.astype(F32)
+    mine, send = hidden_grad(place, go, w_down)
+    chip = mine + swap(send, "core").astype(F32)
     chip_far = swap(chip.astype(BF16), "xh")
     down_first, down_rest = down_grad(place, hidden, hidden_other, go)
 
@@ -298,30 +291,27 @@
 
     near = act_grad(chip, chip_far, gate, up)
     other = [swap(half, "core") for half in near]
-    partial_in = input_grad(place, near_input_grad(near, w_gate, w_up), other, w_gate, w_up)
+    partial_in = input_grad(place, near, other, w_gate, w_up)
     partial_in, own2, first_far = lax.optimization_barrier((partial_in, own2, first_far))
     in_z = lax.psum_scatter(partial_in, "z", scatter_dimension=0, tiled=True).reshape(NY, 32, 1536)
 
     far = [swap(near[0], "dp"), lax.ppermute(near[1], ("dp", "xh"), [(0, 3), (3, 0), (1, 2), (2, 1)])]
     partner1, partner2, partner3 = (from_ahead(partner_z, "y", NY, k) for k in (1, 2, 3))
     own_gate, own_up = weight_grads(place, (0, 1, 2, 3), (own_z, own1, own2, own3), (*near, *other))
-    far, down_rest, own_gate, own_up, partner1, partner3 = lax.optimization_barrier(
-        (far, down_rest, own_gate, own_up, partner1, partner3)
-    )
     rest_far = swap(down_rest, "dp")
+    far, own_gate, own_up, partner1, partner3 = lax.optimization_barrier((far, own_gate, own_up, partner1, partner3))
     far_other = [swap(half, "core") for half in far]
 
     y = place[1]
     slabs = [lax.dynamic_index_in_dim(in_z, (y + k) % NY, 0, keepdims=False) for k in range(NY)]
     grads = (*far, *far_other)
-    most = weight_grads(place, (0, 1, 3), (partner_z, partner1, partner3), grads, (own_gate, own_up))
-    slabs, partner2, most = lax.optimization_barrier((slabs, partner2, most))
+    most = weight_grads(place, (0, 1, 3), (partner_z, partner1, partner3), grads, (own_gate, own_up), held=True)
+    slabs, partner2, most, rest_far = lax.optimization_barrier((slabs, partner2, most, rest_far))
     total = slabs[0].astype(F32)
     for k in range(1, NY):
         total = total + from_ahead(slabs[k], "y", NY, NY - k).astype(F32)
     grad_input = total.astype(BF16)
-    grad_gate, grad_up = weight_grads(place, (2,), (partner2,), grads, most, True)
-    grad_input, grad_gate, grad_up, rest_far = lax.optimization_barrier((grad_input, grad_gate, grad_up, rest_far))
+    grad_gate, grad_up = weight_grads(place, (2,), (partner2,), grads, most, last=True)
     return grad_input, grad_gate, grad_up, add(down_first, first_far, down_rest, rest_far)
 
 

time: 171 us -> 183 us (1.070)
  waiting for transfers between devices: 63.3 us -> 75 us
  Pallas kernels: 48.3 us -> 40.2 us
  local copies, waits for them, and re-layouts: 2.69 us -> 8.68 us
    ppermute x13, waiting for transfers between devices: 18.3 us -> 36.3 us  [swap(): return lax.ppermute(x, axis, [(0, 1), (1, 0)])]
    reduce_scatter x1, waiting for transfers between devices: 10.5 us -> 0.01 us  [body(): lax.psum_scatter(partial_in, 'z', scatter_dimension=0, tiled=True)]
    pallas_call x4 -> x2, Pallas kernels: 15.2 us -> 8.09 us  [the longest x1 4.58 us: hidden_grad(): pl.pallas_call(hidden_grad_kernel, out_shape=(jax.ShapeDtypeStruct((2, 25...]
    unnamed x18 -> x36, local copies, waits for them, and re-layouts: 1.63 us -> 7.62 us
    ppermute x19, waiting for transfers between devices: 30.6 us -> 35 us  [from_ahead(): return lax.ppermute(x, axis, [((d + k) % n, d) for d in range(n)])]
  transfers between devices with their start and end apart: 35 -> 35, of which waited for: 18 -> 20; matrix products, arithmetic and copies ran while one was open for 2% -> 1% of each run, Pallas kernels for 22% -> 19%
where the time goes in v8:
time: 183 us; the launch traced here: 181 us
  waiting for transfers between devices  75 us (41%)
  starting transfers between devices  40.4 us (22%)
  Pallas kernels  40.2 us (22%)
  between operations  14.3 us (8%)
  local copies, waits for them, and re-layouts  8.68 us (5%)
  other arithmetic  2.44 us (1%)
    ppermute x13, waiting for transfers between devices, swap(): return lax.ppermute(x, axis, [(0, 1), (1, 0)])  36.3 us
    ppermute x19, waiting for transfers between devices, from_ahead(): return lax.ppermute(x, axis, [((d + k) % n, d) for d in range(n)])  35 us
    ppermute x19, starting transfers between devices, from_ahead(): return lax.ppermute(x, axis, [((d + k) % n, d) for d in range(n)])  27.9 us
    pallas_call x3, Pallas kernels, weight_grads(): pl.pallas_call(functools.partial(weight_kernel, slots, bool(base)), grid=...  19.2 us
    ppermute x13, starting transfers between devices, swap(): return lax.ppermute(x, axis, [(0, 1), (1, 0)])  10.9 us
    unnamed x36, local copies, waits for them, and re-layouts  7.62 us
    pallas_call x1, Pallas kernels, input_grad(): pl.pallas_call(input_grad_kernel, grid=(3,), out_shape=jax.ShapeDtypeStru...  5.44 us
    pallas_call x1, Pallas kernels, hidden_grad(): pl.pallas_call(hidden_grad_kernel, out_shape=(jax.ShapeDtypeStruct((2, 25...  4.58 us
  transfers between devices with their start and end apart: 35, of which 20 were waited for; matrix products, arithmetic and copies ran while one was open for 1% of the time, Pallas kernels for 19%

profile of v8, /device:TPU:2, one launch (start us, length us, event | category | flops | bytes accessed | tf_op | source)
XLA Modules:
  0.0 181.0 jit_solution(15107835859336824322)
XLA Ops:
  7.2 3.1 %collective-permute-start = (bf16[32,1536]{1,0:T(8,128)(2,1)}, bf16[32,1536]{1,0:T(8,128)(2,1)S(1)}, u32[]{:S(2)}, u32[]{:S(2)}) collective-permute-start(bf16[32,1536]{1,0:T(8,128)(2,1)} %refs_0_.1), channel_id=1, source_target_pairs={{4,0},{8,4},{12,8},{0,12},{5,1},{9,5},{13,9},{1,13},{6,2},{10,6},{... | collective-permute-start | bytes 294920 | tf_op jit(solution)/shard_map/ppermute | solution.py:24
  10.9 1.0 collective-permute-start.2
  11.9 5.9 %collective-permute-start.3 = (bf16[32,1536]{1,0:T(8,128)(2,1)}, bf16[32,1536]{1,0:T(8,128)(2,1)S(1)}, u32[]{:S(2)}, u32[]{:S(2)}) collective-permute-start(bf16[32,1536]{1,0:T(8,128)(2,1)} %refs_0_.2), channel_id=1, source_target_pairs={{16,0},{32,16},{48,32},{64,48},{80,64},{96,80},{112,96},{0,112},{1... | collective-permute-start | bytes 294920 | tf_op jit(solution)/shard_map/ppermute | solution.py:24
  18.4 1.9 %collective-permute-done.3.refs_1_ = bf16[32,1536]{1,0:T(8,128)(2,1)S(1)} collective-permute-done((bf16[32,1536]{1,0:T(8,128)(2,1)}, bf16[32,1536]{1,0:T(8,128)(2,1)S(1)}, u32[]{:S(2)}, u32[]{:S(2)}) %collective-permute-start.3) | collective-permute-done | bytes 98336 | tf_op jit(solution)/shard_map/ppermute | solution.py:24
  20.3 3.5 %collective-permute-done.4.refs_7_ = bf16[32,1536]{1,0:T(8,128)(2,1)S(1)} collective-permute-done((bf16[32,1536]{1,0:T(8,128)(2,1)}, bf16[32,1536]{1,0:T(8,128)(2,1)S(1)}, u32[]{:S(2)}, u32[]{:S(2)}) %collective-permute-start.4) | collective-permute-done | bytes 98336 | tf_op jit(solution)/shard_map/ppermute | solution.py:24
  23.8 1.7 shard_map.102
  25.6 2.2 %collective-permute-start.5 = (bf16[256,512]{1,0:T(8,128)(2,1)}, bf16[256,512]{1,0:T(8,128)(2,1)S(1)}, u32[]{:S(2)}, u32[]{:S(2)}) collective-permute-start(bf16[256,512]{1,0:T(8,128)(2,1)} %param.9), channel_id=1, source_target_pairs={{0,2},{2,0},{1,3},{3,1},{4,6},{6,4},{5,7},{7,5},{8,10},{10,8},{9,1... | collective-permute-start | bytes 786440 | tf_op jit(solution)/shard_map/ppermute | solution.py:28
  28.2 1.6 collective-permute-start.11
  29.8 3.6 %collective-permute-done.8.refs_2_ = bf16[32,1536]{1,0:T(8,128)(2,1)S(1)} collective-permute-done((bf16[32,1536]{1,0:T(8,128)(2,1)S(1)}, bf16[32,1536]{1,0:T(8,128)(2,1)S(1)}, u32[]{:S(2)}, u32[]{:S(2)}) %collective-permute-start.8) | collective-permute-done | bytes 98336 | tf_op jit(solution)/shard_map/ppermute | solution.py:24
  34.0 1.4 collective-permute-start.6
  35.4 1.4 collective-permute-start.12
  36.8 4.2 %collective-permute-done.9.refs_3_ = bf16[32,1536]{1,0:T(8,128)(2,1)S(1)} collective-permute-done((bf16[32,1536]{1,0:T(8,128)(2,1)S(1)}, bf16[32,1536]{1,0:T(8,128)(2,1)S(1)}, u32[]{:S(2)}, u32[]{:S(2)}) %collective-permute-start.9) | collective-permute-done | bytes 98336 | tf_op jit(solution)/shard_map/ppermute | solution.py:24
  42.0 1.0 select_bitcast_fusion.3
  43.4 4.4 %collective-permute-done.10.refs_4_ = bf16[32,1536]{1,0:T(8,128)(2,1)S(1)} collective-permute-done((bf16[32,1536]{1,0:T(8,128)(2,1)S(1)}, bf16[32,1536]{1,0:T(8,128)(2,1)S(1)}, u32[]{:S(2)}, u32[]{:S(2)}) %collective-permute-start.10) | collective-permute-done | bytes 98336 | tf_op jit(solution)/shard_map/ppermute | solution.py:24
  47.7 1.0 shard_map.103
  48.7 1.1 collective-permute-start.13
  49.8 2.2 %collective-permute-start.14 = (bf16[256,1536]{1,0:T(8,128)(2,1)S(1)}, bf16[256,1536]{1,0:T(8,128)(2,1)S(1)}, u32[]{:S(2)}, u32[]{:S(2)}) collective-permute-start(bf16[256,1536]{1,0:T(8,128)(2,1)S(1)} %bitcast.24), channel_id=1, source_target_pairs={{4,0},{8,4},{12,8},{0,12},{5,1},{9,5},{13,9},{1,13},{6,2},{10,6},{... | collective-permute-start | bytes 2359304 | tf_op jit(solution)/shard_map/ppermute | solution.py:24
  52.8 1.8 collective-permute-done.7.hidden_other
  55.3 7.0 %collective-permute-done.13.refs_0_ = bf16[256,1536]{1,0:T(8,128)(2,1)} collective-permute-done((bf16[256,1536]{1,0:T(8,128)(2,1)S(1)}, bf16[256,1536]{1,0:T(8,128)(2,1)}, u32[]{:S(2)}, u32[]{:S(2)}) %collective-permute-start.13) | collective-permute-done | bytes 786464 | tf_op jit(solution)/shard_map/ppermute | solution.py:28
  62.3 1.4 collective-permute-done.14.refs_1_
  63.7 0.9 copy-done.16
  65.3 3.8 %all-gather.2.cloned.1.call-done.go = bf16[1024,1536]{1,0:T(8,128)(2,1)} async-done(((bf16[128,1536]{1,0:T(8,128)(2,1)}), bf16[1024,1536]{1,0:T(8,128)(2,1)}) %all-gather.2.cloned.1.call-update) | async-done | bytes 3145744 | tf_op jit(solution)/shard_map/all_gather | solution.py:269
  69.0 4.6 %shard_map.104 = (f32[2,256,512]{2,1,0:T(8,128)S(1)}, bf16[2,256,512]{2,1,0:T(8,128)(2,1)S(1)}) custom-call(s32[4]{0:T(128)S(1)} %pad_add_fusion.place, bf16[1024,1536]{1,0:T(8,128)(2,1)} %all-gather.2.cloned.1.call-done.go, bf16[512,1536]{1,0:T(8,128)(2,1)} %w_down.1), custom_call_target="tpu_custom_call" | custom-call | tf_op jit(solution)/shard_map/pallas_call | solution.py:83
  73.7 1.9 %collective-permute-done.16 = bf16[2,256,512]{2,1,0:T(8,128)(2,1)S(1)} collective-permute-done((bf16[2,256,512]{2,1,0:T(8,128)(2,1)S(1)}, bf16[2,256,512]{2,1,0:T(8,128)(2,1)S(1)}, u32[]{:S(2)}, u32[]{:S(2)}) %collective-permute-start.16) | collective-permute-done | bytes 524320 | tf_op jit(solution)/shard_map/ppermute | solution.py:28
  75.8 2.2 %collective-permute-start.17 = (bf16[2,256,512]{2,1,0:T(8,128)(2,1)S(1)}, bf16[2,256,512]{2,1,0:T(8,128)(2,1)S(1)}, u32[]{:S(2)}, u32[]{:S(2)}) collective-permute-start(bf16[2,256,512]{2,1,0:T(8,128)(2,1)S(1)} %get-tuple-element.100), channel_id=1, source_target_pairs={{0,2},{2,0},{1,3},{3,1},{4,6},{6,4},{5,7},{7,5},{8,10},{10,8},{9,1... | collective-permute-start | bytes 1572872 | tf_op jit(solution)/shard_map/ppermute | solution.py:28
  78.0 2.0 %collective-permute-start.20 = (bf16[256,1536]{1,0:T(8,128)(2,1)S(1)}, bf16[256,1536]{1,0:T(8,128)(2,1)}, u32[]{:S(2)}, u32[]{:S(2)}) collective-permute-start(bf16[256,1536]{1,0:T(8,128)(2,1)S(1)} %bitcast.26), channel_id=1, source_target_pairs={{8,0},{12,4},{0,8},{4,12},{9,1},{13,5},{1,9},{5,13},{10,2},{14,6},... | collective-permute-start | bytes 2359304 | tf_op jit(solution)/shard_map/ppermute | solution.py:24
  80.0 4.2 %shard_map.105 = (bf16[64,1536]{1,0:T(8,128)(2,1)S(1)}, bf16[448,1536]{1,0:T(8,128)(2,1)S(1)}) custom-call(s32[4]{0:T(128)S(1)} %pad_add_fusion.place, bf16[2,256,512]{2,1,0:T(8,128)(2,1)S(1)} %fusion.4.hidden, bf16[2,256,512]{2,1,0:T(8,128)(2,1)S(1)} %copy-done.10, bf16[1024,1536]{1,0:T(8,128)(2,1)} %all-gather.2.cloned.1.call-done.go), custom_call_target="tpu_custom_call" | custom-call | tf_op jit(solution)/shard_map/pallas_call | solution.py:165
  84.2 1.1 copy-done.7
  85.3 6.1 %collective-permute-done.17.chip_far = bf16[2,256,512]{2,1,0:T(8,128)(2,1)S(1)} collective-permute-done((bf16[2,256,512]{2,1,0:T(8,128)(2,1)S(1)}, bf16[2,256,512]{2,1,0:T(8,128)(2,1)S(1)}, u32[]{:S(2)}, u32[]{:S(2)}) %collective-permute-start.17) | collective-permute-done | bytes 524320 | tf_op jit(solution)/shard_map/ppermute | solution.py:28
  94.7 5.4 %shard_map.107 = bf16[1024,1536]{1,0:T(8,128)(2,1)} custom-call(s32[4]{0:T(128)S(1)} %pad_add_fusion.place, bf16[2,256,512]{2,1,0:T(8,128)(2,1)S(1)} %get-tuple-element.69.near0.refs_4_, bf16[2,256,512]{2,1,0:T(8,128)(2,1)S(1)} %get-tuple-element.70.near1.refs_5_, bf16[2,256,512]{2,1,0:T(8,128)(2,1)S(1)} %collective-permute-done.18.other0.refs_6_, ...), custom_call_target="tpu_custom_call" | custom-call | tf_op jit(solution)/shard_map/pallas_call | solution.py:135
  100.8 2.0 %collective-permute-start.25 = (bf16[256,1536]{1,0:T(8,128)(2,1)}, bf16[256,1536]{1,0:T(8,128)(2,1)}, u32[]{:S(2)}, u32[]{:S(2)}) collective-permute-start(bf16[256,1536]{1,0:T(8,128)(2,1)} %collective-permute-done.13.refs_0_), channel_id=1, source_target_pairs={{4,0},{8,4},{12,8},{0,12},{5,1},{9,5},{13,9},{1,13},{6,2},{10,6},{... | collective-permute-start | bytes 2359304 | tf_op jit(solution)/shard_map/ppermute | solution.py:24
  103.5 1.4 collective-permute-start.23
  104.9 1.5 collective-permute-start.24
  106.4 14.4 %collective-permute-done.25.refs_1_ = bf16[256,1536]{1,0:T(8,128)(2,1)} collective-permute-done((bf16[256,1536]{1,0:T(8,128)(2,1)}, bf16[256,1536]{1,0:T(8,128)(2,1)}, u32[]{:S(2)}, u32[]{:S(2)}) %collective-permute-start.25) | collective-permute-done | bytes 786464 | tf_op jit(solution)/shard_map/ppermute | solution.py:24
  120.7 2.3 %collective-permute-start.22 = (bf16[256,1536]{1,0:T(8,128)(2,1)}, bf16[256,1536]{1,0:T(8,128)(2,1)}, u32[]{:S(2)}, u32[]{:S(2)}) collective-permute-start(bf16[256,1536]{1,0:T(8,128)(2,1)} %collective-permute-done.13.refs_0_), channel_id=1, source_target_pairs={{8,0},{12,4},{0,8},{4,12},{9,1},{13,5},{1,9},{5,13},{10,2},{14,6},... | collective-permute-start | bytes 2359304 | tf_op jit(solution)/shard_map/ppermute | solution.py:24
  123.0 7.5 %shard_map.108 = (bf16[1536,512]{1,0:T(8,128)(2,1)}, bf16[1536,512]{1,0:T(8,128)(2,1)}) custom-call(s32[4]{0:T(128)S(1)} %pad_add_fusion.place, bf16[256,1536]{1,0:T(8,128)(2,1)} %bitcast.27, bf16[256,1536]{1,0:T(8,128)(2,1)} %copy-done.16, bf16[256,1536]{1,0:T(8,128)(2,1)} %collective-permute-done.20.refs_2_, ...), custom_call_target="tpu_custom_call" | custom-call | tf_op jit(solution)/shard_map/pallas_call | solution.py:216
  130.5 15.8 %collective-permute-done.23.refs_3_.refs_1_ = bf16[2,256,512]{2,1,0:T(8,128)(2,1)S(1)} collective-permute-done((bf16[2,256,512]{2,1,0:T(8,128)(2,1)S(1)}, bf16[2,256,512]{2,1,0:T(8,128)(2,1)S(1)}, u32[]{:S(2)}, u32[]{:S(2)}) %collective-permute-start.23) | collective-permute-done | bytes 524320 | tf_op jit(solution)/shard_map/ppermute | solution.py:28
  146.8 1.4 collective-permute-done.27.refs_5_.refs_3_
  148.9 6.4 %shard_map.109 = (bf16[1536,512]{1,0:T(8,128)(2,1)S(1)}, bf16[1536,512]{1,0:T(8,128)(2,1)S(1)}) custom-call(s32[4]{0:T(128)S(1)} %pad_add_fusion.place, bf16[256,1536]{1,0:T(8,128)(2,1)} %collective-permute-done.13.refs_0_, bf16[256,1536]{1,0:T(8,128)(2,1)} %collective-permute-done.25.refs_1_, bf16[256,1536]{1,0:T(8,128)(2,1)} %copy-done.15, ...), custom_call_target="tpu_custom_call" | custom-call | tf_op jit(solution)/shard_map/pallas_call | solution.py:216
  155.3 1.1 copy-done.3
  156.4 1.1 copy-done.5
  157.6 1.1 dynamic-slice_bitcast_fusion
  158.7 3.0 %collective-permute-start.32 = (bf16[32,1536]{1,0:T(8,128)(2,1)S(1)}, bf16[32,1536]{1,0:T(8,128)(2,1)S(1)}, u32[]{:S(2)}, u32[]{:S(2)}) collective-permute-start(bf16[32,1536]{1,0:T(8,128)(2,1)S(1)} %get-tuple-element.92), channel_id=1, source_target_pairs={{4,0},{8,4},{12,8},{0,12},{5,1},{9,5},{13,9},{1,13},{6,2},{10,6},{... | collective-permute-start | bytes 294920 | tf_op jit(solution)/shard_map/ppermute | solution.py:24
  161.7 1.0 collective-permute-start.30
  162.7 0.9 copy-done.12
  163.6 0.9 copy-done.14
  164.5 3.5 %shard_map.111 = bf16[512,1536]{1,0:T(8,128)(2,1)} custom-call(bf16[64,1536]{1,0:T(8,128)(2,1)S(1)} %copy-done.12, bf16[64,1536]{1,0:T(8,128)(2,1)S(1)} %copy-done.14, bf16[448,1536]{1,0:T(8,128)(2,1)S(1)} %copy-done.8, bf16[448,1536]{1,0:T(8,128)(2,1)} %collective-permute-done.29.rest_far), custom_call_target="tpu_custom_call" | custom-call | tf_op jit(solution)/shard_map/pallas_call | solution.py:235
  168.1 5.4 %shard_map.110 = (bf16[1536,512]{1,0:T(8,128)(2,1)}, bf16[1536,512]{1,0:T(8,128)(2,1)}) custom-call(s32[4]{0:T(128)S(1)} %pad_add_fusion.place, bf16[256,1536]{1,0:T(8,128)(2,1)} %collective-permute-done.22.refs_0_, bf16[2,256,512]{2,1,0:T(8,128)(2,1)S(1)} %collective-permute-done.23.refs_3_.refs_1_, ...), custom_call_target="tpu_custom_call" | custom-call | tf_op jit(solution)/shard_map/pallas_call | solution.py:216
  (78 shorter events, 12.8 us)
Async XLA Ops:
  7.2 61.9 %all-gather.2.cloned.1.call-start = ((), (), s32[]{:S(2)}) async-start(), calls=%async_computation.1 | async-start | bytes 3538944 | tf_op jit(solution)/shard_map/all_gather | solution.py:269
  7.2 10.6 %collective-permute-start = (bf16[32,1536]{1,0:T(8,128)(2,1)}, bf16[32,1536]{1,0:T(8,128)(2,1)S(1)}, u32[]{:S(2)}, u32[]{:S(2)}) collective-permute-start(bf16[32,1536]{1,0:T(8,128)(2,1)} %refs_0_.1), channel_id=1, source_target_pairs={{4,0},{8,4},{12,8},{0,12},{5,1},{9,5},{13,9},{1,13},{6,2},{10,6},{... | collective-permute-start | bytes 294920 | tf_op jit(solution)/shard_map/ppermute | solution.py:24
  10.3 7.5 %collective-permute-start.1 = (bf16[32,1536]{1,0:T(8,128)(2,1)}, bf16[32,1536]{1,0:T(8,128)(2,1)S(1)}, u32[]{:S(2)}, u32[]{:S(2)}) collective-permute-start(bf16[32,1536]{1,0:T(8,128)(2,1)} %refs_0_.1), channel_id=1, source_target_pairs={{8,0},{12,4},{0,8},{4,12},{9,1},{13,5},{1,9},{5,13},{10,2},{14,6},... | collective-permute-start | bytes 294920 | tf_op jit(solution)/shard_map/ppermute | solution.py:24
  10.9 7.4 %collective-permute-start.2 = (bf16[32,1536]{1,0:T(8,128)(2,1)}, bf16[32,1536]{1,0:T(8,128)(2,1)S(1)}, u32[]{:S(2)}, u32[]{:S(2)}) collective-permute-start(bf16[32,1536]{1,0:T(8,128)(2,1)} %refs_0_.1), channel_id=1, source_target_pairs={{12,0},{0,4},{4,8},{8,12},{13,1},{1,5},{5,9},{9,13},{14,2},{2,6},{... | collective-permute-start | bytes 294920 | tf_op jit(solution)/shard_map/ppermute | solution.py:24
  11.9 8.4 %collective-permute-start.3 = (bf16[32,1536]{1,0:T(8,128)(2,1)}, bf16[32,1536]{1,0:T(8,128)(2,1)S(1)}, u32[]{:S(2)}, u32[]{:S(2)}) collective-permute-start(bf16[32,1536]{1,0:T(8,128)(2,1)} %refs_0_.2), channel_id=1, source_target_pairs={{16,0},{32,16},{48,32},{64,48},{80,64},{96,80},{112,96},{0,112},{1... | collective-permute-start | bytes 294920 | tf_op jit(solution)/shard_map/ppermute | solution.py:24
  17.8 6.0 %collective-permute-start.4 = (bf16[32,1536]{1,0:T(8,128)(2,1)}, bf16[32,1536]{1,0:T(8,128)(2,1)S(1)}, u32[]{:S(2)}, u32[]{:S(2)}) collective-permute-start(bf16[32,1536]{1,0:T(8,128)(2,1)} %refs_0_.2), channel_id=1, source_target_pairs={{112,0},{0,16},{16,32},{32,48},{48,64},{64,80},{80,96},{96,112},{1... | collective-permute-start | bytes 294920 | tf_op jit(solution)/shard_map/ppermute | solution.py:24
  25.5 26.5 %copy-start.17 = (bf16[256,512]{1,0:T(8,128)(2,1)S(1)}, bf16[256,512]{1,0:T(8,128)(2,1)}, u32[]{:S(2)}) copy-start(bf16[256,512]{1,0:T(8,128)(2,1)} %param.10) | copy-start | bytes 786436
  25.5 132.1 %reduce-scatter.2.cloned.1.call-start = ((), (), s32[]{:S(2)}) async-start(), calls=%async_computation.2 | async-start | bytes 3538944 | tf_op jit(solution)/shard_map/reduce_scatter | solution.py:296
  25.6 16.4 %collective-permute-start.5 = (bf16[256,512]{1,0:T(8,128)(2,1)}, bf16[256,512]{1,0:T(8,128)(2,1)S(1)}, u32[]{:S(2)}, u32[]{:S(2)}) collective-permute-start(bf16[256,512]{1,0:T(8,128)(2,1)} %param.9), channel_id=1, source_target_pairs={{0,2},{2,0},{1,3},{3,1},{4,6},{6,4},{5,7},{7,5},{8,10},{10,8},{9,1... | collective-permute-start | bytes 786440 | tf_op jit(solution)/shard_map/ppermute | solution.py:28
  27.8 5.6 %collective-permute-start.8 = (bf16[32,1536]{1,0:T(8,128)(2,1)S(1)}, bf16[32,1536]{1,0:T(8,128)(2,1)S(1)}, u32[]{:S(2)}, u32[]{:S(2)}) collective-permute-start(bf16[32,1536]{1,0:T(8,128)(2,1)S(1)} %collective-permute-done.3.refs_1_), channel_id=1, source_target_pairs={{16,0},{32,16},{48,32},{64,48},{80,64},{96,80},{112,96},{0,112},{1... | collective-permute-start | bytes 294920 | tf_op jit(solution)/shard_map/ppermute | solution.py:24
  28.2 7.2 %collective-permute-start.11 = (bf16[32,1536]{1,0:T(8,128)(2,1)S(1)}, bf16[32,1536]{1,0:T(8,128)(2,1)S(1)}, u32[]{:S(2)}, u32[]{:S(2)}) collective-permute-start(bf16[32,1536]{1,0:T(8,128)(2,1)S(1)} %collective-permute-done.4.refs_7_), channel_id=1, source_target_pairs={{112,0},{0,16},{16,32},{32,48},{48,64},{64,80},{80,96},{96,112},{1... | collective-permute-start | bytes 294920 | tf_op jit(solution)/shard_map/ppermute | solution.py:24
  33.4 7.7 %collective-permute-start.9 = (bf16[32,1536]{1,0:T(8,128)(2,1)S(1)}, bf16[32,1536]{1,0:T(8,128)(2,1)S(1)}, u32[]{:S(2)}, u32[]{:S(2)}) collective-permute-start(bf16[32,1536]{1,0:T(8,128)(2,1)S(1)} %collective-permute-done.8.refs_2_), channel_id=1, source_target_pairs={{16,0},{32,16},{48,32},{64,48},{80,64},{96,80},{112,96},{0,112},{1... | collective-permute-start | bytes 294920 | tf_op jit(solution)/shard_map/ppermute | solution.py:24
  34.0 17.9 %collective-permute-start.6 = (bf16[256,512]{1,0:T(8,128)(2,1)}, bf16[256,512]{1,0:T(8,128)(2,1)S(1)}, u32[]{:S(2)}, u32[]{:S(2)}) collective-permute-start(bf16[256,512]{1,0:T(8,128)(2,1)} %param.10), channel_id=1, source_target_pairs={{0,2},{2,0},{1,3},{3,1},{4,6},{6,4},{5,7},{7,5},{8,10},{10,8},{9,1... | collective-permute-start | bytes 786440 | tf_op jit(solution)/shard_map/ppermute | solution.py:28
  35.4 7.9 %collective-permute-start.12 = (bf16[32,1536]{1,0:T(8,128)(2,1)S(1)}, bf16[32,1536]{1,0:T(8,128)(2,1)S(1)}, u32[]{:S(2)}, u32[]{:S(2)}) collective-permute-start(bf16[32,1536]{1,0:T(8,128)(2,1)S(1)} %collective-permute-done.11.refs_6_), channel_id=1, source_target_pairs={{112,0},{0,16},{16,32},{32,48},{48,64},{64,80},{80,96},{96,112},{1... | collective-permute-start | bytes 294920 | tf_op jit(solution)/shard_map/ppermute | solution.py:24
  41.1 6.7 %collective-permute-start.10 = (bf16[32,1536]{1,0:T(8,128)(2,1)S(1)}, bf16[32,1536]{1,0:T(8,128)(2,1)S(1)}, u32[]{:S(2)}, u32[]{:S(2)}) collective-permute-start(bf16[32,1536]{1,0:T(8,128)(2,1)S(1)} %collective-permute-done.9.refs_3_), channel_id=1, source_target_pairs={{16,0},{32,16},{48,32},{64,48},{80,64},{96,80},{112,96},{0,112},{1... | collective-permute-start | bytes 294920 | tf_op jit(solution)/shard_map/ppermute | solution.py:24
  48.7 29.3 %copy-start = (bf16[8,32,1536]{2,1,0:T(8,128)(2,1)}, bf16[8,32,1536]{2,1,0:T(8,128)(2,1)S(1)}, u32[]{:S(2)}) copy-start(bf16[8,32,1536]{2,1,0:T(8,128)(2,1)S(1)} %shard_map.103) | copy-start | bytes 2359300
  48.7 13.6 %collective-permute-start.13 = (bf16[256,1536]{1,0:T(8,128)(2,1)S(1)}, bf16[256,1536]{1,0:T(8,128)(2,1)}, u32[]{:S(2)}, u32[]{:S(2)}) collective-permute-start(bf16[256,1536]{1,0:T(8,128)(2,1)S(1)} %bitcast.23), channel_id=1, source_target_pairs={{0,128},{128,0},{1,129},{129,1},{2,130},{130,2},{3,131},{131,3},{4... | collective-permute-start | bytes 2359304 | tf_op jit(solution)/shard_map/ppermute | solution.py:28
  49.8 13.8 %collective-permute-start.14 = (bf16[256,1536]{1,0:T(8,128)(2,1)S(1)}, bf16[256,1536]{1,0:T(8,128)(2,1)S(1)}, u32[]{:S(2)}, u32[]{:S(2)}) collective-permute-start(bf16[256,1536]{1,0:T(8,128)(2,1)S(1)} %bitcast.24), channel_id=1, source_target_pairs={{4,0},{8,4},{12,8},{0,12},{5,1},{9,5},{13,9},{1,13},{6,2},{10,6},{... | collective-permute-start | bytes 2359304 | tf_op jit(solution)/shard_map/ppermute | solution.py:24
  52.0 13.3 %collective-permute-start.15 = (bf16[256,1536]{1,0:T(8,128)(2,1)S(1)}, bf16[256,1536]{1,0:T(8,128)(2,1)}, u32[]{:S(2)}, u32[]{:S(2)}) collective-permute-start(bf16[256,1536]{1,0:T(8,128)(2,1)S(1)} %bitcast.25), channel_id=1, source_target_pairs={{12,0},{0,4},{4,8},{8,12},{13,1},{1,5},{5,9},{9,13},{14,2},{2,6},{... | collective-permute-start | bytes 2359304 | tf_op jit(solution)/shard_map/ppermute | solution.py:24
  52.4 2.2 %collective-permute-start.7 = (bf16[2,256,512]{2,1,0:T(8,128)(2,1)S(1)}, bf16[2,256,512]{2,1,0:T(8,128)(2,1)S(1)}, u32[]{:S(2)}, u32[]{:S(2)}) collective-permute-start(bf16[2,256,512]{2,1,0:T(8,128)(2,1)S(1)} %fusion.4.hidden), channel_id=1, source_target_pairs={{0,1},{1,0},{2,3},{3,2},{4,5},{5,4},{6,7},{7,6},{8,9},{9,8},{10,11... | collective-permute-start | bytes 1572872 | tf_op jit(solution)/shard_map/ppermute | solution.py:28
  73.6 2.0 %collective-permute-start.16 = (bf16[2,256,512]{2,1,0:T(8,128)(2,1)S(1)}, bf16[2,256,512]{2,1,0:T(8,128)(2,1)S(1)}, u32[]{:S(2)}, u32[]{:S(2)}) collective-permute-start(bf16[2,256,512]{2,1,0:T(8,128)(2,1)S(1)} %get-tuple-element.60), channel_id=1, source_target_pairs={{0,1},{1,0},{2,3},{3,2},{4,5},{5,4},{6,7},{7,6},{8,9},{9,8},{10,11... | collective-permute-start | bytes 1572872 | tf_op jit(solution)/shard_map/ppermute | solution.py:28
  75.6 4.3 %copy-start.10 = (bf16[2,256,512]{2,1,0:T(8,128)(2,1)S(1)}, bf16[2,256,512]{2,1,0:T(8,128)(2,1)}, u32[]{:S(2)}) copy-start(bf16[2,256,512]{2,1,0:T(8,128)(2,1)} %copy-done.9) | copy-start | bytes 1572868
  75.8 15.6 %collective-permute-start.17 = (bf16[2,256,512]{2,1,0:T(8,128)(2,1)S(1)}, bf16[2,256,512]{2,1,0:T(8,128)(2,1)S(1)}, u32[]{:S(2)}, u32[]{:S(2)}) collective-permute-start(bf16[2,256,512]{2,1,0:T(8,128)(2,1)S(1)} %get-tuple-element.100), channel_id=1, source_target_pairs={{0,2},{2,0},{1,3},{3,1},{4,6},{6,4},{5,7},{7,5},{8,10},{10,8},{9,1... | collective-permute-start | bytes 1572872 | tf_op jit(solution)/shard_map/ppermute | solution.py:28
  78.0 22.2 %collective-permute-start.20 = (bf16[256,1536]{1,0:T(8,128)(2,1)S(1)}, bf16[256,1536]{1,0:T(8,128)(2,1)}, u32[]{:S(2)}, u32[]{:S(2)}) collective-permute-start(bf16[256,1536]{1,0:T(8,128)(2,1)S(1)} %bitcast.26), channel_id=1, source_target_pairs={{8,0},{12,4},{0,8},{4,12},{9,1},{13,5},{1,9},{5,13},{10,2},{14,6},... | collective-permute-start | bytes 2359304 | tf_op jit(solution)/shard_map/ppermute | solution.py:24
  80.0 14.7 %copy-start.2 = (bf16[1536,512]{1,0:T(8,128)(2,1)S(1)}, bf16[1536,512]{1,0:T(8,128)(2,1)}, u32[]{:S(2)}) copy-start(bf16[1536,512]{1,0:T(8,128)(2,1)} %w_up.1) | copy-start | bytes 4718596
  84.2 1.1 copy-start.7
  85.3 14.9 %copy-start.11 = (bf16[64,1536]{1,0:T(8,128)(2,1)}, bf16[64,1536]{1,0:T(8,128)(2,1)S(1)}, u32[]{:S(2)}) copy-start(bf16[64,1536]{1,0:T(8,128)(2,1)S(1)} %get-tuple-element.72.first) | copy-start | bytes 589828
  85.3 9.4 %copy-start.1 = (bf16[1536,512]{1,0:T(8,128)(2,1)S(1)}, bf16[1536,512]{1,0:T(8,128)(2,1)}, u32[]{:S(2)}) copy-start(bf16[1536,512]{1,0:T(8,128)(2,1)} %w_gate.1) | copy-start | bytes 4718596
  92.0 2.0 %collective-permute-start.18 = (bf16[2,256,512]{2,1,0:T(8,128)(2,1)S(1)}, bf16[2,256,512]{2,1,0:T(8,128)(2,1)S(1)}, u32[]{:S(2)}, u32[]{:S(2)}) collective-permute-start(bf16[2,256,512]{2,1,0:T(8,128)(2,1)S(1)} %get-tuple-element.69.near0.refs_4_), channel_id=1, source_target_pairs={{0,1},{1,0},{2,3},{3,2},{4,5},{5,4},{6,7},{7,6},{8,9},{9,8},{10,11... | collective-permute-start | bytes 1572872 | tf_op jit(solution)/shard_map/ppermute | solution.py:28
  92.1 2.6 %collective-permute-start.19 = (bf16[2,256,512]{2,1,0:T(8,128)(2,1)S(1)}, bf16[2,256,512]{2,1,0:T(8,128)(2,1)S(1)}, u32[]{:S(2)}, u32[]{:S(2)}) collective-permute-start(bf16[2,256,512]{2,1,0:T(8,128)(2,1)S(1)} %get-tuple-element.70.near1.refs_5_), channel_id=1, source_target_pairs={{0,1},{1,0},{2,3},{3,2},{4,5},{5,4},{6,7},{7,6},{8,9},{9,8},{10,11... | collective-permute-start | bytes 1572872 | tf_op jit(solution)/shard_map/ppermute | solution.py:28
  92.6 7.6 %collective-permute-start.21 = (bf16[64,1536]{1,0:T(8,128)(2,1)S(1)}, bf16[64,1536]{1,0:T(8,128)(2,1)S(1)}, u32[]{:S(2)}, u32[]{:S(2)}) collective-permute-start(bf16[64,1536]{1,0:T(8,128)(2,1)S(1)} %get-tuple-element.72.first), channel_id=1, source_target_pairs={{0,128},{128,0},{1,129},{129,1},{2,130},{130,2},{3,131},{131,3},{4... | collective-permute-start | bytes 589832 | tf_op jit(solution)/shard_map/ppermute | solution.py:28
  100.8 19.9 %collective-permute-start.25 = (bf16[256,1536]{1,0:T(8,128)(2,1)}, bf16[256,1536]{1,0:T(8,128)(2,1)}, u32[]{:S(2)}, u32[]{:S(2)}) collective-permute-start(bf16[256,1536]{1,0:T(8,128)(2,1)} %collective-permute-done.13.refs_0_), channel_id=1, source_target_pairs={{4,0},{8,4},{12,8},{0,12},{5,1},{9,5},{13,9},{1,13},{6,2},{10,6},{... | collective-permute-start | bytes 2359304 | tf_op jit(solution)/shard_map/ppermute | solution.py:24
  102.8 27.6 %collective-permute-start.26 = (bf16[256,1536]{1,0:T(8,128)(2,1)}, bf16[256,1536]{1,0:T(8,128)(2,1)S(1)}, u32[]{:S(2)}, u32[]{:S(2)}) collective-permute-start(bf16[256,1536]{1,0:T(8,128)(2,1)} %collective-permute-done.13.refs_0_), channel_id=1, source_target_pairs={{12,0},{0,4},{4,8},{8,12},{13,1},{1,5},{5,9},{9,13},{14,2},{2,6},{... | collective-permute-start | bytes 2359304 | tf_op jit(solution)/shard_map/ppermute | solution.py:24
  102.9 55.8 %collective-permute-start.29 = (bf16[448,1536]{1,0:T(8,128)(2,1)}, bf16[448,1536]{1,0:T(8,128)(2,1)}, u32[]{:S(2)}, u32[]{:S(2)}) collective-permute-start(bf16[448,1536]{1,0:T(8,128)(2,1)} %copy-done.7), channel_id=1, source_target_pairs={{0,128},{128,0},{1,129},{129,1},{2,130},{130,2},{3,131},{131,3},{4... | collective-permute-start | bytes 4128776 | tf_op jit(solution)/shard_map/ppermute | solution.py:28
  103.5 42.8 %collective-permute-start.23 = (bf16[2,256,512]{2,1,0:T(8,128)(2,1)S(1)}, bf16[2,256,512]{2,1,0:T(8,128)(2,1)S(1)}, u32[]{:S(2)}, u32[]{:S(2)}) collective-permute-start(bf16[2,256,512]{2,1,0:T(8,128)(2,1)S(1)} %get-tuple-element.69.near0.refs_4_), channel_id=1, source_target_pairs={{0,128},{128,0},{1,129},{129,1},{2,130},{130,2},{3,131},{131,3},{4... | collective-permute-start | bytes 1572872 | tf_op jit(solution)/shard_map/ppermute | solution.py:28
  104.9 41.4 %collective-permute-start.24 = (bf16[2,256,512]{2,1,0:T(8,128)(2,1)S(1)}, bf16[2,256,512]{2,1,0:T(8,128)(2,1)S(1)}, u32[]{:S(2)}, u32[]{:S(2)}) collective-permute-start(bf16[2,256,512]{2,1,0:T(8,128)(2,1)S(1)} %get-tuple-element.70.near1.refs_5_), channel_id=1, source_target_pairs={{0,130},{130,0},{2,128},{128,2},{1,131},{131,1},{3,129},{129,3},{4... | collective-permute-start | bytes 1572872 | tf_op jit(solution)/shard_map/ppermute | solution.py:298
  120.7 37.9 %collective-permute-start.22 = (bf16[256,1536]{1,0:T(8,128)(2,1)}, bf16[256,1536]{1,0:T(8,128)(2,1)}, u32[]{:S(2)}, u32[]{:S(2)}) collective-permute-start(bf16[256,1536]{1,0:T(8,128)(2,1)} %collective-permute-done.13.refs_0_), channel_id=1, source_target_pairs={{8,0},{12,4},{0,8},{4,12},{9,1},{13,5},{1,9},{5,13},{10,2},{14,6},... | collective-permute-start | bytes 2359304 | tf_op jit(solution)/shard_map/ppermute | solution.py:24
  130.5 15.8 %copy-start.15 = (bf16[256,1536]{1,0:T(8,128)(2,1)}, bf16[256,1536]{1,0:T(8,128)(2,1)S(1)}, u32[]{:S(2)}) copy-start(bf16[256,1536]{1,0:T(8,128)(2,1)S(1)} %collective-permute-done.26.refs_2_) | copy-start | bytes 2359300
  146.2 1.9 %collective-permute-start.27 = (bf16[2,256,512]{2,1,0:T(8,128)(2,1)S(1)}, bf16[2,256,512]{2,1,0:T(8,128)(2,1)S(1)}, u32[]{:S(2)}, u32[]{:S(2)}) collective-permute-start(bf16[2,256,512]{2,1,0:T(8,128)(2,1)S(1)} %collective-permute-done.23.refs_3_.refs_1_), channel_id=1, source_target_pairs={{0,1},{1,0},{2,3},{3,2},{4,5},{5,4},{6,7},{7,6},{8,9},{9,8},{10,11... | collective-permute-start | bytes 1572872 | tf_op jit(solution)/shard_map/ppermute | solution.py:28
  146.2 2.7 %collective-permute-start.28 = (bf16[2,256,512]{2,1,0:T(8,128)(2,1)S(1)}, bf16[2,256,512]{2,1,0:T(8,128)(2,1)S(1)}, u32[]{:S(2)}, u32[]{:S(2)}) collective-permute-start(bf16[2,256,512]{2,1,0:T(8,128)(2,1)S(1)} %collective-permute-done.24.refs_4_.refs_2_), channel_id=1, source_target_pairs={{0,1},{1,0},{2,3},{3,2},{4,5},{5,4},{6,7},{7,6},{8,9},{9,8},{10,11... | collective-permute-start | bytes 1572872 | tf_op jit(solution)/shard_map/ppermute | solution.py:28
  148.9 13.8 %copy-start.8 = (bf16[448,1536]{1,0:T(8,128)(2,1)S(1)}, bf16[448,1536]{1,0:T(8,128)(2,1)}, u32[]{:S(2)}) copy-start(bf16[448,1536]{1,0:T(8,128)(2,1)} %copy-done.7) | copy-start | bytes 4128772
  155.3 1.1 copy-start.3
  156.4 1.1 copy-start.5
  158.7 9.4 %copy-start.4 = (bf16[1536,512]{1,0:T(8,128)(2,1)S(1)}, bf16[1536,512]{1,0:T(8,128)(2,1)}, u32[]{:S(2)}) copy-start(bf16[1536,512]{1,0:T(8,128)(2,1)} %copy-done.3) | copy-start | bytes 4718596
  158.7 9.4 %copy-start.6 = (bf16[1536,512]{1,0:T(8,128)(2,1)S(1)}, bf16[1536,512]{1,0:T(8,128)(2,1)}, u32[]{:S(2)}) copy-start(bf16[1536,512]{1,0:T(8,128)(2,1)} %copy-done.5) | copy-start | bytes 4718596
  158.7 14.7 %collective-permute-start.32 = (bf16[32,1536]{1,0:T(8,128)(2,1)S(1)}, bf16[32,1536]{1,0:T(8,128)(2,1)S(1)}, u32[]{:S(2)}, u32[]{:S(2)}) collective-permute-start(bf16[32,1536]{1,0:T(8,128)(2,1)S(1)} %get-tuple-element.92), channel_id=1, source_target_pairs={{4,0},{8,4},{12,8},{0,12},{5,1},{9,5},{13,9},{1,13},{6,2},{10,6},{... | collective-permute-start | bytes 294920 | tf_op jit(solution)/shard_map/ppermute | solution.py:24
  161.7 11.7 %collective-permute-start.31 = (bf16[32,1536]{1,0:T(8,128)(2,1)S(1)}, bf16[32,1536]{1,0:T(8,128)(2,1)S(1)}, u32[]{:S(2)}, u32[]{:S(2)}) collective-permute-start(bf16[32,1536]{1,0:T(8,128)(2,1)S(1)} %get-tuple-element.91), channel_id=1, source_target_pairs={{8,0},{12,4},{0,8},{4,12},{9,1},{13,5},{1,9},{5,13},{10,2},{14,6},... | collective-permute-start | bytes 294920 | tf_op jit(solution)/shard_map/ppermute | solution.py:24
  161.7 11.7 %collective-permute-start.30 = (bf16[32,1536]{1,0:T(8,128)(2,1)S(1)}, bf16[32,1536]{1,0:T(8,128)(2,1)S(1)}, u32[]{:S(2)}, u32[]{:S(2)}) collective-permute-start(bf16[32,1536]{1,0:T(8,128)(2,1)S(1)} %get-tuple-element.90), channel_id=1, source_target_pairs={{12,0},{0,4},{4,8},{8,12},{13,1},{1,5},{5,9},{9,13},{14,2},{2,6},{... | collective-permute-start | bytes 294920 | tf_op jit(solution)/shard_map/ppermute | solution.py:24
  (5 other events, 4.3 us)
Sparse Core Ops, SparseCore 0:
  25.6 43.3 all-gather.1
  100.3 44.3 reduce-scatter.1

commit v9 on v8

--- a/solution.py
+++ b/solution.py
@@ -34,10 +34,6 @@
 
 def in_hbm(x):
     return pltpu.with_memory_space_constraint(x, pltpu.HBM)
-
-
-def in_vmem(x):
-    return pltpu.with_memory_space_constraint(x, pltpu.VMEM)
 
 
 def arrange_kernel(n, slot, place, *refs):
@@ -196,7 +192,7 @@
                     rows[index, z, :, :512] = grads[half][0, lines, :]
                     rows[index, z, :, 512:] = grads[half][1, lines, :]
 
-    total = jnp.zeros((256, 1024), F32)
+    total = jnp.zeros((d_gate.shape[0], 1024), F32)
     for index, piece in enumerate(pieces):
         total = total + dot(piece[...], rows[index].reshape(256, 1024), 0, 0)
     gate, up = total[:, :512], total[:, 512:]
@@ -207,21 +203,20 @@
     d_up[...] = up.astype(BF16)
 
 
-def weight_grads(place, slots, pieces, grads, base=(), last=False, held=False):
-    piece = pl.BlockSpec((256, 256), lambda i: (0, i))
-    tile = pl.BlockSpec((256, 512), lambda i: (i, 0))
-    space = pltpu.VMEM if held else pltpu.HBM
-    shape = jax.ShapeDtypeStruct((1536, 512), BF16) if last else space((1536, 512), BF16)
-    hold = in_vmem if last else in_hbm
+def weight_grads(place, slots, pieces, grads, base=(), last=False):
+    size = 512 if last else 256
+    piece = pl.BlockSpec((256, size), lambda i: (0, i))
+    tile = pl.BlockSpec((size, 512), lambda i: (i, 0))
+    shape = jax.ShapeDtypeStruct((1536, 512), BF16) if last else pltpu.HBM((1536, 512), BF16)
     return pl.pallas_call(
         functools.partial(weight_kernel, slots, bool(base)),
-        grid=(6,),
+        grid=(1536 // size,),
         out_shape=(shape, shape),
         in_specs=[SMEM] + [piece] * len(slots) + [VMEM] * 4 + [tile] * len(base),
         out_specs=(tile, tile),
         scratch_shapes=[pltpu.VMEM((len(slots), NZ, 32, 1024), BF16)],
         compiler_params=grant(16),
-    )(place, *(x if last else in_hbm(x) for x in pieces), *grads, *(hold(x) for x in base))
+    )(place, *(x if last else in_hbm(x) for x in pieces), *grads, *(in_hbm(x) for x in base))
 
 
 def add_kernel(first, first_far, rest, rest_far, out):
@@ -239,7 +234,7 @@
         in_specs=[top, top, low, low],
         out_specs=pl.BlockSpec((512, 512), lambda i: (0, i)),
         compiler_params=grant(8),
-    )(*(in_vmem(x) for x in parts))
+    )(*parts)
 
 
 def ring(x, up, down, axis, n):
@@ -297,21 +292,23 @@
 
     far = [swap(near[0], "dp"), lax.ppermute(near[1], ("dp", "xh"), [(0, 3), (3, 0), (1, 2), (2, 1)])]
     partner1, partner2, partner3 = (from_ahead(partner_z, "y", NY, k) for k in (1, 2, 3))
+    far, down_rest = lax.optimization_barrier((far, down_rest))
+    rest_far = swap(down_rest, "dp")
+    own_z, partner1, partner3 = lax.optimization_barrier((own_z, partner1, partner3))
     own_gate, own_up = weight_grads(place, (0, 1, 2, 3), (own_z, own1, own2, own3), (*near, *other))
-    rest_far = swap(down_rest, "dp")
-    far, own_gate, own_up, partner1, partner3 = lax.optimization_barrier((far, own_gate, own_up, partner1, partner3))
     far_other = [swap(half, "core") for half in far]
 
     y = place[1]
     slabs = [lax.dynamic_index_in_dim(in_z, (y + k) % NY, 0, keepdims=False) for k in range(NY)]
     grads = (*far, *far_other)
-    most = weight_grads(place, (0, 1, 3), (partner_z, partner1, partner3), grads, (own_gate, own_up), held=True)
-    slabs, partner2, most, rest_far = lax.optimization_barrier((slabs, partner2, most, rest_far))
+    most = weight_grads(place, (0, 1, 3), (partner_z, partner1, partner3), grads, (own_gate, own_up))
+    slabs, partner2, most = lax.optimization_barrier((slabs, partner2, most))
     total = slabs[0].astype(F32)
     for k in range(1, NY):
         total = total + from_ahead(slabs[k], "y", NY, NY - k).astype(F32)
     grad_input = total.astype(BF16)
     grad_gate, grad_up = weight_grads(place, (2,), (partner2,), grads, most, last=True)
+    grad_input, grad_gate, grad_up, rest_far = lax.optimization_barrier((grad_input, grad_gate, grad_up, rest_far))
     return grad_input, grad_gate, grad_up, add(down_first, first_far, down_rest, rest_far)
 
 

time: 183 us -> 179 us (0.978)
  local copies, waits for them, and re-layouts: 8.68 us -> 3.1 us
  Pallas kernels: 40.2 us -> 42.2 us
    ppermute x19, waiting for transfers between devices: 35 us -> 42.6 us  [from_ahead(): return lax.ppermute(x, axis, [((d + k) % n, d) for d in range(n)])]
    ppermute x13, waiting for transfers between devices: 36.3 us -> 29.7 us  [swap(): return lax.ppermute(x, axis, [(0, 1), (1, 0)])]
    unnamed x36 -> x14, local copies, waits for them, and re-layouts: 7.62 us -> 2.03 us
  transfers between devices with their start and end apart: 35 -> 35, of which waited for: 20 -> 20; matrix products, arithmetic and copies ran while one was open for 1% -> 2% of each run, Pallas kernels for 19% -> 18%
where the time goes in v9:
time: 179 us; the launch traced here: 178 us
  waiting for transfers between devices  76.5 us (43%)
  Pallas kernels  42.2 us (24%)
  starting transfers between devices  39.6 us (22%)
  between operations  14.2 us (8%)
  local copies, waits for them, and re-layouts  3.1 us (2%)
  other arithmetic  2.44 us (1%)
    ppermute x19, waiting for transfers between devices, from_ahead(): return lax.ppermute(x, axis, [((d + k) % n, d) for d in range(n)])  42.6 us
    ppermute x13, waiting for transfers between devices, swap(): return lax.ppermute(x, axis, [(0, 1), (1, 0)])  29.7 us
    ppermute x19, starting transfers between devices, from_ahead(): return lax.ppermute(x, axis, [((d + k) % n, d) for d in range(n)])  26.2 us
    pallas_call x3, Pallas kernels, weight_grads(): pl.pallas_call(functools.partial(weight_kernel, slots, bool(base)), grid=...  20.7 us
    ppermute x13, starting transfers between devices, swap(): return lax.ppermute(x, axis, [(0, 1), (1, 0)])  11.6 us
    pallas_call x1, Pallas kernels, input_grad(): pl.pallas_call(input_grad_kernel, grid=(3,), out_shape=jax.ShapeDtypeStru...  5.48 us
    pallas_call x1, Pallas kernels, down_grad(): pl.pallas_call(down_kernel, grid=(3,), out_shape=(jax.ShapeDtypeStruct((F...  4.68 us
    pallas_call x1, Pallas kernels, hidden_grad(): pl.pallas_call(hidden_grad_kernel, out_shape=(jax.ShapeDtypeStruct((2, 25...  4.58 us
  transfers between devices with their start and end apart: 35, of which 20 were waited for; matrix products, arithmetic and copies ran while one was open for 2% of the time, Pallas kernels for 18%

profile of v9, /device:TPU:2, one launch (start us, length us, event | category | flops | bytes accessed | tf_op | source)
XLA Modules:
  0.0 178.0 jit_solution(9962769579439814227)
XLA Ops:
  7.2 3.1 %collective-permute-start = (bf16[32,1536]{1,0:T(8,128)(2,1)}, bf16[32,1536]{1,0:T(8,128)(2,1)S(1)}, u32[]{:S(2)}, u32[]{:S(2)}) collective-permute-start(bf16[32,1536]{1,0:T(8,128)(2,1)} %refs_0_.1), channel_id=1, source_target_pairs={{4,0},{8,4},{12,8},{0,12},{5,1},{9,5},{13,9},{1,13},{6,2},{10,6},{... | collective-permute-start | bytes 294920 | tf_op jit(solution)/shard_map/ppermute | solution.py:24
  10.9 1.0 collective-permute-start.2
  11.9 5.9 %collective-permute-start.3 = (bf16[32,1536]{1,0:T(8,128)(2,1)}, bf16[32,1536]{1,0:T(8,128)(2,1)S(1)}, u32[]{:S(2)}, u32[]{:S(2)}) collective-permute-start(bf16[32,1536]{1,0:T(8,128)(2,1)} %refs_0_.2), channel_id=1, source_target_pairs={{16,0},{32,16},{48,32},{64,48},{80,64},{96,80},{112,96},{0,112},{1... | collective-permute-start | bytes 294920 | tf_op jit(solution)/shard_map/ppermute | solution.py:24
  18.4 1.9 %collective-permute-done.3.refs_1_ = bf16[32,1536]{1,0:T(8,128)(2,1)S(1)} collective-permute-done((bf16[32,1536]{1,0:T(8,128)(2,1)}, bf16[32,1536]{1,0:T(8,128)(2,1)S(1)}, u32[]{:S(2)}, u32[]{:S(2)}) %collective-permute-start.3) | collective-permute-done | bytes 98336 | tf_op jit(solution)/shard_map/ppermute | solution.py:24
  20.3 3.5 %collective-permute-done.4.refs_7_ = bf16[32,1536]{1,0:T(8,128)(2,1)S(1)} collective-permute-done((bf16[32,1536]{1,0:T(8,128)(2,1)}, bf16[32,1536]{1,0:T(8,128)(2,1)S(1)}, u32[]{:S(2)}, u32[]{:S(2)}) %collective-permute-start.4) | collective-permute-done | bytes 98336 | tf_op jit(solution)/shard_map/ppermute | solution.py:24
  23.8 1.7 shard_map.102
  25.6 2.2 %collective-permute-start.6 = (bf16[256,512]{1,0:T(8,128)(2,1)}, bf16[256,512]{1,0:T(8,128)(2,1)S(1)}, u32[]{:S(2)}, u32[]{:S(2)}) collective-permute-start(bf16[256,512]{1,0:T(8,128)(2,1)} %param.10), channel_id=1, source_target_pairs={{0,2},{2,0},{1,3},{3,1},{4,6},{6,4},{5,7},{7,5},{8,10},{10,8},{9,1... | collective-permute-start | bytes 786440 | tf_op jit(solution)/shard_map/ppermute | solution.py:28
  28.2 1.6 collective-permute-start.11
  29.8 3.6 %collective-permute-done.8.refs_2_ = bf16[32,1536]{1,0:T(8,128)(2,1)S(1)} collective-permute-done((bf16[32,1536]{1,0:T(8,128)(2,1)S(1)}, bf16[32,1536]{1,0:T(8,128)(2,1)S(1)}, u32[]{:S(2)}, u32[]{:S(2)}) %collective-permute-start.8) | collective-permute-done | bytes 98336 | tf_op jit(solution)/shard_map/ppermute | solution.py:24
  34.0 1.4 collective-permute-start.5
  35.4 1.4 collective-permute-start.12
  36.8 4.2 %collective-permute-done.9.refs_3_ = bf16[32,1536]{1,0:T(8,128)(2,1)S(1)} collective-permute-done((bf16[32,1536]{1,0:T(8,128)(2,1)S(1)}, bf16[32,1536]{1,0:T(8,128)(2,1)S(1)}, u32[]{:S(2)}, u32[]{:S(2)}) %collective-permute-start.9) | collective-permute-done | bytes 98336 | tf_op jit(solution)/shard_map/ppermute | solution.py:24
  41.1 0.9 collective-permute-start.10
  42.0 1.0 select_bitcast_fusion.1
  43.4 4.4 %collective-permute-done.10.refs_4_ = bf16[32,1536]{1,0:T(8,128)(2,1)S(1)} collective-permute-done((bf16[32,1536]{1,0:T(8,128)(2,1)S(1)}, bf16[32,1536]{1,0:T(8,128)(2,1)S(1)}, u32[]{:S(2)}, u32[]{:S(2)}) %collective-permute-start.10) | collective-permute-done | bytes 98336 | tf_op jit(solution)/shard_map/ppermute | solution.py:24
  47.7 1.0 shard_map.103
  48.7 1.1 collective-permute-start.13
  49.8 2.2 %collective-permute-start.14 = (bf16[256,1536]{1,0:T(8,128)(2,1)S(1)}, bf16[256,1536]{1,0:T(8,128)(2,1)S(1)}, u32[]{:S(2)}, u32[]{:S(2)}) collective-permute-start(bf16[256,1536]{1,0:T(8,128)(2,1)S(1)} %bitcast.24), channel_id=1, source_target_pairs={{4,0},{8,4},{12,8},{0,12},{5,1},{9,5},{13,9},{1,13},{6,2},{10,6},{... | collective-permute-start | bytes 2359304 | tf_op jit(solution)/shard_map/ppermute | solution.py:24
  52.8 1.8 %collective-permute-done.7.hidden_other = bf16[2,256,512]{2,1,0:T(8,128)(2,1)S(1)} collective-permute-done((bf16[2,256,512]{2,1,0:T(8,128)(2,1)S(1)}, bf16[2,256,512]{2,1,0:T(8,128)(2,1)S(1)}, u32[]{:S(2)}, u32[]{:S(2)}) %collective-permute-start.7) | collective-permute-done | bytes 524320 | tf_op jit(solution)/shard_map/ppermute | solution.py:28
  54.5 7.8 %collective-permute-done.13.refs_0_ = bf16[256,1536]{1,0:T(8,128)(2,1)} collective-permute-done((bf16[256,1536]{1,0:T(8,128)(2,1)S(1)}, bf16[256,1536]{1,0:T(8,128)(2,1)}, u32[]{:S(2)}, u32[]{:S(2)}) %collective-permute-start.13) | collective-permute-done | bytes 786464 | tf_op jit(solution)/shard_map/ppermute | solution.py:28
  62.3 1.4 collective-permute-done.14.refs_1_
  63.7 0.9 copy-done.5
  64.6 0.7 collective-permute-done.15.refs_3_
  65.3 3.8 %all-gather.2.cloned.1.call-done.go = bf16[1024,1536]{1,0:T(8,128)(2,1)} async-done(((bf16[128,1536]{1,0:T(8,128)(2,1)}), bf16[1024,1536]{1,0:T(8,128)(2,1)}) %all-gather.2.cloned.1.call-update) | async-done | bytes 3145744 | tf_op jit(solution)/shard_map/all_gather | solution.py:264
  69.0 4.6 %shard_map.104 = (f32[2,256,512]{2,1,0:T(8,128)S(1)}, bf16[2,256,512]{2,1,0:T(8,128)(2,1)S(1)}) custom-call(s32[4]{0:T(128)S(1)} %pad_add_fusion.place, bf16[1024,1536]{1,0:T(8,128)(2,1)} %all-gather.2.cloned.1.call-done.go, bf16[512,1536]{1,0:T(8,128)(2,1)} %w_down.1), custom_call_target="tpu_custom_call" | custom-call | tf_op jit(solution)/shard_map/pallas_call | solution.py:79
  73.7 1.9 %collective-permute-done.16 = bf16[2,256,512]{2,1,0:T(8,128)(2,1)S(1)} collective-permute-done((bf16[2,256,512]{2,1,0:T(8,128)(2,1)S(1)}, bf16[2,256,512]{2,1,0:T(8,128)(2,1)S(1)}, u32[]{:S(2)}, u32[]{:S(2)}) %collective-permute-start.16) | collective-permute-done | bytes 524320 | tf_op jit(solution)/shard_map/ppermute | solution.py:28
  75.8 2.2 %collective-permute-start.17 = (bf16[2,256,512]{2,1,0:T(8,128)(2,1)S(1)}, bf16[2,256,512]{2,1,0:T(8,128)(2,1)S(1)}, u32[]{:S(2)}, u32[]{:S(2)}) collective-permute-start(bf16[2,256,512]{2,1,0:T(8,128)(2,1)S(1)} %get-tuple-element.106), channel_id=1, source_target_pairs={{0,2},{2,0},{1,3},{3,1},{4,6},{6,4},{5,7},{7,5},{8,10},{10,8},{9,1... | collective-permute-start | bytes 1572872 | tf_op jit(solution)/shard_map/ppermute | solution.py:28
  78.0 2.0 %collective-permute-start.20 = (bf16[256,1536]{1,0:T(8,128)(2,1)S(1)}, bf16[256,1536]{1,0:T(8,128)(2,1)}, u32[]{:S(2)}, u32[]{:S(2)}) collective-permute-start(bf16[256,1536]{1,0:T(8,128)(2,1)S(1)} %bitcast.26), channel_id=1, source_target_pairs={{8,0},{12,4},{0,8},{4,12},{9,1},{13,5},{1,9},{5,13},{10,2},{14,6},... | collective-permute-start | bytes 2359304 | tf_op jit(solution)/shard_map/ppermute | solution.py:24
  80.0 4.7 %shard_map.105 = (bf16[64,1536]{1,0:T(8,128)(2,1)}, bf16[448,1536]{1,0:T(8,128)(2,1)S(1)}) custom-call(s32[4]{0:T(128)S(1)} %pad_add_fusion.place, bf16[2,256,512]{2,1,0:T(8,128)(2,1)S(1)} %fusion.4.hidden, bf16[2,256,512]{2,1,0:T(8,128)(2,1)S(1)} %collective-permute-done.7.hidden_other, bf16[1024,1536]{1,0:T(8,128)(2,1)} %all-gather.2.cloned.1.call-done.go), custom_call_target="tpu_custom_call" | custom-call | tf_op jit(solution)/shard_map/pallas_call | solution.py:161
  84.6 1.1 copy-done.3
  85.8 5.6 %collective-permute-done.17.chip_far = bf16[2,256,512]{2,1,0:T(8,128)(2,1)S(1)} collective-permute-done((bf16[2,256,512]{2,1,0:T(8,128)(2,1)S(1)}, bf16[2,256,512]{2,1,0:T(8,128)(2,1)S(1)}, u32[]{:S(2)}, u32[]{:S(2)}) %collective-permute-start.17) | collective-permute-done | bytes 524320 | tf_op jit(solution)/shard_map/ppermute | solution.py:28
  93.1 0.8 collective-permute-done.18.other0.refs_6_
  94.0 0.7 collective-permute-done.19.other1.refs_7_
  94.7 5.5 %shard_map.107 = bf16[1024,1536]{1,0:T(8,128)(2,1)} custom-call(s32[4]{0:T(128)S(1)} %pad_add_fusion.place, bf16[2,256,512]{2,1,0:T(8,128)(2,1)S(1)} %get-tuple-element.72.near0.refs_4_, bf16[2,256,512]{2,1,0:T(8,128)(2,1)S(1)} %get-tuple-element.73.near1.refs_5_, bf16[2,256,512]{2,1,0:T(8,128)(2,1)S(1)} %collective-permute-done.18.other0.refs_6_, ...), custom_call_target="tpu_custom_call" | custom-call | tf_op jit(solution)/shard_map/pallas_call | solution.py:131
  100.2 2.1 %collective-permute-start.23 = (bf16[256,1536]{1,0:T(8,128)(2,1)}, bf16[256,1536]{1,0:T(8,128)(2,1)}, u32[]{:S(2)}, u32[]{:S(2)}) collective-permute-start(bf16[256,1536]{1,0:T(8,128)(2,1)} %collective-permute-done.13.refs_0_), channel_id=1, source_target_pairs={{4,0},{8,4},{12,8},{0,12},{5,1},{9,5},{13,9},{1,13},{6,2},{10,6},{... | collective-permute-start | bytes 2359304 | tf_op jit(solution)/shard_map/ppermute | solution.py:24
  102.9 1.7 collective-permute-start.26
  105.0 11.0 %collective-permute-done.25.refs_3_.refs_1_ = bf16[2,256,512]{2,1,0:T(8,128)(2,1)S(1)} collective-permute-done((bf16[2,256,512]{2,1,0:T(8,128)(2,1)S(1)}, bf16[2,256,512]{2,1,0:T(8,128)(2,1)S(1)}, u32[]{:S(2)}, u32[]{:S(2)}) %collective-permute-start.25) | collective-permute-done | bytes 524320 | tf_op jit(solution)/shard_map/ppermute | solution.py:28
  116.3 2.6 %collective-permute-start.32 = (bf16[448,1536]{1,0:T(8,128)(2,1)}, bf16[448,1536]{1,0:T(8,128)(2,1)}, u32[]{:S(2)}, u32[]{:S(2)}) collective-permute-start(bf16[448,1536]{1,0:T(8,128)(2,1)} %copy-done.3), channel_id=1, source_target_pairs={{0,128},{128,0},{1,129},{129,1},{2,130},{130,2},{3,131},{131,3},{4... | collective-permute-start | bytes 4128776 | tf_op jit(solution)/shard_map/ppermute | solution.py:28
  119.0 0.8 collective-permute-start.22
  119.8 16.9 %collective-permute-done.23.refs_1_ = bf16[256,1536]{1,0:T(8,128)(2,1)} collective-permute-done((bf16[256,1536]{1,0:T(8,128)(2,1)}, bf16[256,1536]{1,0:T(8,128)(2,1)}, u32[]{:S(2)}, u32[]{:S(2)}) %collective-permute-start.23) | collective-permute-done | bytes 786464 | tf_op jit(solution)/shard_map/ppermute | solution.py:24
  136.6 5.1 %collective-permute-done.24.refs_2_ = bf16[256,1536]{1,0:T(8,128)(2,1)} collective-permute-done((bf16[256,1536]{1,0:T(8,128)(2,1)}, bf16[256,1536]{1,0:T(8,128)(2,1)}, u32[]{:S(2)}, u32[]{:S(2)}) %collective-permute-start.24) | collective-permute-done | bytes 786464 | tf_op jit(solution)/shard_map/ppermute | solution.py:24
  141.8 7.5 %shard_map.108 = (bf16[1536,512]{1,0:T(8,128)(2,1)}, bf16[1536,512]{1,0:T(8,128)(2,1)}) custom-call(s32[4]{0:T(128)S(1)} %pad_add_fusion.place, bf16[256,1536]{1,0:T(8,128)(2,1)} %bitcast.27, bf16[256,1536]{1,0:T(8,128)(2,1)} %copy-done.5, bf16[256,1536]{1,0:T(8,128)(2,1)} %collective-permute-done.20.refs_2_, ...), custom_call_target="tpu_custom_call" | custom-call | tf_op jit(solution)/shard_map/pallas_call | solution.py:211
  149.2 7.7 %shard_map.109 = (bf16[1536,512]{1,0:T(8,128)(2,1)}, bf16[1536,512]{1,0:T(8,128)(2,1)}) custom-call(s32[4]{0:T(128)S(1)} %pad_add_fusion.place, bf16[256,1536]{1,0:T(8,128)(2,1)} %collective-permute-done.13.refs_0_, bf16[256,1536]{1,0:T(8,128)(2,1)} %collective-permute-done.23.refs_1_, bf16[256,1536]{1,0:T(8,128)(2,1)} %collective-permute-done.24.refs_2_, ...), custom_call_target="tpu_custom_call" | custom-call | tf_op jit(solution)/shard_map/pallas_call | solution.py:211
  157.0 1.1 dynamic-slice_bitcast_fusion
  158.1 1.0 collective-permute-start.30
  159.2 2.2 %collective-permute-start.31 = (bf16[32,1536]{1,0:T(8,128)(2,1)S(1)}, bf16[32,1536]{1,0:T(8,128)(2,1)S(1)}, u32[]{:S(2)}, u32[]{:S(2)}) collective-permute-start(bf16[32,1536]{1,0:T(8,128)(2,1)S(1)} %get-tuple-element.94), channel_id=1, source_target_pairs={{4,0},{8,4},{12,8},{0,12},{5,1},{9,5},{13,9},{1,13},{6,2},{10,6},{... | collective-permute-start | bytes 294920 | tf_op jit(solution)/shard_map/ppermute | solution.py:24
  161.4 5.5 %shard_map.110 = (bf16[1536,512]{1,0:T(8,128)(2,1)}, bf16[1536,512]{1,0:T(8,128)(2,1)}) custom-call(s32[4]{0:T(128)S(1)} %pad_add_fusion.place, bf16[256,1536]{1,0:T(8,128)(2,1)} %collective-permute-done.22.refs_0_, bf16[2,256,512]{2,1,0:T(8,128)(2,1)S(1)} %collective-permute-done.25.refs_3_.refs_1_, ...), custom_call_target="tpu_custom_call" | custom-call | tf_op jit(solution)/shard_map/pallas_call | solution.py:211
  167.6 3.6 %shard_map.111 = bf16[512,1536]{1,0:T(8,128)(2,1)} custom-call(bf16[64,1536]{1,0:T(8,128)(2,1)} %get-tuple-element.75.first, bf16[64,1536]{1,0:T(8,128)(2,1)S(1)} %collective-permute-done.21.first_far, bf16[448,1536]{1,0:T(8,128)(2,1)S(1)} %copy-done.4, bf16[448,1536]{1,0:T(8,128)(2,1)} %collective-permute-done.32.rest_far), custom_call_target="tpu_custom_call" | custom-call | tf_op jit(solution)/shard_map/pallas_call | solution.py:230
  (56 shorter events, 7.7 us)
Async XLA Ops:
  7.2 61.9 %all-gather.2.cloned.1.call-start = ((), (), s32[]{:S(2)}) async-start(), calls=%async_computation.1 | async-start | bytes 3538944 | tf_op jit(solution)/shard_map/all_gather | solution.py:264
  7.2 10.6 %collective-permute-start = (bf16[32,1536]{1,0:T(8,128)(2,1)}, bf16[32,1536]{1,0:T(8,128)(2,1)S(1)}, u32[]{:S(2)}, u32[]{:S(2)}) collective-permute-start(bf16[32,1536]{1,0:T(8,128)(2,1)} %refs_0_.1), channel_id=1, source_target_pairs={{4,0},{8,4},{12,8},{0,12},{5,1},{9,5},{13,9},{1,13},{6,2},{10,6},{... | collective-permute-start | bytes 294920 | tf_op jit(solution)/shard_map/ppermute | solution.py:24
  10.3 7.5 %collective-permute-start.1 = (bf16[32,1536]{1,0:T(8,128)(2,1)}, bf16[32,1536]{1,0:T(8,128)(2,1)S(1)}, u32[]{:S(2)}, u32[]{:S(2)}) collective-permute-start(bf16[32,1536]{1,0:T(8,128)(2,1)} %refs_0_.1), channel_id=1, source_target_pairs={{8,0},{12,4},{0,8},{4,12},{9,1},{13,5},{1,9},{5,13},{10,2},{14,6},... | collective-permute-start | bytes 294920 | tf_op jit(solution)/shard_map/ppermute | solution.py:24
  10.9 7.4 %collective-permute-start.2 = (bf16[32,1536]{1,0:T(8,128)(2,1)}, bf16[32,1536]{1,0:T(8,128)(2,1)S(1)}, u32[]{:S(2)}, u32[]{:S(2)}) collective-permute-start(bf16[32,1536]{1,0:T(8,128)(2,1)} %refs_0_.1), channel_id=1, source_target_pairs={{12,0},{0,4},{4,8},{8,12},{13,1},{1,5},{5,9},{9,13},{14,2},{2,6},{... | collective-permute-start | bytes 294920 | tf_op jit(solution)/shard_map/ppermute | solution.py:24
  11.9 8.4 %collective-permute-start.3 = (bf16[32,1536]{1,0:T(8,128)(2,1)}, bf16[32,1536]{1,0:T(8,128)(2,1)S(1)}, u32[]{:S(2)}, u32[]{:S(2)}) collective-permute-start(bf16[32,1536]{1,0:T(8,128)(2,1)} %refs_0_.2), channel_id=1, source_target_pairs={{16,0},{32,16},{48,32},{64,48},{80,64},{96,80},{112,96},{0,112},{1... | collective-permute-start | bytes 294920 | tf_op jit(solution)/shard_map/ppermute | solution.py:24
  17.8 6.0 %collective-permute-start.4 = (bf16[32,1536]{1,0:T(8,128)(2,1)}, bf16[32,1536]{1,0:T(8,128)(2,1)S(1)}, u32[]{:S(2)}, u32[]{:S(2)}) collective-permute-start(bf16[32,1536]{1,0:T(8,128)(2,1)} %refs_0_.2), channel_id=1, source_target_pairs={{112,0},{0,16},{16,32},{32,48},{48,64},{64,80},{80,96},{96,112},{1... | collective-permute-start | bytes 294920 | tf_op jit(solution)/shard_map/ppermute | solution.py:24
  25.5 26.5 %copy-start.6 = (bf16[256,512]{1,0:T(8,128)(2,1)S(1)}, bf16[256,512]{1,0:T(8,128)(2,1)}, u32[]{:S(2)}) copy-start(bf16[256,512]{1,0:T(8,128)(2,1)} %param.9) | copy-start | bytes 786436
  25.5 131.4 %reduce-scatter.2.cloned.1.call-start = ((), (), s32[]{:S(2)}) async-start(), calls=%async_computation.2 | async-start | bytes 3538944 | tf_op jit(solution)/shard_map/reduce_scatter | solution.py:291
  25.6 16.4 %collective-permute-start.6 = (bf16[256,512]{1,0:T(8,128)(2,1)}, bf16[256,512]{1,0:T(8,128)(2,1)S(1)}, u32[]{:S(2)}, u32[]{:S(2)}) collective-permute-start(bf16[256,512]{1,0:T(8,128)(2,1)} %param.10), channel_id=1, source_target_pairs={{0,2},{2,0},{1,3},{3,1},{4,6},{6,4},{5,7},{7,5},{8,10},{10,8},{9,1... | collective-permute-start | bytes 786440 | tf_op jit(solution)/shard_map/ppermute | solution.py:28
  27.8 5.6 %collective-permute-start.8 = (bf16[32,1536]{1,0:T(8,128)(2,1)S(1)}, bf16[32,1536]{1,0:T(8,128)(2,1)S(1)}, u32[]{:S(2)}, u32[]{:S(2)}) collective-permute-start(bf16[32,1536]{1,0:T(8,128)(2,1)S(1)} %collective-permute-done.3.refs_1_), channel_id=1, source_target_pairs={{16,0},{32,16},{48,32},{64,48},{80,64},{96,80},{112,96},{0,112},{1... | collective-permute-start | bytes 294920 | tf_op jit(solution)/shard_map/ppermute | solution.py:24
  28.2 7.2 %collective-permute-start.11 = (bf16[32,1536]{1,0:T(8,128)(2,1)S(1)}, bf16[32,1536]{1,0:T(8,128)(2,1)S(1)}, u32[]{:S(2)}, u32[]{:S(2)}) collective-permute-start(bf16[32,1536]{1,0:T(8,128)(2,1)S(1)} %collective-permute-done.4.refs_7_), channel_id=1, source_target_pairs={{112,0},{0,16},{16,32},{32,48},{48,64},{64,80},{80,96},{96,112},{1... | collective-permute-start | bytes 294920 | tf_op jit(solution)/shard_map/ppermute | solution.py:24
  33.4 7.7 %collective-permute-start.9 = (bf16[32,1536]{1,0:T(8,128)(2,1)S(1)}, bf16[32,1536]{1,0:T(8,128)(2,1)S(1)}, u32[]{:S(2)}, u32[]{:S(2)}) collective-permute-start(bf16[32,1536]{1,0:T(8,128)(2,1)S(1)} %collective-permute-done.8.refs_2_), channel_id=1, source_target_pairs={{16,0},{32,16},{48,32},{64,48},{80,64},{96,80},{112,96},{0,112},{1... | collective-permute-start | bytes 294920 | tf_op jit(solution)/shard_map/ppermute | solution.py:24
  34.0 17.9 %collective-permute-start.5 = (bf16[256,512]{1,0:T(8,128)(2,1)}, bf16[256,512]{1,0:T(8,128)(2,1)S(1)}, u32[]{:S(2)}, u32[]{:S(2)}) collective-permute-start(bf16[256,512]{1,0:T(8,128)(2,1)} %param.9), channel_id=1, source_target_pairs={{0,2},{2,0},{1,3},{3,1},{4,6},{6,4},{5,7},{7,5},{8,10},{10,8},{9,1... | collective-permute-start | bytes 786440 | tf_op jit(solution)/shard_map/ppermute | solution.py:28
  35.4 7.9 %collective-permute-start.12 = (bf16[32,1536]{1,0:T(8,128)(2,1)S(1)}, bf16[32,1536]{1,0:T(8,128)(2,1)S(1)}, u32[]{:S(2)}, u32[]{:S(2)}) collective-permute-start(bf16[32,1536]{1,0:T(8,128)(2,1)S(1)} %collective-permute-done.11.refs_6_), channel_id=1, source_target_pairs={{112,0},{0,16},{16,32},{32,48},{48,64},{64,80},{80,96},{96,112},{1... | collective-permute-start | bytes 294920 | tf_op jit(solution)/shard_map/ppermute | solution.py:24
  41.1 6.7 %collective-permute-start.10 = (bf16[32,1536]{1,0:T(8,128)(2,1)S(1)}, bf16[32,1536]{1,0:T(8,128)(2,1)S(1)}, u32[]{:S(2)}, u32[]{:S(2)}) collective-permute-start(bf16[32,1536]{1,0:T(8,128)(2,1)S(1)} %collective-permute-done.9.refs_3_), channel_id=1, source_target_pairs={{16,0},{32,16},{48,32},{64,48},{80,64},{96,80},{112,96},{0,112},{1... | collective-permute-start | bytes 294920 | tf_op jit(solution)/shard_map/ppermute | solution.py:24
  48.7 29.3 %copy-start = (bf16[8,32,1536]{2,1,0:T(8,128)(2,1)}, bf16[8,32,1536]{2,1,0:T(8,128)(2,1)S(1)}, u32[]{:S(2)}) copy-start(bf16[8,32,1536]{2,1,0:T(8,128)(2,1)S(1)} %shard_map.103) | copy-start | bytes 2359300
  48.7 13.6 %collective-permute-start.13 = (bf16[256,1536]{1,0:T(8,128)(2,1)S(1)}, bf16[256,1536]{1,0:T(8,128)(2,1)}, u32[]{:S(2)}, u32[]{:S(2)}) collective-permute-start(bf16[256,1536]{1,0:T(8,128)(2,1)S(1)} %bitcast.23), channel_id=1, source_target_pairs={{0,128},{128,0},{1,129},{129,1},{2,130},{130,2},{3,131},{131,3},{4... | collective-permute-start | bytes 2359304 | tf_op jit(solution)/shard_map/ppermute | solution.py:28
  49.8 13.8 %collective-permute-start.14 = (bf16[256,1536]{1,0:T(8,128)(2,1)S(1)}, bf16[256,1536]{1,0:T(8,128)(2,1)S(1)}, u32[]{:S(2)}, u32[]{:S(2)}) collective-permute-start(bf16[256,1536]{1,0:T(8,128)(2,1)S(1)} %bitcast.24), channel_id=1, source_target_pairs={{4,0},{8,4},{12,8},{0,12},{5,1},{9,5},{13,9},{1,13},{6,2},{10,6},{... | collective-permute-start | bytes 2359304 | tf_op jit(solution)/shard_map/ppermute | solution.py:24
  52.0 13.3 %collective-permute-start.15 = (bf16[256,1536]{1,0:T(8,128)(2,1)S(1)}, bf16[256,1536]{1,0:T(8,128)(2,1)}, u32[]{:S(2)}, u32[]{:S(2)}) collective-permute-start(bf16[256,1536]{1,0:T(8,128)(2,1)S(1)} %bitcast.25), channel_id=1, source_target_pairs={{12,0},{0,4},{4,8},{8,12},{13,1},{1,5},{5,9},{9,13},{14,2},{2,6},{... | collective-permute-start | bytes 2359304 | tf_op jit(solution)/shard_map/ppermute | solution.py:24
  52.4 2.2 %collective-permute-start.7 = (bf16[2,256,512]{2,1,0:T(8,128)(2,1)S(1)}, bf16[2,256,512]{2,1,0:T(8,128)(2,1)S(1)}, u32[]{:S(2)}, u32[]{:S(2)}) collective-permute-start(bf16[2,256,512]{2,1,0:T(8,128)(2,1)S(1)} %fusion.4.hidden), channel_id=1, source_target_pairs={{0,1},{1,0},{2,3},{3,2},{4,5},{5,4},{6,7},{7,6},{8,9},{9,8},{10,11... | collective-permute-start | bytes 1572872 | tf_op jit(solution)/shard_map/ppermute | solution.py:28
  63.7 0.9 copy-start.5
  73.6 2.0 %collective-permute-start.16 = (bf16[2,256,512]{2,1,0:T(8,128)(2,1)S(1)}, bf16[2,256,512]{2,1,0:T(8,128)(2,1)S(1)}, u32[]{:S(2)}, u32[]{:S(2)}) collective-permute-start(bf16[2,256,512]{2,1,0:T(8,128)(2,1)S(1)} %get-tuple-element.63), channel_id=1, source_target_pairs={{0,1},{1,0},{2,3},{3,2},{4,5},{5,4},{6,7},{7,6},{8,9},{9,8},{10,11... | collective-permute-start | bytes 1572872 | tf_op jit(solution)/shard_map/ppermute | solution.py:28
  75.8 15.6 %collective-permute-start.17 = (bf16[2,256,512]{2,1,0:T(8,128)(2,1)S(1)}, bf16[2,256,512]{2,1,0:T(8,128)(2,1)S(1)}, u32[]{:S(2)}, u32[]{:S(2)}) collective-permute-start(bf16[2,256,512]{2,1,0:T(8,128)(2,1)S(1)} %get-tuple-element.106), channel_id=1, source_target_pairs={{0,2},{2,0},{1,3},{3,1},{4,6},{6,4},{5,7},{7,5},{8,10},{10,8},{9,1... | collective-permute-start | bytes 1572872 | tf_op jit(solution)/shard_map/ppermute | solution.py:28
  78.0 22.2 %collective-permute-start.20 = (bf16[256,1536]{1,0:T(8,128)(2,1)S(1)}, bf16[256,1536]{1,0:T(8,128)(2,1)}, u32[]{:S(2)}, u32[]{:S(2)}) collective-permute-start(bf16[256,1536]{1,0:T(8,128)(2,1)S(1)} %bitcast.26), channel_id=1, source_target_pairs={{8,0},{12,4},{0,8},{4,12},{9,1},{13,5},{1,9},{5,13},{10,2},{14,6},... | collective-permute-start | bytes 2359304 | tf_op jit(solution)/shard_map/ppermute | solution.py:24
  80.0 14.7 %copy-start.2 = (bf16[1536,512]{1,0:T(8,128)(2,1)S(1)}, bf16[1536,512]{1,0:T(8,128)(2,1)}, u32[]{:S(2)}) copy-start(bf16[1536,512]{1,0:T(8,128)(2,1)} %w_up.1) | copy-start | bytes 4718596
  84.6 1.1 copy-start.3
  85.8 8.9 %copy-start.1 = (bf16[1536,512]{1,0:T(8,128)(2,1)S(1)}, bf16[1536,512]{1,0:T(8,128)(2,1)}, u32[]{:S(2)}) copy-start(bf16[1536,512]{1,0:T(8,128)(2,1)} %w_gate.1) | copy-start | bytes 4718596
  92.0 2.0 %collective-permute-start.18 = (bf16[2,256,512]{2,1,0:T(8,128)(2,1)S(1)}, bf16[2,256,512]{2,1,0:T(8,128)(2,1)S(1)}, u32[]{:S(2)}, u32[]{:S(2)}) collective-permute-start(bf16[2,256,512]{2,1,0:T(8,128)(2,1)S(1)} %get-tuple-element.72.near0.refs_4_), channel_id=1, source_target_pairs={{0,1},{1,0},{2,3},{3,2},{4,5},{5,4},{6,7},{7,6},{8,9},{9,8},{10,11... | collective-permute-start | bytes 1572872 | tf_op jit(solution)/shard_map/ppermute | solution.py:28
  92.1 2.6 %collective-permute-start.19 = (bf16[2,256,512]{2,1,0:T(8,128)(2,1)S(1)}, bf16[2,256,512]{2,1,0:T(8,128)(2,1)S(1)}, u32[]{:S(2)}, u32[]{:S(2)}) collective-permute-start(bf16[2,256,512]{2,1,0:T(8,128)(2,1)S(1)} %get-tuple-element.73.near1.refs_5_), channel_id=1, source_target_pairs={{0,1},{1,0},{2,3},{3,2},{4,5},{5,4},{6,7},{7,6},{8,9},{9,8},{10,11... | collective-permute-start | bytes 1572872 | tf_op jit(solution)/shard_map/ppermute | solution.py:28
  92.6 7.6 %collective-permute-start.21 = (bf16[64,1536]{1,0:T(8,128)(2,1)}, bf16[64,1536]{1,0:T(8,128)(2,1)S(1)}, u32[]{:S(2)}, u32[]{:S(2)}) collective-permute-start(bf16[64,1536]{1,0:T(8,128)(2,1)} %get-tuple-element.75.first), channel_id=1, source_target_pairs={{0,128},{128,0},{1,129},{129,1},{2,130},{130,2},{3,131},{131,3},{4... | collective-permute-start | bytes 589832 | tf_op jit(solution)/shard_map/ppermute | solution.py:28
  100.2 36.4 %collective-permute-start.23 = (bf16[256,1536]{1,0:T(8,128)(2,1)}, bf16[256,1536]{1,0:T(8,128)(2,1)}, u32[]{:S(2)}, u32[]{:S(2)}) collective-permute-start(bf16[256,1536]{1,0:T(8,128)(2,1)} %collective-permute-done.13.refs_0_), channel_id=1, source_target_pairs={{4,0},{8,4},{12,8},{0,12},{5,1},{9,5},{13,9},{1,13},{6,2},{10,6},{... | collective-permute-start | bytes 2359304 | tf_op jit(solution)/shard_map/ppermute | solution.py:24
  102.3 13.7 %collective-permute-start.25 = (bf16[2,256,512]{2,1,0:T(8,128)(2,1)S(1)}, bf16[2,256,512]{2,1,0:T(8,128)(2,1)S(1)}, u32[]{:S(2)}, u32[]{:S(2)}) collective-permute-start(bf16[2,256,512]{2,1,0:T(8,128)(2,1)S(1)} %get-tuple-element.72.near0.refs_4_), channel_id=1, source_target_pairs={{0,128},{128,0},{1,129},{129,1},{2,130},{130,2},{3,131},{131,3},{4... | collective-permute-start | bytes 1572872 | tf_op jit(solution)/shard_map/ppermute | solution.py:28
  102.9 13.4 %collective-permute-start.26 = (bf16[2,256,512]{2,1,0:T(8,128)(2,1)S(1)}, bf16[2,256,512]{2,1,0:T(8,128)(2,1)S(1)}, u32[]{:S(2)}, u32[]{:S(2)}) collective-permute-start(bf16[2,256,512]{2,1,0:T(8,128)(2,1)S(1)} %get-tuple-element.73.near1.refs_5_), channel_id=1, source_target_pairs={{0,130},{130,0},{2,128},{128,2},{1,131},{131,1},{3,129},{129,3},{4... | collective-permute-start | bytes 1572872 | tf_op jit(solution)/shard_map/ppermute | solution.py:293
  104.6 37.1 %collective-permute-start.24 = (bf16[256,1536]{1,0:T(8,128)(2,1)}, bf16[256,1536]{1,0:T(8,128)(2,1)}, u32[]{:S(2)}, u32[]{:S(2)}) collective-permute-start(bf16[256,1536]{1,0:T(8,128)(2,1)} %collective-permute-done.13.refs_0_), channel_id=1, source_target_pairs={{12,0},{0,4},{4,8},{8,12},{13,1},{1,5},{5,9},{9,13},{14,2},{2,6},{... | collective-permute-start | bytes 2359304 | tf_op jit(solution)/shard_map/ppermute | solution.py:24
  116.3 51.2 %collective-permute-start.32 = (bf16[448,1536]{1,0:T(8,128)(2,1)}, bf16[448,1536]{1,0:T(8,128)(2,1)}, u32[]{:S(2)}, u32[]{:S(2)}) collective-permute-start(bf16[448,1536]{1,0:T(8,128)(2,1)} %copy-done.3), channel_id=1, source_target_pairs={{0,128},{128,0},{1,129},{129,1},{2,130},{130,2},{3,131},{131,3},{4... | collective-permute-start | bytes 4128776 | tf_op jit(solution)/shard_map/ppermute | solution.py:28
  119.0 39.1 %collective-permute-start.22 = (bf16[256,1536]{1,0:T(8,128)(2,1)}, bf16[256,1536]{1,0:T(8,128)(2,1)}, u32[]{:S(2)}, u32[]{:S(2)}) collective-permute-start(bf16[256,1536]{1,0:T(8,128)(2,1)} %collective-permute-done.13.refs_0_), channel_id=1, source_target_pairs={{8,0},{12,4},{0,8},{4,12},{9,1},{13,5},{1,9},{5,13},{10,2},{14,6},... | collective-permute-start | bytes 2359304 | tf_op jit(solution)/shard_map/ppermute | solution.py:24
  119.8 29.5 %collective-permute-start.27 = (bf16[2,256,512]{2,1,0:T(8,128)(2,1)S(1)}, bf16[2,256,512]{2,1,0:T(8,128)(2,1)}, u32[]{:S(2)}, u32[]{:S(2)}) collective-permute-start(bf16[2,256,512]{2,1,0:T(8,128)(2,1)S(1)} %collective-permute-done.25.refs_3_.refs_1_), channel_id=1, source_target_pairs={{0,1},{1,0},{2,3},{3,2},{4,5},{5,4},{6,7},{7,6},{8,9},{9,8},{10,11... | collective-permute-start | bytes 1572872 | tf_op jit(solution)/shard_map/ppermute | solution.py:28
  136.6 12.6 %collective-permute-start.28 = (bf16[2,256,512]{2,1,0:T(8,128)(2,1)S(1)}, bf16[2,256,512]{2,1,0:T(8,128)(2,1)}, u32[]{:S(2)}, u32[]{:S(2)}) collective-permute-start(bf16[2,256,512]{2,1,0:T(8,128)(2,1)S(1)} %collective-permute-done.26.refs_4_.refs_2_), channel_id=1, source_target_pairs={{0,1},{1,0},{2,3},{3,2},{4,5},{5,4},{6,7},{7,6},{8,9},{9,8},{10,11... | collective-permute-start | bytes 1572872 | tf_op jit(solution)/shard_map/ppermute | solution.py:28
  158.0 9.5 %copy-start.4 = (bf16[448,1536]{1,0:T(8,128)(2,1)S(1)}, bf16[448,1536]{1,0:T(8,128)(2,1)}, u32[]{:S(2)}) copy-start(bf16[448,1536]{1,0:T(8,128)(2,1)} %copy-done.3) | copy-start | bytes 4128772
  158.1 8.8 %collective-permute-start.29 = (bf16[32,1536]{1,0:T(8,128)(2,1)S(1)}, bf16[32,1536]{1,0:T(8,128)(2,1)S(1)}, u32[]{:S(2)}, u32[]{:S(2)}) collective-permute-start(bf16[32,1536]{1,0:T(8,128)(2,1)S(1)} %get-tuple-element.92), channel_id=1, source_target_pairs={{12,0},{0,4},{4,8},{8,12},{13,1},{1,5},{5,9},{9,13},{14,2},{2,6},{... | collective-permute-start | bytes 294920 | tf_op jit(solution)/shard_map/ppermute | solution.py:24
  158.1 8.7 %collective-permute-start.30 = (bf16[32,1536]{1,0:T(8,128)(2,1)S(1)}, bf16[32,1536]{1,0:T(8,128)(2,1)S(1)}, u32[]{:S(2)}, u32[]{:S(2)}) collective-permute-start(bf16[32,1536]{1,0:T(8,128)(2,1)S(1)} %get-tuple-element.93), channel_id=1, source_target_pairs={{8,0},{12,4},{0,8},{4,12},{9,1},{13,5},{1,9},{5,13},{10,2},{14,6},... | collective-permute-start | bytes 294920 | tf_op jit(solution)/shard_map/ppermute | solution.py:24
  159.2 7.7 %collective-permute-start.31 = (bf16[32,1536]{1,0:T(8,128)(2,1)S(1)}, bf16[32,1536]{1,0:T(8,128)(2,1)S(1)}, u32[]{:S(2)}, u32[]{:S(2)}) collective-permute-start(bf16[32,1536]{1,0:T(8,128)(2,1)S(1)} %get-tuple-element.94), channel_id=1, source_target_pairs={{4,0},{8,4},{12,8},{0,12},{5,1},{9,5},{13,9},{1,13},{6,2},{10,6},{... | collective-permute-start | bytes 294920 | tf_op jit(solution)/shard_map/ppermute | solution.py:24
Sparse Core Ops, SparseCore 0:
  25.6 43.3 all-gather.1
  100.3 44.3 reduce-scatter.1

commit v10 on v9

--- a/solution.py
+++ b/solution.py
@@ -291,10 +291,11 @@
     in_z = lax.psum_scatter(partial_in, "z", scatter_dimension=0, tiled=True).reshape(NY, 32, 1536)
 
     far = [swap(near[0], "dp"), lax.ppermute(near[1], ("dp", "xh"), [(0, 3), (3, 0), (1, 2), (2, 1)])]
-    partner1, partner2, partner3 = (from_ahead(partner_z, "y", NY, k) for k in (1, 2, 3))
+    partner1, partner3 = from_ahead(partner_z, "y", NY, 1), from_ahead(partner_z, "y", NY, 3)
     far, down_rest = lax.optimization_barrier((far, down_rest))
     rest_far = swap(down_rest, "dp")
-    own_z, partner1, partner3 = lax.optimization_barrier((own_z, partner1, partner3))
+    own_z, partner_z, partner1, partner3 = lax.optimization_barrier((own_z, partner_z, partner1, partner3))
+    partner2 = from_ahead(partner_z, "y", NY, 2)
     own_gate, own_up = weight_grads(place, (0, 1, 2, 3), (own_z, own1, own2, own3), (*near, *other))
     far_other = [swap(half, "core") for half in far]
 

time: 179 us -> 169 us (0.944)
  waiting for transfers between devices: 76.5 us -> 63.5 us
    ppermute x19, waiting for transfers between devices: 42.6 us -> 24.7 us  [from_ahead(): return lax.ppermute(x, axis, [((d + k) % n, d) for d in range(n)])]
    reduce_scatter x1, waiting for transfers between devices: 0.01 us -> 4.97 us  [body(): lax.psum_scatter(partial_in, 'z', scatter_dimension=0, tiled=True)]
  transfers between devices with their start and end apart: 35 -> 35, of which waited for: 20 -> 21; matrix products, arithmetic and copies ran while one was open for 2% -> 2% of each run, Pallas kernels for 18% -> 19%
where the time goes in v10:
time: 169 us; the launch traced here: 168 us
  waiting for transfers between devices  63.5 us (38%)
  Pallas kernels  42.3 us (25%)
  starting transfers between devices  41.1 us (24%)
  between operations  14.2 us (8%)
  local copies, waits for them, and re-layouts  4.54 us (3%)
  other arithmetic  2.44 us (1%)
    ppermute x13, waiting for transfers between devices, swap(): return lax.ppermute(x, axis, [(0, 1), (1, 0)])  29.7 us
    ppermute x19, starting transfers between devices, from_ahead(): return lax.ppermute(x, axis, [((d + k) % n, d) for d in range(n)])  27.3 us
    ppermute x19, waiting for transfers between devices, from_ahead(): return lax.ppermute(x, axis, [((d + k) % n, d) for d in range(n)])  24.7 us
    pallas_call x3, Pallas kernels, weight_grads(): pl.pallas_call(functools.partial(weight_kernel, slots, bool(base)), grid=...  20.7 us
    ppermute x13, starting transfers between devices, swap(): return lax.ppermute(x, axis, [(0, 1), (1, 0)])  11.7 us
    pallas_call x1, Pallas kernels, input_grad(): pl.pallas_call(input_grad_kernel, grid=(3,), out_shape=jax.ShapeDtypeStru...  5.5 us
    reduce_scatter x1, waiting for transfers between devices, body(): lax.psum_scatter(partial_in, 'z', scatter_dimension=0, tiled=True)  4.97 us
    pallas_call x1, Pallas kernels, down_grad(): pl.pallas_call(down_kernel, grid=(3,), out_shape=(jax.ShapeDtypeStruct((F...  4.68 us
  transfers between devices with their start and end apart: 35, of which 21 were waited for; matrix products, arithmetic and copies ran while one was open for 2% of the time, Pallas kernels for 19%

profile of v10, /device:TPU:2, one launch (start us, length us, event | category | flops | bytes accessed | tf_op | source)
XLA Modules:
  0.0 168.1 jit_solution(16950473861572375312)
XLA Ops:
  7.2 3.1 %collective-permute-start = (bf16[32,1536]{1,0:T(8,128)(2,1)}, bf16[32,1536]{1,0:T(8,128)(2,1)S(1)}, u32[]{:S(2)}, u32[]{:S(2)}) collective-permute-start(bf16[32,1536]{1,0:T(8,128)(2,1)} %refs_0_.1), channel_id=1, source_target_pairs={{4,0},{8,4},{12,8},{0,12},{5,1},{9,5},{13,9},{1,13},{6,2},{10,6},{... | collective-permute-start | bytes 294920 | tf_op jit(solution)/shard_map/ppermute | solution.py:24
  10.9 1.0 collective-permute-start.2
  11.9 5.9 %collective-permute-start.3 = (bf16[32,1536]{1,0:T(8,128)(2,1)}, bf16[32,1536]{1,0:T(8,128)(2,1)S(1)}, u32[]{:S(2)}, u32[]{:S(2)}) collective-permute-start(bf16[32,1536]{1,0:T(8,128)(2,1)} %refs_0_.2), channel_id=1, source_target_pairs={{16,0},{32,16},{48,32},{64,48},{80,64},{96,80},{112,96},{0,112},{1... | collective-permute-start | bytes 294920 | tf_op jit(solution)/shard_map/ppermute | solution.py:24
  18.4 1.9 %collective-permute-done.3.refs_1_ = bf16[32,1536]{1,0:T(8,128)(2,1)S(1)} collective-permute-done((bf16[32,1536]{1,0:T(8,128)(2,1)}, bf16[32,1536]{1,0:T(8,128)(2,1)S(1)}, u32[]{:S(2)}, u32[]{:S(2)}) %collective-permute-start.3) | collective-permute-done | bytes 98336 | tf_op jit(solution)/shard_map/ppermute | solution.py:24
  20.3 3.5 %collective-permute-done.4.refs_7_ = bf16[32,1536]{1,0:T(8,128)(2,1)S(1)} collective-permute-done((bf16[32,1536]{1,0:T(8,128)(2,1)}, bf16[32,1536]{1,0:T(8,128)(2,1)S(1)}, u32[]{:S(2)}, u32[]{:S(2)}) %collective-permute-start.4) | collective-permute-done | bytes 98336 | tf_op jit(solution)/shard_map/ppermute | solution.py:24
  23.8 1.7 %shard_map.102 = bf16[4,32,1536]{2,1,0:T(8,128)(2,1)} custom-call(s32[4]{0:T(128)S(1)} %pad_add_fusion.place, bf16[32,1536]{1,0:T(8,128)(2,1)} %refs_0_.1, bf16[32,1536]{1,0:T(8,128)(2,1)S(1)} %collective-permute-done.refs_1_, bf16[32,1536]{1,0:T(8,128)(2,1)S(1)} %collective-permute-done.1.refs_2_, bf16[32,1536]{1,0:T(8,128)(2,1)S(1)} %collective-permute-done.2.refs_3_), custom_call_target="tpu_custom_call" | custom-call | tf_op jit(solution)/shard_map/pallas_call | solution.py:46
  25.6 2.2 %collective-permute-start.6 = (bf16[256,512]{1,0:T(8,128)(2,1)}, bf16[256,512]{1,0:T(8,128)(2,1)S(1)}, u32[]{:S(2)}, u32[]{:S(2)}) collective-permute-start(bf16[256,512]{1,0:T(8,128)(2,1)} %param.10), channel_id=1, source_target_pairs={{0,2},{2,0},{1,3},{3,1},{4,6},{6,4},{5,7},{7,5},{8,10},{10,8},{9,1... | collective-permute-start | bytes 786440 | tf_op jit(solution)/shard_map/ppermute | solution.py:28
  28.2 1.6 collective-permute-start.11
  29.8 3.6 %collective-permute-done.8.refs_2_ = bf16[32,1536]{1,0:T(8,128)(2,1)S(1)} collective-permute-done((bf16[32,1536]{1,0:T(8,128)(2,1)S(1)}, bf16[32,1536]{1,0:T(8,128)(2,1)S(1)}, u32[]{:S(2)}, u32[]{:S(2)}) %collective-permute-start.8) | collective-permute-done | bytes 98336 | tf_op jit(solution)/shard_map/ppermute | solution.py:24
  34.0 1.4 collective-permute-start.5
  35.4 1.4 collective-permute-start.12
  36.8 4.2 %collective-permute-done.9.refs_3_ = bf16[32,1536]{1,0:T(8,128)(2,1)S(1)} collective-permute-done((bf16[32,1536]{1,0:T(8,128)(2,1)S(1)}, bf16[32,1536]{1,0:T(8,128)(2,1)S(1)}, u32[]{:S(2)}, u32[]{:S(2)}) %collective-permute-start.9) | collective-permute-done | bytes 98336 | tf_op jit(solution)/shard_map/ppermute | solution.py:24
  41.1 0.9 collective-permute-start.10
  42.0 1.0 select_bitcast_fusion.1
  43.4 4.4 %collective-permute-done.10.refs_4_ = bf16[32,1536]{1,0:T(8,128)(2,1)S(1)} collective-permute-done((bf16[32,1536]{1,0:T(8,128)(2,1)S(1)}, bf16[32,1536]{1,0:T(8,128)(2,1)S(1)}, u32[]{:S(2)}, u32[]{:S(2)}) %collective-permute-start.10) | collective-permute-done | bytes 98336 | tf_op jit(solution)/shard_map/ppermute | solution.py:24
  47.7 1.0 shard_map.103
  48.7 1.1 collective-permute-start.13
  49.8 2.2 %collective-permute-start.14 = (bf16[256,1536]{1,0:T(8,128)(2,1)S(1)}, bf16[256,1536]{1,0:T(8,128)(2,1)S(1)}, u32[]{:S(2)}, u32[]{:S(2)}) collective-permute-start(bf16[256,1536]{1,0:T(8,128)(2,1)S(1)} %bitcast.24), channel_id=1, source_target_pairs={{4,0},{8,4},{12,8},{0,12},{5,1},{9,5},{13,9},{1,13},{6,2},{10,6},{... | collective-permute-start | bytes 2359304 | tf_op jit(solution)/shard_map/ppermute | solution.py:24
  52.8 1.8 %collective-permute-done.7.hidden_other = bf16[2,256,512]{2,1,0:T(8,128)(2,1)S(1)} collective-permute-done((bf16[2,256,512]{2,1,0:T(8,128)(2,1)S(1)}, bf16[2,256,512]{2,1,0:T(8,128)(2,1)S(1)}, u32[]{:S(2)}, u32[]{:S(2)}) %collective-permute-start.7) | collective-permute-done | bytes 524320 | tf_op jit(solution)/shard_map/ppermute | solution.py:28
  54.5 7.8 %collective-permute-done.13.refs_0_ = bf16[256,1536]{1,0:T(8,128)(2,1)} collective-permute-done((bf16[256,1536]{1,0:T(8,128)(2,1)S(1)}, bf16[256,1536]{1,0:T(8,128)(2,1)}, u32[]{:S(2)}, u32[]{:S(2)}) %collective-permute-start.13) | collective-permute-done | bytes 786464 | tf_op jit(solution)/shard_map/ppermute | solution.py:28
  62.3 1.4 collective-permute-done.14.refs_1_
  63.7 0.9 copy-done.9
  65.3 3.8 %all-gather.2.cloned.1.call-done.go = bf16[1024,1536]{1,0:T(8,128)(2,1)} async-done(((bf16[128,1536]{1,0:T(8,128)(2,1)}), bf16[1024,1536]{1,0:T(8,128)(2,1)}) %all-gather.2.cloned.1.call-update) | async-done | bytes 3145744 | tf_op jit(solution)/shard_map/all_gather | solution.py:264
  69.0 4.6 %shard_map.104 = (f32[2,256,512]{2,1,0:T(8,128)S(1)}, bf16[2,256,512]{2,1,0:T(8,128)(2,1)S(1)}) custom-call(s32[4]{0:T(128)S(1)} %pad_add_fusion.place, bf16[1024,1536]{1,0:T(8,128)(2,1)} %all-gather.2.cloned.1.call-done.go, bf16[512,1536]{1,0:T(8,128)(2,1)} %w_down.1), custom_call_target="tpu_custom_call" | custom-call | tf_op jit(solution)/shard_map/pallas_call | solution.py:79
  73.7 1.9 %collective-permute-done.16 = bf16[2,256,512]{2,1,0:T(8,128)(2,1)S(1)} collective-permute-done((bf16[2,256,512]{2,1,0:T(8,128)(2,1)S(1)}, bf16[2,256,512]{2,1,0:T(8,128)(2,1)S(1)}, u32[]{:S(2)}, u32[]{:S(2)}) %collective-permute-start.16) | collective-permute-done | bytes 524320 | tf_op jit(solution)/shard_map/ppermute | solution.py:28
  75.8 2.2 %collective-permute-start.17 = (bf16[2,256,512]{2,1,0:T(8,128)(2,1)S(1)}, bf16[2,256,512]{2,1,0:T(8,128)(2,1)S(1)}, u32[]{:S(2)}, u32[]{:S(2)}) collective-permute-start(bf16[2,256,512]{2,1,0:T(8,128)(2,1)S(1)} %get-tuple-element.108), channel_id=1, source_target_pairs={{0,2},{2,0},{1,3},{3,1},{4,6},{6,4},{5,7},{7,5},{8,10},{10,8},{9,1... | collective-permute-start | bytes 1572872 | tf_op jit(solution)/shard_map/ppermute | solution.py:28
  78.0 2.0 %collective-permute-start.20 = (bf16[256,1536]{1,0:T(8,128)(2,1)S(1)}, bf16[256,1536]{1,0:T(8,128)(2,1)}, u32[]{:S(2)}, u32[]{:S(2)}) collective-permute-start(bf16[256,1536]{1,0:T(8,128)(2,1)S(1)} %bitcast.26), channel_id=1, source_target_pairs={{8,0},{12,4},{0,8},{4,12},{9,1},{13,5},{1,9},{5,13},{10,2},{14,6},... | collective-permute-start | bytes 2359304 | tf_op jit(solution)/shard_map/ppermute | solution.py:24
  80.0 4.7 %shard_map.105 = (bf16[64,1536]{1,0:T(8,128)(2,1)}, bf16[448,1536]{1,0:T(8,128)(2,1)S(1)}) custom-call(s32[4]{0:T(128)S(1)} %pad_add_fusion.place, bf16[2,256,512]{2,1,0:T(8,128)(2,1)S(1)} %fusion.4.hidden, bf16[2,256,512]{2,1,0:T(8,128)(2,1)S(1)} %collective-permute-done.7.hidden_other, bf16[1024,1536]{1,0:T(8,128)(2,1)} %all-gather.2.cloned.1.call-done.go), custom_call_target="tpu_custom_call" | custom-call | tf_op jit(solution)/shard_map/pallas_call | solution.py:161
  84.6 1.1 copy-done.3
  85.8 5.6 %collective-permute-done.17.chip_far = bf16[2,256,512]{2,1,0:T(8,128)(2,1)S(1)} collective-permute-done((bf16[2,256,512]{2,1,0:T(8,128)(2,1)S(1)}, bf16[2,256,512]{2,1,0:T(8,128)(2,1)S(1)}, u32[]{:S(2)}, u32[]{:S(2)}) %collective-permute-start.17) | collective-permute-done | bytes 524320 | tf_op jit(solution)/shard_map/ppermute | solution.py:28
  93.1 0.8 collective-permute-done.18.other0.refs_6_
  94.7 5.5 %shard_map.107 = bf16[1024,1536]{1,0:T(8,128)(2,1)} custom-call(s32[4]{0:T(128)S(1)} %pad_add_fusion.place, bf16[2,256,512]{2,1,0:T(8,128)(2,1)S(1)} %get-tuple-element.73.near0.refs_4_, bf16[2,256,512]{2,1,0:T(8,128)(2,1)S(1)} %get-tuple-element.74.near1.refs_5_, bf16[2,256,512]{2,1,0:T(8,128)(2,1)S(1)} %collective-permute-done.18.other0.refs_6_, ...), custom_call_target="tpu_custom_call" | custom-call | tf_op jit(solution)/shard_map/pallas_call | solution.py:131
  100.9 2.0 %collective-permute-start.22 = (bf16[256,1536]{1,0:T(8,128)(2,1)}, bf16[256,1536]{1,0:T(8,128)(2,1)S(1)}, u32[]{:S(2)}, u32[]{:S(2)}) collective-permute-start(bf16[256,1536]{1,0:T(8,128)(2,1)} %collective-permute-done.13.refs_0_), channel_id=1, source_target_pairs={{4,0},{8,4},{12,8},{0,12},{5,1},{9,5},{13,9},{1,13},{6,2},{10,6},{... | collective-permute-start | bytes 2359304 | tf_op jit(solution)/shard_map/ppermute | solution.py:24
  103.5 2.0 %collective-permute-start.26 = (bf16[2,256,512]{2,1,0:T(8,128)(2,1)S(1)}, bf16[2,256,512]{2,1,0:T(8,128)(2,1)S(1)}, u32[]{:S(2)}, u32[]{:S(2)}) collective-permute-start(bf16[2,256,512]{2,1,0:T(8,128)(2,1)S(1)} %get-tuple-element.74.near1.refs_5_), channel_id=1, source_target_pairs={{0,130},{130,0},{2,128},{128,2},{1,131},{131,1},{3,129},{129,3},{4... | collective-permute-start | bytes 1572872 | tf_op jit(solution)/shard_map/ppermute | solution.py:293
  105.6 11.0 %collective-permute-done.25.refs_3_.refs_1_ = bf16[2,256,512]{2,1,0:T(8,128)(2,1)S(1)} collective-permute-done((bf16[2,256,512]{2,1,0:T(8,128)(2,1)S(1)}, bf16[2,256,512]{2,1,0:T(8,128)(2,1)S(1)}, u32[]{:S(2)}, u32[]{:S(2)}) %collective-permute-start.25) | collective-permute-done | bytes 524320 | tf_op jit(solution)/shard_map/ppermute | solution.py:28
  116.9 2.6 %collective-permute-start.32 = (bf16[448,1536]{1,0:T(8,128)(2,1)}, bf16[448,1536]{1,0:T(8,128)(2,1)}, u32[]{:S(2)}, u32[]{:S(2)}) collective-permute-start(bf16[448,1536]{1,0:T(8,128)(2,1)} %copy-done.3), channel_id=1, source_target_pairs={{0,128},{128,0},{1,129},{129,1},{2,130},{130,2},{3,131},{131,3},{4... | collective-permute-start | bytes 4128776 | tf_op jit(solution)/shard_map/ppermute | solution.py:28
  119.5 1.1 collective-permute-done.22.refs_1_
  120.7 2.9 %collective-permute-done.23.refs_2_ = bf16[256,1536]{1,0:T(8,128)(2,1)S(1)} collective-permute-done((bf16[256,1536]{1,0:T(8,128)(2,1)}, bf16[256,1536]{1,0:T(8,128)(2,1)S(1)}, u32[]{:S(2)}, u32[]{:S(2)}) %collective-permute-start.23) | collective-permute-done | bytes 786464 | tf_op jit(solution)/shard_map/ppermute | solution.py:24
  123.7 0.8 copy-done.8
  124.5 7.5 %shard_map.108 = (bf16[1536,512]{1,0:T(8,128)(2,1)}, bf16[1536,512]{1,0:T(8,128)(2,1)}) custom-call(s32[4]{0:T(128)S(1)} %pad_add_fusion.place, bf16[256,1536]{1,0:T(8,128)(2,1)} %bitcast.27, bf16[256,1536]{1,0:T(8,128)(2,1)} %copy-done.9, bf16[256,1536]{1,0:T(8,128)(2,1)} %collective-permute-done.20.refs_2_, ...), custom_call_target="tpu_custom_call" | custom-call | tf_op jit(solution)/shard_map/pallas_call | solution.py:211
  132.0 7.8 %shard_map.109 = (bf16[1536,512]{1,0:T(8,128)(2,1)}, bf16[1536,512]{1,0:T(8,128)(2,1)}) custom-call(s32[4]{0:T(128)S(1)} %pad_add_fusion.place, bf16[256,1536]{1,0:T(8,128)(2,1)} %collective-permute-done.13.refs_0_, bf16[256,1536]{1,0:T(8,128)(2,1)} %copy-done.7, bf16[256,1536]{1,0:T(8,128)(2,1)} %copy-done.8, ...), custom_call_target="tpu_custom_call" | custom-call | tf_op jit(solution)/shard_map/pallas_call | solution.py:211
  139.8 5.0 %reduce-scatter.2.cloned.1.call-done = bf16[128,1536]{1,0:T(8,128)(2,1)} async-done(((bf16[1024,1536]{1,0:T(8,128)(2,1)}), bf16[128,1536]{1,0:T(8,128)(2,1)}) %reduce-scatter.2.cloned.1.call-update) | async-done | bytes 393232 | tf_op jit(solution)/shard_map/reduce_scatter | solution.py:291
  144.8 1.1 dynamic-slice_bitcast_fusion
  145.9 1.4 collective-permute-start.29
  147.3 2.8 %collective-permute-start.30 = (bf16[32,1536]{1,0:T(8,128)(2,1)S(1)}, bf16[32,1536]{1,0:T(8,128)(2,1)S(1)}, u32[]{:S(2)}, u32[]{:S(2)}) collective-permute-start(bf16[32,1536]{1,0:T(8,128)(2,1)S(1)} %get-tuple-element.95), channel_id=1, source_target_pairs={{8,0},{12,4},{0,8},{4,12},{9,1},{13,5},{1,9},{5,13},{10,2},{14,6},... | collective-permute-start | bytes 294920 | tf_op jit(solution)/shard_map/ppermute | solution.py:24
  150.1 1.4 collective-permute-start.31
  151.5 5.5 %shard_map.110 = (bf16[1536,512]{1,0:T(8,128)(2,1)}, bf16[1536,512]{1,0:T(8,128)(2,1)}) custom-call(s32[4]{0:T(128)S(1)} %pad_add_fusion.place, bf16[256,1536]{1,0:T(8,128)(2,1)} %collective-permute-done.24.refs_0_, bf16[2,256,512]{2,1,0:T(8,128)(2,1)S(1)} %collective-permute-done.25.refs_3_.refs_1_, ...), custom_call_target="tpu_custom_call" | custom-call | tf_op jit(solution)/shard_map/pallas_call | solution.py:211
  157.7 3.6 %shard_map.111 = bf16[512,1536]{1,0:T(8,128)(2,1)} custom-call(bf16[64,1536]{1,0:T(8,128)(2,1)} %get-tuple-element.76.first, bf16[64,1536]{1,0:T(8,128)(2,1)S(1)} %copy-done.6, bf16[448,1536]{1,0:T(8,128)(2,1)S(1)} %copy-done.4, bf16[448,1536]{1,0:T(8,128)(2,1)} %collective-permute-done.32.rest_far), custom_call_target="tpu_custom_call" | custom-call | tf_op jit(solution)/shard_map/pallas_call | solution.py:230
  (64 shorter events, 9.5 us)
Async XLA Ops:
  7.2 61.9 %all-gather.2.cloned.1.call-start = ((), (), s32[]{:S(2)}) async-start(), calls=%async_computation.1 | async-start | bytes 3538944 | tf_op jit(solution)/shard_map/all_gather | solution.py:264
  7.2 10.6 %collective-permute-start = (bf16[32,1536]{1,0:T(8,128)(2,1)}, bf16[32,1536]{1,0:T(8,128)(2,1)S(1)}, u32[]{:S(2)}, u32[]{:S(2)}) collective-permute-start(bf16[32,1536]{1,0:T(8,128)(2,1)} %refs_0_.1), channel_id=1, source_target_pairs={{4,0},{8,4},{12,8},{0,12},{5,1},{9,5},{13,9},{1,13},{6,2},{10,6},{... | collective-permute-start | bytes 294920 | tf_op jit(solution)/shard_map/ppermute | solution.py:24
  10.3 7.5 %collective-permute-start.1 = (bf16[32,1536]{1,0:T(8,128)(2,1)}, bf16[32,1536]{1,0:T(8,128)(2,1)S(1)}, u32[]{:S(2)}, u32[]{:S(2)}) collective-permute-start(bf16[32,1536]{1,0:T(8,128)(2,1)} %refs_0_.1), channel_id=1, source_target_pairs={{8,0},{12,4},{0,8},{4,12},{9,1},{13,5},{1,9},{5,13},{10,2},{14,6},... | collective-permute-start | bytes 294920 | tf_op jit(solution)/shard_map/ppermute | solution.py:24
  10.9 7.4 %collective-permute-start.2 = (bf16[32,1536]{1,0:T(8,128)(2,1)}, bf16[32,1536]{1,0:T(8,128)(2,1)S(1)}, u32[]{:S(2)}, u32[]{:S(2)}) collective-permute-start(bf16[32,1536]{1,0:T(8,128)(2,1)} %refs_0_.1), channel_id=1, source_target_pairs={{12,0},{0,4},{4,8},{8,12},{13,1},{1,5},{5,9},{9,13},{14,2},{2,6},{... | collective-permute-start | bytes 294920 | tf_op jit(solution)/shard_map/ppermute | solution.py:24
  11.9 8.4 %collective-permute-start.3 = (bf16[32,1536]{1,0:T(8,128)(2,1)}, bf16[32,1536]{1,0:T(8,128)(2,1)S(1)}, u32[]{:S(2)}, u32[]{:S(2)}) collective-permute-start(bf16[32,1536]{1,0:T(8,128)(2,1)} %refs_0_.2), channel_id=1, source_target_pairs={{16,0},{32,16},{48,32},{64,48},{80,64},{96,80},{112,96},{0,112},{1... | collective-permute-start | bytes 294920 | tf_op jit(solution)/shard_map/ppermute | solution.py:24
  17.8 6.0 %collective-permute-start.4 = (bf16[32,1536]{1,0:T(8,128)(2,1)}, bf16[32,1536]{1,0:T(8,128)(2,1)S(1)}, u32[]{:S(2)}, u32[]{:S(2)}) collective-permute-start(bf16[32,1536]{1,0:T(8,128)(2,1)} %refs_0_.2), channel_id=1, source_target_pairs={{112,0},{0,16},{16,32},{32,48},{48,64},{64,80},{80,96},{96,112},{1... | collective-permute-start | bytes 294920 | tf_op jit(solution)/shard_map/ppermute | solution.py:24
  25.5 26.5 %copy-start.10 = (bf16[256,512]{1,0:T(8,128)(2,1)S(1)}, bf16[256,512]{1,0:T(8,128)(2,1)}, u32[]{:S(2)}) copy-start(bf16[256,512]{1,0:T(8,128)(2,1)} %param.9) | copy-start | bytes 786436
  25.5 119.3 %reduce-scatter.2.cloned.1.call-start = ((), (), s32[]{:S(2)}) async-start(), calls=%async_computation.2 | async-start | bytes 3538944 | tf_op jit(solution)/shard_map/reduce_scatter | solution.py:291
  25.6 16.4 %collective-permute-start.6 = (bf16[256,512]{1,0:T(8,128)(2,1)}, bf16[256,512]{1,0:T(8,128)(2,1)S(1)}, u32[]{:S(2)}, u32[]{:S(2)}) collective-permute-start(bf16[256,512]{1,0:T(8,128)(2,1)} %param.10), channel_id=1, source_target_pairs={{0,2},{2,0},{1,3},{3,1},{4,6},{6,4},{5,7},{7,5},{8,10},{10,8},{9,1... | collective-permute-start | bytes 786440 | tf_op jit(solution)/shard_map/ppermute | solution.py:28
  27.8 5.6 %collective-permute-start.8 = (bf16[32,1536]{1,0:T(8,128)(2,1)S(1)}, bf16[32,1536]{1,0:T(8,128)(2,1)S(1)}, u32[]{:S(2)}, u32[]{:S(2)}) collective-permute-start(bf16[32,1536]{1,0:T(8,128)(2,1)S(1)} %collective-permute-done.3.refs_1_), channel_id=1, source_target_pairs={{16,0},{32,16},{48,32},{64,48},{80,64},{96,80},{112,96},{0,112},{1... | collective-permute-start | bytes 294920 | tf_op jit(solution)/shard_map/ppermute | solution.py:24
  28.2 7.2 %collective-permute-start.11 = (bf16[32,1536]{1,0:T(8,128)(2,1)S(1)}, bf16[32,1536]{1,0:T(8,128)(2,1)S(1)}, u32[]{:S(2)}, u32[]{:S(2)}) collective-permute-start(bf16[32,1536]{1,0:T(8,128)(2,1)S(1)} %collective-permute-done.4.refs_7_), channel_id=1, source_target_pairs={{112,0},{0,16},{16,32},{32,48},{48,64},{64,80},{80,96},{96,112},{1... | collective-permute-start | bytes 294920 | tf_op jit(solution)/shard_map/ppermute | solution.py:24
  33.4 7.7 %collective-permute-start.9 = (bf16[32,1536]{1,0:T(8,128)(2,1)S(1)}, bf16[32,1536]{1,0:T(8,128)(2,1)S(1)}, u32[]{:S(2)}, u32[]{:S(2)}) collective-permute-start(bf16[32,1536]{1,0:T(8,128)(2,1)S(1)} %collective-permute-done.8.refs_2_), channel_id=1, source_target_pairs={{16,0},{32,16},{48,32},{64,48},{80,64},{96,80},{112,96},{0,112},{1... | collective-permute-start | bytes 294920 | tf_op jit(solution)/shard_map/ppermute | solution.py:24
  34.0 17.9 %collective-permute-start.5 = (bf16[256,512]{1,0:T(8,128)(2,1)}, bf16[256,512]{1,0:T(8,128)(2,1)S(1)}, u32[]{:S(2)}, u32[]{:S(2)}) collective-permute-start(bf16[256,512]{1,0:T(8,128)(2,1)} %param.9), channel_id=1, source_target_pairs={{0,2},{2,0},{1,3},{3,1},{4,6},{6,4},{5,7},{7,5},{8,10},{10,8},{9,1... | collective-permute-start | bytes 786440 | tf_op jit(solution)/shard_map/ppermute | solution.py:28
  35.4 7.9 %collective-permute-start.12 = (bf16[32,1536]{1,0:T(8,128)(2,1)S(1)}, bf16[32,1536]{1,0:T(8,128)(2,1)S(1)}, u32[]{:S(2)}, u32[]{:S(2)}) collective-permute-start(bf16[32,1536]{1,0:T(8,128)(2,1)S(1)} %collective-permute-done.11.refs_6_), channel_id=1, source_target_pairs={{112,0},{0,16},{16,32},{32,48},{48,64},{64,80},{80,96},{96,112},{1... | collective-permute-start | bytes 294920 | tf_op jit(solution)/shard_map/ppermute | solution.py:24
  41.1 6.7 %collective-permute-start.10 = (bf16[32,1536]{1,0:T(8,128)(2,1)S(1)}, bf16[32,1536]{1,0:T(8,128)(2,1)S(1)}, u32[]{:S(2)}, u32[]{:S(2)}) collective-permute-start(bf16[32,1536]{1,0:T(8,128)(2,1)S(1)} %collective-permute-done.9.refs_3_), channel_id=1, source_target_pairs={{16,0},{32,16},{48,32},{64,48},{80,64},{96,80},{112,96},{0,112},{1... | collective-permute-start | bytes 294920 | tf_op jit(solution)/shard_map/ppermute | solution.py:24
  48.7 29.3 %copy-start = (bf16[8,32,1536]{2,1,0:T(8,128)(2,1)}, bf16[8,32,1536]{2,1,0:T(8,128)(2,1)S(1)}, u32[]{:S(2)}) copy-start(bf16[8,32,1536]{2,1,0:T(8,128)(2,1)S(1)} %shard_map.103) | copy-start | bytes 2359300
  48.7 13.6 %collective-permute-start.13 = (bf16[256,1536]{1,0:T(8,128)(2,1)S(1)}, bf16[256,1536]{1,0:T(8,128)(2,1)}, u32[]{:S(2)}, u32[]{:S(2)}) collective-permute-start(bf16[256,1536]{1,0:T(8,128)(2,1)S(1)} %bitcast.23), channel_id=1, source_target_pairs={{0,128},{128,0},{1,129},{129,1},{2,130},{130,2},{3,131},{131,3},{4... | collective-permute-start | bytes 2359304 | tf_op jit(solution)/shard_map/ppermute | solution.py:28
  49.8 13.8 %collective-permute-start.14 = (bf16[256,1536]{1,0:T(8,128)(2,1)S(1)}, bf16[256,1536]{1,0:T(8,128)(2,1)S(1)}, u32[]{:S(2)}, u32[]{:S(2)}) collective-permute-start(bf16[256,1536]{1,0:T(8,128)(2,1)S(1)} %bitcast.24), channel_id=1, source_target_pairs={{4,0},{8,4},{12,8},{0,12},{5,1},{9,5},{13,9},{1,13},{6,2},{10,6},{... | collective-permute-start | bytes 2359304 | tf_op jit(solution)/shard_map/ppermute | solution.py:24
  52.0 13.3 %collective-permute-start.15 = (bf16[256,1536]{1,0:T(8,128)(2,1)S(1)}, bf16[256,1536]{1,0:T(8,128)(2,1)}, u32[]{:S(2)}, u32[]{:S(2)}) collective-permute-start(bf16[256,1536]{1,0:T(8,128)(2,1)S(1)} %bitcast.25), channel_id=1, source_target_pairs={{12,0},{0,4},{4,8},{8,12},{13,1},{1,5},{5,9},{9,13},{14,2},{2,6},{... | collective-permute-start | bytes 2359304 | tf_op jit(solution)/shard_map/ppermute | solution.py:24
  52.4 2.2 %collective-permute-start.7 = (bf16[2,256,512]{2,1,0:T(8,128)(2,1)S(1)}, bf16[2,256,512]{2,1,0:T(8,128)(2,1)S(1)}, u32[]{:S(2)}, u32[]{:S(2)}) collective-permute-start(bf16[2,256,512]{2,1,0:T(8,128)(2,1)S(1)} %fusion.4.hidden), channel_id=1, source_target_pairs={{0,1},{1,0},{2,3},{3,2},{4,5},{5,4},{6,7},{7,6},{8,9},{9,8},{10,11... | collective-permute-start | bytes 1572872 | tf_op jit(solution)/shard_map/ppermute | solution.py:28
  63.7 0.9 copy-start.9
  73.6 2.0 %collective-permute-start.16 = (bf16[2,256,512]{2,1,0:T(8,128)(2,1)S(1)}, bf16[2,256,512]{2,1,0:T(8,128)(2,1)S(1)}, u32[]{:S(2)}, u32[]{:S(2)}) collective-permute-start(bf16[2,256,512]{2,1,0:T(8,128)(2,1)S(1)} %get-tuple-element.64), channel_id=1, source_target_pairs={{0,1},{1,0},{2,3},{3,2},{4,5},{5,4},{6,7},{7,6},{8,9},{9,8},{10,11... | collective-permute-start | bytes 1572872 | tf_op jit(solution)/shard_map/ppermute | solution.py:28
  75.8 15.6 %collective-permute-start.17 = (bf16[2,256,512]{2,1,0:T(8,128)(2,1)S(1)}, bf16[2,256,512]{2,1,0:T(8,128)(2,1)S(1)}, u32[]{:S(2)}, u32[]{:S(2)}) collective-permute-start(bf16[2,256,512]{2,1,0:T(8,128)(2,1)S(1)} %get-tuple-element.108), channel_id=1, source_target_pairs={{0,2},{2,0},{1,3},{3,1},{4,6},{6,4},{5,7},{7,5},{8,10},{10,8},{9,1... | collective-permute-start | bytes 1572872 | tf_op jit(solution)/shard_map/ppermute | solution.py:28
  78.0 22.2 %collective-permute-start.20 = (bf16[256,1536]{1,0:T(8,128)(2,1)S(1)}, bf16[256,1536]{1,0:T(8,128)(2,1)}, u32[]{:S(2)}, u32[]{:S(2)}) collective-permute-start(bf16[256,1536]{1,0:T(8,128)(2,1)S(1)} %bitcast.26), channel_id=1, source_target_pairs={{8,0},{12,4},{0,8},{4,12},{9,1},{13,5},{1,9},{5,13},{10,2},{14,6},... | collective-permute-start | bytes 2359304 | tf_op jit(solution)/shard_map/ppermute | solution.py:24
  80.0 14.7 %copy-start.2 = (bf16[1536,512]{1,0:T(8,128)(2,1)S(1)}, bf16[1536,512]{1,0:T(8,128)(2,1)}, u32[]{:S(2)}) copy-start(bf16[1536,512]{1,0:T(8,128)(2,1)} %w_up.1) | copy-start | bytes 4718596
  84.6 1.1 copy-start.3
  85.8 8.9 %copy-start.1 = (bf16[1536,512]{1,0:T(8,128)(2,1)S(1)}, bf16[1536,512]{1,0:T(8,128)(2,1)}, u32[]{:S(2)}) copy-start(bf16[1536,512]{1,0:T(8,128)(2,1)} %w_gate.1) | copy-start | bytes 4718596
  92.0 2.0 %collective-permute-start.18 = (bf16[2,256,512]{2,1,0:T(8,128)(2,1)S(1)}, bf16[2,256,512]{2,1,0:T(8,128)(2,1)S(1)}, u32[]{:S(2)}, u32[]{:S(2)}) collective-permute-start(bf16[2,256,512]{2,1,0:T(8,128)(2,1)S(1)} %get-tuple-element.73.near0.refs_4_), channel_id=1, source_target_pairs={{0,1},{1,0},{2,3},{3,2},{4,5},{5,4},{6,7},{7,6},{8,9},{9,8},{10,11... | collective-permute-start | bytes 1572872 | tf_op jit(solution)/shard_map/ppermute | solution.py:28
  92.1 2.6 %collective-permute-start.19 = (bf16[2,256,512]{2,1,0:T(8,128)(2,1)S(1)}, bf16[2,256,512]{2,1,0:T(8,128)(2,1)S(1)}, u32[]{:S(2)}, u32[]{:S(2)}) collective-permute-start(bf16[2,256,512]{2,1,0:T(8,128)(2,1)S(1)} %get-tuple-element.74.near1.refs_5_), channel_id=1, source_target_pairs={{0,1},{1,0},{2,3},{3,2},{4,5},{5,4},{6,7},{7,6},{8,9},{9,8},{10,11... | collective-permute-start | bytes 1572872 | tf_op jit(solution)/shard_map/ppermute | solution.py:28
  92.6 7.7 %collective-permute-start.21 = (bf16[64,1536]{1,0:T(8,128)(2,1)}, bf16[64,1536]{1,0:T(8,128)(2,1)S(1)}, u32[]{:S(2)}, u32[]{:S(2)}) collective-permute-start(bf16[64,1536]{1,0:T(8,128)(2,1)} %get-tuple-element.76.first), channel_id=1, source_target_pairs={{0,128},{128,0},{1,129},{129,1},{2,130},{130,2},{3,131},{131,3},{4... | collective-permute-start | bytes 589832 | tf_op jit(solution)/shard_map/ppermute | solution.py:28
  100.2 0.7 copy-start.5
  100.9 19.8 %collective-permute-start.22 = (bf16[256,1536]{1,0:T(8,128)(2,1)}, bf16[256,1536]{1,0:T(8,128)(2,1)S(1)}, u32[]{:S(2)}, u32[]{:S(2)}) collective-permute-start(bf16[256,1536]{1,0:T(8,128)(2,1)} %collective-permute-done.13.refs_0_), channel_id=1, source_target_pairs={{4,0},{8,4},{12,8},{0,12},{5,1},{9,5},{13,9},{1,13},{6,2},{10,6},{... | collective-permute-start | bytes 2359304 | tf_op jit(solution)/shard_map/ppermute | solution.py:24
  102.9 20.7 %collective-permute-start.23 = (bf16[256,1536]{1,0:T(8,128)(2,1)}, bf16[256,1536]{1,0:T(8,128)(2,1)S(1)}, u32[]{:S(2)}, u32[]{:S(2)}) collective-permute-start(bf16[256,1536]{1,0:T(8,128)(2,1)} %collective-permute-done.13.refs_0_), channel_id=1, source_target_pairs={{12,0},{0,4},{4,8},{8,12},{13,1},{1,5},{5,9},{9,13},{14,2},{2,6},{... | collective-permute-start | bytes 2359304 | tf_op jit(solution)/shard_map/ppermute | solution.py:24
  102.9 13.7 %collective-permute-start.25 = (bf16[2,256,512]{2,1,0:T(8,128)(2,1)S(1)}, bf16[2,256,512]{2,1,0:T(8,128)(2,1)S(1)}, u32[]{:S(2)}, u32[]{:S(2)}) collective-permute-start(bf16[2,256,512]{2,1,0:T(8,128)(2,1)S(1)} %get-tuple-element.73.near0.refs_4_), channel_id=1, source_target_pairs={{0,128},{128,0},{1,129},{129,1},{2,130},{130,2},{3,131},{131,3},{4... | collective-permute-start | bytes 1572872 | tf_op jit(solution)/shard_map/ppermute | solution.py:28
  103.5 13.4 %collective-permute-start.26 = (bf16[2,256,512]{2,1,0:T(8,128)(2,1)S(1)}, bf16[2,256,512]{2,1,0:T(8,128)(2,1)S(1)}, u32[]{:S(2)}, u32[]{:S(2)}) collective-permute-start(bf16[2,256,512]{2,1,0:T(8,128)(2,1)S(1)} %get-tuple-element.74.near1.refs_5_), channel_id=1, source_target_pairs={{0,130},{130,0},{2,128},{128,2},{1,131},{131,1},{3,129},{129,3},{4... | collective-permute-start | bytes 1572872 | tf_op jit(solution)/shard_map/ppermute | solution.py:293
  116.9 40.7 %collective-permute-start.32 = (bf16[448,1536]{1,0:T(8,128)(2,1)}, bf16[448,1536]{1,0:T(8,128)(2,1)}, u32[]{:S(2)}, u32[]{:S(2)}) collective-permute-start(bf16[448,1536]{1,0:T(8,128)(2,1)} %copy-done.3), channel_id=1, source_target_pairs={{0,128},{128,0},{1,129},{129,1},{2,130},{130,2},{3,131},{131,3},{4... | collective-permute-start | bytes 4128776 | tf_op jit(solution)/shard_map/ppermute | solution.py:28
  120.7 2.9 %copy-start.7 = (bf16[256,1536]{1,0:T(8,128)(2,1)}, bf16[256,1536]{1,0:T(8,128)(2,1)S(1)}, u32[]{:S(2)}) copy-start(bf16[256,1536]{1,0:T(8,128)(2,1)S(1)} %collective-permute-done.22.refs_1_) | copy-start | bytes 2359300
  123.6 0.9 copy-start.8
  123.6 22.2 %collective-permute-start.24 = (bf16[256,1536]{1,0:T(8,128)(2,1)}, bf16[256,1536]{1,0:T(8,128)(2,1)}, u32[]{:S(2)}, u32[]{:S(2)}) collective-permute-start(bf16[256,1536]{1,0:T(8,128)(2,1)} %collective-permute-done.13.refs_0_), channel_id=1, source_target_pairs={{8,0},{12,4},{0,8},{4,12},{9,1},{13,5},{1,9},{5,13},{10,2},{14,6},... | collective-permute-start | bytes 2359304 | tf_op jit(solution)/shard_map/ppermute | solution.py:24
  123.6 8.4 %collective-permute-start.27 = (bf16[2,256,512]{2,1,0:T(8,128)(2,1)S(1)}, bf16[2,256,512]{2,1,0:T(8,128)(2,1)}, u32[]{:S(2)}, u32[]{:S(2)}) collective-permute-start(bf16[2,256,512]{2,1,0:T(8,128)(2,1)S(1)} %collective-permute-done.25.refs_3_.refs_1_), channel_id=1, source_target_pairs={{0,1},{1,0},{2,3},{3,2},{4,5},{5,4},{6,7},{7,6},{8,9},{9,8},{10,11... | collective-permute-start | bytes 1572872 | tf_op jit(solution)/shard_map/ppermute | solution.py:28
  124.5 7.5 %collective-permute-start.28 = (bf16[2,256,512]{2,1,0:T(8,128)(2,1)S(1)}, bf16[2,256,512]{2,1,0:T(8,128)(2,1)}, u32[]{:S(2)}, u32[]{:S(2)}) collective-permute-start(bf16[2,256,512]{2,1,0:T(8,128)(2,1)S(1)} %collective-permute-done.26.refs_4_.refs_2_), channel_id=1, source_target_pairs={{0,1},{1,0},{2,3},{3,2},{4,5},{5,4},{6,7},{7,6},{8,9},{9,8},{10,11... | collective-permute-start | bytes 1572872 | tf_op jit(solution)/shard_map/ppermute | solution.py:28
  145.8 11.8 %copy-start.4 = (bf16[448,1536]{1,0:T(8,128)(2,1)S(1)}, bf16[448,1536]{1,0:T(8,128)(2,1)}, u32[]{:S(2)}) copy-start(bf16[448,1536]{1,0:T(8,128)(2,1)} %copy-done.3) | copy-start | bytes 4128772
  145.9 11.8 %copy-start.6 = (bf16[64,1536]{1,0:T(8,128)(2,1)S(1)}, bf16[64,1536]{1,0:T(8,128)(2,1)}, u32[]{:S(2)}) copy-start(bf16[64,1536]{1,0:T(8,128)(2,1)} %copy-done.5) | copy-start | bytes 589828
  145.9 11.1 %collective-permute-start.29 = (bf16[32,1536]{1,0:T(8,128)(2,1)S(1)}, bf16[32,1536]{1,0:T(8,128)(2,1)S(1)}, u32[]{:S(2)}, u32[]{:S(2)}) collective-permute-start(bf16[32,1536]{1,0:T(8,128)(2,1)S(1)} %get-tuple-element.94), channel_id=1, source_target_pairs={{12,0},{0,4},{4,8},{8,12},{13,1},{1,5},{5,9},{9,13},{14,2},{2,6},{... | collective-permute-start | bytes 294920 | tf_op jit(solution)/shard_map/ppermute | solution.py:24
  147.3 9.7 %collective-permute-start.30 = (bf16[32,1536]{1,0:T(8,128)(2,1)S(1)}, bf16[32,1536]{1,0:T(8,128)(2,1)S(1)}, u32[]{:S(2)}, u32[]{:S(2)}) collective-permute-start(bf16[32,1536]{1,0:T(8,128)(2,1)S(1)} %get-tuple-element.95), channel_id=1, source_target_pairs={{8,0},{12,4},{0,8},{4,12},{9,1},{13,5},{1,9},{5,13},{10,2},{14,6},... | collective-permute-start | bytes 294920 | tf_op jit(solution)/shard_map/ppermute | solution.py:24
  150.1 6.9 %collective-permute-start.31 = (bf16[32,1536]{1,0:T(8,128)(2,1)S(1)}, bf16[32,1536]{1,0:T(8,128)(2,1)S(1)}, u32[]{:S(2)}, u32[]{:S(2)}) collective-permute-start(bf16[32,1536]{1,0:T(8,128)(2,1)S(1)} %get-tuple-element.96), channel_id=1, source_target_pairs={{4,0},{8,4},{12,8},{0,12},{5,1},{9,5},{13,9},{1,13},{6,2},{10,6},{... | collective-permute-start | bytes 294920 | tf_op jit(solution)/shard_map/ppermute | solution.py:24
Sparse Core Ops, SparseCore 0:
  25.6 43.3 all-gather.1
  100.4 44.3 reduce-scatter.1

commit v11 on v9

--- a/solution.py
+++ b/solution.py
@@ -176,7 +176,7 @@
 
 
 def weight_kernel(slots, based, place, *refs):
-    count = len(slots)
+    count, turns = len(slots), sorted({k for k, _, _ in slots})
     pieces, grads, base = refs[:count], refs[count:count + 4], refs[count + 4:-3]
     d_gate, d_up, rows = refs[-3:]
 
@@ -186,15 +186,16 @@
             core = place[3] if half < 2 else 1 - place[3]
             for pair in range(2):
                 z = 4 * (half % 2) + 2 * core + pair
-                for index, k in enumerate(slots):
+                for index, k in enumerate(turns):
                     start = pair * 128 + (place[1] + k) % NY * 32
                     lines = pl.ds(pl.multiple_of(start, 32), 32)
                     rows[index, z, :, :512] = grads[half][0, lines, :]
                     rows[index, z, :, 512:] = grads[half][1, lines, :]
 
     total = jnp.zeros((d_gate.shape[0], 1024), F32)
-    for index, piece in enumerate(pieces):
-        total = total + dot(piece[...], rows[index].reshape(256, 1024), 0, 0)
+    for (k, low, high), piece in zip(slots, pieces):
+        lines = rows[turns.index(k), low:high].reshape(32 * (high - low), 1024)
+        total = total + dot(piece[...], lines, 0, 0)
     gate, up = total[:, :512], total[:, 512:]
     if based:
         gate = gate + base[0][...].astype(F32)
@@ -205,16 +206,16 @@
 
 def weight_grads(place, slots, pieces, grads, base=(), last=False):
     size = 512 if last else 256
-    piece = pl.BlockSpec((256, size), lambda i: (0, i))
+    pieces_in = [pl.BlockSpec((32 * (high - low), size), lambda i: (0, i)) for _, low, high in slots]
     tile = pl.BlockSpec((size, 512), lambda i: (i, 0))
     shape = jax.ShapeDtypeStruct((1536, 512), BF16) if last else pltpu.HBM((1536, 512), BF16)
     return pl.pallas_call(
         functools.partial(weight_kernel, slots, bool(base)),
         grid=(1536 // size,),
         out_shape=(shape, shape),
-        in_specs=[SMEM] + [piece] * len(slots) + [VMEM] * 4 + [tile] * len(base),
+        in_specs=[SMEM] + pieces_in + [VMEM] * 4 + [tile] * len(base),
         out_specs=(tile, tile),
-        scratch_shapes=[pltpu.VMEM((len(slots), NZ, 32, 1024), BF16)],
+        scratch_shapes=[pltpu.VMEM((len({k for k, _, _ in slots}), NZ, 32, 1024), BF16)],
         compiler_params=grant(16),
     )(place, *(x if last else in_hbm(x) for x in pieces), *grads, *(in_hbm(x) for x in base))
 
@@ -248,6 +249,18 @@
     return [x] + ahead + behind[::-1]
 
 
+def whole(*turns):
+    return tuple((k, 0, NZ) for k in turns)
+
+
+OPPOSITE = ((2, 0, NZ // 2), (2, NZ // 2, NZ))
+
+
+def opposite(ahead, behind):
+    top = from_ahead(ahead[:128], "y", NY, 1)
+    return top, from_ahead(behind[128:], "y", NY, NY - 1)
+
+
 def ordered(mine, other, index):
     low = jnp.where(index == 0, mine, other)
     high = jnp.where(index == 0, other, mine)
@@ -291,24 +304,25 @@
     in_z = lax.psum_scatter(partial_in, "z", scatter_dimension=0, tiled=True).reshape(NY, 32, 1536)
 
     far = [swap(near[0], "dp"), lax.ppermute(near[1], ("dp", "xh"), [(0, 3), (3, 0), (1, 2), (2, 1)])]
-    partner1, partner2, partner3 = (from_ahead(partner_z, "y", NY, k) for k in (1, 2, 3))
+    partner1, partner3 = from_ahead(partner_z, "y", NY, 1), from_ahead(partner_z, "y", NY, 3)
     far, down_rest = lax.optimization_barrier((far, down_rest))
     rest_far = swap(down_rest, "dp")
     own_z, partner1, partner3 = lax.optimization_barrier((own_z, partner1, partner3))
-    own_gate, own_up = weight_grads(place, (0, 1, 2, 3), (own_z, own1, own2, own3), (*near, *other))
+    partner2 = opposite(partner1, partner3)
+    own_gate, own_up = weight_grads(place, whole(0, 1, 2, 3), (own_z, own1, own2, own3), (*near, *other))
     far_other = [swap(half, "core") for half in far]
 
     y = place[1]
     slabs = [lax.dynamic_index_in_dim(in_z, (y + k) % NY, 0, keepdims=False) for k in range(NY)]
     grads = (*far, *far_other)
-    most = weight_grads(place, (0, 1, 3), (partner_z, partner1, partner3), grads, (own_gate, own_up))
-    slabs, partner2, most = lax.optimization_barrier((slabs, partner2, most))
+    most = weight_grads(place, whole(0, 1, 3), (partner_z, partner1, partner3), grads, (own_gate, own_up))
+    grad_gate, grad_up = weight_grads(place, OPPOSITE, partner2, grads, most, last=True)
+    slabs, grad_gate, grad_up = lax.optimization_barrier((slabs, grad_gate, grad_up))
     total = slabs[0].astype(F32)
     for k in range(1, NY):
         total = total + from_ahead(slabs[k], "y", NY, NY - k).astype(F32)
     grad_input = total.astype(BF16)
-    grad_gate, grad_up = weight_grads(place, (2,), (partner2,), grads, most, last=True)
-    grad_input, grad_gate, grad_up, rest_far = lax.optimization_barrier((grad_input, grad_gate, grad_up, rest_far))
+    grad_input, rest_far = lax.optimization_barrier((grad_input, rest_far))
     return grad_input, grad_gate, grad_up, add(down_first, first_far, down_rest, rest_far)
 
 

time: 179 us -> 169 us (0.944)
  waiting for transfers between devices: 76.5 us -> 62.6 us
  local copies, waits for them, and re-layouts: 3.1 us -> 5.39 us
  starting transfers between devices: 39.6 us -> 41.8 us
    ppermute x19 -> x20, waiting for transfers between devices: 42.6 us -> 28.8 us  [from_ahead(): return lax.ppermute(x, axis, [((d + k) % n, d) for d in range(n)])]
    ppermute x19 -> x20, starting transfers between devices: 26.2 us -> 27.6 us  [from_ahead(): return lax.ppermute(x, axis, [((d + k) % n, d) for d in range(n)])]
  transfers between devices with their start and end apart: 35 -> 36, of which waited for: 20 -> 23; matrix products, arithmetic and copies ran while one was open for 2% -> 3% of each run, Pallas kernels for 18% -> 19%
where the time goes in v11:
time: 169 us
  waiting for transfers between devices  62.6 us (37%)
  Pallas kernels  42.3 us (25%)
  starting transfers between devices  41.8 us (25%)
  between operations  14.2 us (8%)
  local copies, waits for them, and re-layouts  5.39 us (3%)
  other arithmetic  2.43 us (1%)
    ppermute x13, waiting for transfers between devices, swap(): return lax.ppermute(x, axis, [(0, 1), (1, 0)])  29.7 us
    ppermute x20, waiting for transfers between devices, from_ahead(): return lax.ppermute(x, axis, [((d + k) % n, d) for d in range(n)])  28.8 us
    ppermute x20, starting transfers between devices, from_ahead(): return lax.ppermute(x, axis, [((d + k) % n, d) for d in range(n)])  27.6 us
    pallas_call x3, Pallas kernels, weight_grads(): pl.pallas_call(functools.partial(weight_kernel, slots, bool(base)), grid=...  20.8 us
    ppermute x13, starting transfers between devices, swap(): return lax.ppermute(x, axis, [(0, 1), (1, 0)])  12.1 us
    pallas_call x1, Pallas kernels, input_grad(): pl.pallas_call(input_grad_kernel, grid=(3,), out_shape=jax.ShapeDtypeStru...  5.45 us
    pallas_call x1, Pallas kernels, down_grad(): pl.pallas_call(down_kernel, grid=(3,), out_shape=(jax.ShapeDtypeStruct((F...  4.68 us
    pallas_call x1, Pallas kernels, hidden_grad(): pl.pallas_call(hidden_grad_kernel, out_shape=(jax.ShapeDtypeStruct((2, 25...  4.58 us
  transfers between devices with their start and end apart: 36, of which 23 were waited for; matrix products, arithmetic and copies ran while one was open for 3% of the time, Pallas kernels for 19%

profile of v11, /device:TPU:2, one launch (start us, length us, event | category | flops | bytes accessed | tf_op | source)
XLA Modules:
  0.0 168.8 jit_solution(5755123870206305514)
XLA Ops:
  7.2 3.1 %collective-permute-start = (bf16[32,1536]{1,0:T(8,128)(2,1)}, bf16[32,1536]{1,0:T(8,128)(2,1)S(1)}, u32[]{:S(2)}, u32[]{:S(2)}) collective-permute-start(bf16[32,1536]{1,0:T(8,128)(2,1)} %refs_0_.1), channel_id=1, source_target_pairs={{4,0},{8,4},{12,8},{0,12},{5,1},{9,5},{13,9},{1,13},{6,2},{10,6},{... | collective-permute-start | bytes 294920 | tf_op jit(solution)/shard_map/ppermute | solution.py:24
  10.9 1.0 collective-permute-start.2
  11.9 5.9 %collective-permute-start.3 = (bf16[32,1536]{1,0:T(8,128)(2,1)}, bf16[32,1536]{1,0:T(8,128)(2,1)S(1)}, u32[]{:S(2)}, u32[]{:S(2)}) collective-permute-start(bf16[32,1536]{1,0:T(8,128)(2,1)} %refs_0_.2), channel_id=1, source_target_pairs={{16,0},{32,16},{48,32},{64,48},{80,64},{96,80},{112,96},{0,112},{1... | collective-permute-start | bytes 294920 | tf_op jit(solution)/shard_map/ppermute | solution.py:24
  18.4 1.9 %collective-permute-done.3.refs_1_ = bf16[32,1536]{1,0:T(8,128)(2,1)S(1)} collective-permute-done((bf16[32,1536]{1,0:T(8,128)(2,1)}, bf16[32,1536]{1,0:T(8,128)(2,1)S(1)}, u32[]{:S(2)}, u32[]{:S(2)}) %collective-permute-start.3) | collective-permute-done | bytes 98336 | tf_op jit(solution)/shard_map/ppermute | solution.py:24
  20.3 3.5 %collective-permute-done.4.refs_7_ = bf16[32,1536]{1,0:T(8,128)(2,1)S(1)} collective-permute-done((bf16[32,1536]{1,0:T(8,128)(2,1)}, bf16[32,1536]{1,0:T(8,128)(2,1)S(1)}, u32[]{:S(2)}, u32[]{:S(2)}) %collective-permute-start.4) | collective-permute-done | bytes 98336 | tf_op jit(solution)/shard_map/ppermute | solution.py:24
  23.8 1.7 shard_map.102
  25.6 2.2 %collective-permute-start.6 = (bf16[256,512]{1,0:T(8,128)(2,1)}, bf16[256,512]{1,0:T(8,128)(2,1)S(1)}, u32[]{:S(2)}, u32[]{:S(2)}) collective-permute-start(bf16[256,512]{1,0:T(8,128)(2,1)} %param.10), channel_id=1, source_target_pairs={{0,2},{2,0},{1,3},{3,1},{4,6},{6,4},{5,7},{7,5},{8,10},{10,8},{9,1... | collective-permute-start | bytes 786440 | tf_op jit(solution)/shard_map/ppermute | solution.py:28
  28.2 1.6 collective-permute-start.11
  29.8 3.6 %collective-permute-done.8.refs_2_ = bf16[32,1536]{1,0:T(8,128)(2,1)S(1)} collective-permute-done((bf16[32,1536]{1,0:T(8,128)(2,1)S(1)}, bf16[32,1536]{1,0:T(8,128)(2,1)S(1)}, u32[]{:S(2)}, u32[]{:S(2)}) %collective-permute-start.8) | collective-permute-done | bytes 98336 | tf_op jit(solution)/shard_map/ppermute | solution.py:24
  34.0 1.4 collective-permute-start.5
  35.4 1.4 collective-permute-start.12
  36.8 4.2 %collective-permute-done.9.refs_3_ = bf16[32,1536]{1,0:T(8,128)(2,1)S(1)} collective-permute-done((bf16[32,1536]{1,0:T(8,128)(2,1)S(1)}, bf16[32,1536]{1,0:T(8,128)(2,1)S(1)}, u32[]{:S(2)}, u32[]{:S(2)}) %collective-permute-start.9) | collective-permute-done | bytes 98336 | tf_op jit(solution)/shard_map/ppermute | solution.py:24
  41.1 0.9 collective-permute-start.10
  42.0 1.0 select_bitcast_fusion.1
  43.4 4.4 %collective-permute-done.10.refs_4_ = bf16[32,1536]{1,0:T(8,128)(2,1)S(1)} collective-permute-done((bf16[32,1536]{1,0:T(8,128)(2,1)S(1)}, bf16[32,1536]{1,0:T(8,128)(2,1)S(1)}, u32[]{:S(2)}, u32[]{:S(2)}) %collective-permute-start.10) | collective-permute-done | bytes 98336 | tf_op jit(solution)/shard_map/ppermute | solution.py:24
  47.7 1.0 shard_map.103
  48.7 1.1 collective-permute-start.13
  49.8 2.2 %collective-permute-start.14 = (bf16[256,1536]{1,0:T(8,128)(2,1)S(1)}, bf16[256,1536]{1,0:T(8,128)(2,1)S(1)}, u32[]{:S(2)}, u32[]{:S(2)}) collective-permute-start(bf16[256,1536]{1,0:T(8,128)(2,1)S(1)} %bitcast.24), channel_id=1, source_target_pairs={{4,0},{8,4},{12,8},{0,12},{5,1},{9,5},{13,9},{1,13},{6,2},{10,6},{... | collective-permute-start | bytes 2359304 | tf_op jit(solution)/shard_map/ppermute | solution.py:24
  52.8 1.8 %collective-permute-done.7.hidden_other = bf16[2,256,512]{2,1,0:T(8,128)(2,1)S(1)} collective-permute-done((bf16[2,256,512]{2,1,0:T(8,128)(2,1)S(1)}, bf16[2,256,512]{2,1,0:T(8,128)(2,1)S(1)}, u32[]{:S(2)}, u32[]{:S(2)}) %collective-permute-start.7) | collective-permute-done | bytes 524320 | tf_op jit(solution)/shard_map/ppermute | solution.py:28
  54.5 7.8 %collective-permute-done.13.refs_0_ = bf16[256,1536]{1,0:T(8,128)(2,1)} collective-permute-done((bf16[256,1536]{1,0:T(8,128)(2,1)S(1)}, bf16[256,1536]{1,0:T(8,128)(2,1)}, u32[]{:S(2)}, u32[]{:S(2)}) %collective-permute-start.13) | collective-permute-done | bytes 786464 | tf_op jit(solution)/shard_map/ppermute | solution.py:28
  62.3 1.4 collective-permute-done.14.refs_1_
  63.7 0.9 copy-done.9
  65.3 3.8 %all-gather.2.cloned.1.call-done.go = bf16[1024,1536]{1,0:T(8,128)(2,1)} async-done(((bf16[128,1536]{1,0:T(8,128)(2,1)}), bf16[1024,1536]{1,0:T(8,128)(2,1)}) %all-gather.2.cloned.1.call-update) | async-done | bytes 3145744 | tf_op jit(solution)/shard_map/all_gather | solution.py:277
  69.0 4.6 %shard_map.104 = (f32[2,256,512]{2,1,0:T(8,128)S(1)}, bf16[2,256,512]{2,1,0:T(8,128)(2,1)S(1)}) custom-call(s32[4]{0:T(128)S(1)} %pad_add_fusion.place, bf16[1024,1536]{1,0:T(8,128)(2,1)} %all-gather.2.cloned.1.call-done.go, bf16[512,1536]{1,0:T(8,128)(2,1)} %w_down.1), custom_call_target="tpu_custom_call" | custom-call | tf_op jit(solution)/shard_map/pallas_call | solution.py:79
  73.7 1.9 %collective-permute-done.16 = bf16[2,256,512]{2,1,0:T(8,128)(2,1)S(1)} collective-permute-done((bf16[2,256,512]{2,1,0:T(8,128)(2,1)S(1)}, bf16[2,256,512]{2,1,0:T(8,128)(2,1)S(1)}, u32[]{:S(2)}, u32[]{:S(2)}) %collective-permute-start.16) | collective-permute-done | bytes 524320 | tf_op jit(solution)/shard_map/ppermute | solution.py:28
  75.8 2.2 %collective-permute-start.17 = (bf16[2,256,512]{2,1,0:T(8,128)(2,1)S(1)}, bf16[2,256,512]{2,1,0:T(8,128)(2,1)S(1)}, u32[]{:S(2)}, u32[]{:S(2)}) collective-permute-start(bf16[2,256,512]{2,1,0:T(8,128)(2,1)S(1)} %get-tuple-element.100), channel_id=1, source_target_pairs={{0,2},{2,0},{1,3},{3,1},{4,6},{6,4},{5,7},{7,5},{8,10},{10,8},{9,1... | collective-permute-start | bytes 1572872 | tf_op jit(solution)/shard_map/ppermute | solution.py:28
  78.0 2.0 %collective-permute-start.20 = (bf16[256,1536]{1,0:T(8,128)(2,1)S(1)}, bf16[256,1536]{1,0:T(8,128)(2,1)}, u32[]{:S(2)}, u32[]{:S(2)}) collective-permute-start(bf16[256,1536]{1,0:T(8,128)(2,1)S(1)} %bitcast.26), channel_id=1, source_target_pairs={{8,0},{12,4},{0,8},{4,12},{9,1},{13,5},{1,9},{5,13},{10,2},{14,6},... | collective-permute-start | bytes 2359304 | tf_op jit(solution)/shard_map/ppermute | solution.py:24
  80.0 4.7 %shard_map.105 = (bf16[64,1536]{1,0:T(8,128)(2,1)}, bf16[448,1536]{1,0:T(8,128)(2,1)S(1)}) custom-call(s32[4]{0:T(128)S(1)} %pad_add_fusion.place, bf16[2,256,512]{2,1,0:T(8,128)(2,1)S(1)} %fusion.4.hidden, bf16[2,256,512]{2,1,0:T(8,128)(2,1)S(1)} %collective-permute-done.7.hidden_other, bf16[1024,1536]{1,0:T(8,128)(2,1)} %all-gather.2.cloned.1.call-done.go), custom_call_target="tpu_custom_call" | custom-call | tf_op jit(solution)/shard_map/pallas_call | solution.py:161
  84.6 1.1 copy-done.3
  85.8 5.6 %collective-permute-done.17.chip_far = bf16[2,256,512]{2,1,0:T(8,128)(2,1)S(1)} collective-permute-done((bf16[2,256,512]{2,1,0:T(8,128)(2,1)S(1)}, bf16[2,256,512]{2,1,0:T(8,128)(2,1)S(1)}, u32[]{:S(2)}, u32[]{:S(2)}) %collective-permute-start.17) | collective-permute-done | bytes 524320 | tf_op jit(solution)/shard_map/ppermute | solution.py:28
  94.7 5.5 %shard_map.107 = bf16[1024,1536]{1,0:T(8,128)(2,1)} custom-call(s32[4]{0:T(128)S(1)} %pad_add_fusion.place, bf16[2,256,512]{2,1,0:T(8,128)(2,1)S(1)} %get-tuple-element.69.near0.refs_4_, bf16[2,256,512]{2,1,0:T(8,128)(2,1)S(1)} %get-tuple-element.70.near1.refs_5_, bf16[2,256,512]{2,1,0:T(8,128)(2,1)S(1)} %collective-permute-done.18.other0.refs_6_, ...), custom_call_target="tpu_custom_call" | custom-call | tf_op jit(solution)/shard_map/pallas_call | solution.py:131
  100.8 2.0 %collective-permute-start.22 = (bf16[256,1536]{1,0:T(8,128)(2,1)}, bf16[256,1536]{1,0:T(8,128)(2,1)S(1)}, u32[]{:S(2)}, u32[]{:S(2)}) collective-permute-start(bf16[256,1536]{1,0:T(8,128)(2,1)} %collective-permute-done.13.refs_0_), channel_id=1, source_target_pairs={{4,0},{8,4},{12,8},{0,12},{5,1},{9,5},{13,9},{1,13},{6,2},{10,6},{... | collective-permute-start | bytes 2359304 | tf_op jit(solution)/shard_map/ppermute | solution.py:24
  103.5 2.0 %collective-permute-start.27 = (bf16[2,256,512]{2,1,0:T(8,128)(2,1)S(1)}, bf16[2,256,512]{2,1,0:T(8,128)(2,1)S(1)}, u32[]{:S(2)}, u32[]{:S(2)}) collective-permute-start(bf16[2,256,512]{2,1,0:T(8,128)(2,1)S(1)} %get-tuple-element.70.near1.refs_5_), channel_id=1, source_target_pairs={{0,130},{130,0},{2,128},{128,2},{1,131},{131,1},{3,129},{129,3},{4... | collective-permute-start | bytes 1572872 | tf_op jit(solution)/shard_map/ppermute | solution.py:306
  105.5 11.0 %collective-permute-done.26.refs_3_.refs_2_ = bf16[2,256,512]{2,1,0:T(8,128)(2,1)S(1)} collective-permute-done((bf16[2,256,512]{2,1,0:T(8,128)(2,1)S(1)}, bf16[2,256,512]{2,1,0:T(8,128)(2,1)S(1)}, u32[]{:S(2)}, u32[]{:S(2)}) %collective-permute-start.26) | collective-permute-done | bytes 524320 | tf_op jit(solution)/shard_map/ppermute | solution.py:28
  116.9 2.6 %collective-permute-start.33 = (bf16[448,1536]{1,0:T(8,128)(2,1)}, bf16[448,1536]{1,0:T(8,128)(2,1)}, u32[]{:S(2)}, u32[]{:S(2)}) collective-permute-start(bf16[448,1536]{1,0:T(8,128)(2,1)} %copy-done.3), channel_id=1, source_target_pairs={{0,128},{128,0},{1,129},{129,1},{2,130},{130,2},{3,131},{131,3},{4... | collective-permute-start | bytes 4128776 | tf_op jit(solution)/shard_map/ppermute | solution.py:28
  120.6 2.9 %collective-permute-done.23.refs_2_ = bf16[256,1536]{1,0:T(8,128)(2,1)S(1)} collective-permute-done((bf16[256,1536]{1,0:T(8,128)(2,1)}, bf16[256,1536]{1,0:T(8,128)(2,1)S(1)}, u32[]{:S(2)}, u32[]{:S(2)}) %collective-permute-start.23) | collective-permute-done | bytes 786464 | tf_op jit(solution)/shard_map/ppermute | solution.py:24
  123.6 0.9 slice.6
  124.4 1.2 collective-permute-start.24
  126.4 0.9 collective-permute-start.25
  127.2 7.5 %shard_map.108 = (bf16[1536,512]{1,0:T(8,128)(2,1)}, bf16[1536,512]{1,0:T(8,128)(2,1)}) custom-call(s32[4]{0:T(128)S(1)} %pad_add_fusion.place, bf16[256,1536]{1,0:T(8,128)(2,1)} %bitcast.27, bf16[256,1536]{1,0:T(8,128)(2,1)} %copy-done.9, bf16[256,1536]{1,0:T(8,128)(2,1)} %collective-permute-done.20.refs_2_, ...), custom_call_target="tpu_custom_call" | custom-call | tf_op jit(solution)/shard_map/pallas_call | solution.py:212
  134.7 7.8 %shard_map.109 = (bf16[1536,512]{1,0:T(8,128)(2,1)}, bf16[1536,512]{1,0:T(8,128)(2,1)}) custom-call(s32[4]{0:T(128)S(1)} %pad_add_fusion.place, bf16[256,1536]{1,0:T(8,128)(2,1)} %collective-permute-done.13.refs_0_, bf16[256,1536]{1,0:T(8,128)(2,1)} %copy-done.7, bf16[256,1536]{1,0:T(8,128)(2,1)} %copy-done.8, ...), custom_call_target="tpu_custom_call" | custom-call | tf_op jit(solution)/shard_map/pallas_call | solution.py:212
  142.5 5.6 %shard_map.110 = (bf16[1536,512]{1,0:T(8,128)(2,1)}, bf16[1536,512]{1,0:T(8,128)(2,1)}) custom-call(s32[4]{0:T(128)S(1)} %pad_add_fusion.place, bf16[128,1536]{1,0:T(8,128)(2,1)S(1)} %collective-permute-done.24.refs_0_, bf16[128,1536]{1,0:T(8,128)(2,1)} %collective-permute-done.25.refs_1_, bf16[2,256,512]{2,1,0:T(8,128)(2,1)S(1)} %collective-permute-done.26.refs_3_.refs_2_, ...), custom_call_target="tpu_custom_call" | custom-call | tf_op jit(solution)/shard_map/pallas_call | solution.py:212
  148.1 1.1 dynamic-slice_bitcast_fusion
  149.3 3.8 %collective-permute-start.31 = (bf16[32,1536]{1,0:T(8,128)(2,1)S(1)}, bf16[32,1536]{1,0:T(8,128)(2,1)S(1)}, u32[]{:S(2)}, u32[]{:S(2)}) collective-permute-start(bf16[32,1536]{1,0:T(8,128)(2,1)S(1)} %get-tuple-element.92), channel_id=1, source_target_pairs={{8,0},{12,4},{0,8},{4,12},{9,1},{13,5},{1,9},{5,13},{10,2},{14,6},... | collective-permute-start | bytes 294920 | tf_op jit(solution)/shard_map/ppermute | solution.py:24
  153.1 2.6 %collective-permute-done.30 = bf16[32,1536]{1,0:T(8,128)(2,1)S(1)} collective-permute-done((bf16[32,1536]{1,0:T(8,128)(2,1)S(1)}, bf16[32,1536]{1,0:T(8,128)(2,1)S(1)}, u32[]{:S(2)}, u32[]{:S(2)}) %collective-permute-start.30) | collective-permute-done | bytes 98336 | tf_op jit(solution)/shard_map/ppermute | solution.py:24
  155.7 1.1 collective-permute-done.31
  156.7 0.9 collective-permute-done.32
  158.4 3.6 %shard_map.111 = bf16[512,1536]{1,0:T(8,128)(2,1)} custom-call(bf16[64,1536]{1,0:T(8,128)(2,1)} %get-tuple-element.72.first, bf16[64,1536]{1,0:T(8,128)(2,1)S(1)} %copy-done.6, bf16[448,1536]{1,0:T(8,128)(2,1)S(1)} %copy-done.4, bf16[448,1536]{1,0:T(8,128)(2,1)} %collective-permute-done.33.rest_far), custom_call_target="tpu_custom_call" | custom-call | tf_op jit(solution)/shard_map/pallas_call | solution.py:231
  (68 shorter events, 12.3 us)
Async XLA Ops:
  7.2 61.9 %all-gather.2.cloned.1.call-start = ((), (), s32[]{:S(2)}) async-start(), calls=%async_computation.1 | async-start | bytes 3538944 | tf_op jit(solution)/shard_map/all_gather | solution.py:277
  7.2 10.6 %collective-permute-start = (bf16[32,1536]{1,0:T(8,128)(2,1)}, bf16[32,1536]{1,0:T(8,128)(2,1)S(1)}, u32[]{:S(2)}, u32[]{:S(2)}) collective-permute-start(bf16[32,1536]{1,0:T(8,128)(2,1)} %refs_0_.1), channel_id=1, source_target_pairs={{4,0},{8,4},{12,8},{0,12},{5,1},{9,5},{13,9},{1,13},{6,2},{10,6},{... | collective-permute-start | bytes 294920 | tf_op jit(solution)/shard_map/ppermute | solution.py:24
  10.3 7.5 %collective-permute-start.1 = (bf16[32,1536]{1,0:T(8,128)(2,1)}, bf16[32,1536]{1,0:T(8,128)(2,1)S(1)}, u32[]{:S(2)}, u32[]{:S(2)}) collective-permute-start(bf16[32,1536]{1,0:T(8,128)(2,1)} %refs_0_.1), channel_id=1, source_target_pairs={{8,0},{12,4},{0,8},{4,12},{9,1},{13,5},{1,9},{5,13},{10,2},{14,6},... | collective-permute-start | bytes 294920 | tf_op jit(solution)/shard_map/ppermute | solution.py:24
  10.9 7.4 %collective-permute-start.2 = (bf16[32,1536]{1,0:T(8,128)(2,1)}, bf16[32,1536]{1,0:T(8,128)(2,1)S(1)}, u32[]{:S(2)}, u32[]{:S(2)}) collective-permute-start(bf16[32,1536]{1,0:T(8,128)(2,1)} %refs_0_.1), channel_id=1, source_target_pairs={{12,0},{0,4},{4,8},{8,12},{13,1},{1,5},{5,9},{9,13},{14,2},{2,6},{... | collective-permute-start | bytes 294920 | tf_op jit(solution)/shard_map/ppermute | solution.py:24
  11.9 8.4 %collective-permute-start.3 = (bf16[32,1536]{1,0:T(8,128)(2,1)}, bf16[32,1536]{1,0:T(8,128)(2,1)S(1)}, u32[]{:S(2)}, u32[]{:S(2)}) collective-permute-start(bf16[32,1536]{1,0:T(8,128)(2,1)} %refs_0_.2), channel_id=1, source_target_pairs={{16,0},{32,16},{48,32},{64,48},{80,64},{96,80},{112,96},{0,112},{1... | collective-permute-start | bytes 294920 | tf_op jit(solution)/shard_map/ppermute | solution.py:24
  17.8 6.0 %collective-permute-start.4 = (bf16[32,1536]{1,0:T(8,128)(2,1)}, bf16[32,1536]{1,0:T(8,128)(2,1)S(1)}, u32[]{:S(2)}, u32[]{:S(2)}) collective-permute-start(bf16[32,1536]{1,0:T(8,128)(2,1)} %refs_0_.2), channel_id=1, source_target_pairs={{112,0},{0,16},{16,32},{32,48},{48,64},{64,80},{80,96},{96,112},{1... | collective-permute-start | bytes 294920 | tf_op jit(solution)/shard_map/ppermute | solution.py:24
  25.5 26.5 %copy-start.10 = (bf16[256,512]{1,0:T(8,128)(2,1)S(1)}, bf16[256,512]{1,0:T(8,128)(2,1)}, u32[]{:S(2)}) copy-start(bf16[256,512]{1,0:T(8,128)(2,1)} %param.9) | copy-start | bytes 786436
  25.5 122.6 %reduce-scatter.2.cloned.1.call-start = ((), (), s32[]{:S(2)}) async-start(), calls=%async_computation.2 | async-start | bytes 3538944 | tf_op jit(solution)/shard_map/reduce_scatter | solution.py:304
  25.6 16.4 %collective-permute-start.6 = (bf16[256,512]{1,0:T(8,128)(2,1)}, bf16[256,512]{1,0:T(8,128)(2,1)S(1)}, u32[]{:S(2)}, u32[]{:S(2)}) collective-permute-start(bf16[256,512]{1,0:T(8,128)(2,1)} %param.10), channel_id=1, source_target_pairs={{0,2},{2,0},{1,3},{3,1},{4,6},{6,4},{5,7},{7,5},{8,10},{10,8},{9,1... | collective-permute-start | bytes 786440 | tf_op jit(solution)/shard_map/ppermute | solution.py:28
  27.8 5.6 %collective-permute-start.8 = (bf16[32,1536]{1,0:T(8,128)(2,1)S(1)}, bf16[32,1536]{1,0:T(8,128)(2,1)S(1)}, u32[]{:S(2)}, u32[]{:S(2)}) collective-permute-start(bf16[32,1536]{1,0:T(8,128)(2,1)S(1)} %collective-permute-done.3.refs_1_), channel_id=1, source_target_pairs={{16,0},{32,16},{48,32},{64,48},{80,64},{96,80},{112,96},{0,112},{1... | collective-permute-start | bytes 294920 | tf_op jit(solution)/shard_map/ppermute | solution.py:24
  28.2 7.2 %collective-permute-start.11 = (bf16[32,1536]{1,0:T(8,128)(2,1)S(1)}, bf16[32,1536]{1,0:T(8,128)(2,1)S(1)}, u32[]{:S(2)}, u32[]{:S(2)}) collective-permute-start(bf16[32,1536]{1,0:T(8,128)(2,1)S(1)} %collective-permute-done.4.refs_7_), channel_id=1, source_target_pairs={{112,0},{0,16},{16,32},{32,48},{48,64},{64,80},{80,96},{96,112},{1... | collective-permute-start | bytes 294920 | tf_op jit(solution)/shard_map/ppermute | solution.py:24
  33.4 7.7 %collective-permute-start.9 = (bf16[32,1536]{1,0:T(8,128)(2,1)S(1)}, bf16[32,1536]{1,0:T(8,128)(2,1)S(1)}, u32[]{:S(2)}, u32[]{:S(2)}) collective-permute-start(bf16[32,1536]{1,0:T(8,128)(2,1)S(1)} %collective-permute-done.8.refs_2_), channel_id=1, source_target_pairs={{16,0},{32,16},{48,32},{64,48},{80,64},{96,80},{112,96},{0,112},{1... | collective-permute-start | bytes 294920 | tf_op jit(solution)/shard_map/ppermute | solution.py:24
  34.0 17.9 %collective-permute-start.5 = (bf16[256,512]{1,0:T(8,128)(2,1)}, bf16[256,512]{1,0:T(8,128)(2,1)S(1)}, u32[]{:S(2)}, u32[]{:S(2)}) collective-permute-start(bf16[256,512]{1,0:T(8,128)(2,1)} %param.9), channel_id=1, source_target_pairs={{0,2},{2,0},{1,3},{3,1},{4,6},{6,4},{5,7},{7,5},{8,10},{10,8},{9,1... | collective-permute-start | bytes 786440 | tf_op jit(solution)/shard_map/ppermute | solution.py:28
  35.4 7.9 %collective-permute-start.12 = (bf16[32,1536]{1,0:T(8,128)(2,1)S(1)}, bf16[32,1536]{1,0:T(8,128)(2,1)S(1)}, u32[]{:S(2)}, u32[]{:S(2)}) collective-permute-start(bf16[32,1536]{1,0:T(8,128)(2,1)S(1)} %collective-permute-done.11.refs_6_), channel_id=1, source_target_pairs={{112,0},{0,16},{16,32},{32,48},{48,64},{64,80},{80,96},{96,112},{1... | collective-permute-start | bytes 294920 | tf_op jit(solution)/shard_map/ppermute | solution.py:24
  41.1 6.7 %collective-permute-start.10 = (bf16[32,1536]{1,0:T(8,128)(2,1)S(1)}, bf16[32,1536]{1,0:T(8,128)(2,1)S(1)}, u32[]{:S(2)}, u32[]{:S(2)}) collective-permute-start(bf16[32,1536]{1,0:T(8,128)(2,1)S(1)} %collective-permute-done.9.refs_3_), channel_id=1, source_target_pairs={{16,0},{32,16},{48,32},{64,48},{80,64},{96,80},{112,96},{0,112},{1... | collective-permute-start | bytes 294920 | tf_op jit(solution)/shard_map/ppermute | solution.py:24
  48.7 29.3 %copy-start = (bf16[8,32,1536]{2,1,0:T(8,128)(2,1)}, bf16[8,32,1536]{2,1,0:T(8,128)(2,1)S(1)}, u32[]{:S(2)}) copy-start(bf16[8,32,1536]{2,1,0:T(8,128)(2,1)S(1)} %shard_map.103) | copy-start | bytes 2359300
  48.7 13.6 %collective-permute-start.13 = (bf16[256,1536]{1,0:T(8,128)(2,1)S(1)}, bf16[256,1536]{1,0:T(8,128)(2,1)}, u32[]{:S(2)}, u32[]{:S(2)}) collective-permute-start(bf16[256,1536]{1,0:T(8,128)(2,1)S(1)} %bitcast.23), channel_id=1, source_target_pairs={{0,128},{128,0},{1,129},{129,1},{2,130},{130,2},{3,131},{131,3},{4... | collective-permute-start | bytes 2359304 | tf_op jit(solution)/shard_map/ppermute | solution.py:28
  49.8 13.8 %collective-permute-start.14 = (bf16[256,1536]{1,0:T(8,128)(2,1)S(1)}, bf16[256,1536]{1,0:T(8,128)(2,1)S(1)}, u32[]{:S(2)}, u32[]{:S(2)}) collective-permute-start(bf16[256,1536]{1,0:T(8,128)(2,1)S(1)} %bitcast.24), channel_id=1, source_target_pairs={{4,0},{8,4},{12,8},{0,12},{5,1},{9,5},{13,9},{1,13},{6,2},{10,6},{... | collective-permute-start | bytes 2359304 | tf_op jit(solution)/shard_map/ppermute | solution.py:24
  52.0 13.3 %collective-permute-start.15 = (bf16[256,1536]{1,0:T(8,128)(2,1)S(1)}, bf16[256,1536]{1,0:T(8,128)(2,1)}, u32[]{:S(2)}, u32[]{:S(2)}) collective-permute-start(bf16[256,1536]{1,0:T(8,128)(2,1)S(1)} %bitcast.25), channel_id=1, source_target_pairs={{12,0},{0,4},{4,8},{8,12},{13,1},{1,5},{5,9},{9,13},{14,2},{2,6},{... | collective-permute-start | bytes 2359304 | tf_op jit(solution)/shard_map/ppermute | solution.py:24
  52.4 2.2 %collective-permute-start.7 = (bf16[2,256,512]{2,1,0:T(8,128)(2,1)S(1)}, bf16[2,256,512]{2,1,0:T(8,128)(2,1)S(1)}, u32[]{:S(2)}, u32[]{:S(2)}) collective-permute-start(bf16[2,256,512]{2,1,0:T(8,128)(2,1)S(1)} %fusion.4.hidden), channel_id=1, source_target_pairs={{0,1},{1,0},{2,3},{3,2},{4,5},{5,4},{6,7},{7,6},{8,9},{9,8},{10,11... | collective-permute-start | bytes 1572872 | tf_op jit(solution)/shard_map/ppermute | solution.py:28
  63.7 0.9 copy-start.9
  73.6 2.0 %collective-permute-start.16 = (bf16[2,256,512]{2,1,0:T(8,128)(2,1)S(1)}, bf16[2,256,512]{2,1,0:T(8,128)(2,1)S(1)}, u32[]{:S(2)}, u32[]{:S(2)}) collective-permute-start(bf16[2,256,512]{2,1,0:T(8,128)(2,1)S(1)} %get-tuple-element.60), channel_id=1, source_target_pairs={{0,1},{1,0},{2,3},{3,2},{4,5},{5,4},{6,7},{7,6},{8,9},{9,8},{10,11... | collective-permute-start | bytes 1572872 | tf_op jit(solution)/shard_map/ppermute | solution.py:28
  75.8 15.6 %collective-permute-start.17 = (bf16[2,256,512]{2,1,0:T(8,128)(2,1)S(1)}, bf16[2,256,512]{2,1,0:T(8,128)(2,1)S(1)}, u32[]{:S(2)}, u32[]{:S(2)}) collective-permute-start(bf16[2,256,512]{2,1,0:T(8,128)(2,1)S(1)} %get-tuple-element.100), channel_id=1, source_target_pairs={{0,2},{2,0},{1,3},{3,1},{4,6},{6,4},{5,7},{7,5},{8,10},{10,8},{9,1... | collective-permute-start | bytes 1572872 | tf_op jit(solution)/shard_map/ppermute | solution.py:28
  78.0 22.2 %collective-permute-start.20 = (bf16[256,1536]{1,0:T(8,128)(2,1)S(1)}, bf16[256,1536]{1,0:T(8,128)(2,1)}, u32[]{:S(2)}, u32[]{:S(2)}) collective-permute-start(bf16[256,1536]{1,0:T(8,128)(2,1)S(1)} %bitcast.26), channel_id=1, source_target_pairs={{8,0},{12,4},{0,8},{4,12},{9,1},{13,5},{1,9},{5,13},{10,2},{14,6},... | collective-permute-start | bytes 2359304 | tf_op jit(solution)/shard_map/ppermute | solution.py:24
  80.0 14.7 %copy-start.2 = (bf16[1536,512]{1,0:T(8,128)(2,1)S(1)}, bf16[1536,512]{1,0:T(8,128)(2,1)}, u32[]{:S(2)}) copy-start(bf16[1536,512]{1,0:T(8,128)(2,1)} %w_up.1) | copy-start | bytes 4718596
  84.6 1.1 copy-start.3
  85.8 8.9 %copy-start.1 = (bf16[1536,512]{1,0:T(8,128)(2,1)S(1)}, bf16[1536,512]{1,0:T(8,128)(2,1)}, u32[]{:S(2)}) copy-start(bf16[1536,512]{1,0:T(8,128)(2,1)} %w_gate.1) | copy-start | bytes 4718596
  92.0 2.0 %collective-permute-start.18 = (bf16[2,256,512]{2,1,0:T(8,128)(2,1)S(1)}, bf16[2,256,512]{2,1,0:T(8,128)(2,1)S(1)}, u32[]{:S(2)}, u32[]{:S(2)}) collective-permute-start(bf16[2,256,512]{2,1,0:T(8,128)(2,1)S(1)} %get-tuple-element.69.near0.refs_4_), channel_id=1, source_target_pairs={{0,1},{1,0},{2,3},{3,2},{4,5},{5,4},{6,7},{7,6},{8,9},{9,8},{10,11... | collective-permute-start | bytes 1572872 | tf_op jit(solution)/shard_map/ppermute | solution.py:28
  92.1 2.6 %collective-permute-start.19 = (bf16[2,256,512]{2,1,0:T(8,128)(2,1)S(1)}, bf16[2,256,512]{2,1,0:T(8,128)(2,1)S(1)}, u32[]{:S(2)}, u32[]{:S(2)}) collective-permute-start(bf16[2,256,512]{2,1,0:T(8,128)(2,1)S(1)} %get-tuple-element.70.near1.refs_5_), channel_id=1, source_target_pairs={{0,1},{1,0},{2,3},{3,2},{4,5},{5,4},{6,7},{7,6},{8,9},{9,8},{10,11... | collective-permute-start | bytes 1572872 | tf_op jit(solution)/shard_map/ppermute | solution.py:28
  92.6 7.6 %collective-permute-start.21 = (bf16[64,1536]{1,0:T(8,128)(2,1)}, bf16[64,1536]{1,0:T(8,128)(2,1)S(1)}, u32[]{:S(2)}, u32[]{:S(2)}) collective-permute-start(bf16[64,1536]{1,0:T(8,128)(2,1)} %get-tuple-element.72.first), channel_id=1, source_target_pairs={{0,128},{128,0},{1,129},{129,1},{2,130},{130,2},{3,131},{131,3},{4... | collective-permute-start | bytes 589832 | tf_op jit(solution)/shard_map/ppermute | solution.py:28
  100.2 0.7 copy-start.5
  100.8 19.8 %collective-permute-start.22 = (bf16[256,1536]{1,0:T(8,128)(2,1)}, bf16[256,1536]{1,0:T(8,128)(2,1)S(1)}, u32[]{:S(2)}, u32[]{:S(2)}) collective-permute-start(bf16[256,1536]{1,0:T(8,128)(2,1)} %collective-permute-done.13.refs_0_), channel_id=1, source_target_pairs={{4,0},{8,4},{12,8},{0,12},{5,1},{9,5},{13,9},{1,13},{6,2},{10,6},{... | collective-permute-start | bytes 2359304 | tf_op jit(solution)/shard_map/ppermute | solution.py:24
  102.9 20.7 %collective-permute-start.23 = (bf16[256,1536]{1,0:T(8,128)(2,1)}, bf16[256,1536]{1,0:T(8,128)(2,1)S(1)}, u32[]{:S(2)}, u32[]{:S(2)}) collective-permute-start(bf16[256,1536]{1,0:T(8,128)(2,1)} %collective-permute-done.13.refs_0_), channel_id=1, source_target_pairs={{12,0},{0,4},{4,8},{8,12},{13,1},{1,5},{5,9},{9,13},{14,2},{2,6},{... | collective-permute-start | bytes 2359304 | tf_op jit(solution)/shard_map/ppermute | solution.py:24
  102.9 13.7 %collective-permute-start.26 = (bf16[2,256,512]{2,1,0:T(8,128)(2,1)S(1)}, bf16[2,256,512]{2,1,0:T(8,128)(2,1)S(1)}, u32[]{:S(2)}, u32[]{:S(2)}) collective-permute-start(bf16[2,256,512]{2,1,0:T(8,128)(2,1)S(1)} %get-tuple-element.69.near0.refs_4_), channel_id=1, source_target_pairs={{0,128},{128,0},{1,129},{129,1},{2,130},{130,2},{3,131},{131,3},{4... | collective-permute-start | bytes 1572872 | tf_op jit(solution)/shard_map/ppermute | solution.py:28
  103.5 13.4 %collective-permute-start.27 = (bf16[2,256,512]{2,1,0:T(8,128)(2,1)S(1)}, bf16[2,256,512]{2,1,0:T(8,128)(2,1)S(1)}, u32[]{:S(2)}, u32[]{:S(2)}) collective-permute-start(bf16[2,256,512]{2,1,0:T(8,128)(2,1)S(1)} %get-tuple-element.70.near1.refs_5_), channel_id=1, source_target_pairs={{0,130},{130,0},{2,128},{128,2},{1,131},{131,1},{3,129},{129,3},{4... | collective-permute-start | bytes 1572872 | tf_op jit(solution)/shard_map/ppermute | solution.py:306
  116.9 41.5 %collective-permute-start.33 = (bf16[448,1536]{1,0:T(8,128)(2,1)}, bf16[448,1536]{1,0:T(8,128)(2,1)}, u32[]{:S(2)}, u32[]{:S(2)}) collective-permute-start(bf16[448,1536]{1,0:T(8,128)(2,1)} %copy-done.3), channel_id=1, source_target_pairs={{0,128},{128,0},{1,129},{129,1},{2,130},{130,2},{3,131},{131,3},{4... | collective-permute-start | bytes 4128776 | tf_op jit(solution)/shard_map/ppermute | solution.py:28
  119.5 15.2 %collective-permute-start.28 = (bf16[2,256,512]{2,1,0:T(8,128)(2,1)S(1)}, bf16[2,256,512]{2,1,0:T(8,128)(2,1)}, u32[]{:S(2)}, u32[]{:S(2)}) collective-permute-start(bf16[2,256,512]{2,1,0:T(8,128)(2,1)S(1)} %collective-permute-done.26.refs_3_.refs_2_), channel_id=1, source_target_pairs={{0,1},{1,0},{2,3},{3,2},{4,5},{5,4},{6,7},{7,6},{8,9},{9,8},{10,11... | collective-permute-start | bytes 1572872 | tf_op jit(solution)/shard_map/ppermute | solution.py:28
  119.5 15.2 %collective-permute-start.29 = (bf16[2,256,512]{2,1,0:T(8,128)(2,1)S(1)}, bf16[2,256,512]{2,1,0:T(8,128)(2,1)}, u32[]{:S(2)}, u32[]{:S(2)}) collective-permute-start(bf16[2,256,512]{2,1,0:T(8,128)(2,1)S(1)} %collective-permute-done.27.refs_4_.refs_3_), channel_id=1, source_target_pairs={{0,1},{1,0},{2,3},{3,2},{4,5},{5,4},{6,7},{7,6},{8,9},{9,8},{10,11... | collective-permute-start | bytes 1572872 | tf_op jit(solution)/shard_map/ppermute | solution.py:28
  120.6 2.9 %copy-start.7 = (bf16[256,1536]{1,0:T(8,128)(2,1)}, bf16[256,1536]{1,0:T(8,128)(2,1)S(1)}, u32[]{:S(2)}) copy-start(bf16[256,1536]{1,0:T(8,128)(2,1)S(1)} %collective-permute-done.22.refs_1_) | copy-start | bytes 2359300
  123.6 2.0 %copy-start.8 = (bf16[256,1536]{1,0:T(8,128)(2,1)}, bf16[256,1536]{1,0:T(8,128)(2,1)S(1)}, u32[]{:S(2)}) copy-start(bf16[256,1536]{1,0:T(8,128)(2,1)S(1)} %collective-permute-done.23.refs_2_) | copy-start | bytes 2359300
  124.4 18.0 %collective-permute-start.24 = (bf16[128,1536]{1,0:T(8,128)(2,1)}, bf16[128,1536]{1,0:T(8,128)(2,1)S(1)}, u32[]{:S(2)}, u32[]{:S(2)}) collective-permute-start(bf16[128,1536]{1,0:T(8,128)(2,1)} %slice.6), channel_id=1, source_target_pairs={{4,0},{8,4},{12,8},{0,12},{5,1},{9,5},{13,9},{1,13},{6,2},{10,6},{... | collective-permute-start | bytes 1179656 | tf_op jit(solution)/shard_map/ppermute | solution.py:24
  126.4 16.1 %collective-permute-start.25 = (bf16[128,1536]{1,0:T(8,128)(2,1)}, bf16[128,1536]{1,0:T(8,128)(2,1)}, u32[]{:S(2)}, u32[]{:S(2)}) collective-permute-start(bf16[128,1536]{1,0:T(8,128)(2,1)} %slice.7), channel_id=1, source_target_pairs={{12,0},{0,4},{4,8},{8,12},{13,1},{1,5},{5,9},{9,13},{14,2},{2,6},{... | collective-permute-start | bytes 1179656 | tf_op jit(solution)/shard_map/ppermute | solution.py:24
  142.5 15.9 %copy-start.4 = (bf16[448,1536]{1,0:T(8,128)(2,1)S(1)}, bf16[448,1536]{1,0:T(8,128)(2,1)}, u32[]{:S(2)}) copy-start(bf16[448,1536]{1,0:T(8,128)(2,1)} %copy-done.3) | copy-start | bytes 4128772
  142.5 15.9 %copy-start.6 = (bf16[64,1536]{1,0:T(8,128)(2,1)S(1)}, bf16[64,1536]{1,0:T(8,128)(2,1)}, u32[]{:S(2)}) copy-start(bf16[64,1536]{1,0:T(8,128)(2,1)} %copy-done.5) | copy-start | bytes 589828
  149.2 6.5 %collective-permute-start.30 = (bf16[32,1536]{1,0:T(8,128)(2,1)S(1)}, bf16[32,1536]{1,0:T(8,128)(2,1)S(1)}, u32[]{:S(2)}, u32[]{:S(2)}) collective-permute-start(bf16[32,1536]{1,0:T(8,128)(2,1)S(1)} %get-tuple-element.91), channel_id=1, source_target_pairs={{12,0},{0,4},{4,8},{8,12},{13,1},{1,5},{5,9},{9,13},{14,2},{2,6},{... | collective-permute-start | bytes 294920 | tf_op jit(solution)/shard_map/ppermute | solution.py:24
  149.3 7.4 %collective-permute-start.31 = (bf16[32,1536]{1,0:T(8,128)(2,1)S(1)}, bf16[32,1536]{1,0:T(8,128)(2,1)S(1)}, u32[]{:S(2)}, u32[]{:S(2)}) collective-permute-start(bf16[32,1536]{1,0:T(8,128)(2,1)S(1)} %get-tuple-element.92), channel_id=1, source_target_pairs={{8,0},{12,4},{0,8},{4,12},{9,1},{13,5},{1,9},{5,13},{10,2},{14,6},... | collective-permute-start | bytes 294920 | tf_op jit(solution)/shard_map/ppermute | solution.py:24
  153.1 4.6 %collective-permute-start.32 = (bf16[32,1536]{1,0:T(8,128)(2,1)S(1)}, bf16[32,1536]{1,0:T(8,128)(2,1)S(1)}, u32[]{:S(2)}, u32[]{:S(2)}) collective-permute-start(bf16[32,1536]{1,0:T(8,128)(2,1)S(1)} %get-tuple-element.93), channel_id=1, source_target_pairs={{4,0},{8,4},{12,8},{0,12},{5,1},{9,5},{13,9},{1,13},{6,2},{10,6},{... | collective-permute-start | bytes 294920 | tf_op jit(solution)/shard_map/ppermute | solution.py:24
Sparse Core Ops, SparseCore 0:
  25.6 43.3 all-gather.1
  100.3 44.3 reduce-scatter.1

commit v12 on v11

--- a/solution.py
+++ b/solution.py
@@ -305,11 +305,11 @@
 
     far = [swap(near[0], "dp"), lax.ppermute(near[1], ("dp", "xh"), [(0, 3), (3, 0), (1, 2), (2, 1)])]
     partner1, partner3 = from_ahead(partner_z, "y", NY, 1), from_ahead(partner_z, "y", NY, 3)
-    far, down_rest = lax.optimization_barrier((far, down_rest))
+    own_gate, own_up = weight_grads(place, whole(0, 1, 2, 3), (own_z, own1, own2, own3), (*near, *other))
+    far, down_rest, own_gate, own_up = lax.optimization_barrier((far, down_rest, own_gate, own_up))
     rest_far = swap(down_rest, "dp")
-    own_z, partner1, partner3 = lax.optimization_barrier((own_z, partner1, partner3))
+    partner1, partner3 = lax.optimization_barrier((partner1, partner3))
     partner2 = opposite(partner1, partner3)
-    own_gate, own_up = weight_grads(place, whole(0, 1, 2, 3), (own_z, own1, own2, own3), (*near, *other))
     far_other = [swap(half, "core") for half in far]
 
     y = place[1]
@@ -322,7 +322,6 @@
     for k in range(1, NY):
         total = total + from_ahead(slabs[k], "y", NY, NY - k).astype(F32)
     grad_input = total.astype(BF16)
-    grad_input, rest_far = lax.optimization_barrier((grad_input, rest_far))
     return grad_input, grad_gate, grad_up, add(down_first, first_far, down_rest, rest_far)
 
 

time: 169 us -> 164 us (0.970)
  waiting for transfers between devices: 62.6 us -> 58.6 us
  local copies, waits for them, and re-layouts: 5.39 us -> 3.45 us
    ppermute x13, waiting for transfers between devices: 29.7 us -> 21.1 us  [swap(): return lax.ppermute(x, axis, [(0, 1), (1, 0)])]
    ppermute x20, waiting for transfers between devices: 28.8 us -> 31.2 us  [from_ahead(): return lax.ppermute(x, axis, [((d + k) % n, d) for d in range(n)])]
    reduce_scatter x1, waiting for transfers between devices: 0.01 us -> 1.97 us  [body(): lax.psum_scatter(partial_in, 'z', scatter_dimension=0, tiled=True)]
  transfers between devices with their start and end apart: 36 -> 36, of which waited for: 23 -> 24; matrix products, arithmetic and copies ran while one was open for 3% -> 2% of each run, Pallas kernels for 19% -> 22%
where the time goes in v12:
time: 164 us; the launch traced here: 163 us
  waiting for transfers between devices  58.6 us (36%)
  starting transfers between devices  42.4 us (26%)
  Pallas kernels  42.2 us (26%)
  between operations  14.2 us (9%)
  local copies, waits for them, and re-layouts  3.45 us (2%)
  other arithmetic  2.44 us (1%)
    ppermute x20, waiting for transfers between devices, from_ahead(): return lax.ppermute(x, axis, [((d + k) % n, d) for d in range(n)])  31.2 us
    ppermute x20, starting transfers between devices, from_ahead(): return lax.ppermute(x, axis, [((d + k) % n, d) for d in range(n)])  28.4 us
    ppermute x13, waiting for transfers between devices, swap(): return lax.ppermute(x, axis, [(0, 1), (1, 0)])  21.1 us
    pallas_call x3, Pallas kernels, weight_grads(): pl.pallas_call(functools.partial(weight_kernel, slots, bool(base)), grid=...  20 us
    ppermute x13, starting transfers between devices, swap(): return lax.ppermute(x, axis, [(0, 1), (1, 0)])  11.8 us
    pallas_call x1, Pallas kernels, input_grad(): pl.pallas_call(input_grad_kernel, grid=(3,), out_shape=jax.ShapeDtypeStru...  5.46 us
    pallas_call x1, Pallas kernels, down_grad(): pl.pallas_call(down_kernel, grid=(3,), out_shape=(jax.ShapeDtypeStruct((F...  5.13 us
    pallas_call x1, Pallas kernels, hidden_grad(): pl.pallas_call(hidden_grad_kernel, out_shape=(jax.ShapeDtypeStruct((2, 25...  4.58 us
  transfers between devices with their start and end apart: 36, of which 24 were waited for; matrix products, arithmetic and copies ran while one was open for 2% of the time, Pallas kernels for 22%

profile of v12, /device:TPU:2, one launch (start us, length us, event | category | flops | bytes accessed | tf_op | source)
XLA Modules:
  0.0 163.2 jit_solution(4288469423754183401)
XLA Ops:
  7.2 3.1 %collective-permute-start = (bf16[32,1536]{1,0:T(8,128)(2,1)}, bf16[32,1536]{1,0:T(8,128)(2,1)S(1)}, u32[]{:S(2)}, u32[]{:S(2)}) collective-permute-start(bf16[32,1536]{1,0:T(8,128)(2,1)} %refs_0_.1), channel_id=1, source_target_pairs={{4,0},{8,4},{12,8},{0,12},{5,1},{9,5},{13,9},{1,13},{6,2},{10,6},{... | collective-permute-start | bytes 294920 | tf_op jit(solution)/shard_map/ppermute | solution.py:24
  10.9 1.0 collective-permute-start.2
  11.9 5.9 %collective-permute-start.3 = (bf16[32,1536]{1,0:T(8,128)(2,1)}, bf16[32,1536]{1,0:T(8,128)(2,1)S(1)}, u32[]{:S(2)}, u32[]{:S(2)}) collective-permute-start(bf16[32,1536]{1,0:T(8,128)(2,1)} %refs_0_.2), channel_id=1, source_target_pairs={{16,0},{32,16},{48,32},{64,48},{80,64},{96,80},{112,96},{0,112},{1... | collective-permute-start | bytes 294920 | tf_op jit(solution)/shard_map/ppermute | solution.py:24
  18.4 1.9 %collective-permute-done.3.refs_1_ = bf16[32,1536]{1,0:T(8,128)(2,1)S(1)} collective-permute-done((bf16[32,1536]{1,0:T(8,128)(2,1)}, bf16[32,1536]{1,0:T(8,128)(2,1)S(1)}, u32[]{:S(2)}, u32[]{:S(2)}) %collective-permute-start.3) | collective-permute-done | bytes 98336 | tf_op jit(solution)/shard_map/ppermute | solution.py:24
  20.3 3.5 %collective-permute-done.4.refs_7_ = bf16[32,1536]{1,0:T(8,128)(2,1)S(1)} collective-permute-done((bf16[32,1536]{1,0:T(8,128)(2,1)}, bf16[32,1536]{1,0:T(8,128)(2,1)S(1)}, u32[]{:S(2)}, u32[]{:S(2)}) %collective-permute-start.4) | collective-permute-done | bytes 98336 | tf_op jit(solution)/shard_map/ppermute | solution.py:24
  23.8 1.7 %shard_map.102 = bf16[4,32,1536]{2,1,0:T(8,128)(2,1)} custom-call(s32[4]{0:T(128)S(1)} %pad_add_fusion.place, bf16[32,1536]{1,0:T(8,128)(2,1)} %refs_0_.1, bf16[32,1536]{1,0:T(8,128)(2,1)S(1)} %collective-permute-done.refs_1_, bf16[32,1536]{1,0:T(8,128)(2,1)S(1)} %collective-permute-done.1.refs_2_, bf16[32,1536]{1,0:T(8,128)(2,1)S(1)} %collective-permute-done.2.refs_3_), custom_call_target="tpu_custom_call" | custom-call | tf_op jit(solution)/shard_map/pallas_call | solution.py:46
  25.6 2.2 %collective-permute-start.5 = (bf16[256,512]{1,0:T(8,128)(2,1)}, bf16[256,512]{1,0:T(8,128)(2,1)S(1)}, u32[]{:S(2)}, u32[]{:S(2)}) collective-permute-start(bf16[256,512]{1,0:T(8,128)(2,1)} %param.9), channel_id=1, source_target_pairs={{0,2},{2,0},{1,3},{3,1},{4,6},{6,4},{5,7},{7,5},{8,10},{10,8},{9,1... | collective-permute-start | bytes 786440 | tf_op jit(solution)/shard_map/ppermute | solution.py:28
  28.2 1.6 collective-permute-start.11
  29.8 3.6 %collective-permute-done.8.refs_2_ = bf16[32,1536]{1,0:T(8,128)(2,1)S(1)} collective-permute-done((bf16[32,1536]{1,0:T(8,128)(2,1)S(1)}, bf16[32,1536]{1,0:T(8,128)(2,1)S(1)}, u32[]{:S(2)}, u32[]{:S(2)}) %collective-permute-start.8) | collective-permute-done | bytes 98336 | tf_op jit(solution)/shard_map/ppermute | solution.py:24
  34.0 1.4 collective-permute-start.6
  35.4 1.4 collective-permute-start.12
  36.8 4.2 %collective-permute-done.9.refs_3_ = bf16[32,1536]{1,0:T(8,128)(2,1)S(1)} collective-permute-done((bf16[32,1536]{1,0:T(8,128)(2,1)S(1)}, bf16[32,1536]{1,0:T(8,128)(2,1)S(1)}, u32[]{:S(2)}, u32[]{:S(2)}) %collective-permute-start.9) | collective-permute-done | bytes 98336 | tf_op jit(solution)/shard_map/ppermute | solution.py:24
  41.1 0.9 collective-permute-start.10
  42.0 1.0 select_bitcast_fusion.3
  43.4 4.4 %collective-permute-done.10.refs_4_ = bf16[32,1536]{1,0:T(8,128)(2,1)S(1)} collective-permute-done((bf16[32,1536]{1,0:T(8,128)(2,1)S(1)}, bf16[32,1536]{1,0:T(8,128)(2,1)S(1)}, u32[]{:S(2)}, u32[]{:S(2)}) %collective-permute-start.10) | collective-permute-done | bytes 98336 | tf_op jit(solution)/shard_map/ppermute | solution.py:24
  47.7 1.0 shard_map.103
  48.7 1.1 collective-permute-start.13
  49.8 2.2 %collective-permute-start.14 = (bf16[256,1536]{1,0:T(8,128)(2,1)S(1)}, bf16[256,1536]{1,0:T(8,128)(2,1)S(1)}, u32[]{:S(2)}, u32[]{:S(2)}) collective-permute-start(bf16[256,1536]{1,0:T(8,128)(2,1)S(1)} %bitcast.24), channel_id=1, source_target_pairs={{4,0},{8,4},{12,8},{0,12},{5,1},{9,5},{13,9},{1,13},{6,2},{10,6},{... | collective-permute-start | bytes 2359304 | tf_op jit(solution)/shard_map/ppermute | solution.py:24
  52.8 1.8 %collective-permute-done.7.hidden_other = bf16[2,256,512]{2,1,0:T(8,128)(2,1)S(1)} collective-permute-done((bf16[2,256,512]{2,1,0:T(8,128)(2,1)S(1)}, bf16[2,256,512]{2,1,0:T(8,128)(2,1)S(1)}, u32[]{:S(2)}, u32[]{:S(2)}) %collective-permute-start.7) | collective-permute-done | bytes 524320 | tf_op jit(solution)/shard_map/ppermute | solution.py:28
  54.5 7.7 %collective-permute-done.13.refs_0_ = bf16[256,1536]{1,0:T(8,128)(2,1)S(1)} collective-permute-done((bf16[256,1536]{1,0:T(8,128)(2,1)S(1)}, bf16[256,1536]{1,0:T(8,128)(2,1)S(1)}, u32[]{:S(2)}, u32[]{:S(2)}) %collective-permute-start.13) | collective-permute-done | bytes 786464 | tf_op jit(solution)/shard_map/ppermute | solution.py:28
  62.2 1.5 collective-permute-done.14.refs_1_
  63.7 0.9 copy-done.10
  65.3 3.8 %all-gather.2.cloned.1.call-done.go = bf16[1024,1536]{1,0:T(8,128)(2,1)} async-done(((bf16[128,1536]{1,0:T(8,128)(2,1)}), bf16[1024,1536]{1,0:T(8,128)(2,1)}) %all-gather.2.cloned.1.call-update) | async-done | bytes 3145744 | tf_op jit(solution)/shard_map/all_gather | solution.py:277
  69.0 4.6 %shard_map.104 = (f32[2,256,512]{2,1,0:T(8,128)S(1)}, bf16[2,256,512]{2,1,0:T(8,128)(2,1)S(1)}) custom-call(s32[4]{0:T(128)S(1)} %pad_add_fusion.place, bf16[1024,1536]{1,0:T(8,128)(2,1)} %all-gather.2.cloned.1.call-done.go, bf16[512,1536]{1,0:T(8,128)(2,1)} %w_down.1), custom_call_target="tpu_custom_call" | custom-call | tf_op jit(solution)/shard_map/pallas_call | solution.py:79
  73.7 1.9 %collective-permute-done.16 = bf16[2,256,512]{2,1,0:T(8,128)(2,1)S(1)} collective-permute-done((bf16[2,256,512]{2,1,0:T(8,128)(2,1)S(1)}, bf16[2,256,512]{2,1,0:T(8,128)(2,1)S(1)}, u32[]{:S(2)}, u32[]{:S(2)}) %collective-permute-start.16) | collective-permute-done | bytes 524320 | tf_op jit(solution)/shard_map/ppermute | solution.py:28
  75.8 2.2 %collective-permute-start.17 = (bf16[2,256,512]{2,1,0:T(8,128)(2,1)S(1)}, bf16[2,256,512]{2,1,0:T(8,128)(2,1)S(1)}, u32[]{:S(2)}, u32[]{:S(2)}) collective-permute-start(bf16[2,256,512]{2,1,0:T(8,128)(2,1)S(1)} %get-tuple-element.98), channel_id=1, source_target_pairs={{0,2},{2,0},{1,3},{3,1},{4,6},{6,4},{5,7},{7,5},{8,10},{10,8},{9,1... | collective-permute-start | bytes 1572872 | tf_op jit(solution)/shard_map/ppermute | solution.py:28
  78.0 2.0 %collective-permute-start.20 = (bf16[256,1536]{1,0:T(8,128)(2,1)S(1)}, bf16[256,1536]{1,0:T(8,128)(2,1)}, u32[]{:S(2)}, u32[]{:S(2)}) collective-permute-start(bf16[256,1536]{1,0:T(8,128)(2,1)S(1)} %bitcast.26), channel_id=1, source_target_pairs={{8,0},{12,4},{0,8},{4,12},{9,1},{13,5},{1,9},{5,13},{10,2},{14,6},... | collective-permute-start | bytes 2359304 | tf_op jit(solution)/shard_map/ppermute | solution.py:24
  80.0 5.1 %shard_map.105 = (bf16[64,1536]{1,0:T(8,128)(2,1)S(1)}, bf16[448,1536]{1,0:T(8,128)(2,1)}) custom-call(s32[4]{0:T(128)S(1)} %pad_add_fusion.place, bf16[2,256,512]{2,1,0:T(8,128)(2,1)S(1)} %fusion.4.hidden, bf16[2,256,512]{2,1,0:T(8,128)(2,1)S(1)} %collective-permute-done.7.hidden_other, bf16[1024,1536]{1,0:T(8,128)(2,1)} %all-gather.2.cloned.1.call-done.go), custom_call_target="tpu_custom_call" | custom-call | tf_op jit(solution)/shard_map/pallas_call | solution.py:161
  85.1 6.3 %collective-permute-done.17.chip_far = bf16[2,256,512]{2,1,0:T(8,128)(2,1)S(1)} collective-permute-done((bf16[2,256,512]{2,1,0:T(8,128)(2,1)S(1)}, bf16[2,256,512]{2,1,0:T(8,128)(2,1)S(1)}, u32[]{:S(2)}, u32[]{:S(2)}) %collective-permute-start.17) | collective-permute-done | bytes 524320 | tf_op jit(solution)/shard_map/ppermute | solution.py:28
  93.1 0.8 collective-permute-done.18.other0.refs_6_
  94.7 5.5 %shard_map.107 = bf16[1024,1536]{1,0:T(8,128)(2,1)} custom-call(s32[4]{0:T(128)S(1)} %pad_add_fusion.place, bf16[2,256,512]{2,1,0:T(8,128)(2,1)S(1)} %get-tuple-element.68.near0.refs_4_, bf16[2,256,512]{2,1,0:T(8,128)(2,1)S(1)} %get-tuple-element.69.near1.refs_5_, bf16[2,256,512]{2,1,0:T(8,128)(2,1)S(1)} %collective-permute-done.18.other0.refs_6_, ...), custom_call_target="tpu_custom_call" | custom-call | tf_op jit(solution)/shard_map/pallas_call | solution.py:131
  101.4 2.1 %collective-permute-start.27 = (bf16[2,256,512]{2,1,0:T(8,128)(2,1)S(1)}, bf16[2,256,512]{2,1,0:T(8,128)(2,1)S(1)}, u32[]{:S(2)}, u32[]{:S(2)}) collective-permute-start(bf16[2,256,512]{2,1,0:T(8,128)(2,1)S(1)} %get-tuple-element.69.near1.refs_5_), channel_id=1, source_target_pairs={{0,130},{130,0},{2,128},{128,2},{1,131},{131,1},{3,129},{129,3},{4... | collective-permute-start | bytes 1572872 | tf_op jit(solution)/shard_map/ppermute | solution.py:306
  103.5 1.7 %collective-permute-start.22 = (bf16[256,1536]{1,0:T(8,128)(2,1)}, bf16[256,1536]{1,0:T(8,128)(2,1)S(1)}, u32[]{:S(2)}, u32[]{:S(2)}) collective-permute-start(bf16[256,1536]{1,0:T(8,128)(2,1)} %copy-done.9), channel_id=1, source_target_pairs={{4,0},{8,4},{12,8},{0,12},{5,1},{9,5},{13,9},{1,13},{6,2},{10,6},{... | collective-permute-start | bytes 2359304 | tf_op jit(solution)/shard_map/ppermute | solution.py:24
  105.5 7.5 %shard_map.108 = (bf16[1536,512]{1,0:T(8,128)(2,1)}, bf16[1536,512]{1,0:T(8,128)(2,1)}) custom-call(s32[4]{0:T(128)S(1)} %pad_add_fusion.place, bf16[256,1536]{1,0:T(8,128)(2,1)} %bitcast.27, bf16[256,1536]{1,0:T(8,128)(2,1)} %copy-done.10, bf16[256,1536]{1,0:T(8,128)(2,1)} %collective-permute-done.20.refs_2_, ...), custom_call_target="tpu_custom_call" | custom-call | tf_op jit(solution)/shard_map/pallas_call | solution.py:212
  113.0 1.8 %collective-permute-done.26.refs_3_.refs_2_ = bf16[2,256,512]{2,1,0:T(8,128)(2,1)S(1)} collective-permute-done((bf16[2,256,512]{2,1,0:T(8,128)(2,1)S(1)}, bf16[2,256,512]{2,1,0:T(8,128)(2,1)S(1)}, u32[]{:S(2)}, u32[]{:S(2)}) %collective-permute-start.26) | collective-permute-done | bytes 524320 | tf_op jit(solution)/shard_map/ppermute | solution.py:28
  115.4 2.3 %collective-permute-start.33 = (bf16[448,1536]{1,0:T(8,128)(2,1)}, bf16[448,1536]{1,0:T(8,128)(2,1)}, u32[]{:S(2)}, u32[]{:S(2)}) collective-permute-start(bf16[448,1536]{1,0:T(8,128)(2,1)} %get-tuple-element.97.rest), channel_id=1, source_target_pairs={{0,128},{128,0},{1,129},{129,1},{2,130},{130,2},{3,131},{131,3},{4... | collective-permute-start | bytes 4128776 | tf_op jit(solution)/shard_map/ppermute | solution.py:28
  118.3 4.4 %collective-permute-done.22.refs_1_ = bf16[256,1536]{1,0:T(8,128)(2,1)S(1)} collective-permute-done((bf16[256,1536]{1,0:T(8,128)(2,1)}, bf16[256,1536]{1,0:T(8,128)(2,1)S(1)}, u32[]{:S(2)}, u32[]{:S(2)}) %collective-permute-start.22) | collective-permute-done | bytes 786464 | tf_op jit(solution)/shard_map/ppermute | solution.py:24
  122.7 2.6 %collective-permute-done.23.refs_2_ = bf16[256,1536]{1,0:T(8,128)(2,1)S(1)} collective-permute-done((bf16[256,1536]{1,0:T(8,128)(2,1)}, bf16[256,1536]{1,0:T(8,128)(2,1)S(1)}, u32[]{:S(2)}, u32[]{:S(2)}) %collective-permute-start.23) | collective-permute-done | bytes 786464 | tf_op jit(solution)/shard_map/ppermute | solution.py:24
  126.7 1.7 %collective-permute-start.25 = (bf16[128,1536]{1,0:T(8,128)(2,1)}, bf16[128,1536]{1,0:T(8,128)(2,1)S(1)}, u32[]{:S(2)}, u32[]{:S(2)}) collective-permute-start(bf16[128,1536]{1,0:T(8,128)(2,1)} %slice.7), channel_id=1, source_target_pairs={{12,0},{0,4},{4,8},{8,12},{13,1},{1,5},{5,9},{9,13},{14,2},{2,6},{... | collective-permute-start | bytes 1179656 | tf_op jit(solution)/shard_map/ppermute | solution.py:24
  128.5 7.3 %shard_map.109 = (bf16[1536,512]{1,0:T(8,128)(2,1)}, bf16[1536,512]{1,0:T(8,128)(2,1)}) custom-call(s32[4]{0:T(128)S(1)} %pad_add_fusion.place, bf16[256,1536]{1,0:T(8,128)(2,1)} %copy-done.9, bf16[256,1536]{1,0:T(8,128)(2,1)} %copy-done.7, bf16[256,1536]{1,0:T(8,128)(2,1)} %copy-done.8, bf16[2,256,512]{2,1,0:T(8,128)(2,1)S(1)} %collective-permute-done.26.refs_3_.refs_2_, ...), custom_call_target="tpu_custom_call" | custom-call | tf_op jit(solution)/shard_map/pallas_call | solution.py:212
  135.8 1.9 %collective-permute-done.25.refs_1_ = bf16[128,1536]{1,0:T(8,128)(2,1)S(1)} collective-permute-done((bf16[128,1536]{1,0:T(8,128)(2,1)}, bf16[128,1536]{1,0:T(8,128)(2,1)S(1)}, u32[]{:S(2)}, u32[]{:S(2)}) %collective-permute-start.25) | collective-permute-done | bytes 393248 | tf_op jit(solution)/shard_map/ppermute | solution.py:24
  137.7 5.2 %shard_map.110 = (bf16[1536,512]{1,0:T(8,128)(2,1)}, bf16[1536,512]{1,0:T(8,128)(2,1)}) custom-call(s32[4]{0:T(128)S(1)} %pad_add_fusion.place, bf16[128,1536]{1,0:T(8,128)(2,1)S(1)} %collective-permute-done.24.refs_0_, bf16[128,1536]{1,0:T(8,128)(2,1)S(1)} %collective-permute-done.25.refs_1_, ...), custom_call_target="tpu_custom_call" | custom-call | tf_op jit(solution)/shard_map/pallas_call | solution.py:212
  142.9 2.0 %reduce-scatter.2.cloned.1.call-done = bf16[128,1536]{1,0:T(8,128)(2,1)} async-done(((bf16[1024,1536]{1,0:T(8,128)(2,1)}), bf16[128,1536]{1,0:T(8,128)(2,1)}) %reduce-scatter.2.cloned.1.call-update) | async-done | bytes 393232 | tf_op jit(solution)/shard_map/reduce_scatter | solution.py:304
  144.9 1.1 dynamic-slice_bitcast_fusion
  145.9 2.6 %collective-permute-start.32 = (bf16[32,1536]{1,0:T(8,128)(2,1)S(1)}, bf16[32,1536]{1,0:T(8,128)(2,1)S(1)}, u32[]{:S(2)}, u32[]{:S(2)}) collective-permute-start(bf16[32,1536]{1,0:T(8,128)(2,1)S(1)} %get-tuple-element.93), channel_id=1, source_target_pairs={{4,0},{8,4},{12,8},{0,12},{5,1},{9,5},{13,9},{1,13},{6,2},{10,6},{... | collective-permute-start | bytes 294920 | tf_op jit(solution)/shard_map/ppermute | solution.py:24
  149.3 1.0 collective-permute-start.30
  150.3 3.8 %shard_map.111 = bf16[512,1536]{1,0:T(8,128)(2,1)} custom-call(bf16[64,1536]{1,0:T(8,128)(2,1)S(1)} %copy-done.4, bf16[64,1536]{1,0:T(8,128)(2,1)S(1)} %copy-done.6, bf16[448,1536]{1,0:T(8,128)(2,1)} %get-tuple-element.97.rest, bf16[448,1536]{1,0:T(8,128)(2,1)} %collective-permute-done.33.rest_far), custom_call_target="tpu_custom_call" | custom-call | tf_op jit(solution)/shard_map/pallas_call | solution.py:231
  154.7 1.0 collective-permute-done.30
  (70 shorter events, 13.1 us)
Async XLA Ops:
  7.2 61.9 %all-gather.2.cloned.1.call-start = ((), (), s32[]{:S(2)}) async-start(), calls=%async_computation.1 | async-start | bytes 3538944 | tf_op jit(solution)/shard_map/all_gather | solution.py:277
  7.2 10.6 %collective-permute-start = (bf16[32,1536]{1,0:T(8,128)(2,1)}, bf16[32,1536]{1,0:T(8,128)(2,1)S(1)}, u32[]{:S(2)}, u32[]{:S(2)}) collective-permute-start(bf16[32,1536]{1,0:T(8,128)(2,1)} %refs_0_.1), channel_id=1, source_target_pairs={{4,0},{8,4},{12,8},{0,12},{5,1},{9,5},{13,9},{1,13},{6,2},{10,6},{... | collective-permute-start | bytes 294920 | tf_op jit(solution)/shard_map/ppermute | solution.py:24
  10.3 7.5 %collective-permute-start.1 = (bf16[32,1536]{1,0:T(8,128)(2,1)}, bf16[32,1536]{1,0:T(8,128)(2,1)S(1)}, u32[]{:S(2)}, u32[]{:S(2)}) collective-permute-start(bf16[32,1536]{1,0:T(8,128)(2,1)} %refs_0_.1), channel_id=1, source_target_pairs={{8,0},{12,4},{0,8},{4,12},{9,1},{13,5},{1,9},{5,13},{10,2},{14,6},... | collective-permute-start | bytes 294920 | tf_op jit(solution)/shard_map/ppermute | solution.py:24
  10.9 7.4 %collective-permute-start.2 = (bf16[32,1536]{1,0:T(8,128)(2,1)}, bf16[32,1536]{1,0:T(8,128)(2,1)S(1)}, u32[]{:S(2)}, u32[]{:S(2)}) collective-permute-start(bf16[32,1536]{1,0:T(8,128)(2,1)} %refs_0_.1), channel_id=1, source_target_pairs={{12,0},{0,4},{4,8},{8,12},{13,1},{1,5},{5,9},{9,13},{14,2},{2,6},{... | collective-permute-start | bytes 294920 | tf_op jit(solution)/shard_map/ppermute | solution.py:24
  11.9 8.4 %collective-permute-start.3 = (bf16[32,1536]{1,0:T(8,128)(2,1)}, bf16[32,1536]{1,0:T(8,128)(2,1)S(1)}, u32[]{:S(2)}, u32[]{:S(2)}) collective-permute-start(bf16[32,1536]{1,0:T(8,128)(2,1)} %refs_0_.2), channel_id=1, source_target_pairs={{16,0},{32,16},{48,32},{64,48},{80,64},{96,80},{112,96},{0,112},{1... | collective-permute-start | bytes 294920 | tf_op jit(solution)/shard_map/ppermute | solution.py:24
  17.8 6.0 %collective-permute-start.4 = (bf16[32,1536]{1,0:T(8,128)(2,1)}, bf16[32,1536]{1,0:T(8,128)(2,1)S(1)}, u32[]{:S(2)}, u32[]{:S(2)}) collective-permute-start(bf16[32,1536]{1,0:T(8,128)(2,1)} %refs_0_.2), channel_id=1, source_target_pairs={{112,0},{0,16},{16,32},{32,48},{48,64},{64,80},{80,96},{96,112},{1... | collective-permute-start | bytes 294920 | tf_op jit(solution)/shard_map/ppermute | solution.py:24
  25.5 26.5 %copy-start.11 = (bf16[256,512]{1,0:T(8,128)(2,1)S(1)}, bf16[256,512]{1,0:T(8,128)(2,1)}, u32[]{:S(2)}) copy-start(bf16[256,512]{1,0:T(8,128)(2,1)} %param.10) | copy-start | bytes 786436
  25.5 119.3 %reduce-scatter.2.cloned.1.call-start = ((), (), s32[]{:S(2)}) async-start(), calls=%async_computation.2 | async-start | bytes 3538944 | tf_op jit(solution)/shard_map/reduce_scatter | solution.py:304
  25.6 16.4 %collective-permute-start.5 = (bf16[256,512]{1,0:T(8,128)(2,1)}, bf16[256,512]{1,0:T(8,128)(2,1)S(1)}, u32[]{:S(2)}, u32[]{:S(2)}) collective-permute-start(bf16[256,512]{1,0:T(8,128)(2,1)} %param.9), channel_id=1, source_target_pairs={{0,2},{2,0},{1,3},{3,1},{4,6},{6,4},{5,7},{7,5},{8,10},{10,8},{9,1... | collective-permute-start | bytes 786440 | tf_op jit(solution)/shard_map/ppermute | solution.py:28
  27.8 5.6 %collective-permute-start.8 = (bf16[32,1536]{1,0:T(8,128)(2,1)S(1)}, bf16[32,1536]{1,0:T(8,128)(2,1)S(1)}, u32[]{:S(2)}, u32[]{:S(2)}) collective-permute-start(bf16[32,1536]{1,0:T(8,128)(2,1)S(1)} %collective-permute-done.3.refs_1_), channel_id=1, source_target_pairs={{16,0},{32,16},{48,32},{64,48},{80,64},{96,80},{112,96},{0,112},{1... | collective-permute-start | bytes 294920 | tf_op jit(solution)/shard_map/ppermute | solution.py:24
  28.2 7.2 %collective-permute-start.11 = (bf16[32,1536]{1,0:T(8,128)(2,1)S(1)}, bf16[32,1536]{1,0:T(8,128)(2,1)S(1)}, u32[]{:S(2)}, u32[]{:S(2)}) collective-permute-start(bf16[32,1536]{1,0:T(8,128)(2,1)S(1)} %collective-permute-done.4.refs_7_), channel_id=1, source_target_pairs={{112,0},{0,16},{16,32},{32,48},{48,64},{64,80},{80,96},{96,112},{1... | collective-permute-start | bytes 294920 | tf_op jit(solution)/shard_map/ppermute | solution.py:24
  33.4 7.7 %collective-permute-start.9 = (bf16[32,1536]{1,0:T(8,128)(2,1)S(1)}, bf16[32,1536]{1,0:T(8,128)(2,1)S(1)}, u32[]{:S(2)}, u32[]{:S(2)}) collective-permute-start(bf16[32,1536]{1,0:T(8,128)(2,1)S(1)} %collective-permute-done.8.refs_2_), channel_id=1, source_target_pairs={{16,0},{32,16},{48,32},{64,48},{80,64},{96,80},{112,96},{0,112},{1... | collective-permute-start | bytes 294920 | tf_op jit(solution)/shard_map/ppermute | solution.py:24
  34.0 17.9 %collective-permute-start.6 = (bf16[256,512]{1,0:T(8,128)(2,1)}, bf16[256,512]{1,0:T(8,128)(2,1)S(1)}, u32[]{:S(2)}, u32[]{:S(2)}) collective-permute-start(bf16[256,512]{1,0:T(8,128)(2,1)} %param.10), channel_id=1, source_target_pairs={{0,2},{2,0},{1,3},{3,1},{4,6},{6,4},{5,7},{7,5},{8,10},{10,8},{9,1... | collective-permute-start | bytes 786440 | tf_op jit(solution)/shard_map/ppermute | solution.py:28
  35.4 7.9 %collective-permute-start.12 = (bf16[32,1536]{1,0:T(8,128)(2,1)S(1)}, bf16[32,1536]{1,0:T(8,128)(2,1)S(1)}, u32[]{:S(2)}, u32[]{:S(2)}) collective-permute-start(bf16[32,1536]{1,0:T(8,128)(2,1)S(1)} %collective-permute-done.11.refs_6_), channel_id=1, source_target_pairs={{112,0},{0,16},{16,32},{32,48},{48,64},{64,80},{80,96},{96,112},{1... | collective-permute-start | bytes 294920 | tf_op jit(solution)/shard_map/ppermute | solution.py:24
  41.1 6.7 %collective-permute-start.10 = (bf16[32,1536]{1,0:T(8,128)(2,1)S(1)}, bf16[32,1536]{1,0:T(8,128)(2,1)S(1)}, u32[]{:S(2)}, u32[]{:S(2)}) collective-permute-start(bf16[32,1536]{1,0:T(8,128)(2,1)S(1)} %collective-permute-done.9.refs_3_), channel_id=1, source_target_pairs={{16,0},{32,16},{48,32},{64,48},{80,64},{96,80},{112,96},{0,112},{1... | collective-permute-start | bytes 294920 | tf_op jit(solution)/shard_map/ppermute | solution.py:24
  48.7 29.3 %copy-start = (bf16[8,32,1536]{2,1,0:T(8,128)(2,1)}, bf16[8,32,1536]{2,1,0:T(8,128)(2,1)S(1)}, u32[]{:S(2)}) copy-start(bf16[8,32,1536]{2,1,0:T(8,128)(2,1)S(1)} %shard_map.103) | copy-start | bytes 2359300
  48.7 13.5 %collective-permute-start.13 = (bf16[256,1536]{1,0:T(8,128)(2,1)S(1)}, bf16[256,1536]{1,0:T(8,128)(2,1)S(1)}, u32[]{:S(2)}, u32[]{:S(2)}) collective-permute-start(bf16[256,1536]{1,0:T(8,128)(2,1)S(1)} %bitcast.23), channel_id=1, source_target_pairs={{0,128},{128,0},{1,129},{129,1},{2,130},{130,2},{3,131},{131,3},{4... | collective-permute-start | bytes 2359304 | tf_op jit(solution)/shard_map/ppermute | solution.py:28
  49.8 13.8 %collective-permute-start.14 = (bf16[256,1536]{1,0:T(8,128)(2,1)S(1)}, bf16[256,1536]{1,0:T(8,128)(2,1)S(1)}, u32[]{:S(2)}, u32[]{:S(2)}) collective-permute-start(bf16[256,1536]{1,0:T(8,128)(2,1)S(1)} %bitcast.24), channel_id=1, source_target_pairs={{4,0},{8,4},{12,8},{0,12},{5,1},{9,5},{13,9},{1,13},{6,2},{10,6},{... | collective-permute-start | bytes 2359304 | tf_op jit(solution)/shard_map/ppermute | solution.py:24
  52.0 13.3 %collective-permute-start.15 = (bf16[256,1536]{1,0:T(8,128)(2,1)S(1)}, bf16[256,1536]{1,0:T(8,128)(2,1)}, u32[]{:S(2)}, u32[]{:S(2)}) collective-permute-start(bf16[256,1536]{1,0:T(8,128)(2,1)S(1)} %bitcast.25), channel_id=1, source_target_pairs={{12,0},{0,4},{4,8},{8,12},{13,1},{1,5},{5,9},{9,13},{14,2},{2,6},{... | collective-permute-start | bytes 2359304 | tf_op jit(solution)/shard_map/ppermute | solution.py:24
  52.4 2.2 %collective-permute-start.7 = (bf16[2,256,512]{2,1,0:T(8,128)(2,1)S(1)}, bf16[2,256,512]{2,1,0:T(8,128)(2,1)S(1)}, u32[]{:S(2)}, u32[]{:S(2)}) collective-permute-start(bf16[2,256,512]{2,1,0:T(8,128)(2,1)S(1)} %fusion.4.hidden), channel_id=1, source_target_pairs={{0,1},{1,0},{2,3},{3,2},{4,5},{5,4},{6,7},{7,6},{8,9},{9,8},{10,11... | collective-permute-start | bytes 1572872 | tf_op jit(solution)/shard_map/ppermute | solution.py:28
  62.2 1.5 copy-start.9
  63.7 0.9 copy-start.10
  73.6 2.0 %collective-permute-start.16 = (bf16[2,256,512]{2,1,0:T(8,128)(2,1)S(1)}, bf16[2,256,512]{2,1,0:T(8,128)(2,1)S(1)}, u32[]{:S(2)}, u32[]{:S(2)}) collective-permute-start(bf16[2,256,512]{2,1,0:T(8,128)(2,1)S(1)} %get-tuple-element.59), channel_id=1, source_target_pairs={{0,1},{1,0},{2,3},{3,2},{4,5},{5,4},{6,7},{7,6},{8,9},{9,8},{10,11... | collective-permute-start | bytes 1572872 | tf_op jit(solution)/shard_map/ppermute | solution.py:28
  75.8 15.6 %collective-permute-start.17 = (bf16[2,256,512]{2,1,0:T(8,128)(2,1)S(1)}, bf16[2,256,512]{2,1,0:T(8,128)(2,1)S(1)}, u32[]{:S(2)}, u32[]{:S(2)}) collective-permute-start(bf16[2,256,512]{2,1,0:T(8,128)(2,1)S(1)} %get-tuple-element.98), channel_id=1, source_target_pairs={{0,2},{2,0},{1,3},{3,1},{4,6},{6,4},{5,7},{7,5},{8,10},{10,8},{9,1... | collective-permute-start | bytes 1572872 | tf_op jit(solution)/shard_map/ppermute | solution.py:28
  78.0 22.2 %collective-permute-start.20 = (bf16[256,1536]{1,0:T(8,128)(2,1)S(1)}, bf16[256,1536]{1,0:T(8,128)(2,1)}, u32[]{:S(2)}, u32[]{:S(2)}) collective-permute-start(bf16[256,1536]{1,0:T(8,128)(2,1)S(1)} %bitcast.26), channel_id=1, source_target_pairs={{8,0},{12,4},{0,8},{4,12},{9,1},{13,5},{1,9},{5,13},{10,2},{14,6},... | collective-permute-start | bytes 2359304 | tf_op jit(solution)/shard_map/ppermute | solution.py:24
  80.0 14.7 %copy-start.2 = (bf16[1536,512]{1,0:T(8,128)(2,1)S(1)}, bf16[1536,512]{1,0:T(8,128)(2,1)}, u32[]{:S(2)}) copy-start(bf16[1536,512]{1,0:T(8,128)(2,1)} %w_up.1) | copy-start | bytes 4718596
  85.1 15.1 %copy-start.3 = (bf16[64,1536]{1,0:T(8,128)(2,1)}, bf16[64,1536]{1,0:T(8,128)(2,1)S(1)}, u32[]{:S(2)}) copy-start(bf16[64,1536]{1,0:T(8,128)(2,1)S(1)} %get-tuple-element.71.first) | copy-start | bytes 589828
  85.1 9.6 %copy-start.1 = (bf16[1536,512]{1,0:T(8,128)(2,1)S(1)}, bf16[1536,512]{1,0:T(8,128)(2,1)}, u32[]{:S(2)}) copy-start(bf16[1536,512]{1,0:T(8,128)(2,1)} %w_gate.1) | copy-start | bytes 4718596
  92.0 2.0 %collective-permute-start.18 = (bf16[2,256,512]{2,1,0:T(8,128)(2,1)S(1)}, bf16[2,256,512]{2,1,0:T(8,128)(2,1)S(1)}, u32[]{:S(2)}, u32[]{:S(2)}) collective-permute-start(bf16[2,256,512]{2,1,0:T(8,128)(2,1)S(1)} %get-tuple-element.68.near0.refs_4_), channel_id=1, source_target_pairs={{0,1},{1,0},{2,3},{3,2},{4,5},{5,4},{6,7},{7,6},{8,9},{9,8},{10,11... | collective-permute-start | bytes 1572872 | tf_op jit(solution)/shard_map/ppermute | solution.py:28
  92.1 2.6 %collective-permute-start.19 = (bf16[2,256,512]{2,1,0:T(8,128)(2,1)S(1)}, bf16[2,256,512]{2,1,0:T(8,128)(2,1)S(1)}, u32[]{:S(2)}, u32[]{:S(2)}) collective-permute-start(bf16[2,256,512]{2,1,0:T(8,128)(2,1)S(1)} %get-tuple-element.69.near1.refs_5_), channel_id=1, source_target_pairs={{0,1},{1,0},{2,3},{3,2},{4,5},{5,4},{6,7},{7,6},{8,9},{9,8},{10,11... | collective-permute-start | bytes 1572872 | tf_op jit(solution)/shard_map/ppermute | solution.py:28
  92.6 7.6 %collective-permute-start.21 = (bf16[64,1536]{1,0:T(8,128)(2,1)S(1)}, bf16[64,1536]{1,0:T(8,128)(2,1)S(1)}, u32[]{:S(2)}, u32[]{:S(2)}) collective-permute-start(bf16[64,1536]{1,0:T(8,128)(2,1)S(1)} %get-tuple-element.71.first), channel_id=1, source_target_pairs={{0,128},{128,0},{1,129},{129,1},{2,130},{130,2},{3,131},{131,3},{4... | collective-permute-start | bytes 589832 | tf_op jit(solution)/shard_map/ppermute | solution.py:28
  100.2 0.7 copy-start.5
  100.9 14.0 %collective-permute-start.26 = (bf16[2,256,512]{2,1,0:T(8,128)(2,1)S(1)}, bf16[2,256,512]{2,1,0:T(8,128)(2,1)S(1)}, u32[]{:S(2)}, u32[]{:S(2)}) collective-permute-start(bf16[2,256,512]{2,1,0:T(8,128)(2,1)S(1)} %get-tuple-element.68.near0.refs_4_), channel_id=1, source_target_pairs={{0,128},{128,0},{1,129},{129,1},{2,130},{130,2},{3,131},{131,3},{4... | collective-permute-start | bytes 1572872 | tf_op jit(solution)/shard_map/ppermute | solution.py:28
  101.4 14.0 %collective-permute-start.27 = (bf16[2,256,512]{2,1,0:T(8,128)(2,1)S(1)}, bf16[2,256,512]{2,1,0:T(8,128)(2,1)S(1)}, u32[]{:S(2)}, u32[]{:S(2)}) collective-permute-start(bf16[2,256,512]{2,1,0:T(8,128)(2,1)S(1)} %get-tuple-element.69.near1.refs_5_), channel_id=1, source_target_pairs={{0,130},{130,0},{2,128},{128,2},{1,131},{131,1},{3,129},{129,3},{4... | collective-permute-start | bytes 1572872 | tf_op jit(solution)/shard_map/ppermute | solution.py:306
  103.5 19.2 %collective-permute-start.22 = (bf16[256,1536]{1,0:T(8,128)(2,1)}, bf16[256,1536]{1,0:T(8,128)(2,1)S(1)}, u32[]{:S(2)}, u32[]{:S(2)}) collective-permute-start(bf16[256,1536]{1,0:T(8,128)(2,1)} %copy-done.9), channel_id=1, source_target_pairs={{4,0},{8,4},{12,8},{0,12},{5,1},{9,5},{13,9},{1,13},{6,2},{10,6},{... | collective-permute-start | bytes 2359304 | tf_op jit(solution)/shard_map/ppermute | solution.py:24
  105.2 20.2 %collective-permute-start.23 = (bf16[256,1536]{1,0:T(8,128)(2,1)}, bf16[256,1536]{1,0:T(8,128)(2,1)S(1)}, u32[]{:S(2)}, u32[]{:S(2)}) collective-permute-start(bf16[256,1536]{1,0:T(8,128)(2,1)} %copy-done.9), channel_id=1, source_target_pairs={{12,0},{0,4},{4,8},{8,12},{13,1},{1,5},{5,9},{9,13},{14,2},{2,6},{... | collective-permute-start | bytes 2359304 | tf_op jit(solution)/shard_map/ppermute | solution.py:24
  115.4 34.9 %collective-permute-start.33 = (bf16[448,1536]{1,0:T(8,128)(2,1)}, bf16[448,1536]{1,0:T(8,128)(2,1)}, u32[]{:S(2)}, u32[]{:S(2)}) collective-permute-start(bf16[448,1536]{1,0:T(8,128)(2,1)} %get-tuple-element.97.rest), channel_id=1, source_target_pairs={{0,128},{128,0},{1,129},{129,1},{2,130},{130,2},{3,131},{131,3},{4... | collective-permute-start | bytes 4128776 | tf_op jit(solution)/shard_map/ppermute | solution.py:28
  117.8 10.7 %collective-permute-start.28 = (bf16[2,256,512]{2,1,0:T(8,128)(2,1)S(1)}, bf16[2,256,512]{2,1,0:T(8,128)(2,1)S(1)}, u32[]{:S(2)}, u32[]{:S(2)}) collective-permute-start(bf16[2,256,512]{2,1,0:T(8,128)(2,1)S(1)} %collective-permute-done.26.refs_3_.refs_2_), channel_id=1, source_target_pairs={{0,1},{1,0},{2,3},{3,2},{4,5},{5,4},{6,7},{7,6},{8,9},{9,8},{10,11... | collective-permute-start | bytes 1572872 | tf_op jit(solution)/shard_map/ppermute | solution.py:28
  117.8 10.7 %collective-permute-start.29 = (bf16[2,256,512]{2,1,0:T(8,128)(2,1)S(1)}, bf16[2,256,512]{2,1,0:T(8,128)(2,1)S(1)}, u32[]{:S(2)}, u32[]{:S(2)}) collective-permute-start(bf16[2,256,512]{2,1,0:T(8,128)(2,1)S(1)} %collective-permute-done.27.refs_4_.refs_3_), channel_id=1, source_target_pairs={{0,1},{1,0},{2,3},{3,2},{4,5},{5,4},{6,7},{7,6},{8,9},{9,8},{10,11... | collective-permute-start | bytes 1572872 | tf_op jit(solution)/shard_map/ppermute | solution.py:28
  122.7 3.2 %copy-start.7 = (bf16[256,1536]{1,0:T(8,128)(2,1)}, bf16[256,1536]{1,0:T(8,128)(2,1)S(1)}, u32[]{:S(2)}) copy-start(bf16[256,1536]{1,0:T(8,128)(2,1)S(1)} %collective-permute-done.22.refs_1_) | copy-start | bytes 2359300
  125.4 1.4 copy-start.8
  125.4 10.4 %collective-permute-start.24 = (bf16[128,1536]{1,0:T(8,128)(2,1)S(1)}, bf16[128,1536]{1,0:T(8,128)(2,1)S(1)}, u32[]{:S(2)}, u32[]{:S(2)}) collective-permute-start(bf16[128,1536]{1,0:T(8,128)(2,1)S(1)} %slice.6), channel_id=1, source_target_pairs={{4,0},{8,4},{12,8},{0,12},{5,1},{9,5},{13,9},{1,13},{6,2},{10,6},{... | collective-permute-start | bytes 1179656 | tf_op jit(solution)/shard_map/ppermute | solution.py:24
  126.7 10.9 %collective-permute-start.25 = (bf16[128,1536]{1,0:T(8,128)(2,1)}, bf16[128,1536]{1,0:T(8,128)(2,1)S(1)}, u32[]{:S(2)}, u32[]{:S(2)}) collective-permute-start(bf16[128,1536]{1,0:T(8,128)(2,1)} %slice.7), channel_id=1, source_target_pairs={{12,0},{0,4},{4,8},{8,12},{13,1},{1,5},{5,9},{9,13},{14,2},{2,6},{... | collective-permute-start | bytes 1179656 | tf_op jit(solution)/shard_map/ppermute | solution.py:24
  137.7 12.7 %copy-start.4 = (bf16[64,1536]{1,0:T(8,128)(2,1)S(1)}, bf16[64,1536]{1,0:T(8,128)(2,1)}, u32[]{:S(2)}) copy-start(bf16[64,1536]{1,0:T(8,128)(2,1)} %copy-done.3) | copy-start | bytes 589828
  137.7 12.7 %copy-start.6 = (bf16[64,1536]{1,0:T(8,128)(2,1)S(1)}, bf16[64,1536]{1,0:T(8,128)(2,1)}, u32[]{:S(2)}) copy-start(bf16[64,1536]{1,0:T(8,128)(2,1)} %copy-done.5) | copy-start | bytes 589828
  145.9 8.3 %collective-permute-start.32 = (bf16[32,1536]{1,0:T(8,128)(2,1)S(1)}, bf16[32,1536]{1,0:T(8,128)(2,1)S(1)}, u32[]{:S(2)}, u32[]{:S(2)}) collective-permute-start(bf16[32,1536]{1,0:T(8,128)(2,1)S(1)} %get-tuple-element.93), channel_id=1, source_target_pairs={{4,0},{8,4},{12,8},{0,12},{5,1},{9,5},{13,9},{1,13},{6,2},{10,6},{... | collective-permute-start | bytes 294920 | tf_op jit(solution)/shard_map/ppermute | solution.py:24
  148.5 6.2 %collective-permute-start.31 = (bf16[32,1536]{1,0:T(8,128)(2,1)S(1)}, bf16[32,1536]{1,0:T(8,128)(2,1)S(1)}, u32[]{:S(2)}, u32[]{:S(2)}) collective-permute-start(bf16[32,1536]{1,0:T(8,128)(2,1)S(1)} %get-tuple-element.92), channel_id=1, source_target_pairs={{8,0},{12,4},{0,8},{4,12},{9,1},{13,5},{1,9},{5,13},{10,2},{14,6},... | collective-permute-start | bytes 294920 | tf_op jit(solution)/shard_map/ppermute | solution.py:24
  149.3 6.4 %collective-permute-start.30 = (bf16[32,1536]{1,0:T(8,128)(2,1)S(1)}, bf16[32,1536]{1,0:T(8,128)(2,1)S(1)}, u32[]{:S(2)}, u32[]{:S(2)}) collective-permute-start(bf16[32,1536]{1,0:T(8,128)(2,1)S(1)} %get-tuple-element.91), channel_id=1, source_target_pairs={{12,0},{0,4},{4,8},{8,12},{13,1},{1,5},{5,9},{9,13},{14,2},{2,6},{... | collective-permute-start | bytes 294920 | tf_op jit(solution)/shard_map/ppermute | solution.py:24
Sparse Core Ops, SparseCore 0:
  25.6 43.3 all-gather.1
  100.3 44.4 reduce-scatter.1

commit v13 on v12

--- a/solution.py
+++ b/solution.py
@@ -273,7 +273,7 @@
 
     go_parts = [grad_output] + [from_ahead(grad_output, "y", NY, k) for k in (1, 2, 3)]
     z_up, z_down = from_ahead(layer_input, "z", NZ, 1), from_ahead(layer_input, "z", NZ, NZ - 1)
-    go_parts, z_up, z_down = lax.optimization_barrier((go_parts, z_up, z_down))
+    go_parts, z_up = lax.optimization_barrier((go_parts, z_up))
     go = lax.all_gather(arrange(place, 1, go_parts), "z", axis=0, tiled=True)
     own_z = arrange(place, 0, ring(layer_input, z_up, z_down, "z", NZ))
     partner_z = swap(own_z, "dp")

time: 164 us -> 164 us (level)
  waiting for transfers between devices: 58.6 us -> 52.6 us
  starting transfers between devices: 42.4 us -> 48.2 us
    ppermute x20, waiting for transfers between devices: 31.2 us -> 24.9 us  [from_ahead(): return lax.ppermute(x, axis, [((d + k) % n, d) for d in range(n)])]
    ppermute x20, starting transfers between devices: 28.4 us -> 34.7 us  [from_ahead(): return lax.ppermute(x, axis, [((d + k) % n, d) for d in range(n)])]
  transfers between devices with their start and end apart: 36 -> 36, of which waited for: 24 -> 22; matrix products, arithmetic and copies ran while one was open for 2% -> 2% of each run, Pallas kernels for 22% -> 22%
where the time goes in v13:
time: 164 us; the launch traced here: 163 us
  waiting for transfers between devices  52.6 us (32%)
  starting transfers between devices  48.2 us (29%)
  Pallas kernels  42.2 us (26%)
  between operations  14.2 us (9%)
  local copies, waits for them, and re-layouts  3.45 us (2%)
  other arithmetic  2.44 us (1%)
    ppermute x20, starting transfers between devices, from_ahead(): return lax.ppermute(x, axis, [((d + k) % n, d) for d in range(n)])  34.7 us
    ppermute x20, waiting for transfers between devices, from_ahead(): return lax.ppermute(x, axis, [((d + k) % n, d) for d in range(n)])  24.9 us
    ppermute x13, waiting for transfers between devices, swap(): return lax.ppermute(x, axis, [(0, 1), (1, 0)])  21.5 us
    pallas_call x3, Pallas kernels, weight_grads(): pl.pallas_call(functools.partial(weight_kernel, slots, bool(base)), grid=...  20 us
    ppermute x13, starting transfers between devices, swap(): return lax.ppermute(x, axis, [(0, 1), (1, 0)])  12.2 us
    pallas_call x1, Pallas kernels, input_grad(): pl.pallas_call(input_grad_kernel, grid=(3,), out_shape=jax.ShapeDtypeStru...  5.46 us
    pallas_call x1, Pallas kernels, down_grad(): pl.pallas_call(down_kernel, grid=(3,), out_shape=(jax.ShapeDtypeStruct((F...  5.13 us
    pallas_call x1, Pallas kernels, hidden_grad(): pl.pallas_call(hidden_grad_kernel, out_shape=(jax.ShapeDtypeStruct((2, 25...  4.58 us
  transfers between devices with their start and end apart: 36, of which 22 were waited for; matrix products, arithmetic and copies ran while one was open for 2% of the time, Pallas kernels for 22%

profile of v13, /device:TPU:2, one launch (start us, length us, event | category | flops | bytes accessed | tf_op | source)
XLA Modules:
  0.0 163.1 jit_solution(3229753505853452758)
XLA Ops:
  7.2 3.1 %collective-permute-start = (bf16[32,1536]{1,0:T(8,128)(2,1)}, bf16[32,1536]{1,0:T(8,128)(2,1)S(1)}, u32[]{:S(2)}, u32[]{:S(2)}) collective-permute-start(bf16[32,1536]{1,0:T(8,128)(2,1)} %refs_0_.1), channel_id=1, source_target_pairs={{4,0},{8,4},{12,8},{0,12},{5,1},{9,5},{13,9},{1,13},{6,2},{10,6},{... | collective-permute-start | bytes 294920 | tf_op jit(solution)/shard_map/ppermute | solution.py:24
  10.9 1.0 collective-permute-start.2
  11.9 5.9 %collective-permute-start.3 = (bf16[32,1536]{1,0:T(8,128)(2,1)}, bf16[32,1536]{1,0:T(8,128)(2,1)S(1)}, u32[]{:S(2)}, u32[]{:S(2)}) collective-permute-start(bf16[32,1536]{1,0:T(8,128)(2,1)} %refs_0_.2), channel_id=1, source_target_pairs={{16,0},{32,16},{48,32},{64,48},{80,64},{96,80},{112,96},{0,112},{1... | collective-permute-start | bytes 294920 | tf_op jit(solution)/shard_map/ppermute | solution.py:24
  18.4 1.9 %collective-permute-done.3.refs_1_ = bf16[32,1536]{1,0:T(8,128)(2,1)S(1)} collective-permute-done((bf16[32,1536]{1,0:T(8,128)(2,1)}, bf16[32,1536]{1,0:T(8,128)(2,1)S(1)}, u32[]{:S(2)}, u32[]{:S(2)}) %collective-permute-start.3) | collective-permute-done | bytes 98336 | tf_op jit(solution)/shard_map/ppermute | solution.py:24
  20.3 1.7 %shard_map.102 = bf16[4,32,1536]{2,1,0:T(8,128)(2,1)} custom-call(s32[4]{0:T(128)S(1)} %pad_add_fusion.place, bf16[32,1536]{1,0:T(8,128)(2,1)} %refs_0_.1, bf16[32,1536]{1,0:T(8,128)(2,1)S(1)} %collective-permute-done.refs_1_, bf16[32,1536]{1,0:T(8,128)(2,1)S(1)} %collective-permute-done.1.refs_2_, bf16[32,1536]{1,0:T(8,128)(2,1)S(1)} %collective-permute-done.2.refs_3_), custom_call_target="tpu_custom_call" | custom-call | tf_op jit(solution)/shard_map/pallas_call | solution.py:46
  22.0 2.2 %collective-permute-start.4 = (bf16[256,512]{1,0:T(8,128)(2,1)}, bf16[256,512]{1,0:T(8,128)(2,1)S(1)}, u32[]{:S(2)}, u32[]{:S(2)}) collective-permute-start(bf16[256,512]{1,0:T(8,128)(2,1)} %param.9), channel_id=1, source_target_pairs={{0,2},{2,0},{1,3},{3,1},{4,6},{6,4},{5,7},{7,5},{8,10},{10,8},{9,1... | collective-permute-start | bytes 786440 | tf_op jit(solution)/shard_map/ppermute | solution.py:28
  24.3 3.9 %collective-permute-start.7 = (bf16[32,1536]{1,0:T(8,128)(2,1)S(1)}, bf16[32,1536]{1,0:T(8,128)(2,1)S(1)}, u32[]{:S(2)}, u32[]{:S(2)}) collective-permute-start(bf16[32,1536]{1,0:T(8,128)(2,1)S(1)} %collective-permute-done.3.refs_1_), channel_id=1, source_target_pairs={{16,0},{32,16},{48,32},{64,48},{80,64},{96,80},{112,96},{0,112},{1... | collective-permute-start | bytes 294920 | tf_op jit(solution)/shard_map/ppermute | solution.py:24
  28.2 2.8 %collective-permute-done.10.refs_7_ = bf16[32,1536]{1,0:T(8,128)(2,1)S(1)} collective-permute-done((bf16[32,1536]{1,0:T(8,128)(2,1)}, bf16[32,1536]{1,0:T(8,128)(2,1)S(1)}, u32[]{:S(2)}, u32[]{:S(2)}) %collective-permute-start.10) | collective-permute-done | bytes 98336 | tf_op jit(solution)/shard_map/ppermute | solution.py:24
  31.0 3.2 %collective-permute-start.8 = (bf16[32,1536]{1,0:T(8,128)(2,1)S(1)}, bf16[32,1536]{1,0:T(8,128)(2,1)S(1)}, u32[]{:S(2)}, u32[]{:S(2)}) collective-permute-start(bf16[32,1536]{1,0:T(8,128)(2,1)S(1)} %collective-permute-done.7.refs_2_), channel_id=1, source_target_pairs={{16,0},{32,16},{48,32},{64,48},{80,64},{96,80},{112,96},{0,112},{1... | collective-permute-start | bytes 294920 | tf_op jit(solution)/shard_map/ppermute | solution.py:24
  34.3 1.4 collective-permute-start.5
  35.7 3.3 %collective-permute-done.11.refs_6_ = bf16[32,1536]{1,0:T(8,128)(2,1)S(1)} collective-permute-done((bf16[32,1536]{1,0:T(8,128)(2,1)S(1)}, bf16[32,1536]{1,0:T(8,128)(2,1)S(1)}, u32[]{:S(2)}, u32[]{:S(2)}) %collective-permute-start.11) | collective-permute-done | bytes 98336 | tf_op jit(solution)/shard_map/ppermute | solution.py:24
  39.0 3.2 %collective-permute-start.9 = (bf16[32,1536]{1,0:T(8,128)(2,1)S(1)}, bf16[32,1536]{1,0:T(8,128)(2,1)S(1)}, u32[]{:S(2)}, u32[]{:S(2)}) collective-permute-start(bf16[32,1536]{1,0:T(8,128)(2,1)S(1)} %collective-permute-done.8.refs_3_), channel_id=1, source_target_pairs={{16,0},{32,16},{48,32},{64,48},{80,64},{96,80},{112,96},{0,112},{1... | collective-permute-start | bytes 294920 | tf_op jit(solution)/shard_map/ppermute | solution.py:24
  42.2 1.0 select_bitcast_fusion.3
  43.2 3.7 %collective-permute-done.12.refs_5_ = bf16[32,1536]{1,0:T(8,128)(2,1)S(1)} collective-permute-done((bf16[32,1536]{1,0:T(8,128)(2,1)S(1)}, bf16[32,1536]{1,0:T(8,128)(2,1)S(1)}, u32[]{:S(2)}, u32[]{:S(2)}) %collective-permute-start.12) | collective-permute-done | bytes 98336 | tf_op jit(solution)/shard_map/ppermute | solution.py:24
  46.9 1.0 shard_map.103
  47.9 1.2 collective-permute-start.13
  49.1 2.7 %collective-permute-start.14 = (bf16[256,1536]{1,0:T(8,128)(2,1)S(1)}, bf16[256,1536]{1,0:T(8,128)(2,1)S(1)}, u32[]{:S(2)}, u32[]{:S(2)}) collective-permute-start(bf16[256,1536]{1,0:T(8,128)(2,1)S(1)} %bitcast.24), channel_id=1, source_target_pairs={{4,0},{8,4},{12,8},{0,12},{5,1},{9,5},{13,9},{1,13},{6,2},{10,6},{... | collective-permute-start | bytes 2359304 | tf_op jit(solution)/shard_map/ppermute | solution.py:24
  52.5 1.8 %collective-permute-done.6.hidden_other = bf16[2,256,512]{2,1,0:T(8,128)(2,1)S(1)} collective-permute-done((bf16[2,256,512]{2,1,0:T(8,128)(2,1)S(1)}, bf16[2,256,512]{2,1,0:T(8,128)(2,1)S(1)}, u32[]{:S(2)}, u32[]{:S(2)}) %collective-permute-start.6) | collective-permute-done | bytes 524320 | tf_op jit(solution)/shard_map/ppermute | solution.py:28
  54.3 7.8 %collective-permute-done.13.refs_0_ = bf16[256,1536]{1,0:T(8,128)(2,1)S(1)} collective-permute-done((bf16[256,1536]{1,0:T(8,128)(2,1)S(1)}, bf16[256,1536]{1,0:T(8,128)(2,1)S(1)}, u32[]{:S(2)}, u32[]{:S(2)}) %collective-permute-start.13) | collective-permute-done | bytes 786464 | tf_op jit(solution)/shard_map/ppermute | solution.py:28
  62.1 1.1 collective-permute-done.14.refs_1_
  63.2 0.9 copy-done.10
  64.1 1.0 collective-permute-done.15.refs_3_
  65.1 3.8 %all-gather.2.cloned.1.call-done.go = bf16[1024,1536]{1,0:T(8,128)(2,1)} async-done(((bf16[128,1536]{1,0:T(8,128)(2,1)}), bf16[1024,1536]{1,0:T(8,128)(2,1)}) %all-gather.2.cloned.1.call-update) | async-done | bytes 3145744 | tf_op jit(solution)/shard_map/all_gather | solution.py:277
  68.8 4.6 %shard_map.104 = (f32[2,256,512]{2,1,0:T(8,128)S(1)}, bf16[2,256,512]{2,1,0:T(8,128)(2,1)S(1)}) custom-call(s32[4]{0:T(128)S(1)} %pad_add_fusion.place, bf16[1024,1536]{1,0:T(8,128)(2,1)} %all-gather.2.cloned.1.call-done.go, bf16[512,1536]{1,0:T(8,128)(2,1)} %w_down.1), custom_call_target="tpu_custom_call" | custom-call | tf_op jit(solution)/shard_map/pallas_call | solution.py:79
  73.5 1.9 %collective-permute-done.16 = bf16[2,256,512]{2,1,0:T(8,128)(2,1)S(1)} collective-permute-done((bf16[2,256,512]{2,1,0:T(8,128)(2,1)S(1)}, bf16[2,256,512]{2,1,0:T(8,128)(2,1)S(1)}, u32[]{:S(2)}, u32[]{:S(2)}) %collective-permute-start.16) | collective-permute-done | bytes 524320 | tf_op jit(solution)/shard_map/ppermute | solution.py:28
  75.6 1.7 %collective-permute-start.17 = (bf16[2,256,512]{2,1,0:T(8,128)(2,1)S(1)}, bf16[2,256,512]{2,1,0:T(8,128)(2,1)S(1)}, u32[]{:S(2)}, u32[]{:S(2)}) collective-permute-start(bf16[2,256,512]{2,1,0:T(8,128)(2,1)S(1)} %get-tuple-element.96), channel_id=1, source_target_pairs={{0,2},{2,0},{1,3},{3,1},{4,6},{6,4},{5,7},{7,5},{8,10},{10,8},{9,1... | collective-permute-start | bytes 1572872 | tf_op jit(solution)/shard_map/ppermute | solution.py:28
  77.4 2.0 %collective-permute-start.20 = (bf16[256,1536]{1,0:T(8,128)(2,1)S(1)}, bf16[256,1536]{1,0:T(8,128)(2,1)}, u32[]{:S(2)}, u32[]{:S(2)}) collective-permute-start(bf16[256,1536]{1,0:T(8,128)(2,1)S(1)} %bitcast.26), channel_id=1, source_target_pairs={{8,0},{12,4},{0,8},{4,12},{9,1},{13,5},{1,9},{5,13},{10,2},{14,6},... | collective-permute-start | bytes 2359304 | tf_op jit(solution)/shard_map/ppermute | solution.py:24
  79.4 5.1 %shard_map.105 = (bf16[64,1536]{1,0:T(8,128)(2,1)S(1)}, bf16[448,1536]{1,0:T(8,128)(2,1)}) custom-call(s32[4]{0:T(128)S(1)} %pad_add_fusion.place, bf16[2,256,512]{2,1,0:T(8,128)(2,1)S(1)} %fusion.4.hidden, bf16[2,256,512]{2,1,0:T(8,128)(2,1)S(1)} %collective-permute-done.6.hidden_other, bf16[1024,1536]{1,0:T(8,128)(2,1)} %all-gather.2.cloned.1.call-done.go), custom_call_target="tpu_custom_call" | custom-call | tf_op jit(solution)/shard_map/pallas_call | solution.py:161
  84.5 6.7 %collective-permute-done.17.chip_far = bf16[2,256,512]{2,1,0:T(8,128)(2,1)S(1)} collective-permute-done((bf16[2,256,512]{2,1,0:T(8,128)(2,1)S(1)}, bf16[2,256,512]{2,1,0:T(8,128)(2,1)S(1)}, u32[]{:S(2)}, u32[]{:S(2)}) %collective-permute-start.17) | collective-permute-done | bytes 524320 | tf_op jit(solution)/shard_map/ppermute | solution.py:28
  92.4 1.0 collective-permute-start.21
  94.5 5.5 %shard_map.107 = bf16[1024,1536]{1,0:T(8,128)(2,1)} custom-call(s32[4]{0:T(128)S(1)} %pad_add_fusion.place, bf16[2,256,512]{2,1,0:T(8,128)(2,1)S(1)} %get-tuple-element.66.near0.refs_4_, bf16[2,256,512]{2,1,0:T(8,128)(2,1)S(1)} %get-tuple-element.67.near1.refs_5_, bf16[2,256,512]{2,1,0:T(8,128)(2,1)S(1)} %collective-permute-done.18.other0.refs_6_, ...), custom_call_target="tpu_custom_call" | custom-call | tf_op jit(solution)/shard_map/pallas_call | solution.py:131
  100.7 1.0 collective-permute-start.26
  101.6 1.2 collective-permute-start.27
  102.9 2.1 %collective-permute-start.22 = (bf16[256,1536]{1,0:T(8,128)(2,1)}, bf16[256,1536]{1,0:T(8,128)(2,1)S(1)}, u32[]{:S(2)}, u32[]{:S(2)}) collective-permute-start(bf16[256,1536]{1,0:T(8,128)(2,1)} %copy-done.9), channel_id=1, source_target_pairs={{4,0},{8,4},{12,8},{0,12},{5,1},{9,5},{13,9},{1,13},{6,2},{10,6},{... | collective-permute-start | bytes 2359304 | tf_op jit(solution)/shard_map/ppermute | solution.py:24
  104.9 7.5 %shard_map.108 = (bf16[1536,512]{1,0:T(8,128)(2,1)}, bf16[1536,512]{1,0:T(8,128)(2,1)}) custom-call(s32[4]{0:T(128)S(1)} %pad_add_fusion.place, bf16[256,1536]{1,0:T(8,128)(2,1)} %bitcast.27, bf16[256,1536]{1,0:T(8,128)(2,1)} %copy-done.10, bf16[256,1536]{1,0:T(8,128)(2,1)} %collective-permute-done.20.refs_2_, ...), custom_call_target="tpu_custom_call" | custom-call | tf_op jit(solution)/shard_map/pallas_call | solution.py:212
  112.4 2.2 %collective-permute-done.26.refs_3_.refs_2_ = bf16[2,256,512]{2,1,0:T(8,128)(2,1)S(1)} collective-permute-done((bf16[2,256,512]{2,1,0:T(8,128)(2,1)S(1)}, bf16[2,256,512]{2,1,0:T(8,128)(2,1)S(1)}, u32[]{:S(2)}, u32[]{:S(2)}) %collective-permute-start.26) | collective-permute-done | bytes 524320 | tf_op jit(solution)/shard_map/ppermute | solution.py:28
  115.3 2.3 %collective-permute-start.33 = (bf16[448,1536]{1,0:T(8,128)(2,1)}, bf16[448,1536]{1,0:T(8,128)(2,1)}, u32[]{:S(2)}, u32[]{:S(2)}) collective-permute-start(bf16[448,1536]{1,0:T(8,128)(2,1)} %get-tuple-element.95.rest), channel_id=1, source_target_pairs={{0,128},{128,0},{1,129},{129,1},{2,130},{130,2},{3,131},{131,3},{4... | collective-permute-start | bytes 4128776 | tf_op jit(solution)/shard_map/ppermute | solution.py:28
  118.1 4.0 %collective-permute-done.22.refs_1_ = bf16[256,1536]{1,0:T(8,128)(2,1)S(1)} collective-permute-done((bf16[256,1536]{1,0:T(8,128)(2,1)}, bf16[256,1536]{1,0:T(8,128)(2,1)S(1)}, u32[]{:S(2)}, u32[]{:S(2)}) %collective-permute-start.22) | collective-permute-done | bytes 786464 | tf_op jit(solution)/shard_map/ppermute | solution.py:24
  122.1 3.0 %collective-permute-done.23.refs_2_ = bf16[256,1536]{1,0:T(8,128)(2,1)S(1)} collective-permute-done((bf16[256,1536]{1,0:T(8,128)(2,1)}, bf16[256,1536]{1,0:T(8,128)(2,1)S(1)}, u32[]{:S(2)}, u32[]{:S(2)}) %collective-permute-start.23) | collective-permute-done | bytes 786464 | tf_op jit(solution)/shard_map/ppermute | solution.py:24
  126.5 1.7 %collective-permute-start.25 = (bf16[128,1536]{1,0:T(8,128)(2,1)}, bf16[128,1536]{1,0:T(8,128)(2,1)S(1)}, u32[]{:S(2)}, u32[]{:S(2)}) collective-permute-start(bf16[128,1536]{1,0:T(8,128)(2,1)} %slice.7), channel_id=1, source_target_pairs={{12,0},{0,4},{4,8},{8,12},{13,1},{1,5},{5,9},{9,13},{14,2},{2,6},{... | collective-permute-start | bytes 1179656 | tf_op jit(solution)/shard_map/ppermute | solution.py:24
  128.2 7.3 %shard_map.109 = (bf16[1536,512]{1,0:T(8,128)(2,1)}, bf16[1536,512]{1,0:T(8,128)(2,1)}) custom-call(s32[4]{0:T(128)S(1)} %pad_add_fusion.place, bf16[256,1536]{1,0:T(8,128)(2,1)} %copy-done.9, bf16[256,1536]{1,0:T(8,128)(2,1)} %copy-done.7, bf16[256,1536]{1,0:T(8,128)(2,1)} %copy-done.8, bf16[2,256,512]{2,1,0:T(8,128)(2,1)S(1)} %collective-permute-done.26.refs_3_.refs_2_, ...), custom_call_target="tpu_custom_call" | custom-call | tf_op jit(solution)/shard_map/pallas_call | solution.py:212
  135.5 1.9 %collective-permute-done.25.refs_1_ = bf16[128,1536]{1,0:T(8,128)(2,1)S(1)} collective-permute-done((bf16[128,1536]{1,0:T(8,128)(2,1)}, bf16[128,1536]{1,0:T(8,128)(2,1)S(1)}, u32[]{:S(2)}, u32[]{:S(2)}) %collective-permute-start.25) | collective-permute-done | bytes 393248 | tf_op jit(solution)/shard_map/ppermute | solution.py:24
  137.4 5.2 %shard_map.110 = (bf16[1536,512]{1,0:T(8,128)(2,1)}, bf16[1536,512]{1,0:T(8,128)(2,1)}) custom-call(s32[4]{0:T(128)S(1)} %pad_add_fusion.place, bf16[128,1536]{1,0:T(8,128)(2,1)S(1)} %collective-permute-done.24.refs_0_, bf16[128,1536]{1,0:T(8,128)(2,1)S(1)} %collective-permute-done.25.refs_1_, ...), custom_call_target="tpu_custom_call" | custom-call | tf_op jit(solution)/shard_map/pallas_call | solution.py:212
  142.6 1.7 %reduce-scatter.2.cloned.1.call-done = bf16[128,1536]{1,0:T(8,128)(2,1)} async-done(((bf16[1024,1536]{1,0:T(8,128)(2,1)}), bf16[128,1536]{1,0:T(8,128)(2,1)}) %reduce-scatter.2.cloned.1.call-update) | async-done | bytes 393232 | tf_op jit(solution)/shard_map/reduce_scatter | solution.py:304
  144.4 1.1 dynamic-slice_bitcast_fusion
  145.4 3.0 %collective-permute-start.32 = (bf16[32,1536]{1,0:T(8,128)(2,1)S(1)}, bf16[32,1536]{1,0:T(8,128)(2,1)S(1)}, u32[]{:S(2)}, u32[]{:S(2)}) collective-permute-start(bf16[32,1536]{1,0:T(8,128)(2,1)S(1)} %get-tuple-element.91), channel_id=1, source_target_pairs={{4,0},{8,4},{12,8},{0,12},{5,1},{9,5},{13,9},{1,13},{6,2},{10,6},{... | collective-permute-start | bytes 294920 | tf_op jit(solution)/shard_map/ppermute | solution.py:24
  150.0 3.8 %shard_map.111 = bf16[512,1536]{1,0:T(8,128)(2,1)} custom-call(bf16[64,1536]{1,0:T(8,128)(2,1)S(1)} %copy-done.4, bf16[64,1536]{1,0:T(8,128)(2,1)S(1)} %copy-done.6, bf16[448,1536]{1,0:T(8,128)(2,1)} %get-tuple-element.95.rest, bf16[448,1536]{1,0:T(8,128)(2,1)} %collective-permute-done.33.rest_far), custom_call_target="tpu_custom_call" | custom-call | tf_op jit(solution)/shard_map/pallas_call | solution.py:231
  154.6 1.0 collective-permute-done.30
  (70 shorter events, 11.1 us)
Async XLA Ops:
  7.2 61.7 %all-gather.2.cloned.1.call-start = ((), (), s32[]{:S(2)}) async-start(), calls=%async_computation.1 | async-start | bytes 3538944 | tf_op jit(solution)/shard_map/all_gather | solution.py:277
  7.2 10.6 %collective-permute-start = (bf16[32,1536]{1,0:T(8,128)(2,1)}, bf16[32,1536]{1,0:T(8,128)(2,1)S(1)}, u32[]{:S(2)}, u32[]{:S(2)}) collective-permute-start(bf16[32,1536]{1,0:T(8,128)(2,1)} %refs_0_.1), channel_id=1, source_target_pairs={{4,0},{8,4},{12,8},{0,12},{5,1},{9,5},{13,9},{1,13},{6,2},{10,6},{... | collective-permute-start | bytes 294920 | tf_op jit(solution)/shard_map/ppermute | solution.py:24
  10.3 7.5 %collective-permute-start.1 = (bf16[32,1536]{1,0:T(8,128)(2,1)}, bf16[32,1536]{1,0:T(8,128)(2,1)S(1)}, u32[]{:S(2)}, u32[]{:S(2)}) collective-permute-start(bf16[32,1536]{1,0:T(8,128)(2,1)} %refs_0_.1), channel_id=1, source_target_pairs={{8,0},{12,4},{0,8},{4,12},{9,1},{13,5},{1,9},{5,13},{10,2},{14,6},... | collective-permute-start | bytes 294920 | tf_op jit(solution)/shard_map/ppermute | solution.py:24
  10.9 7.4 %collective-permute-start.2 = (bf16[32,1536]{1,0:T(8,128)(2,1)}, bf16[32,1536]{1,0:T(8,128)(2,1)S(1)}, u32[]{:S(2)}, u32[]{:S(2)}) collective-permute-start(bf16[32,1536]{1,0:T(8,128)(2,1)} %refs_0_.1), channel_id=1, source_target_pairs={{12,0},{0,4},{4,8},{8,12},{13,1},{1,5},{5,9},{9,13},{14,2},{2,6},{... | collective-permute-start | bytes 294920 | tf_op jit(solution)/shard_map/ppermute | solution.py:24
  11.9 8.4 %collective-permute-start.3 = (bf16[32,1536]{1,0:T(8,128)(2,1)}, bf16[32,1536]{1,0:T(8,128)(2,1)S(1)}, u32[]{:S(2)}, u32[]{:S(2)}) collective-permute-start(bf16[32,1536]{1,0:T(8,128)(2,1)} %refs_0_.2), channel_id=1, source_target_pairs={{16,0},{32,16},{48,32},{64,48},{80,64},{96,80},{112,96},{0,112},{1... | collective-permute-start | bytes 294920 | tf_op jit(solution)/shard_map/ppermute | solution.py:24
  22.0 29.8 %copy-start.11 = (bf16[256,512]{1,0:T(8,128)(2,1)S(1)}, bf16[256,512]{1,0:T(8,128)(2,1)}, u32[]{:S(2)}) copy-start(bf16[256,512]{1,0:T(8,128)(2,1)} %param.10) | copy-start | bytes 786436
  22.0 122.4 %reduce-scatter.2.cloned.1.call-start = ((), (), s32[]{:S(2)}) async-start(), calls=%async_computation.2 | async-start | bytes 3538944 | tf_op jit(solution)/shard_map/reduce_scatter | solution.py:304
  22.0 20.2 %collective-permute-start.4 = (bf16[256,512]{1,0:T(8,128)(2,1)}, bf16[256,512]{1,0:T(8,128)(2,1)S(1)}, u32[]{:S(2)}, u32[]{:S(2)}) collective-permute-start(bf16[256,512]{1,0:T(8,128)(2,1)} %param.9), channel_id=1, source_target_pairs={{0,2},{2,0},{1,3},{3,1},{4,6},{6,4},{5,7},{7,5},{8,10},{10,8},{9,1... | collective-permute-start | bytes 786440 | tf_op jit(solution)/shard_map/ppermute | solution.py:28
  24.3 6.8 %collective-permute-start.10 = (bf16[32,1536]{1,0:T(8,128)(2,1)}, bf16[32,1536]{1,0:T(8,128)(2,1)S(1)}, u32[]{:S(2)}, u32[]{:S(2)}) collective-permute-start(bf16[32,1536]{1,0:T(8,128)(2,1)} %refs_0_.2), channel_id=1, source_target_pairs={{112,0},{0,16},{16,32},{32,48},{48,64},{64,80},{80,96},{96,112},{1... | collective-permute-start | bytes 294920 | tf_op jit(solution)/shard_map/ppermute | solution.py:24
  24.3 6.7 %collective-permute-start.7 = (bf16[32,1536]{1,0:T(8,128)(2,1)S(1)}, bf16[32,1536]{1,0:T(8,128)(2,1)S(1)}, u32[]{:S(2)}, u32[]{:S(2)}) collective-permute-start(bf16[32,1536]{1,0:T(8,128)(2,1)S(1)} %collective-permute-done.3.refs_1_), channel_id=1, source_target_pairs={{16,0},{32,16},{48,32},{64,48},{80,64},{96,80},{112,96},{0,112},{1... | collective-permute-start | bytes 294920 | tf_op jit(solution)/shard_map/ppermute | solution.py:24
  31.0 8.0 %collective-permute-start.11 = (bf16[32,1536]{1,0:T(8,128)(2,1)S(1)}, bf16[32,1536]{1,0:T(8,128)(2,1)S(1)}, u32[]{:S(2)}, u32[]{:S(2)}) collective-permute-start(bf16[32,1536]{1,0:T(8,128)(2,1)S(1)} %collective-permute-done.10.refs_7_), channel_id=1, source_target_pairs={{112,0},{0,16},{16,32},{32,48},{48,64},{64,80},{80,96},{96,112},{1... | collective-permute-start | bytes 294920 | tf_op jit(solution)/shard_map/ppermute | solution.py:24
  31.0 8.0 %collective-permute-start.8 = (bf16[32,1536]{1,0:T(8,128)(2,1)S(1)}, bf16[32,1536]{1,0:T(8,128)(2,1)S(1)}, u32[]{:S(2)}, u32[]{:S(2)}) collective-permute-start(bf16[32,1536]{1,0:T(8,128)(2,1)S(1)} %collective-permute-done.7.refs_2_), channel_id=1, source_target_pairs={{16,0},{32,16},{48,32},{64,48},{80,64},{96,80},{112,96},{0,112},{1... | collective-permute-start | bytes 294920 | tf_op jit(solution)/shard_map/ppermute | solution.py:24
  34.3 17.5 %collective-permute-start.5 = (bf16[256,512]{1,0:T(8,128)(2,1)}, bf16[256,512]{1,0:T(8,128)(2,1)S(1)}, u32[]{:S(2)}, u32[]{:S(2)}) collective-permute-start(bf16[256,512]{1,0:T(8,128)(2,1)} %param.10), channel_id=1, source_target_pairs={{0,2},{2,0},{1,3},{3,1},{4,6},{6,4},{5,7},{7,5},{8,10},{10,8},{9,1... | collective-permute-start | bytes 786440 | tf_op jit(solution)/shard_map/ppermute | solution.py:28
  39.0 7.9 %collective-permute-start.12 = (bf16[32,1536]{1,0:T(8,128)(2,1)S(1)}, bf16[32,1536]{1,0:T(8,128)(2,1)S(1)}, u32[]{:S(2)}, u32[]{:S(2)}) collective-permute-start(bf16[32,1536]{1,0:T(8,128)(2,1)S(1)} %collective-permute-done.11.refs_6_), channel_id=1, source_target_pairs={{112,0},{0,16},{16,32},{32,48},{48,64},{64,80},{80,96},{96,112},{1... | collective-permute-start | bytes 294920 | tf_op jit(solution)/shard_map/ppermute | solution.py:24
  39.0 7.9 %collective-permute-start.9 = (bf16[32,1536]{1,0:T(8,128)(2,1)S(1)}, bf16[32,1536]{1,0:T(8,128)(2,1)S(1)}, u32[]{:S(2)}, u32[]{:S(2)}) collective-permute-start(bf16[32,1536]{1,0:T(8,128)(2,1)S(1)} %collective-permute-done.8.refs_3_), channel_id=1, source_target_pairs={{16,0},{32,16},{48,32},{64,48},{80,64},{96,80},{112,96},{0,112},{1... | collective-permute-start | bytes 294920 | tf_op jit(solution)/shard_map/ppermute | solution.py:24
  47.8 29.5 %copy-start = (bf16[8,32,1536]{2,1,0:T(8,128)(2,1)}, bf16[8,32,1536]{2,1,0:T(8,128)(2,1)S(1)}, u32[]{:S(2)}) copy-start(bf16[8,32,1536]{2,1,0:T(8,128)(2,1)S(1)} %shard_map.103) | copy-start | bytes 2359300
  47.9 14.2 %collective-permute-start.13 = (bf16[256,1536]{1,0:T(8,128)(2,1)S(1)}, bf16[256,1536]{1,0:T(8,128)(2,1)S(1)}, u32[]{:S(2)}, u32[]{:S(2)}) collective-permute-start(bf16[256,1536]{1,0:T(8,128)(2,1)S(1)} %bitcast.23), channel_id=1, source_target_pairs={{0,128},{128,0},{1,129},{129,1},{2,130},{130,2},{3,131},{131,3},{4... | collective-permute-start | bytes 2359304 | tf_op jit(solution)/shard_map/ppermute | solution.py:28
  49.1 14.1 %collective-permute-start.14 = (bf16[256,1536]{1,0:T(8,128)(2,1)S(1)}, bf16[256,1536]{1,0:T(8,128)(2,1)S(1)}, u32[]{:S(2)}, u32[]{:S(2)}) collective-permute-start(bf16[256,1536]{1,0:T(8,128)(2,1)S(1)} %bitcast.24), channel_id=1, source_target_pairs={{4,0},{8,4},{12,8},{0,12},{5,1},{9,5},{13,9},{1,13},{6,2},{10,6},{... | collective-permute-start | bytes 2359304 | tf_op jit(solution)/shard_map/ppermute | solution.py:24
  51.7 13.3 %collective-permute-start.15 = (bf16[256,1536]{1,0:T(8,128)(2,1)S(1)}, bf16[256,1536]{1,0:T(8,128)(2,1)}, u32[]{:S(2)}, u32[]{:S(2)}) collective-permute-start(bf16[256,1536]{1,0:T(8,128)(2,1)S(1)} %bitcast.25), channel_id=1, source_target_pairs={{12,0},{0,4},{4,8},{8,12},{13,1},{1,5},{5,9},{9,13},{14,2},{2,6},{... | collective-permute-start | bytes 2359304 | tf_op jit(solution)/shard_map/ppermute | solution.py:24
  52.2 2.2 %collective-permute-start.6 = (bf16[2,256,512]{2,1,0:T(8,128)(2,1)S(1)}, bf16[2,256,512]{2,1,0:T(8,128)(2,1)S(1)}, u32[]{:S(2)}, u32[]{:S(2)}) collective-permute-start(bf16[2,256,512]{2,1,0:T(8,128)(2,1)S(1)} %fusion.4.hidden), channel_id=1, source_target_pairs={{0,1},{1,0},{2,3},{3,2},{4,5},{5,4},{6,7},{7,6},{8,9},{9,8},{10,11... | collective-permute-start | bytes 1572872 | tf_op jit(solution)/shard_map/ppermute | solution.py:28
  62.1 1.1 copy-start.9
  63.2 0.9 copy-start.10
  73.4 2.0 %collective-permute-start.16 = (bf16[2,256,512]{2,1,0:T(8,128)(2,1)S(1)}, bf16[2,256,512]{2,1,0:T(8,128)(2,1)S(1)}, u32[]{:S(2)}, u32[]{:S(2)}) collective-permute-start(bf16[2,256,512]{2,1,0:T(8,128)(2,1)S(1)} %get-tuple-element.57), channel_id=1, source_target_pairs={{0,1},{1,0},{2,3},{3,2},{4,5},{5,4},{6,7},{7,6},{8,9},{9,8},{10,11... | collective-permute-start | bytes 1572872 | tf_op jit(solution)/shard_map/ppermute | solution.py:28
  75.6 15.6 %collective-permute-start.17 = (bf16[2,256,512]{2,1,0:T(8,128)(2,1)S(1)}, bf16[2,256,512]{2,1,0:T(8,128)(2,1)S(1)}, u32[]{:S(2)}, u32[]{:S(2)}) collective-permute-start(bf16[2,256,512]{2,1,0:T(8,128)(2,1)S(1)} %get-tuple-element.96), channel_id=1, source_target_pairs={{0,2},{2,0},{1,3},{3,1},{4,6},{6,4},{5,7},{7,5},{8,10},{10,8},{9,1... | collective-permute-start | bytes 1572872 | tf_op jit(solution)/shard_map/ppermute | solution.py:28
  77.4 22.6 %collective-permute-start.20 = (bf16[256,1536]{1,0:T(8,128)(2,1)S(1)}, bf16[256,1536]{1,0:T(8,128)(2,1)}, u32[]{:S(2)}, u32[]{:S(2)}) collective-permute-start(bf16[256,1536]{1,0:T(8,128)(2,1)S(1)} %bitcast.26), channel_id=1, source_target_pairs={{8,0},{12,4},{0,8},{4,12},{9,1},{13,5},{1,9},{5,13},{10,2},{14,6},... | collective-permute-start | bytes 2359304 | tf_op jit(solution)/shard_map/ppermute | solution.py:24
  79.4 15.1 %copy-start.2 = (bf16[1536,512]{1,0:T(8,128)(2,1)S(1)}, bf16[1536,512]{1,0:T(8,128)(2,1)}, u32[]{:S(2)}) copy-start(bf16[1536,512]{1,0:T(8,128)(2,1)} %w_up.1) | copy-start | bytes 4718596
  84.5 15.5 %copy-start.3 = (bf16[64,1536]{1,0:T(8,128)(2,1)}, bf16[64,1536]{1,0:T(8,128)(2,1)S(1)}, u32[]{:S(2)}) copy-start(bf16[64,1536]{1,0:T(8,128)(2,1)S(1)} %get-tuple-element.69.first) | copy-start | bytes 589828
  84.5 10.0 %copy-start.1 = (bf16[1536,512]{1,0:T(8,128)(2,1)S(1)}, bf16[1536,512]{1,0:T(8,128)(2,1)}, u32[]{:S(2)}) copy-start(bf16[1536,512]{1,0:T(8,128)(2,1)} %w_gate.1) | copy-start | bytes 4718596
  91.8 2.0 %collective-permute-start.18 = (bf16[2,256,512]{2,1,0:T(8,128)(2,1)S(1)}, bf16[2,256,512]{2,1,0:T(8,128)(2,1)S(1)}, u32[]{:S(2)}, u32[]{:S(2)}) collective-permute-start(bf16[2,256,512]{2,1,0:T(8,128)(2,1)S(1)} %get-tuple-element.66.near0.refs_4_), channel_id=1, source_target_pairs={{0,1},{1,0},{2,3},{3,2},{4,5},{5,4},{6,7},{7,6},{8,9},{9,8},{10,11... | collective-permute-start | bytes 1572872 | tf_op jit(solution)/shard_map/ppermute | solution.py:28
  91.9 2.6 %collective-permute-start.19 = (bf16[2,256,512]{2,1,0:T(8,128)(2,1)S(1)}, bf16[2,256,512]{2,1,0:T(8,128)(2,1)S(1)}, u32[]{:S(2)}, u32[]{:S(2)}) collective-permute-start(bf16[2,256,512]{2,1,0:T(8,128)(2,1)S(1)} %get-tuple-element.67.near1.refs_5_), channel_id=1, source_target_pairs={{0,1},{1,0},{2,3},{3,2},{4,5},{5,4},{6,7},{7,6},{8,9},{9,8},{10,11... | collective-permute-start | bytes 1572872 | tf_op jit(solution)/shard_map/ppermute | solution.py:28
  92.4 7.6 %collective-permute-start.21 = (bf16[64,1536]{1,0:T(8,128)(2,1)S(1)}, bf16[64,1536]{1,0:T(8,128)(2,1)S(1)}, u32[]{:S(2)}, u32[]{:S(2)}) collective-permute-start(bf16[64,1536]{1,0:T(8,128)(2,1)S(1)} %get-tuple-element.69.first), channel_id=1, source_target_pairs={{0,128},{128,0},{1,129},{129,1},{2,130},{130,2},{3,131},{131,3},{4... | collective-permute-start | bytes 589832 | tf_op jit(solution)/shard_map/ppermute | solution.py:28
  100.0 0.7 copy-start.5
  100.7 14.0 %collective-permute-start.26 = (bf16[2,256,512]{2,1,0:T(8,128)(2,1)S(1)}, bf16[2,256,512]{2,1,0:T(8,128)(2,1)S(1)}, u32[]{:S(2)}, u32[]{:S(2)}) collective-permute-start(bf16[2,256,512]{2,1,0:T(8,128)(2,1)S(1)} %get-tuple-element.66.near0.refs_4_), channel_id=1, source_target_pairs={{0,128},{128,0},{1,129},{129,1},{2,130},{130,2},{3,131},{131,3},{4... | collective-permute-start | bytes 1572872 | tf_op jit(solution)/shard_map/ppermute | solution.py:28
  101.6 13.7 %collective-permute-start.27 = (bf16[2,256,512]{2,1,0:T(8,128)(2,1)S(1)}, bf16[2,256,512]{2,1,0:T(8,128)(2,1)S(1)}, u32[]{:S(2)}, u32[]{:S(2)}) collective-permute-start(bf16[2,256,512]{2,1,0:T(8,128)(2,1)S(1)} %get-tuple-element.67.near1.refs_5_), channel_id=1, source_target_pairs={{0,130},{130,0},{2,128},{128,2},{1,131},{131,1},{3,129},{129,3},{4... | collective-permute-start | bytes 1572872 | tf_op jit(solution)/shard_map/ppermute | solution.py:306
  102.9 19.2 %collective-permute-start.22 = (bf16[256,1536]{1,0:T(8,128)(2,1)}, bf16[256,1536]{1,0:T(8,128)(2,1)S(1)}, u32[]{:S(2)}, u32[]{:S(2)}) collective-permute-start(bf16[256,1536]{1,0:T(8,128)(2,1)} %copy-done.9), channel_id=1, source_target_pairs={{4,0},{8,4},{12,8},{0,12},{5,1},{9,5},{13,9},{1,13},{6,2},{10,6},{... | collective-permute-start | bytes 2359304 | tf_op jit(solution)/shard_map/ppermute | solution.py:24
  104.9 20.2 %collective-permute-start.23 = (bf16[256,1536]{1,0:T(8,128)(2,1)}, bf16[256,1536]{1,0:T(8,128)(2,1)S(1)}, u32[]{:S(2)}, u32[]{:S(2)}) collective-permute-start(bf16[256,1536]{1,0:T(8,128)(2,1)} %copy-done.9), channel_id=1, source_target_pairs={{12,0},{0,4},{4,8},{8,12},{13,1},{1,5},{5,9},{9,13},{14,2},{2,6},{... | collective-permute-start | bytes 2359304 | tf_op jit(solution)/shard_map/ppermute | solution.py:24
  115.3 34.7 %collective-permute-start.33 = (bf16[448,1536]{1,0:T(8,128)(2,1)}, bf16[448,1536]{1,0:T(8,128)(2,1)}, u32[]{:S(2)}, u32[]{:S(2)}) collective-permute-start(bf16[448,1536]{1,0:T(8,128)(2,1)} %get-tuple-element.95.rest), channel_id=1, source_target_pairs={{0,128},{128,0},{1,129},{129,1},{2,130},{130,2},{3,131},{131,3},{4... | collective-permute-start | bytes 4128776 | tf_op jit(solution)/shard_map/ppermute | solution.py:28
  117.6 10.6 %collective-permute-start.28 = (bf16[2,256,512]{2,1,0:T(8,128)(2,1)S(1)}, bf16[2,256,512]{2,1,0:T(8,128)(2,1)S(1)}, u32[]{:S(2)}, u32[]{:S(2)}) collective-permute-start(bf16[2,256,512]{2,1,0:T(8,128)(2,1)S(1)} %collective-permute-done.26.refs_3_.refs_2_), channel_id=1, source_target_pairs={{0,1},{1,0},{2,3},{3,2},{4,5},{5,4},{6,7},{7,6},{8,9},{9,8},{10,11... | collective-permute-start | bytes 1572872 | tf_op jit(solution)/shard_map/ppermute | solution.py:28
  117.6 10.6 %collective-permute-start.29 = (bf16[2,256,512]{2,1,0:T(8,128)(2,1)S(1)}, bf16[2,256,512]{2,1,0:T(8,128)(2,1)S(1)}, u32[]{:S(2)}, u32[]{:S(2)}) collective-permute-start(bf16[2,256,512]{2,1,0:T(8,128)(2,1)S(1)} %collective-permute-done.27.refs_4_.refs_3_), channel_id=1, source_target_pairs={{0,1},{1,0},{2,3},{3,2},{4,5},{5,4},{6,7},{7,6},{8,9},{9,8},{10,11... | collective-permute-start | bytes 1572872 | tf_op jit(solution)/shard_map/ppermute | solution.py:28
  122.1 3.6 %copy-start.7 = (bf16[256,1536]{1,0:T(8,128)(2,1)}, bf16[256,1536]{1,0:T(8,128)(2,1)S(1)}, u32[]{:S(2)}) copy-start(bf16[256,1536]{1,0:T(8,128)(2,1)S(1)} %collective-permute-done.22.refs_1_) | copy-start | bytes 2359300
  125.1 1.4 copy-start.8
  125.1 10.4 %collective-permute-start.24 = (bf16[128,1536]{1,0:T(8,128)(2,1)S(1)}, bf16[128,1536]{1,0:T(8,128)(2,1)S(1)}, u32[]{:S(2)}, u32[]{:S(2)}) collective-permute-start(bf16[128,1536]{1,0:T(8,128)(2,1)S(1)} %slice.6), channel_id=1, source_target_pairs={{4,0},{8,4},{12,8},{0,12},{5,1},{9,5},{13,9},{1,13},{6,2},{10,6},{... | collective-permute-start | bytes 1179656 | tf_op jit(solution)/shard_map/ppermute | solution.py:24
  126.5 10.9 %collective-permute-start.25 = (bf16[128,1536]{1,0:T(8,128)(2,1)}, bf16[128,1536]{1,0:T(8,128)(2,1)S(1)}, u32[]{:S(2)}, u32[]{:S(2)}) collective-permute-start(bf16[128,1536]{1,0:T(8,128)(2,1)} %slice.7), channel_id=1, source_target_pairs={{12,0},{0,4},{4,8},{8,12},{13,1},{1,5},{5,9},{9,13},{14,2},{2,6},{... | collective-permute-start | bytes 1179656 | tf_op jit(solution)/shard_map/ppermute | solution.py:24
  137.4 12.6 %copy-start.4 = (bf16[64,1536]{1,0:T(8,128)(2,1)S(1)}, bf16[64,1536]{1,0:T(8,128)(2,1)}, u32[]{:S(2)}) copy-start(bf16[64,1536]{1,0:T(8,128)(2,1)} %copy-done.3) | copy-start | bytes 589828
  137.4 12.6 %copy-start.6 = (bf16[64,1536]{1,0:T(8,128)(2,1)S(1)}, bf16[64,1536]{1,0:T(8,128)(2,1)}, u32[]{:S(2)}) copy-start(bf16[64,1536]{1,0:T(8,128)(2,1)} %copy-done.5) | copy-start | bytes 589828
  145.4 8.4 %collective-permute-start.32 = (bf16[32,1536]{1,0:T(8,128)(2,1)S(1)}, bf16[32,1536]{1,0:T(8,128)(2,1)S(1)}, u32[]{:S(2)}, u32[]{:S(2)}) collective-permute-start(bf16[32,1536]{1,0:T(8,128)(2,1)S(1)} %get-tuple-element.91), channel_id=1, source_target_pairs={{4,0},{8,4},{12,8},{0,12},{5,1},{9,5},{13,9},{1,13},{6,2},{10,6},{... | collective-permute-start | bytes 294920 | tf_op jit(solution)/shard_map/ppermute | solution.py:24
  148.4 6.2 %collective-permute-start.31 = (bf16[32,1536]{1,0:T(8,128)(2,1)S(1)}, bf16[32,1536]{1,0:T(8,128)(2,1)S(1)}, u32[]{:S(2)}, u32[]{:S(2)}) collective-permute-start(bf16[32,1536]{1,0:T(8,128)(2,1)S(1)} %get-tuple-element.90), channel_id=1, source_target_pairs={{8,0},{12,4},{0,8},{4,12},{9,1},{13,5},{1,9},{5,13},{10,2},{14,6},... | collective-permute-start | bytes 294920 | tf_op jit(solution)/shard_map/ppermute | solution.py:24
  149.2 6.4 %collective-permute-start.30 = (bf16[32,1536]{1,0:T(8,128)(2,1)S(1)}, bf16[32,1536]{1,0:T(8,128)(2,1)S(1)}, u32[]{:S(2)}, u32[]{:S(2)}) collective-permute-start(bf16[32,1536]{1,0:T(8,128)(2,1)S(1)} %get-tuple-element.89), channel_id=1, source_target_pairs={{12,0},{0,4},{4,8},{8,12},{13,1},{1,5},{5,9},{9,13},{14,2},{2,6},{... | collective-permute-start | bytes 294920 | tf_op jit(solution)/shard_map/ppermute | solution.py:24
Sparse Core Ops, SparseCore 0:
  22.1 46.6 all-gather.1
  100.2 44.1 reduce-scatter.1
